TPU v7x, 32 devices: a whole 2x2x4 slice. The times are simulated.
32 devices in a mesh: subj: 8 (over z, y), vox: 4 (over x, core).
Axes of the slice: x: 2, y: 2, z: 4, core: 2. Of those that a mesh axis runs over, the one named last changes fastest.
Arguments:
- scans: bfloat16 [5120, 49152], P('subj', 'vox'), may hold values from -6 to 6
- test_matrix: bfloat16 [49152, 128], P('vox'), may hold values from -6 to 6
- lengths: int32 [8], replicated, may hold values from 160 to 640, as said below
- block_subject: int32 [8], replicated, may hold values from 0 to 7, each once
Outputs:
- basis: float32 [49152, 128], P('vox')
Inputs may be any that keep to these rules, and one draw needn't show every extreme that they name: `lengths`: one subject has exactly 640 rows and one exactly 160. `block_subject`: each subject appears once.
All inputs are finite; a program needn't handle non-finite values.
Results may differ from a plain program's by a relative error of at most 0.0046.
Values may be sent and summed in bfloat16 or wider, within the bound.
No kernel may reach another device: no remote copies, remote signals or barrier semaphores. Data moves between devices by JAX's collectives and lax.ppermute only.
A program may use at most 128 MiB of HBM per device.

v0:
```python
import functools

import jax
import jax.numpy as jnp
from jax import lax
from jax.experimental import pallas as pl
from jax.experimental.pallas import tpu as pltpu
from jax.sharding import PartitionSpec as P

F32 = jnp.float32
BF16 = jnp.bfloat16
I16 = jnp.int16
HIGHEST = lax.Precision.HIGHEST
STEPS = 64.0
LOW = 2
GROUP = 8
VMEM_BYTES = 48 << 20
WHOLE = pl.BlockSpec(memory_space=pltpu.VMEM)


def exchange(value, axis, size, mask):
    return lax.ppermute(value, axis, [(i, i ^ mask) for i in range(size)])


def butterfly(value, axis, size):
    mask = 1
    while 2 * mask < size:
        value = value + exchange(value, axis, size, mask)
        mask *= 2
    return value, exchange(value, axis, size, mask)


class Plain:
    pad = 0
    dtype = BF16

    @staticmethod
    def encode(value):
        return value.astype(BF16)

    @staticmethod
    def decode(sent):
        return sent.astype(F32)


class Fixed:
    pad = 16
    dtype = I16

    @staticmethod
    def encode(value):
        top = jnp.maximum(jnp.max(jnp.abs(value), axis=0, keepdims=True), 1e-30)
        power = jnp.ceil(jnp.log2(top * (1.0 / 32000.0)) * STEPS)
        codes = jnp.round(value * jnp.exp2(power * (-1.0 / STEPS)))
        codes = jnp.clip(codes, -32767.0, 32767.0)
        rows = jnp.broadcast_to(power, (Fixed.pad, value.shape[1]))
        return jnp.concatenate([codes, rows]).astype(jnp.int32).astype(I16)

    @staticmethod
    def decode(sent):
        wide = sent.astype(jnp.int32).astype(F32)
        rows = wide.shape[0] - Fixed.pad
        return wide[:rows] * jnp.exp2(wide[rows : rows + 1] * (1.0 / STEPS))


def params():
    return pltpu.CompilerParams(vmem_limit_bytes=VMEM_BYTES)


def sketch_kernel(code, count, pos_ref, scores_ref, *refs):
    for u in range(count):
        product = lax.dot_general(
            scores_ref[...], refs[u][...], (((0,), (0,)), ((), ())), preferred_element_type=F32
        )
        out = refs[count + u] if len(refs) == 2 * count else refs[count].at[u]
        out[...] = code.encode(product.T)


def unit_of(high, j, k, pos):
    if j is None:
        return LOW * high + (pos[1] ^ k)
    return (pos[0] ^ j) * high + (pos[1] ^ k)


def sketch_part(scans, scores, pos, high, j, ks, code, apart, per_step):
    time_rows, voxels = scans.shape
    rank = scores.shape[1]
    n = voxels // ((LOW + 1) * high)
    rows = n + code.pad
    first = ks[0]
    steps = len(ks) // per_step

    def column(u):
        return lambda g, pos: (0, unit_of(high, j, first + g * per_step + u, pos))

    if apart:
        out_shape = [jax.ShapeDtypeStruct((rows, rank), code.dtype)] * len(ks)
        out_specs = [pl.BlockSpec((rows, rank), lambda g, pos: (0, 0))] * len(ks)
    else:
        out_shape = jax.ShapeDtypeStruct((len(ks), rows, rank), code.dtype)
        out_specs = pl.BlockSpec((per_step, rows, rank), lambda g, pos: (g, 0, 0))
    return pl.pallas_call(
        functools.partial(sketch_kernel, code, per_step),
        out_shape=out_shape,
        grid_spec=pltpu.PrefetchScalarGridSpec(
            num_scalar_prefetch=1,
            grid=(steps,),
            in_specs=[pl.BlockSpec((time_rows, rank), lambda g, pos: (0, 0))]
            + [pl.BlockSpec((time_rows, n), column(u)) for u in range(per_step)],
            out_specs=out_specs,
        ),
        compiler_params=params(),
        cost_estimate=pl.CostEstimate(
            flops=2 * time_rows * n * rank * len(ks),
            bytes_accessed=time_rows * n * 2 * len(ks),
            transcendentals=0,
        ),
    )(pos, scores, *([scans] * per_step))


def small_call(kernel, out_shape, *args):
    return pl.pallas_call(
        kernel,
        out_shape=out_shape,
        in_specs=[WHOLE] * len(args),
        out_specs=jax.tree.map(lambda _: WHOLE, out_shape),
        compiler_params=params(),
    )(*args)


def add_pieces_kernel(code, count, own_ref, got_ref, *outs):
    for k in range(count):
        outs[k][...] = code.encode(code.decode(own_ref[k]) + code.decode(got_ref[k]))


def add_all_kernel(code, with_gram, *refs):
    outs = refs[-2:] if with_gram else refs[-1:]
    parts = refs[: len(refs) - len(outs)]
    total = code.decode(parts[0][...])
    for part in parts[1:]:
        total = total + code.decode(part[...])
    outs[0][...] = code.encode(total)
    if with_gram:
        outs[1][...] = lax.dot_general(
            total, total, (((0,), (0,)), ((), ())), precision=HIGHEST,
            preferred_element_type=F32,
        )


def add_halves_kernel(code, pos_ref, *refs):
    parts, (keep_ref, send_ref) = refs[:-2], refs[-2:]
    total = code.decode(parts[0][...])
    for part in parts[1:]:
        total = total + code.decode(part[...])
    half = total.shape[0] // 2
    lower = pos_ref[0] == 0
    keep_ref[...] = code.encode(jnp.where(lower, total[:half], total[half:]))
    send_ref[...] = code.encode(jnp.where(lower, total[half:], total[:half]))


def add_all(code, with_gram, parts):
    rank = parts[0].shape[1]
    out = [jax.ShapeDtypeStruct(parts[0].shape, code.dtype)]
    if with_gram:
        out.append(jax.ShapeDtypeStruct((rank, rank), F32))
    return small_call(functools.partial(add_all_kernel, code, with_gram), out, *parts)


def project_kernel(has_base, with_own, count, pos_ref, *refs):
    refs = list(refs)
    base = refs.pop(0) if has_base else None
    out = refs.pop()
    scans, pieces = refs[:count], refs[count:]
    time_rows = scans[0].shape[0]
    rank = out.shape[1]
    total = jnp.zeros((time_rows, rank), F32)
    gram = jnp.zeros((rank, rank), F32)
    for u in range(count):
        piece = pieces[u][...] if len(pieces) == count else pieces[0][u]
        total += jnp.dot(scans[u][...], piece, preferred_element_type=F32)
        gram += lax.dot_general(
            piece, piece, (((0,), (0,)), ((), ())), preferred_element_type=F32
        )
    if has_base:
        out[:time_rows] = base[:time_rows] + total
        out[time_rows:] = base[time_rows:] + gram
    else:
        out[:time_rows] = total
        out[time_rows:] = gram


def project(scans, pieces, pos, high, j, base=None):
    time_rows, voxels = scans.shape
    n = voxels // ((LOW + 1) * high)
    rank = pieces[0].shape[-1]

    def column(u):
        return lambda g, pos: (0, unit_of(high, j, u, pos))

    full = lambda shape: pl.BlockSpec(shape, lambda g, pos: (0,) * len(shape))
    bases = [] if base is None else [base]
    return pl.pallas_call(
        functools.partial(project_kernel, base is not None, True, high),
        out_shape=jax.ShapeDtypeStruct((time_rows + rank, rank), F32),
        grid_spec=pltpu.PrefetchScalarGridSpec(
            num_scalar_prefetch=1,
            grid=(1,),
            in_specs=[full(b.shape) for b in bases]
            + [pl.BlockSpec((time_rows, n), column(u)) for u in range(high)]
            + [full(p.shape) for p in pieces],
            out_specs=full((time_rows + rank, rank)),
        ),
        compiler_params=params(),
        cost_estimate=pl.CostEstimate(
            flops=2 * (time_rows + rank) * n * rank * high,
            bytes_accessed=time_rows * n * 2 * high,
            transcendentals=0,
        ),
    )(pos, *bases, *([scans] * high), *pieces)


def finish_kernel(high, n, pos_ref, inverse_ref, *refs):
    refs, (out, held, sems) = refs[:-3], refs[-3:]
    first, low_got, second = refs[:high], refs[high], refs[high + 1 :]
    copies = []

    def emit(slot, codes, unit, offset, rows):
        scaled = Fixed.decode(codes)
        value = times_transpose(scaled, inverse_ref[...])
        held[slot, offset : offset + rows] = value
        start = pl.multiple_of(unit * n, n)
        if offset + rows == n:
            copy = pltpu.make_async_copy(held.at[slot], out.at[pl.ds(start, n)], sems.at[slot])
            copy.start()
            copies.append(copy)

    pos = (pos_ref[0], pos_ref[1])
    for k in range(high):
        emit(k, first[k][...], unit_of(high, 0, k, pos), 0, n)
    for k in range(high):
        emit(high + k, low_got[k], unit_of(high, 1, k, pos), 0, n)
    half = n // 2
    for k in range(high):
        for side in range(2):
            codes = second[k][side]
            emit(2 * high + k, codes, unit_of(high, None, k, pos), side * half, half)
    for copy in copies:
        copy.wait()


def finish(first, low_got, second, inverse, pos, high, n):
    rank = inverse.shape[0]
    units = (LOW + 1) * high
    args = [inverse, *first, low_got, *second]
    return pl.pallas_call(
        functools.partial(finish_kernel, high, n),
        out_shape=jax.ShapeDtypeStruct((units * n, rank), F32),
        in_specs=[pl.BlockSpec(memory_space=pltpu.SMEM)] + [WHOLE] * len(args),
        out_specs=pl.BlockSpec(memory_space=pl.ANY),
        scratch_shapes=[
            pltpu.VMEM((units, n, rank), F32),
            pltpu.SemaphoreType.DMA((units,)),
        ],
        compiler_params=params(),
    )(pos, *args)


def inverse_factor(gram):
    size = gram.shape[0]
    groups = size // GROUP
    shape = (GROUP, size)
    sub = lax.broadcasted_iota(jnp.int32, shape, 0)
    lane = lax.broadcasted_iota(jnp.int32, shape, 1)
    left = [gram[GROUP * i : GROUP * (i + 1)] for i in range(groups)]
    right = [jnp.where(sub + GROUP * i == lane, 1.0, 0.0).astype(F32) for i in range(groups)]
    for g in range(groups):
        first = g * GROUP
        wide = lambda value: jnp.broadcast_to(value, shape)
        rows = [wide(left[g][t : t + 1]) for t in range(GROUP)]
        inverse_rows = [wide(right[g][t : t + 1]) for t in range(GROUP)]
        block = [
            [wide(left[g][t : t + 1, first + u : first + u + 1]) for u in range(GROUP)]
            for t in range(GROUP)
        ]
        below = range(g + 1, groups)
        columns = {
            i: [wide(left[i][:, first + u : first + u + 1]) for u in range(GROUP)] for i in below
        }
        scaled = []
        for t in range(GROUP):
            pivot = 1.0 / block[t][t]
            scaled.append((rows[t] * pivot, inverse_rows[t] * pivot))
            for u in range(t + 1, GROUP):
                factor = block[t][u] * pivot
                for w in range(u, GROUP):
                    block[u][w] = block[u][w] - factor * block[t][w]
                rows[u] = rows[u] - factor * rows[t]
                inverse_rows[u] = inverse_rows[u] - factor * inverse_rows[t]
                for i in below:
                    columns[i][u] = columns[i][u] - factor * columns[i][t]
        for i in below:
            for t in range(GROUP):
                left[i] = left[i] - columns[i][t] * scaled[t][0]
                right[i] = right[i] - columns[i][t] * scaled[t][1]
        for t in range(GROUP):
            left[g] = jnp.where(sub == t, rows[t], left[g])
            right[g] = jnp.where(sub == t, inverse_rows[t], right[g])
    out = []
    for g in range(groups):
        pivots = jnp.sum(
            jnp.where(sub + GROUP * g == lane, left[g], 0.0), axis=1, keepdims=True
        )
        out.append(right[g] * lax.rsqrt(pivots))
    return jnp.concatenate(out)


def times_transpose(value, inverse):
    return lax.dot_general(
        value, inverse, (((1,), (1,)), ((), ())), precision=HIGHEST, preferred_element_type=F32
    )


def normalise_kernel(all_voxels, length_ref, mine_ref, got_ref, out_ref):
    time_rows = out_ref.shape[0]
    both = mine_ref[...] + got_ref[...]
    inverse = inverse_factor(both[time_rows:] * (1.0 / all_voxels))
    scores = times_transpose(both[:time_rows], inverse)
    live = lax.broadcasted_iota(jnp.int32, scores.shape, 0) < length_ref[0]
    out_ref[...] = jnp.where(live, scores, 0.0).astype(BF16)


def invert_kernel(all_voxels, mine_ref, got_ref, out_ref):
    out_ref[...] = inverse_factor((mine_ref[...] + got_ref[...]) * (1.0 / all_voxels))


def make(mesh):
    subjects, blocks = mesh.shape["subj"], mesh.shape["vox"]
    high = subjects // LOW
    swap = functools.partial(exchange, axis="subj", size=subjects)

    def on_device(scans, test_matrix, lengths, block_subject):
        time_rows, voxels = scans.shape
        rank = test_matrix.shape[1]
        all_voxels = voxels * blocks
        n = voxels // ((LOW + 1) * high)
        me = lax.axis_index("subj")
        pos = jnp.stack([me % LOW, me // LOW]).astype(jnp.int32)
        slot_ids = jnp.arange(block_subject.shape[0], dtype=jnp.int32)
        subject = jnp.sum(jnp.where(slot_ids == me, block_subject, 0))
        length = jnp.sum(jnp.where(slot_ids == subject, lengths, 0))
        live_rows = (jnp.arange(time_rows, dtype=jnp.int32) < length)[:, None]

        def sketch_sum(scores, code, with_gram):
            rows = n + code.pad
            part = functools.partial(sketch_part, scans, scores, pos, high)
            ks = list(range(high))
            away = part(1, ks, code, False, high // 2)
            got_away = swap(away, mask=1)
            second = part(None, ks[1:], code, True, high - 1)
            got_second = [swap(second[k - 1], mask=k * LOW) for k in ks[1:]]
            got_away, *got_second = lax.optimization_barrier((got_away, *got_second))
            home = part(0, ks, code, False, high // 2)
            (second_own,) = part(None, ks[:1], code, True, 1)
            piece = jax.ShapeDtypeStruct((rows, rank), code.dtype)
            half = jax.ShapeDtypeStruct((n // 2 + code.pad, rank), code.dtype)
            first = small_call(
                functools.partial(add_pieces_kernel, code, high), [piece] * high, home, got_away
            )
            got_first = [swap(first[k], mask=k * LOW) for k in ks[1:]]
            keep, send = pl.pallas_call(
                functools.partial(add_halves_kernel, code),
                out_shape=[half, half],
                in_specs=[pl.BlockSpec(memory_space=pltpu.SMEM)] + [WHOLE] * high,
                out_specs=[WHOLE, WHOLE],
                compiler_params=params(),
            )(pos, second_own, *got_second)
            got_send = swap(send, mask=1)
            return (
                add_all(code, with_gram, [first[0], *got_first]),
                add_all(code, with_gram, [keep, got_send]),
            )

        def gather(first, second, *others):
            ks = list(range(1, high))
            firsts = [first] + [swap(first, mask=k * LOW) for k in ks]
            got = swap(second, mask=1)
            lower = pos[0] == 0
            pair = jnp.stack([jnp.where(lower, second, got), jnp.where(lower, got, second)])
            firsts, pair, others = lax.optimization_barrier((firsts, pair, others))
            low_got = swap(jnp.stack(firsts), mask=1)
            seconds = [pair] + [swap(pair, mask=k * LOW) for k in ks]
            return firsts, low_got, seconds, others

        partial = jnp.dot(scans, test_matrix, preferred_element_type=F32)
        summed = sum(butterfly(partial, "vox", blocks))
        scores = jnp.where(live_rows, summed, 0.0).astype(BF16)

        (first,), (second,) = sketch_sum(scores, Plain, False)
        firsts, low_got, seconds, _ = gather(first, second)
        both = project(scans, firsts, pos, high, 0)
        seconds = [part.reshape(n, rank) for part in seconds]
        both = project(scans, seconds, pos, high, None, both)
        both = project(scans, [low_got], pos, high, 1, both)
        mine, got = butterfly(both, "vox", blocks)
        scores = pl.pallas_call(
            functools.partial(normalise_kernel, all_voxels),
            out_shape=jax.ShapeDtypeStruct((time_rows, rank), BF16),
            in_specs=[pl.BlockSpec(memory_space=pltpu.SMEM), WHOLE, WHOLE],
            out_specs=WHOLE,
            compiler_params=params(),
        )(length[None], mine, got)

        (first, gram_first), (second, gram_second) = sketch_sum(scores, Fixed, True)
        gram = sum(butterfly(gram_first + gram_second, "vox", blocks))
        mine, got = butterfly(gram, "subj", subjects)
        inverse = small_call(
            functools.partial(invert_kernel, all_voxels),
            jax.ShapeDtypeStruct((rank, rank), F32), mine, got,
        )
        firsts, low_got, seconds, (inverse,) = gather(first, second, inverse)
        return finish(firsts, low_got, seconds, inverse, pos, high, n)

    return on_device


def solution(mesh):
    placed = (P("subj", "vox"), P("vox", None), P(), P())
    return jax.shard_map(
        make(mesh), mesh=mesh, in_specs=placed, out_specs=P("vox", None), check_vma=False
    )
```

profile of v0, /device:TPU:0, one launch (start us, length us, event | category | flops | bytes accessed | tf_op | source)
XLA Modules:
  0.0 292.2 jit_solution(15295216776672092377)
XLA Ops:
  1.9 7.7 %fusion.2 = f32[640,128]{1,0:T(8,128)S(1)} fusion(bf16[640,12288]{1,0:T(8,128)(2,1)} %refs_0_.17, bf16[12288,128]{1,0:T(8,128)(2,1)S(1)} %copy-done), kind=kOutput, calls=%fused_computation.15 | convolution fusion | flops 2013265920 | bytes 19202048 | tf_op jit(solution)/shard_map/dot_general | solution.py:394
  17.5 5.9 %collective-permute-done.1 = f32[640,128]{1,0:T(8,128)S(1)} collective-permute-done((f32[640,128]{1,0:T(8,128)S(1)}, f32[640,128]{1,0:T(8,128)S(1)}, u32[]{:S(2)}, u32[]{:S(2)}) %collective-permute-start.1) | collective-permute-done | bytes 327712 | tf_op jit(solution)/shard_map/ppermute | solution.py:22
  44.5 11.3 %collective-permute-done.4.refs_2_ = bf16[1024,128]{1,0:T(8,128)(2,1)S(1)} collective-permute-done((bf16[1024,128]{1,0:T(8,128)(2,1)S(1)}, bf16[1024,128]{1,0:T(8,128)(2,1)S(1)}, u32[]{:S(2)}, u32[]{:S(2)}) %collective-permute-start.4) | collective-permute-done | bytes 262176 | tf_op jit(solution)/shard_map/ppermute | solution.py:22
  64.5 5.3 %collective-permute-done.12.refs_1_ = bf16[512,128]{1,0:T(8,128)(2,1)S(1)} collective-permute-done((bf16[512,128]{1,0:T(8,128)(2,1)S(1)}, bf16[512,128]{1,0:T(8,128)(2,1)S(1)}, u32[]{:S(2)}, u32[]{:S(2)}) %collective-permute-start.12) | collective-permute-done | bytes 131104 | tf_op jit(solution)/shard_map/ppermute | solution.py:22
  70.3 14.3 %collective-permute-done.7.refs_2_ = bf16[1024,128]{1,0:T(8,128)(2,1)} collective-permute-done((bf16[1024,128]{1,0:T(8,128)(2,1)}, bf16[1024,128]{1,0:T(8,128)(2,1)}, u32[]{:S(2)}, u32[]{:S(2)}) %collective-permute-start.7) | collective-permute-done | bytes 262176 | tf_op jit(solution)/shard_map/ppermute | solution.py:22
  91.9 5.0 %collective-permute-done.11.refs_7_ = bf16[1024,128]{1,0:T(8,128)(2,1)S(1)} collective-permute-done((bf16[1024,128]{1,0:T(8,128)(2,1)S(1)}, bf16[1024,128]{1,0:T(8,128)(2,1)S(1)}, u32[]{:S(2)}, u32[]{:S(2)}) %collective-permute-start.11) | collective-permute-done | bytes 262176 | tf_op jit(solution)/shard_map/ppermute | solution.py:22
  96.9 11.9 %collective-permute-done.10.refs_6_ = bf16[1024,128]{1,0:T(8,128)(2,1)S(1)} collective-permute-done((bf16[1024,128]{1,0:T(8,128)(2,1)S(1)}, bf16[1024,128]{1,0:T(8,128)(2,1)S(1)}, u32[]{:S(2)}, u32[]{:S(2)}) %collective-permute-start.10) | collective-permute-done | bytes 262176 | tf_op jit(solution)/shard_map/ppermute | solution.py:22
  113.8 4.9 %shard_map.54.refs_0_ = f32[768,128]{1,0:T(8,128)S(1)} custom-call(s32[2]{0:T(128)S(1)} %pad_add_fusion.2.pos_ref, bf16[640,12288]{1,0:T(8,128)(2,1)} %refs_0_.17, bf16[640,12288]{1,0:T(8,128)(2,1)} %refs_0_.17, bf16[640,12288]{1,0:T(8,128)(2,1)} %refs_0_.17, bf16[640,12288]{1,0:T(8,128)(2,1)} %refs_0_.17, bf16[1024,128]{1,0:T(8,128)(2,1)S(1)} %shard_map.50.refs_4_, ...), custom_call_target="tpu_custom_call" | custom-call | flops 805306368 | bytes 5242880 | tf_op jit(solution)/shard_map/pallas_call | solution.py:202
  120.4 12.0 %collective-permute-done.15 = bf16[2,512,128]{2,1,0:T(8,128)(2,1)S(1)} collective-permute-done((bf16[2,512,128]{2,1,0:T(8,128)(2,1)S(1)}, bf16[2,512,128]{2,1,0:T(8,128)(2,1)S(1)}, u32[]{:S(2)}, u32[]{:S(2)}) %collective-permute-start.15) | collective-permute-done | bytes 262176 | tf_op jit(solution)/shard_map/ppermute | solution.py:22
  132.4 4.9 %shard_map.55.refs_0_ = f32[768,128]{1,0:T(8,128)S(1)} custom-call(s32[2]{0:T(128)S(1)} %pad_add_fusion.2.pos_ref, f32[768,128]{1,0:T(8,128)S(1)} %shard_map.54.refs_0_, bf16[640,12288]{1,0:T(8,128)(2,1)} %refs_0_.17, bf16[640,12288]{1,0:T(8,128)(2,1)} %refs_0_.17, bf16[640,12288]{1,0:T(8,128)(2,1)} %refs_0_.17, bf16[640,12288]{1,0:T(8,128)(2,1)} %refs_0_.17, ...), custom_call_target="tpu_custom_call" | custom-call | flops 805306368 | bytes 5242880 | tf_op jit(solution)/shard_map/pallas_call | solution.py:202
  137.3 4.9 %shard_map.56 = f32[768,128]{1,0:T(8,128)S(1)} custom-call(s32[2]{0:T(128)S(1)} %pad_add_fusion.2.pos_ref, f32[768,128]{1,0:T(8,128)S(1)} %shard_map.55.refs_0_, bf16[640,12288]{1,0:T(8,128)(2,1)} %refs_0_.17, bf16[640,12288]{1,0:T(8,128)(2,1)} %refs_0_.17, bf16[640,12288]{1,0:T(8,128)(2,1)} %refs_0_.17, bf16[640,12288]{1,0:T(8,128)(2,1)} %refs_0_.17, ...), custom_call_target="tpu_custom_call" | custom-call | flops 805306368 | bytes 5242880 | tf_op jit(solution)/shard_map/pallas_call | solution.py:202
  145.7 9.6 %collective-permute-done.19.got_ref = f32[768,128]{1,0:T(8,128)S(1)} collective-permute-done((f32[768,128]{1,0:T(8,128)S(1)}, f32[768,128]{1,0:T(8,128)S(1)}, u32[]{:S(2)}, u32[]{:S(2)}) %collective-permute-start.19) | collective-permute-done | bytes 393248 | tf_op jit(solution)/shard_map/ppermute | solution.py:22
  155.3 5.5 %shard_map.57.scores_ref = bf16[640,128]{1,0:T(8,128)(2,1)S(1)} custom-call(s32[1]{0:T(128)} %bitcast.2.length_ref, f32[768,128]{1,0:T(8,128)S(1)} %add.32.mine_ref, f32[768,128]{1,0:T(8,128)S(1)} %collective-permute-done.19.got_ref), custom_call_target="tpu_custom_call" | custom-call | tf_op jit(solution)/shard_map/pallas_call | solution.py:405
  175.0 4.3 %shard_map.58.own_ref = s16[4,1040,128]{2,1,0:T(8,128)(2,1)S(1)} custom-call(s32[2]{0:T(128)S(1)} %pad_add_fusion.2.pos_ref, bf16[640,128]{1,0:T(8,128)(2,1)S(1)} %shard_map.57.scores_ref, bf16[640,12288]{1,0:T(8,128)(2,1)} %refs_0_.17, bf16[640,12288]{1,0:T(8,128)(2,1)} %refs_0_.17), custom_call_target="tpu_custom_call" | custom-call | flops 671088640 | bytes 5242880 | tf_op jit(solution)/shard_map/pallas_call | solution.py:102
  182.4 9.9 %collective-permute-done.22.refs_2_ = s16[1040,128]{1,0:T(8,128)(2,1)S(1)} collective-permute-done((s16[1040,128]{1,0:T(8,128)(2,1)S(1)}, s16[1040,128]{1,0:T(8,128)(2,1)S(1)}, u32[]{:S(2)}, u32[]{:S(2)}) %collective-permute-start.22) | collective-permute-done | bytes 266272 | tf_op jit(solution)/shard_map/ppermute | solution.py:22
  193.3 4.4 %collective-permute-start.24 = (s16[1040,128]{1,0:T(8,128)(2,1)S(1)}, s16[1040,128]{1,0:T(8,128)(2,1)S(1)}, u32[]{:S(2)}, u32[]{:S(2)}) collective-permute-start(s16[1040,128]{1,0:T(8,128)(2,1)S(1)} %get-tuple-element.69), channel_id=1, source_target_pairs={{0,8},{4,12},{8,0},{12,4},{16,24},{20,28},{24,16},{28,20},{1,9},{5... | collective-permute-start | bytes 798728 | tf_op jit(solution)/shard_map/ppermute | solution.py:22
  204.0 4.6 %collective-permute-done.30.refs_1_ = s16[528,128]{1,0:T(8,128)(2,1)S(1)} collective-permute-done((s16[528,128]{1,0:T(8,128)(2,1)S(1)}, s16[528,128]{1,0:T(8,128)(2,1)S(1)}, u32[]{:S(2)}, u32[]{:S(2)}) %collective-permute-start.30) | collective-permute-done | bytes 135200 | tf_op jit(solution)/shard_map/ppermute | solution.py:22
  209.1 9.5 %collective-permute-done.25.refs_2_ = s16[1040,128]{1,0:T(8,128)(2,1)S(1)} collective-permute-done((s16[1040,128]{1,0:T(8,128)(2,1)S(1)}, s16[1040,128]{1,0:T(8,128)(2,1)S(1)}, u32[]{:S(2)}, u32[]{:S(2)}) %collective-permute-start.25) | collective-permute-done | bytes 266272 | tf_op jit(solution)/shard_map/ppermute | solution.py:22
  233.6 12.0 %collective-permute-done.35 = f32[128,128]{1,0:T(8,128)S(1)} collective-permute-done((f32[128,128]{1,0:T(8,128)S(1)}, f32[128,128]{1,0:T(8,128)S(1)}, u32[]{:S(2)}, u32[]{:S(2)}) %collective-permute-start.35) | collective-permute-done | bytes 65568 | tf_op jit(solution)/shard_map/ppermute | solution.py:22
  248.7 6.4 %collective-permute-done.36.got_ref = f32[128,128]{1,0:T(8,128)S(1)} collective-permute-done((f32[128,128]{1,0:T(8,128)S(1)}, f32[128,128]{1,0:T(8,128)S(1)}, u32[]{:S(2)}, u32[]{:S(2)}) %collective-permute-start.36) | collective-permute-done | bytes 65568 | tf_op jit(solution)/shard_map/ppermute | solution.py:22
  255.1 4.1 %shard_map.66.inverse_ref = f32[128,128]{1,0:T(8,128)S(1)} custom-call(f32[128,128]{1,0:T(8,128)S(1)} %add.37.mine_ref, f32[128,128]{1,0:T(8,128)S(1)} %collective-permute-done.36.got_ref), custom_call_target="tpu_custom_call" | custom-call | tf_op jit(solution)/shard_map/pallas_call | solution.py:122
  264.9 6.9 %collective-permute-done.40.refs_8_ = s16[2,528,128]{2,1,0:T(8,128)(2,1)S(1)} collective-permute-done((s16[2,528,128]{2,1,0:T(8,128)(2,1)S(1)}, s16[2,528,128]{2,1,0:T(8,128)(2,1)S(1)}, u32[]{:S(2)}, u32[]{:S(2)}) %collective-permute-start.40) | collective-permute-done | bytes 270368 | tf_op jit(solution)/shard_map/ppermute | solution.py:22
  271.8 12.7 %collective-permute-done.39.refs_7_ = s16[2,528,128]{2,1,0:T(8,128)(2,1)S(1)} collective-permute-done((s16[2,528,128]{2,1,0:T(8,128)(2,1)S(1)}, s16[2,528,128]{2,1,0:T(8,128)(2,1)S(1)}, u32[]{:S(2)}, u32[]{:S(2)}) %collective-permute-start.39) | collective-permute-done | bytes 270368 | tf_op jit(solution)/shard_map/ppermute | solution.py:22
  284.8 7.2 %shard_map.67 = f32[12288,128]{1,0:T(8,128)} custom-call(s32[2]{0:T(128)S(1)} %pad_add_fusion.2.pos_ref, f32[128,128]{1,0:T(8,128)S(1)} %shard_map.66.inverse_ref, s16[1040,128]{1,0:T(8,128)(2,1)S(1)} %get-tuple-element.82.refs_0_, s16[1040,128]{1,0:T(8,128)(2,1)S(1)} %collective-permute-done.27.refs_1_, ...), custom_call_target="tpu_custom_call" | custom-call | tf_op jit(solution)/shard_map/pallas_call | solution.py:255
  (105 shorter events, 106.6 us)
Async XLA Ops:
  27.4 28.4 %collective-permute-start.2 = (bf16[4,1024,128]{2,1,0:T(8,128)(2,1)S(1)}, bf16[4,1024,128]{2,1,0:T(8,128)(2,1)S(1)}, u32[]{:S(2)}, u32[]{:S(2)}) collective-permute-start(bf16[4,1024,128]{2,1,0:T(8,128)(2,1)S(1)} %shard_map.47), channel_id=1, source_target_pairs={{0,4},{4,0},{8,12},{12,8},{16,20},{20,16},{24,28},{28,24},{1,5},{5... | collective-permute-start | bytes 3145736 | tf_op jit(solution)/shard_map/ppermute | solution.py:22
  34.4 21.4 %collective-permute-start.4 = (bf16[1024,128]{1,0:T(8,128)(2,1)S(1)}, bf16[1024,128]{1,0:T(8,128)(2,1)S(1)}, u32[]{:S(2)}, u32[]{:S(2)}) collective-permute-start(bf16[1024,128]{1,0:T(8,128)(2,1)S(1)} %get-tuple-element.47), channel_id=1, source_target_pairs={{0,16},{4,20},{8,24},{12,28},{16,0},{20,4},{24,8},{28,12},{1,17},{... | collective-permute-start | bytes 786440 | tf_op jit(solution)/shard_map/ppermute | solution.py:22
  37.0 18.8 %collective-permute-start.5 = (bf16[1024,128]{1,0:T(8,128)(2,1)S(1)}, bf16[1024,128]{1,0:T(8,128)(2,1)S(1)}, u32[]{:S(2)}, u32[]{:S(2)}) collective-permute-start(bf16[1024,128]{1,0:T(8,128)(2,1)S(1)} %get-tuple-element.48), channel_id=1, source_target_pairs={{0,24},{4,28},{8,16},{12,20},{16,8},{20,12},{24,0},{28,4},{1,25},{... | collective-permute-start | bytes 786440 | tf_op jit(solution)/shard_map/ppermute | solution.py:22
  60.7 23.9 %collective-permute-start.7 = (bf16[1024,128]{1,0:T(8,128)(2,1)}, bf16[1024,128]{1,0:T(8,128)(2,1)}, u32[]{:S(2)}, u32[]{:S(2)}) collective-permute-start(bf16[1024,128]{1,0:T(8,128)(2,1)} %get-tuple-element.52), channel_id=1, source_target_pairs={{0,16},{4,20},{8,24},{12,28},{16,0},{20,4},{24,8},{28,12},{1,17},{... | collective-permute-start | bytes 786440 | tf_op jit(solution)/shard_map/ppermute | solution.py:22
  61.8 22.9 %collective-permute-start.8 = (bf16[1024,128]{1,0:T(8,128)(2,1)}, bf16[1024,128]{1,0:T(8,128)(2,1)}, u32[]{:S(2)}, u32[]{:S(2)}) collective-permute-start(bf16[1024,128]{1,0:T(8,128)(2,1)} %get-tuple-element.53), channel_id=1, source_target_pairs={{0,24},{4,28},{8,16},{12,20},{16,8},{20,12},{24,0},{28,4},{1,25},{... | collective-permute-start | bytes 786440 | tf_op jit(solution)/shard_map/ppermute | solution.py:22
  69.8 21.2 %collective-permute-start.13 = (bf16[512,128]{1,0:T(8,128)(2,1)S(1)}, bf16[512,128]{1,0:T(8,128)(2,1)}, u32[]{:S(2)}, u32[]{:S(2)}) collective-permute-start(bf16[512,128]{1,0:T(8,128)(2,1)S(1)} %shard_map.53), channel_id=1, source_target_pairs={{0,4},{4,0},{8,12},{12,8},{16,20},{20,16},{24,28},{28,24},{1,5},{5... | collective-permute-start | bytes 393224 | tf_op jit(solution)/shard_map/ppermute | solution.py:22
  87.9 20.8 %collective-permute-start.10 = (bf16[1024,128]{1,0:T(8,128)(2,1)S(1)}, bf16[1024,128]{1,0:T(8,128)(2,1)S(1)}, u32[]{:S(2)}, u32[]{:S(2)}) collective-permute-start(bf16[1024,128]{1,0:T(8,128)(2,1)S(1)} %shard_map.50.refs_4_), channel_id=1, source_target_pairs={{0,16},{4,20},{8,24},{12,28},{16,0},{20,4},{24,8},{28,12},{1,17},{... | collective-permute-start | bytes 786440 | tf_op jit(solution)/shard_map/ppermute | solution.py:22
  90.8 18.0 %collective-permute-start.9 = (bf16[1024,128]{1,0:T(8,128)(2,1)S(1)}, bf16[1024,128]{1,0:T(8,128)(2,1)S(1)}, u32[]{:S(2)}, u32[]{:S(2)}) collective-permute-start(bf16[1024,128]{1,0:T(8,128)(2,1)S(1)} %shard_map.50.refs_4_), channel_id=1, source_target_pairs={{0,8},{4,12},{8,0},{12,4},{16,24},{20,28},{24,16},{28,20},{1,9},{5... | collective-permute-start | bytes 786440 | tf_op jit(solution)/shard_map/ppermute | solution.py:22
  108.9 28.4 %collective-permute-start.17 = (bf16[4,1024,128]{2,1,0:T(8,128)(2,1)S(1)}, bf16[4,1024,128]{2,1,0:T(8,128)(2,1)S(1)}, u32[]{:S(2)}, u32[]{:S(2)}) collective-permute-start(bf16[4,1024,128]{2,1,0:T(8,128)(2,1)S(1)} %pad_maximum_fusion), channel_id=1, source_target_pairs={{0,4},{4,0},{8,12},{12,8},{16,20},{20,16},{24,28},{28,24},{1,5},{5... | collective-permute-start | bytes 3145736 | tf_op jit(solution)/shard_map/ppermute | solution.py:22
  112.0 20.4 %collective-permute-start.15 = (bf16[2,512,128]{2,1,0:T(8,128)(2,1)S(1)}, bf16[2,512,128]{2,1,0:T(8,128)(2,1)S(1)}, u32[]{:S(2)}, u32[]{:S(2)}) collective-permute-start(bf16[2,512,128]{2,1,0:T(8,128)(2,1)S(1)} %pad_maximum_fusion.1), channel_id=1, source_target_pairs={{0,16},{4,20},{8,24},{12,28},{16,0},{20,4},{24,8},{28,12},{1,17},{... | collective-permute-start | bytes 786440 | tf_op jit(solution)/shard_map/ppermute | solution.py:22
  112.0 20.4 %collective-permute-start.14 = (bf16[2,512,128]{2,1,0:T(8,128)(2,1)S(1)}, bf16[2,512,128]{2,1,0:T(8,128)(2,1)S(1)}, u32[]{:S(2)}, u32[]{:S(2)}) collective-permute-start(bf16[2,512,128]{2,1,0:T(8,128)(2,1)S(1)} %pad_maximum_fusion.1), channel_id=1, source_target_pairs={{0,8},{4,12},{8,0},{12,4},{16,24},{20,28},{24,16},{28,20},{1,9},{5... | collective-permute-start | bytes 786440 | tf_op jit(solution)/shard_map/ppermute | solution.py:22
  164.9 27.4 %collective-permute-start.20 = (s16[4,1040,128]{2,1,0:T(8,128)(2,1)S(1)}, s16[4,1040,128]{2,1,0:T(8,128)(2,1)S(1)}, u32[]{:S(2)}, u32[]{:S(2)}) collective-permute-start(s16[4,1040,128]{2,1,0:T(8,128)(2,1)S(1)} %shard_map.59), channel_id=1, source_target_pairs={{0,4},{4,0},{8,12},{12,8},{16,20},{20,16},{24,28},{28,24},{1,5},{5... | collective-permute-start | bytes 3194888 | tf_op jit(solution)/shard_map/ppermute | solution.py:22
  170.6 21.7 %collective-permute-start.22 = (s16[1040,128]{1,0:T(8,128)(2,1)S(1)}, s16[1040,128]{1,0:T(8,128)(2,1)S(1)}, u32[]{:S(2)}, u32[]{:S(2)}) collective-permute-start(s16[1040,128]{1,0:T(8,128)(2,1)S(1)} %get-tuple-element.65), channel_id=1, source_target_pairs={{0,16},{4,20},{8,24},{12,28},{16,0},{20,4},{24,8},{28,12},{1,17},{... | collective-permute-start | bytes 798728 | tf_op jit(solution)/shard_map/ppermute | solution.py:22
  172.4 19.9 %collective-permute-start.23 = (s16[1040,128]{1,0:T(8,128)(2,1)S(1)}, s16[1040,128]{1,0:T(8,128)(2,1)S(1)}, u32[]{:S(2)}, u32[]{:S(2)}) collective-permute-start(s16[1040,128]{1,0:T(8,128)(2,1)S(1)} %get-tuple-element.66), channel_id=1, source_target_pairs={{0,24},{4,28},{8,16},{12,20},{16,8},{20,12},{24,0},{28,4},{1,25},{... | collective-permute-start | bytes 798728 | tf_op jit(solution)/shard_map/ppermute | solution.py:22
  193.3 15.8 %collective-permute-start.24 = (s16[1040,128]{1,0:T(8,128)(2,1)S(1)}, s16[1040,128]{1,0:T(8,128)(2,1)S(1)}, u32[]{:S(2)}, u32[]{:S(2)}) collective-permute-start(s16[1040,128]{1,0:T(8,128)(2,1)S(1)} %get-tuple-element.69), channel_id=1, source_target_pairs={{0,8},{4,12},{8,0},{12,4},{16,24},{20,28},{24,16},{28,20},{1,9},{5... | collective-permute-start | bytes 798728 | tf_op jit(solution)/shard_map/ppermute | solution.py:22
  197.7 20.9 %collective-permute-start.25 = (s16[1040,128]{1,0:T(8,128)(2,1)S(1)}, s16[1040,128]{1,0:T(8,128)(2,1)S(1)}, u32[]{:S(2)}, u32[]{:S(2)}) collective-permute-start(s16[1040,128]{1,0:T(8,128)(2,1)S(1)} %get-tuple-element.70), channel_id=1, source_target_pairs={{0,16},{4,20},{8,24},{12,28},{16,0},{20,4},{24,8},{28,12},{1,17},{... | collective-permute-start | bytes 798728 | tf_op jit(solution)/shard_map/ppermute | solution.py:22
  197.7 20.9 %collective-permute-start.26 = (s16[1040,128]{1,0:T(8,128)(2,1)S(1)}, s16[1040,128]{1,0:T(8,128)(2,1)S(1)}, u32[]{:S(2)}, u32[]{:S(2)}) collective-permute-start(s16[1040,128]{1,0:T(8,128)(2,1)S(1)} %get-tuple-element.71), channel_id=1, source_target_pairs={{0,24},{4,28},{8,16},{12,20},{16,8},{20,12},{24,0},{28,4},{1,25},{... | collective-permute-start | bytes 798728 | tf_op jit(solution)/shard_map/ppermute | solution.py:22
  226.1 33.1 %collective-permute-start.29 = (s16[1040,128]{1,0:T(8,128)(2,1)S(1)}, s16[1040,128]{1,0:T(8,128)(2,1)S(1)}, u32[]{:S(2)}, u32[]{:S(2)}) collective-permute-start(s16[1040,128]{1,0:T(8,128)(2,1)S(1)} %get-tuple-element.82.refs_0_), channel_id=1, source_target_pairs={{0,24},{4,28},{8,16},{12,20},{16,8},{20,12},{24,0},{28,4},{1,25},{... | collective-permute-start | bytes 798728 | tf_op jit(solution)/shard_map/ppermute | solution.py:22
  228.0 31.3 %collective-permute-start.28 = (s16[1040,128]{1,0:T(8,128)(2,1)S(1)}, s16[1040,128]{1,0:T(8,128)(2,1)S(1)}, u32[]{:S(2)}, u32[]{:S(2)}) collective-permute-start(s16[1040,128]{1,0:T(8,128)(2,1)S(1)} %get-tuple-element.82.refs_0_), channel_id=1, source_target_pairs={{0,16},{4,20},{8,24},{12,28},{16,0},{20,4},{24,8},{28,12},{1,17},{... | collective-permute-start | bytes 798728 | tf_op jit(solution)/shard_map/ppermute | solution.py:22
  231.5 27.8 %collective-permute-start.27 = (s16[1040,128]{1,0:T(8,128)(2,1)S(1)}, s16[1040,128]{1,0:T(8,128)(2,1)S(1)}, u32[]{:S(2)}, u32[]{:S(2)}) collective-permute-start(s16[1040,128]{1,0:T(8,128)(2,1)S(1)} %get-tuple-element.82.refs_0_), channel_id=1, source_target_pairs={{0,8},{4,12},{8,0},{12,4},{16,24},{20,28},{24,16},{28,20},{1,9},{5... | collective-permute-start | bytes 798728 | tf_op jit(solution)/shard_map/ppermute | solution.py:22
  231.5 14.2 %collective-permute-start.35 = (f32[128,128]{1,0:T(8,128)S(1)}, f32[128,128]{1,0:T(8,128)S(1)}, u32[]{:S(2)}, u32[]{:S(2)}) collective-permute-start(f32[128,128]{1,0:T(8,128)S(1)} %add.36), channel_id=1, source_target_pairs={{0,8},{4,12},{8,0},{12,4},{16,24},{20,28},{24,16},{28,20},{1,9},{5... | collective-permute-start | bytes 196616 | tf_op jit(solution)/shard_map/ppermute | solution.py:22
  259.3 25.5 %collective-permute-start.37 = (s16[4,1040,128]{2,1,0:T(8,128)(2,1)S(1)}, s16[4,1040,128]{2,1,0:T(8,128)(2,1)S(1)}, u32[]{:S(2)}, u32[]{:S(2)}) collective-permute-start(s16[4,1040,128]{2,1,0:T(8,128)(2,1)S(1)} %pad_add_fusion), channel_id=1, source_target_pairs={{0,4},{4,0},{8,12},{12,8},{16,20},{20,16},{24,28},{28,24},{1,5},{5... | collective-permute-start | bytes 3194888 | tf_op jit(solution)/shard_map/ppermute | solution.py:22
  262.4 22.1 %collective-permute-start.39 = (s16[2,528,128]{2,1,0:T(8,128)(2,1)S(1)}, s16[2,528,128]{2,1,0:T(8,128)(2,1)S(1)}, u32[]{:S(2)}, u32[]{:S(2)}) collective-permute-start(s16[2,528,128]{2,1,0:T(8,128)(2,1)S(1)} %pad_add_fusion.1.refs_5_), channel_id=1, source_target_pairs={{0,16},{4,20},{8,24},{12,28},{16,0},{20,4},{24,8},{28,12},{1,17},{... | collective-permute-start | bytes 811016 | tf_op jit(solution)/shard_map/ppermute | solution.py:22
  262.4 22.1 %collective-permute-start.38 = (s16[2,528,128]{2,1,0:T(8,128)(2,1)S(1)}, s16[2,528,128]{2,1,0:T(8,128)(2,1)S(1)}, u32[]{:S(2)}, u32[]{:S(2)}) collective-permute-start(s16[2,528,128]{2,1,0:T(8,128)(2,1)S(1)} %pad_add_fusion.1.refs_5_), channel_id=1, source_target_pairs={{0,8},{4,12},{8,0},{12,4},{16,24},{20,28},{24,16},{28,20},{1,9},{5... | collective-permute-start | bytes 811016 | tf_op jit(solution)/shard_map/ppermute | solution.py:22
  (20 other events, 168.3 us)
where the time goes:
time: 293 us; the launch traced here: 292 us
  waiting for transfers between devices  150 us (51%)
  Pallas kernels  66 us (23%)
  starting transfers between devices  61.3 us (21%)
  matrix products  7.68 us (3%)
  other arithmetic  5.33 us (2%)
    ppermute x41, waiting for transfers between devices, exchange(): return lax.ppermute(value, axis, [(i, i ^ mask) for i in range(size)])  150 us
    ppermute x41, starting transfers between devices, exchange(): return lax.ppermute(value, axis, [(i, i ^ mask) for i in range(size)])  61.3 us
    pallas_call x8, Pallas kernels, sketch_part(): pl.pallas_call(functools.partial(sketch_kernel, code, per_step), out_shap...  28.3 us
    pallas_call x3, Pallas kernels, project(): pl.pallas_call(functools.partial(project_kernel, base is not None, True,...  14.7 us
    pallas_call x7, Pallas kernels, small_call(): pl.pallas_call(kernel, out_shape=out_shape, in_specs=[WHOLE] * len(args),...  8.62 us
    dot_general x1, matrix products, on_device(): partial = jnp.dot(scans, test_matrix, preferred_element_type=F32)  7.68 us
    pallas_call x1, Pallas kernels, finish(): pl.pallas_call(functools.partial(finish_kernel, high, n), out_shape=jax.S...  7.18 us
  transfers between devices with their start and end apart: 41, of which 23 were waited for; matrix products, arithmetic and copies ran while one was open for 1% of the time, Pallas kernels for 13%

commit v1 on v0

v1 whole, which is shorter than its diff:
```python
import functools

import jax
import jax.numpy as jnp
from jax import lax
from jax.experimental import pallas as pl
from jax.experimental.pallas import tpu as pltpu
from jax.sharding import PartitionSpec as P

F32 = jnp.float32
BF16 = jnp.bfloat16
I16 = jnp.int16
HIGHEST = lax.Precision.HIGHEST
STEPS = 64.0
LOW = 2
GROUP = 8
LANES = 128
VMEM_BYTES = 48 << 20
WHOLE = pl.BlockSpec(memory_space=pltpu.VMEM)


def exchange(value, axis, size, mask):
    return lax.ppermute(value, axis, [(i, i ^ mask) for i in range(size)])


def butterfly(value, axis, size):
    mask = 1
    while 2 * mask < size:
        value = value + exchange(value, axis, size, mask)
        mask *= 2
    return value, exchange(value, axis, size, mask)


class Plain:
    pad = 0
    dtype = BF16

    @staticmethod
    def encode(value):
        return value.astype(BF16)

    @staticmethod
    def decode(sent):
        return sent.astype(F32)


class Fixed:
    pad = 16
    dtype = I16

    @staticmethod
    def encode(value):
        top = jnp.maximum(jnp.max(jnp.abs(value), axis=0, keepdims=True), 1e-30)
        power = jnp.ceil(jnp.log2(top * (1.0 / 32000.0)) * STEPS)
        codes = jnp.round(value * jnp.exp2(power * (-1.0 / STEPS)))
        codes = jnp.clip(codes, -32767.0, 32767.0)
        rows = jnp.broadcast_to(power, (Fixed.pad, value.shape[1]))
        return jnp.concatenate([codes, rows]).astype(jnp.int32).astype(I16)

    @staticmethod
    def decode(sent):
        wide = sent.astype(jnp.int32).astype(F32)
        rows = wide.shape[0] - Fixed.pad
        return wide[:rows] * jnp.exp2(wide[rows : rows + 1] * (1.0 / STEPS))


def params():
    return pltpu.CompilerParams(vmem_limit_bytes=VMEM_BYTES)


class Layout:
    def __init__(self, voxels, subjects):
        self.high = subjects // LOW
        unit = subjects * LANES
        for top, bottom in ((5, 6), (3, 4), (2, 3), (1, 2)):
            self.cut = voxels * top // bottom
            self.pair = (voxels - self.cut) // self.high
            if self.cut % unit == 0 and voxels % unit == 0 and self.cut % self.pair == 0:
                break
        self.single = self.cut // subjects

    def columns(self, j):
        return self.pair if j is None else self.single

    def block(self, j, k, pos):
        if j is None:
            return self.cut // self.pair + (pos[1] ^ k)
        return (pos[0] ^ j) * self.high + (pos[1] ^ k)


def sketch_kernel(code, apart, count, pos_ref, scores_ref, *refs):
    for u in range(count):
        product = lax.dot_general(
            scores_ref[...], refs[u][...], (((0,), (0,)), ((), ())), preferred_element_type=F32
        )
        out = refs[count + u] if apart else refs[count].at[u]
        out[...] = code.encode(product.T)


def sketch_part(scans, layout, pos, scores, j, ks, code, apart, per_step):
    time_rows = scans.shape[0]
    rank = scores.shape[1]
    n = layout.columns(j)
    rows = n + code.pad
    steps = len(ks) // per_step

    def column(u):
        return lambda g, pos: (0, layout.block(j, ks[0] + g * per_step + u, pos))

    if apart:
        out_shape = [jax.ShapeDtypeStruct((rows, rank), code.dtype)] * len(ks)
        out_specs = [pl.BlockSpec((rows, rank), lambda g, pos: (0, 0))] * len(ks)
    else:
        out_shape = jax.ShapeDtypeStruct((len(ks), rows, rank), code.dtype)
        out_specs = pl.BlockSpec((per_step, rows, rank), lambda g, pos: (g, 0, 0))
    return pl.pallas_call(
        functools.partial(sketch_kernel, code, apart, per_step),
        out_shape=out_shape,
        grid_spec=pltpu.PrefetchScalarGridSpec(
            num_scalar_prefetch=1,
            grid=(steps,),
            in_specs=[pl.BlockSpec((time_rows, rank), lambda g, pos: (0, 0))]
            + [pl.BlockSpec((time_rows, n), column(u)) for u in range(per_step)],
            out_specs=out_specs,
        ),
        compiler_params=params(),
        cost_estimate=pl.CostEstimate(
            flops=2 * time_rows * n * rank * len(ks),
            bytes_accessed=time_rows * n * 2 * len(ks),
            transcendentals=0,
        ),
    )(pos, scores, *([scans] * per_step))


def small_call(kernel, out_shape, *args):
    return pl.pallas_call(
        kernel,
        out_shape=out_shape,
        in_specs=[WHOLE] * len(args),
        out_specs=jax.tree.map(lambda _: WHOLE, out_shape),
        compiler_params=params(),
    )(*args)


def add_pieces_kernel(code, count, own_ref, got_ref, *outs):
    for k in range(count):
        outs[k][...] = code.encode(code.decode(own_ref[k]) + code.decode(got_ref[k]))


def add_all_kernel(code, with_gram, *refs):
    outs = refs[-2:] if with_gram else refs[-1:]
    parts = refs[: len(refs) - len(outs)]
    total = code.decode(parts[0][...])
    for part in parts[1:]:
        total = total + code.decode(part[...])
    outs[0][...] = code.encode(total)
    if with_gram:
        outs[1][...] = lax.dot_general(
            total, total, (((0,), (0,)), ((), ())), precision=HIGHEST,
            preferred_element_type=F32,
        )


def add_halves_kernel(code, pos_ref, *refs):
    parts, (keep_ref, send_ref) = refs[:-2], refs[-2:]
    total = code.decode(parts[0][...])
    for part in parts[1:]:
        total = total + code.decode(part[...])
    half = total.shape[0] // 2
    lower = pos_ref[0] == 0
    keep_ref[...] = code.encode(jnp.where(lower, total[:half], total[half:]))
    send_ref[...] = code.encode(jnp.where(lower, total[half:], total[:half]))


def add_all(code, with_gram, parts):
    rank = parts[0].shape[1]
    out = [jax.ShapeDtypeStruct(parts[0].shape, code.dtype)]
    if with_gram:
        out.append(jax.ShapeDtypeStruct((rank, rank), F32))
    return small_call(functools.partial(add_all_kernel, code, with_gram), out, *parts)


def project_kernel(has_base, split, items, pos_ref, *refs):
    refs = list(refs)
    base = refs.pop(0) if has_base else None
    outs = [refs.pop() for _ in range(2 if split else 1)][::-1]
    scans, pieces = refs[: len(items)], refs[len(items) :]
    time_rows = scans[0].shape[0]
    rank = outs[0].shape[1]
    total = jnp.zeros((time_rows, rank), F32)
    gram = jnp.zeros((rank, rank), F32)
    for scan, (source, index) in zip(scans, items):
        piece = pieces[source][...] if index is None else pieces[source][index]
        total += jnp.dot(scan[...], piece, preferred_element_type=F32)
        gram += lax.dot_general(
            piece, piece, (((0,), (0,)), ((), ())), preferred_element_type=F32
        )
    if has_base:
        total += base[:time_rows]
        gram += base[time_rows:]
    if not split:
        outs[0][:time_rows] = total
        outs[0][time_rows:] = gram
        return
    both = jnp.concatenate([total, gram])
    half = both.shape[0] // 2
    lower = pos_ref[2] == 0
    outs[0][...] = jnp.where(lower, both[:half], both[half:])
    outs[1][...] = jnp.where(lower, both[half:], both[:half])


def project(scans, layout, pos, groups, base=None, split=False):
    time_rows = scans.shape[0]
    rank = groups[0][2].shape[-1]
    items, names = [], []
    for source, (j, ks, array) in enumerate(groups):
        for i, k in enumerate(ks):
            items.append((source, None if array.ndim == 2 else i))
            names.append((j, k))

    def column(j, k):
        return lambda g, pos: (0, layout.block(j, k, pos))

    full = lambda shape: pl.BlockSpec(shape, lambda g, pos: (0,) * len(shape))
    bases = [] if base is None else [base]
    arrays = [array for _, _, array in groups]
    rows = time_rows + rank
    shape = (rows // 2, rank) if split else (rows, rank)
    out_shape = [jax.ShapeDtypeStruct(shape, F32)] * (2 if split else 1)
    columns = sum(layout.columns(j) for j, _ in names)
    out = pl.pallas_call(
        functools.partial(project_kernel, base is not None, split, items),
        out_shape=out_shape,
        grid_spec=pltpu.PrefetchScalarGridSpec(
            num_scalar_prefetch=1,
            grid=(1,),
            in_specs=[full(b.shape) for b in bases]
            + [pl.BlockSpec((time_rows, layout.columns(j)), column(j, k)) for j, k in names]
            + [full(p.shape) for p in arrays],
            out_specs=[full(shape)] * len(out_shape),
        ),
        compiler_params=params(),
        cost_estimate=pl.CostEstimate(
            flops=2 * rows * columns * rank, bytes_accessed=time_rows * columns * 2,
            transcendentals=0,
        ),
    )(pos, *bases, *([scans] * len(items)), *arrays)
    return out if split else out[0]


def finish_kernel(layout, items, has_base, pos_ref, inverse_ref, *refs):
    refs, (out, held, sems) = refs[:-3], refs[-3:]
    if has_base:
        refs = refs[1:]
    copies = []
    used = 0
    pos = (pos_ref[0], pos_ref[1])
    for number, (source, index, j, k) in enumerate(items):
        n = layout.columns(j)
        codes = refs[source][...] if index is None else refs[source][index]
        if j is None:
            value = jnp.concatenate([Fixed.decode(codes[side]) for side in range(LOW)])
        else:
            value = Fixed.decode(codes)
        rows = pl.ds(used, n)
        held[rows] = times_transpose(value, inverse_ref[...])
        used += n
        start = pl.multiple_of(layout.block(j, k, pos) * n, n)
        copy = pltpu.make_async_copy(held.at[rows], out.at[pl.ds(start, n)], sems.at[number])
        copy.start()
        copies.append(copy)
    for copy in copies:
        copy.wait()


def finish(layout, pos, groups, inverse, voxels, base=None):
    rank = inverse.shape[0]
    items = []
    for source, (j, ks, array) in enumerate(groups):
        alone = array.ndim == (2 if j is not None else 3)
        for i, k in enumerate(ks):
            items.append((source, None if alone else i, j, k))
    columns = sum(layout.columns(j) for _, _, j, _ in items)
    bases = [] if base is None else [base]
    arrays = [array for _, _, array in groups]
    return pl.pallas_call(
        functools.partial(finish_kernel, layout, items, base is not None),
        out_shape=jax.ShapeDtypeStruct((voxels, rank), F32),
        in_specs=[pl.BlockSpec(memory_space=pltpu.SMEM), WHOLE]
        + [pl.BlockSpec(memory_space=pl.ANY)] * len(bases)
        + [WHOLE] * len(arrays),
        out_specs=pl.BlockSpec(memory_space=pl.ANY),
        scratch_shapes=[
            pltpu.VMEM((columns, rank), F32),
            pltpu.SemaphoreType.DMA((len(items),)),
        ],
        input_output_aliases={2: 0} if bases else {},
        compiler_params=params(),
    )(pos, inverse, *bases, *arrays)


def inverse_factor(gram):
    size = gram.shape[0]
    groups = size // GROUP
    shape = (GROUP, size)
    sub = lax.broadcasted_iota(jnp.int32, shape, 0)
    lane = lax.broadcasted_iota(jnp.int32, shape, 1)
    left = [gram[GROUP * i : GROUP * (i + 1)] for i in range(groups)]
    right = [jnp.where(sub + GROUP * i == lane, 1.0, 0.0).astype(F32) for i in range(groups)]
    for g in range(groups):
        first = g * GROUP
        wide = lambda value: jnp.broadcast_to(value, shape)
        rows = [wide(left[g][t : t + 1]) for t in range(GROUP)]
        inverse_rows = [wide(right[g][t : t + 1]) for t in range(GROUP)]
        block = [
            [wide(left[g][t : t + 1, first + u : first + u + 1]) for u in range(GROUP)]
            for t in range(GROUP)
        ]
        below = range(g + 1, groups)
        columns = {
            i: [wide(left[i][:, first + u : first + u + 1]) for u in range(GROUP)] for i in below
        }
        scaled = []
        for t in range(GROUP):
            pivot = 1.0 / block[t][t]
            scaled.append((rows[t] * pivot, inverse_rows[t] * pivot))
            for u in range(t + 1, GROUP):
                factor = block[t][u] * pivot
                for w in range(u, GROUP):
                    block[u][w] = block[u][w] - factor * block[t][w]
                rows[u] = rows[u] - factor * rows[t]
                inverse_rows[u] = inverse_rows[u] - factor * inverse_rows[t]
                for i in below:
                    columns[i][u] = columns[i][u] - factor * columns[i][t]
        for i in below:
            for t in range(GROUP):
                left[i] = left[i] - columns[i][t] * scaled[t][0]
                right[i] = right[i] - columns[i][t] * scaled[t][1]
        for t in range(GROUP):
            left[g] = jnp.where(sub == t, rows[t], left[g])
            right[g] = jnp.where(sub == t, inverse_rows[t], right[g])
    out = []
    for g in range(groups):
        pivots = jnp.sum(
            jnp.where(sub + GROUP * g == lane, left[g], 0.0), axis=1, keepdims=True
        )
        out.append(right[g] * lax.rsqrt(pivots))
    return jnp.concatenate(out)


def times_transpose(value, inverse):
    return lax.dot_general(
        value, inverse, (((1,), (1,)), ((), ())), precision=HIGHEST, preferred_element_type=F32
    )


def normalise_kernel(all_voxels, length_ref, pos_ref, mine_ref, other_ref, out_ref):
    time_rows = out_ref.shape[0]
    mine, other = mine_ref[...], other_ref[...]
    lower = pos_ref[2] == 0
    both = jnp.concatenate([jnp.where(lower, mine, other), jnp.where(lower, other, mine)])
    inverse = inverse_factor(both[time_rows:] * (1.0 / all_voxels))
    scores = times_transpose(both[:time_rows], inverse)
    live = lax.broadcasted_iota(jnp.int32, scores.shape, 0) < length_ref[0]
    out_ref[...] = jnp.where(live, scores, 0.0).astype(BF16)


def invert_kernel(all_voxels, *refs):
    terms = [ref[...] for ref in refs[:-1]]
    while len(terms) > 1:
        terms = [terms[i] + terms[i + 1] for i in range(0, len(terms), 2)]
    refs[-1][...] = inverse_factor(terms[0] * (1.0 / all_voxels))


def make(mesh):
    subjects, blocks = mesh.shape["subj"], mesh.shape["vox"]
    swap = functools.partial(exchange, axis="subj", size=subjects)
    swap_vox = functools.partial(exchange, axis="vox", size=blocks)

    def on_device(scans, test_matrix, lengths, block_subject):
        time_rows, voxels = scans.shape
        rank = test_matrix.shape[1]
        all_voxels = voxels * blocks
        layout = Layout(voxels, subjects)
        high = layout.high
        ks = list(range(high))
        near, far = ks[: high // 2], ks[high // 2 :]
        me = lax.axis_index("subj")
        core = lax.axis_index("vox") % 2
        pos = jnp.stack([me % LOW, me // LOW, core]).astype(jnp.int32)
        slot_ids = jnp.arange(block_subject.shape[0], dtype=jnp.int32)
        subject = jnp.sum(jnp.where(slot_ids == me, block_subject, 0))
        length = jnp.sum(jnp.where(slot_ids == subject, lengths, 0))
        live_rows = (jnp.arange(time_rows, dtype=jnp.int32) < length)[:, None]

        def sketch_sum(scores, code, with_gram):
            def part(after, j, ks, apart, per_step):
                ordered = scores if after is None else lax.optimization_barrier((scores, after))[0]
                return sketch_part(
                    scans, layout, pos, ordered, j, ks, code, apart, per_step
                )

            def add_pieces(home, got, count):
                piece = jax.ShapeDtypeStruct((layout.single + code.pad, rank), code.dtype)
                return small_call(
                    functools.partial(add_pieces_kernel, code, count), [piece] * count, home, got
                )

            away_far = part(None, 1, far, False, 1)
            got_far = swap(away_far, mask=1)
            second = part(away_far, None, ks[1:], True, high - 1)
            got_second = [swap(second[k - 1], mask=k * LOW) for k in ks[1:]]
            away_near = part(second[0], 1, near, False, 1)
            got_near = swap(away_near, mask=1)
            home_far = part(away_near, 0, far, False, 1)
            home_near = part(home_far, 0, near, False, 1)
            (second_own,) = part(home_near, None, ks[:1], True, 1)

            first_far = add_pieces(home_far, got_far, len(far))
            got_first = [swap(first_far[k - far[0]], mask=k * LOW) for k in far]
            got_near, *got_second = lax.optimization_barrier((got_near, *got_second))
            first_near = add_pieces(home_near, got_near, len(near))
            got_first += [swap(first_near[k], mask=k * LOW) for k in near[1:]]

            half = jax.ShapeDtypeStruct((layout.pair // 2 + code.pad, rank), code.dtype)
            keep, send = pl.pallas_call(
                functools.partial(add_halves_kernel, code),
                out_shape=[half, half],
                in_specs=[pl.BlockSpec(memory_space=pltpu.SMEM)] + [WHOLE] * high,
                out_specs=[WHOLE, WHOLE],
                compiler_params=params(),
            )(pos, second_own, *got_second)
            got_send = swap(send, mask=1)
            return (
                add_all(code, with_gram, [first_near[0], *got_first]),
                add_all(code, with_gram, [keep, got_send]),
            )

        def gather(first, second, gram=None):
            far_in = [swap(first, mask=k * LOW) for k in far]
            near_in = [first] + [swap(first, mask=k * LOW) for k in near[1:]]
            low_near = swap(jnp.stack(near_in), mask=1)
            got = swap(second, mask=1)
            lower = pos[0] == 0
            pair = jnp.stack([jnp.where(lower, second, got), jnp.where(lower, got, second)])
            if gram is not None:
                gram = gram + swap_vox(gram, mask=1)
                mask = 2
                while mask < blocks:
                    gram = gram + swap_vox(gram, mask=mask)
                    mask *= 2
                gram = gram + swap(gram, mask=1)
            far_in, pair, gram = lax.optimization_barrier((far_in, pair, gram))
            low_far = swap(jnp.stack(far_in), mask=1)
            seconds = [pair] + [swap(pair, mask=k * LOW) for k in ks[1:]]
            if gram is not None:
                gram = [gram] + [swap(gram, mask=k * LOW) for k in ks[1:]]
            early = [(0, [k], array) for k, array in zip(near + far, near_in + far_in)]
            early.append((1, near, low_near))
            pairs = [(None, [k], array) for k, array in zip(ks, seconds)]
            return early, pairs, (1, far, low_far), gram

        partial = jnp.dot(scans, test_matrix, preferred_element_type=F32)
        summed = sum(butterfly(partial, "vox", blocks))
        scores = jnp.where(live_rows, summed, 0.0).astype(BF16)

        (first,), (second,) = sketch_sum(scores, Plain, False)
        early, pairs, last, _ = gather(first, second)
        pairs = [(j, k, array.reshape(layout.pair, rank)) for j, k, array in pairs]
        both = project(scans, layout, pos, early)
        both = project(scans, layout, pos, pairs, both)
        mine, send = project(scans, layout, pos, [last], both, True)
        mine = mine + swap_vox(send, mask=1)
        mask = 2
        while mask < blocks:
            mine = mine + swap_vox(mine, mask=mask)
            mask *= 2
        other = swap_vox(mine, mask=1)
        scores = pl.pallas_call(
            functools.partial(normalise_kernel, all_voxels),
            out_shape=jax.ShapeDtypeStruct((time_rows, rank), BF16),
            in_specs=[pl.BlockSpec(memory_space=pltpu.SMEM)] * 2 + [WHOLE, WHOLE],
            out_specs=WHOLE,
            compiler_params=params(),
        )(length[None], pos, mine, other)

        (first, gram_first), (second, gram_second) = sketch_sum(scores, Fixed, True)
        early, pairs, last, grams = gather(first, second, gram_first + gram_second)
        inverse = small_call(
            functools.partial(invert_kernel, all_voxels),
            jax.ShapeDtypeStruct((rank, rank), F32), *grams,
        )
        out = finish(layout, pos, early, inverse, voxels)
        return finish(layout, pos, pairs + [last], inverse, voxels, out)

    return on_device


def solution(mesh):
    placed = (P("subj", "vox"), P("vox", None), P(), P())
    return jax.shard_map(
        make(mesh), mesh=mesh, in_specs=placed, out_specs=P("vox", None), check_vma=False
    )
```

time: 293 us -> 317 us (1.082)
  starting transfers between devices: 61.3 us -> 78 us
  Pallas kernels: 66 us -> 77.1 us
    ppermute x41 -> x47, starting transfers between devices: 61.3 us -> 78 us  [exchange(): return lax.ppermute(value, axis, [(i, i ^ mask) for i in range(size)])]
    pallas_call x12 -> x17, Pallas kernels: 50.2 us -> 59.9 us  [the longest x12 35.8 us: sketch_part(): pl.pallas_call(functools.partial(sketch_kernel, code, apart, per_step), o...]
    ppermute x41 -> x47, waiting for transfers between devices: 150 us -> 147 us  [exchange(): return lax.ppermute(value, axis, [(i, i ^ mask) for i in range(size)])]
    pallas_call x7 -> x9, Pallas kernels: 8.62 us -> 9.8 us  [small_call(): pl.pallas_call(kernel, out_shape=out_shape, in_specs=[WHOLE] * len(args),...]
  transfers between devices with their start and end apart: 41 -> 47, of which waited for: 23 -> 28; matrix products, arithmetic and copies ran while one was open for 1% -> 1% of each run, Pallas kernels for 13% -> 14%
where the time goes in v1:
time: 317 us
  waiting for transfers between devices  147 us (46%)
  starting transfers between devices  78 us (25%)
  Pallas kernels  77.1 us (24%)
  matrix products  7.68 us (2%)
  other arithmetic  5.1 us (2%)
    ppermute x47, waiting for transfers between devices, exchange(): return lax.ppermute(value, axis, [(i, i ^ mask) for i in range(size)])  147 us
    ppermute x47, starting transfers between devices, exchange(): return lax.ppermute(value, axis, [(i, i ^ mask) for i in range(size)])  78 us
    pallas_call x12, Pallas kernels, sketch_part(): pl.pallas_call(functools.partial(sketch_kernel, code, apart, per_step), o...  35.8 us
    pallas_call x3, Pallas kernels, project(): pl.pallas_call(functools.partial(project_kernel, base is not None, split,...  14.6 us
    pallas_call x9, Pallas kernels, small_call(): pl.pallas_call(kernel, out_shape=out_shape, in_specs=[WHOLE] * len(args),...  9.8 us
    pallas_call x2, Pallas kernels, finish(): pl.pallas_call(functools.partial(finish_kernel, layout, items, base is no...  9.53 us
    dot_general x1, matrix products, on_device(): partial = jnp.dot(scans, test_matrix, preferred_element_type=F32)  7.68 us
  transfers between devices with their start and end apart: 47, of which 28 were waited for; matrix products, arithmetic and copies ran while one was open for 1% of the time, Pallas kernels for 14%

profile of v1, /device:TPU:0, one launch (start us, length us, event | category | flops | bytes accessed | tf_op | source)
XLA Modules:
  0.0 316.9 jit_solution(17670771843256870191)
XLA Ops:
  1.9 7.7 %fusion.2 = f32[640,128]{1,0:T(8,128)S(1)} fusion(bf16[640,12288]{1,0:T(8,128)(2,1)} %refs_0_.25, bf16[12288,128]{1,0:T(8,128)(2,1)S(1)} %copy-done), kind=kOutput, calls=%fused_computation.17 | convolution fusion | flops 2013265920 | bytes 19202048 | tf_op jit(solution)/shard_map/dot_general | solution.py:463
  17.4 6.0 %collective-permute-done.1 = f32[640,128]{1,0:T(8,128)S(1)} collective-permute-done((f32[640,128]{1,0:T(8,128)S(1)}, f32[640,128]{1,0:T(8,128)S(1)}, u32[]{:S(2)}, u32[]{:S(2)}) %collective-permute-start.1) | collective-permute-done | bytes 327712 | tf_op jit(solution)/shard_map/ppermute | solution.py:23
  52.8 10.0 %collective-permute-done.6.got_ref = bf16[2,1280,128]{2,1,0:T(8,128)(2,1)S(1)} collective-permute-done((bf16[2,1280,128]{2,1,0:T(8,128)(2,1)S(1)}, bf16[2,1280,128]{2,1,0:T(8,128)(2,1)S(1)}, u32[]{:S(2)}, u32[]{:S(2)}) %collective-permute-start.6) | collective-permute-done | bytes 655392 | tf_op jit(solution)/shard_map/ppermute | solution.py:23
  76.8 11.3 %collective-permute-done.7.refs_1_ = bf16[1280,128]{1,0:T(8,128)(2,1)} collective-permute-done((bf16[1280,128]{1,0:T(8,128)(2,1)}, bf16[1280,128]{1,0:T(8,128)(2,1)}, u32[]{:S(2)}, u32[]{:S(2)}) %collective-permute-start.7) | collective-permute-done | bytes 327712 | tf_op jit(solution)/shard_map/ppermute | solution.py:23
  91.9 13.1 %collective-permute-start.11 = (bf16[1280,128]{1,0:T(8,128)(2,1)S(1)}, bf16[1280,128]{1,0:T(8,128)(2,1)S(1)}, u32[]{:S(2)}, u32[]{:S(2)}) collective-permute-start(bf16[1280,128]{1,0:T(8,128)(2,1)S(1)} %shard_map.53.refs_6_), channel_id=1, source_target_pairs={{0,16},{4,20},{8,24},{12,28},{16,0},{20,4},{24,8},{28,12},{1,17},{... | collective-permute-start | bytes 983048 | tf_op jit(solution)/shard_map/ppermute | solution.py:23
  106.4 20.5 %collective-permute-done.11.refs_8_ = bf16[1280,128]{1,0:T(8,128)(2,1)S(1)} collective-permute-done((bf16[1280,128]{1,0:T(8,128)(2,1)S(1)}, bf16[1280,128]{1,0:T(8,128)(2,1)S(1)}, u32[]{:S(2)}, u32[]{:S(2)}) %collective-permute-start.11) | collective-permute-done | bytes 327712 | tf_op jit(solution)/shard_map/ppermute | solution.py:23
  133.5 11.1 %collective-permute-done.15.refs_10_ = bf16[2,1280,128]{2,1,0:T(8,128)(2,1)S(1)} collective-permute-done((bf16[2,1280,128]{2,1,0:T(8,128)(2,1)S(1)}, bf16[2,1280,128]{2,1,0:T(8,128)(2,1)S(1)}, u32[]{:S(2)}, u32[]{:S(2)}) %collective-permute-start.15) | collective-permute-done | bytes 655392 | tf_op jit(solution)/shard_map/ppermute | solution.py:23
  144.7 7.7 %shard_map.57.refs_0_ = f32[768,128]{1,0:T(8,128)S(1)} custom-call(s32[3]{0:T(128)S(1)} %pad_add_fusion.3.pos_ref, bf16[640,12288]{1,0:T(8,128)(2,1)} %refs_0_.25, bf16[640,12288]{1,0:T(8,128)(2,1)} %refs_0_.25, bf16[640,12288]{1,0:T(8,128)(2,1)} %refs_0_.25, bf16[640,12288]{1,0:T(8,128)(2,1)} %refs_0_.25, bf16[640,12288]{1,0:T(8,128)(2,1)} %refs_0_.25, ...), custom_call_target="tpu_custom_call" | custom-call | flops 1509949440 | bytes 9830400 | tf_op jit(solution)/shard_map/pallas_call | solution.py:231
  157.2 3.7 %shard_map.59 = (f32[384,128]{1,0:T(8,128)S(1)}, f32[384,128]{1,0:T(8,128)S(1)}) custom-call(s32[3]{0:T(128)S(1)} %pad_add_fusion.3.pos_ref, f32[768,128]{1,0:T(8,128)S(1)} %shard_map.58.refs_0_, bf16[640,12288]{1,0:T(8,128)(2,1)} %refs_0_.25, bf16[640,12288]{1,0:T(8,128)(2,1)} %refs_0_.25, bf16[2,1280,128]{2,1,0:T(8,128)(2,1)S(1)} %collective-permute-done.19.refs_3_), custom_call_target="tpu_custom_call" | custom-call | flops 503316480 | bytes 3276800 | tf_op jit(solution)/shard_map/pallas_call | solution.py:231
  164.0 5.4 %collective-permute-done.21 = f32[384,128]{1,0:T(8,128)S(1)} collective-permute-done((f32[384,128]{1,0:T(8,128)S(1)}, f32[384,128]{1,0:T(8,128)S(1)}, u32[]{:S(2)}, u32[]{:S(2)}) %collective-permute-start.21) | collective-permute-done | bytes 196640 | tf_op jit(solution)/shard_map/ppermute | solution.py:23
  170.9 6.0 %shard_map.60.scores_ref = bf16[640,128]{1,0:T(8,128)(2,1)S(1)} custom-call(s32[1]{0:T(128)} %bitcast.3.length_ref, s32[3]{0:T(128)S(1)} %pad_add_fusion.3.pos_ref, f32[384,128]{1,0:T(8,128)S(1)} %add.37.mine_ref, f32[384,128]{1,0:T(8,128)S(1)} %collective-permute-done.22.other_ref), custom_call_target="tpu_custom_call" | custom-call | tf_op jit(solution)/shard_map/pallas_call | solution.py:479
  177.0 3.4 %shard_map.61 = s16[2,1296,128]{2,1,0:T(8,128)(2,1)S(1)} custom-call(s32[3]{0:T(128)S(1)} %pad_add_fusion.3.pos_ref, bf16[640,128]{1,0:T(8,128)(2,1)S(1)} %shard_map.60.scores_ref, bf16[640,12288]{1,0:T(8,128)(2,1)} %refs_0_.25), custom_call_target="tpu_custom_call" | custom-call | flops 419430400 | bytes 3276800 | tf_op jit(solution)/shard_map/pallas_call | solution.py:116
  183.1 3.4 %shard_map.63 = s16[2,1296,128]{2,1,0:T(8,128)(2,1)S(1)} custom-call(s32[3]{0:T(128)S(1)} %pad_add_fusion.3.pos_ref, bf16[640,128]{1,0:T(8,128)(2,1)S(1)} %shard_map.60.scores_ref, bf16[640,12288]{1,0:T(8,128)(2,1)} %refs_0_.25), custom_call_target="tpu_custom_call" | custom-call | flops 419430400 | bytes 3276800 | tf_op jit(solution)/shard_map/pallas_call | solution.py:116
  192.1 3.4 %shard_map.64.own_ref = s16[2,1296,128]{2,1,0:T(8,128)(2,1)S(1)} custom-call(s32[3]{0:T(128)S(1)} %pad_add_fusion.3.pos_ref, bf16[640,128]{1,0:T(8,128)(2,1)S(1)} %shard_map.60.scores_ref, bf16[640,12288]{1,0:T(8,128)(2,1)} %refs_0_.25), custom_call_target="tpu_custom_call" | custom-call | flops 419430400 | bytes 3276800 | tf_op jit(solution)/shard_map/pallas_call | solution.py:116
  195.5 3.6 %shard_map.65.own_ref = s16[2,1296,128]{2,1,0:T(8,128)(2,1)S(1)} custom-call(s32[3]{0:T(128)S(1)} %pad_add_fusion.3.pos_ref, bf16[640,128]{1,0:T(8,128)(2,1)S(1)} %shard_map.60.scores_ref, bf16[640,12288]{1,0:T(8,128)(2,1)} %refs_0_.25), custom_call_target="tpu_custom_call" | custom-call | flops 419430400 | bytes 3276800 | tf_op jit(solution)/shard_map/pallas_call | solution.py:116
  205.1 12.7 %collective-permute-done.27.got_ref = s16[2,1296,128]{2,1,0:T(8,128)(2,1)S(1)} collective-permute-done((s16[2,1296,128]{2,1,0:T(8,128)(2,1)S(1)}, s16[2,1296,128]{2,1,0:T(8,128)(2,1)S(1)}, u32[]{:S(2)}, u32[]{:S(2)}) %collective-permute-start.27) | collective-permute-done | bytes 663584 | tf_op jit(solution)/shard_map/ppermute | solution.py:23
  230.0 12.3 %collective-permute-done.28.refs_1_ = s16[1296,128]{1,0:T(8,128)(2,1)S(1)} collective-permute-done((s16[1296,128]{1,0:T(8,128)(2,1)S(1)}, s16[1296,128]{1,0:T(8,128)(2,1)S(1)}, u32[]{:S(2)}, u32[]{:S(2)}) %collective-permute-start.28) | collective-permute-done | bytes 331808 | tf_op jit(solution)/shard_map/ppermute | solution.py:23
  243.5 7.6 %collective-permute-start.41 = (s16[1296,128]{1,0:T(8,128)(2,1)S(1)}, s16[1296,128]{1,0:T(8,128)(2,1)S(1)}, u32[]{:S(2)}, u32[]{:S(2)}) collective-permute-start(s16[1296,128]{1,0:T(8,128)(2,1)S(1)} %get-tuple-element.89.refs_0_), channel_id=1, source_target_pairs={{0,8},{4,12},{8,0},{12,4},{16,24},{20,28},{24,16},{28,20},{1,9},{5... | collective-permute-start | bytes 995336 | tf_op jit(solution)/shard_map/ppermute | solution.py:23
  261.4 7.0 %collective-permute-done.32.refs_3_ = s16[1296,128]{1,0:T(8,128)(2,1)S(1)} collective-permute-done((s16[1296,128]{1,0:T(8,128)(2,1)S(1)}, s16[1296,128]{1,0:T(8,128)(2,1)S(1)}, u32[]{:S(2)}, u32[]{:S(2)}) %collective-permute-start.32) | collective-permute-done | bytes 331808 | tf_op jit(solution)/shard_map/ppermute | solution.py:23
  268.5 13.6 %collective-permute-done.31.refs_2_ = s16[1296,128]{1,0:T(8,128)(2,1)S(1)} collective-permute-done((s16[1296,128]{1,0:T(8,128)(2,1)S(1)}, s16[1296,128]{1,0:T(8,128)(2,1)S(1)}, u32[]{:S(2)}, u32[]{:S(2)}) %collective-permute-start.31) | collective-permute-done | bytes 331808 | tf_op jit(solution)/shard_map/ppermute | solution.py:23
  295.7 4.1 %shard_map.72.inverse_ref = f32[128,128]{1,0:T(8,128)S(1)} custom-call(f32[128,128]{1,0:T(8,128)S(1)} %add.41.refs_0_, f32[128,128]{1,0:T(8,128)S(1)} %collective-permute-done.38.refs_1_, f32[128,128]{1,0:T(8,128)S(1)} %collective-permute-done.39.refs_2_, f32[128,128]{1,0:T(8,128)S(1)} %collective-permute-done.40.refs_3_), custom_call_target="tpu_custom_call" | custom-call | tf_op jit(solution)/shard_map/pallas_call | solution.py:136
  300.1 5.7 %shard_map.73.refs_0_ = f32[12288,128]{1,0:T(8,128)} custom-call(s32[3]{0:T(128)S(1)} %pad_add_fusion.3.pos_ref, f32[128,128]{1,0:T(8,128)S(1)} %shard_map.72.inverse_ref, s16[1296,128]{1,0:T(8,128)(2,1)S(1)} %get-tuple-element.89.refs_0_, s16[1296,128]{1,0:T(8,128)(2,1)S(1)} %collective-permute-done.41.refs_1_, ...), custom_call_target="tpu_custom_call" | custom-call | tf_op jit(solution)/shard_map/pallas_call | solution.py:286
  305.8 7.1 %collective-permute-done.46.refs_5_ = s16[2,1296,128]{2,1,0:T(8,128)(2,1)S(1)} collective-permute-done((s16[2,1296,128]{2,1,0:T(8,128)(2,1)S(1)}, s16[2,1296,128]{2,1,0:T(8,128)(2,1)S(1)}, u32[]{:S(2)}, u32[]{:S(2)}) %collective-permute-start.46) | collective-permute-done | bytes 663584 | tf_op jit(solution)/shard_map/ppermute | solution.py:23
  312.8 3.9 %shard_map.74 = f32[12288,128]{1,0:T(8,128)} custom-call(s32[3]{0:T(128)S(1)} %pad_add_fusion.3.pos_ref, f32[128,128]{1,0:T(8,128)S(1)} %shard_map.72.inverse_ref, f32[12288,128]{1,0:T(8,128)} %shard_map.73.refs_0_, s16[2,272,128]{2,1,0:T(8,128)(2,1)S(1)} %pad_add_fusion.2.refs_1_, ...), custom_call_target="tpu_custom_call", output_to_operand_aliasing={{}: (2, {})} | custom-call | tf_op jit(solution)/shard_map/pallas_call | solution.py:286
  (126 shorter events, 125.9 us)
Async XLA Ops:
  32.4 17.7 %collective-permute-start.2 = (bf16[2,1280,128]{2,1,0:T(8,128)(2,1)S(1)}, bf16[2,1280,128]{2,1,0:T(8,128)(2,1)S(1)}, u32[]{:S(2)}, u32[]{:S(2)}) collective-permute-start(bf16[2,1280,128]{2,1,0:T(8,128)(2,1)S(1)} %shard_map.48), channel_id=1, source_target_pairs={{0,4},{4,0},{8,12},{12,8},{16,20},{20,16},{24,28},{28,24},{1,5},{5... | collective-permute-start | bytes 1966088 | tf_op jit(solution)/shard_map/ppermute | solution.py:23
  34.2 28.5 %collective-permute-start.6 = (bf16[2,1280,128]{2,1,0:T(8,128)(2,1)S(1)}, bf16[2,1280,128]{2,1,0:T(8,128)(2,1)S(1)}, u32[]{:S(2)}, u32[]{:S(2)}) collective-permute-start(bf16[2,1280,128]{2,1,0:T(8,128)(2,1)S(1)} %shard_map.46), channel_id=1, source_target_pairs={{0,4},{4,0},{8,12},{12,8},{16,20},{20,16},{24,28},{28,24},{1,5},{5... | collective-permute-start | bytes 1966088 | tf_op jit(solution)/shard_map/ppermute | solution.py:23
  50.9 25.8 %collective-permute-start.9 = (bf16[1280,128]{1,0:T(8,128)(2,1)}, bf16[1280,128]{1,0:T(8,128)(2,1)}, u32[]{:S(2)}, u32[]{:S(2)}) collective-permute-start(bf16[1280,128]{1,0:T(8,128)(2,1)} %get-tuple-element.65), channel_id=1, source_target_pairs={{0,8},{4,12},{8,0},{12,4},{16,24},{20,28},{24,16},{28,20},{1,9},{5... | collective-permute-start | bytes 983048 | tf_op jit(solution)/shard_map/ppermute | solution.py:23
  63.7 24.4 %collective-permute-start.7 = (bf16[1280,128]{1,0:T(8,128)(2,1)}, bf16[1280,128]{1,0:T(8,128)(2,1)}, u32[]{:S(2)}, u32[]{:S(2)}) collective-permute-start(bf16[1280,128]{1,0:T(8,128)(2,1)} %get-tuple-element.63), channel_id=1, source_target_pairs={{0,16},{4,20},{8,24},{12,28},{16,0},{20,4},{24,8},{28,12},{1,17},{... | collective-permute-start | bytes 983048 | tf_op jit(solution)/shard_map/ppermute | solution.py:23
  66.2 21.8 %collective-permute-start.8 = (bf16[1280,128]{1,0:T(8,128)(2,1)}, bf16[1280,128]{1,0:T(8,128)(2,1)}, u32[]{:S(2)}, u32[]{:S(2)}) collective-permute-start(bf16[1280,128]{1,0:T(8,128)(2,1)} %get-tuple-element.64), channel_id=1, source_target_pairs={{0,24},{4,28},{8,16},{12,20},{16,8},{20,12},{24,0},{28,4},{1,25},{... | collective-permute-start | bytes 983048 | tf_op jit(solution)/shard_map/ppermute | solution.py:23
  75.2 30.3 %collective-permute-start.14 = (bf16[256,128]{1,0:T(8,128)(2,1)S(1)}, bf16[256,128]{1,0:T(8,128)(2,1)}, u32[]{:S(2)}, u32[]{:S(2)}) collective-permute-start(bf16[256,128]{1,0:T(8,128)(2,1)S(1)} %shard_map.56), channel_id=1, source_target_pairs={{0,4},{4,0},{8,12},{12,8},{16,20},{20,16},{24,28},{28,24},{1,5},{5... | collective-permute-start | bytes 196616 | tf_op jit(solution)/shard_map/ppermute | solution.py:23
  91.9 35.0 %collective-permute-start.11 = (bf16[1280,128]{1,0:T(8,128)(2,1)S(1)}, bf16[1280,128]{1,0:T(8,128)(2,1)S(1)}, u32[]{:S(2)}, u32[]{:S(2)}) collective-permute-start(bf16[1280,128]{1,0:T(8,128)(2,1)S(1)} %shard_map.53.refs_6_), channel_id=1, source_target_pairs={{0,16},{4,20},{8,24},{12,28},{16,0},{20,4},{24,8},{28,12},{1,17},{... | collective-permute-start | bytes 983048 | tf_op jit(solution)/shard_map/ppermute | solution.py:23
  105.0 21.9 %collective-permute-start.10 = (bf16[1280,128]{1,0:T(8,128)(2,1)S(1)}, bf16[1280,128]{1,0:T(8,128)(2,1)S(1)}, u32[]{:S(2)}, u32[]{:S(2)}) collective-permute-start(bf16[1280,128]{1,0:T(8,128)(2,1)S(1)} %shard_map.53.refs_6_), channel_id=1, source_target_pairs={{0,8},{4,12},{8,0},{12,4},{16,24},{20,28},{24,16},{28,20},{1,9},{5... | collective-permute-start | bytes 983048 | tf_op jit(solution)/shard_map/ppermute | solution.py:23
  126.9 17.7 %collective-permute-start.15 = (bf16[2,1280,128]{2,1,0:T(8,128)(2,1)S(1)}, bf16[2,1280,128]{2,1,0:T(8,128)(2,1)S(1)}, u32[]{:S(2)}, u32[]{:S(2)}) collective-permute-start(bf16[2,1280,128]{2,1,0:T(8,128)(2,1)S(1)} %pad_maximum_fusion), channel_id=1, source_target_pairs={{0,4},{4,0},{8,12},{12,8},{16,20},{20,16},{24,28},{28,24},{1,5},{5... | collective-permute-start | bytes 1966088 | tf_op jit(solution)/shard_map/ppermute | solution.py:23
  128.6 28.6 %collective-permute-start.19 = (bf16[2,1280,128]{2,1,0:T(8,128)(2,1)S(1)}, bf16[2,1280,128]{2,1,0:T(8,128)(2,1)S(1)}, u32[]{:S(2)}, u32[]{:S(2)}) collective-permute-start(bf16[2,1280,128]{2,1,0:T(8,128)(2,1)S(1)} %pad_maximum_fusion.1), channel_id=1, source_target_pairs={{0,4},{4,0},{8,12},{12,8},{16,20},{20,16},{24,28},{28,24},{1,5},{5... | collective-permute-start | bytes 1966088 | tf_op jit(solution)/shard_map/ppermute | solution.py:23
  129.1 23.2 %collective-permute-start.18 = (bf16[2,256,128]{2,1,0:T(8,128)(2,1)S(1)}, bf16[2,256,128]{2,1,0:T(8,128)(2,1)S(1)}, u32[]{:S(2)}, u32[]{:S(2)}) collective-permute-start(bf16[2,256,128]{2,1,0:T(8,128)(2,1)S(1)} %pad_maximum_fusion.2), channel_id=1, source_target_pairs={{0,24},{4,28},{8,16},{12,20},{16,8},{20,12},{24,0},{28,4},{1,25},{... | collective-permute-start | bytes 393224 | tf_op jit(solution)/shard_map/ppermute | solution.py:23
  131.8 20.6 %collective-permute-start.17 = (bf16[2,256,128]{2,1,0:T(8,128)(2,1)S(1)}, bf16[2,256,128]{2,1,0:T(8,128)(2,1)S(1)}, u32[]{:S(2)}, u32[]{:S(2)}) collective-permute-start(bf16[2,256,128]{2,1,0:T(8,128)(2,1)S(1)} %pad_maximum_fusion.2), channel_id=1, source_target_pairs={{0,16},{4,20},{8,24},{12,28},{16,0},{20,4},{24,8},{28,12},{1,17},{... | collective-permute-start | bytes 393224 | tf_op jit(solution)/shard_map/ppermute | solution.py:23
  131.8 20.6 %collective-permute-start.16 = (bf16[2,256,128]{2,1,0:T(8,128)(2,1)S(1)}, bf16[2,256,128]{2,1,0:T(8,128)(2,1)S(1)}, u32[]{:S(2)}, u32[]{:S(2)}) collective-permute-start(bf16[2,256,128]{2,1,0:T(8,128)(2,1)S(1)} %pad_maximum_fusion.2), channel_id=1, source_target_pairs={{0,8},{4,12},{8,0},{12,4},{16,24},{20,28},{24,16},{28,20},{1,9},{5... | collective-permute-start | bytes 393224 | tf_op jit(solution)/shard_map/ppermute | solution.py:23
  186.5 17.8 %collective-permute-start.23 = (s16[2,1296,128]{2,1,0:T(8,128)(2,1)S(1)}, s16[2,1296,128]{2,1,0:T(8,128)(2,1)S(1)}, u32[]{:S(2)}, u32[]{:S(2)}) collective-permute-start(s16[2,1296,128]{2,1,0:T(8,128)(2,1)S(1)} %shard_map.63), channel_id=1, source_target_pairs={{0,4},{4,0},{8,12},{12,8},{16,20},{20,16},{24,28},{28,24},{1,5},{5... | collective-permute-start | bytes 1990664 | tf_op jit(solution)/shard_map/ppermute | solution.py:23
  188.1 29.6 %collective-permute-start.27 = (s16[2,1296,128]{2,1,0:T(8,128)(2,1)S(1)}, s16[2,1296,128]{2,1,0:T(8,128)(2,1)S(1)}, u32[]{:S(2)}, u32[]{:S(2)}) collective-permute-start(s16[2,1296,128]{2,1,0:T(8,128)(2,1)S(1)} %shard_map.61), channel_id=1, source_target_pairs={{0,4},{4,0},{8,12},{12,8},{16,20},{20,16},{24,28},{28,24},{1,5},{5... | collective-permute-start | bytes 1990664 | tf_op jit(solution)/shard_map/ppermute | solution.py:23
  205.0 25.0 %collective-permute-start.30 = (s16[1296,128]{1,0:T(8,128)(2,1)S(1)}, s16[1296,128]{1,0:T(8,128)(2,1)S(1)}, u32[]{:S(2)}, u32[]{:S(2)}) collective-permute-start(s16[1296,128]{1,0:T(8,128)(2,1)S(1)} %get-tuple-element.88), channel_id=1, source_target_pairs={{0,8},{4,12},{8,0},{12,4},{16,24},{20,28},{24,16},{28,20},{1,9},{5... | collective-permute-start | bytes 995336 | tf_op jit(solution)/shard_map/ppermute | solution.py:23
  218.4 24.0 %collective-permute-start.28 = (s16[1296,128]{1,0:T(8,128)(2,1)S(1)}, s16[1296,128]{1,0:T(8,128)(2,1)S(1)}, u32[]{:S(2)}, u32[]{:S(2)}) collective-permute-start(s16[1296,128]{1,0:T(8,128)(2,1)S(1)} %get-tuple-element.86), channel_id=1, source_target_pairs={{0,16},{4,20},{8,24},{12,28},{16,0},{20,4},{24,8},{28,12},{1,17},{... | collective-permute-start | bytes 995336 | tf_op jit(solution)/shard_map/ppermute | solution.py:23
  218.5 23.9 %collective-permute-start.29 = (s16[1296,128]{1,0:T(8,128)(2,1)S(1)}, s16[1296,128]{1,0:T(8,128)(2,1)S(1)}, u32[]{:S(2)}, u32[]{:S(2)}) collective-permute-start(s16[1296,128]{1,0:T(8,128)(2,1)S(1)} %get-tuple-element.87), channel_id=1, source_target_pairs={{0,24},{4,28},{8,16},{12,20},{16,8},{20,12},{24,0},{28,4},{1,25},{... | collective-permute-start | bytes 995336 | tf_op jit(solution)/shard_map/ppermute | solution.py:23
  228.4 25.9 %collective-permute-start.34 = (s16[272,128]{1,0:T(8,128)(2,1)S(1)}, s16[272,128]{1,0:T(8,128)(2,1)S(1)}, u32[]{:S(2)}, u32[]{:S(2)}) collective-permute-start(s16[272,128]{1,0:T(8,128)(2,1)S(1)} %get-tuple-element.96), channel_id=1, source_target_pairs={{0,4},{4,0},{8,12},{12,8},{16,20},{20,16},{24,28},{28,24},{1,5},{5... | collective-permute-start | bytes 208904 | tf_op jit(solution)/shard_map/ppermute | solution.py:23
  243.5 38.5 %collective-permute-start.41 = (s16[1296,128]{1,0:T(8,128)(2,1)S(1)}, s16[1296,128]{1,0:T(8,128)(2,1)S(1)}, u32[]{:S(2)}, u32[]{:S(2)}) collective-permute-start(s16[1296,128]{1,0:T(8,128)(2,1)S(1)} %get-tuple-element.89.refs_0_), channel_id=1, source_target_pairs={{0,8},{4,12},{8,0},{12,4},{16,24},{20,28},{24,16},{28,20},{1,9},{5... | collective-permute-start | bytes 995336 | tf_op jit(solution)/shard_map/ppermute | solution.py:23
  251.2 17.3 %collective-permute-start.32 = (s16[1296,128]{1,0:T(8,128)(2,1)S(1)}, s16[1296,128]{1,0:T(8,128)(2,1)S(1)}, u32[]{:S(2)}, u32[]{:S(2)}) collective-permute-start(s16[1296,128]{1,0:T(8,128)(2,1)S(1)} %get-tuple-element.89.refs_0_), channel_id=1, source_target_pairs={{0,24},{4,28},{8,16},{12,20},{16,8},{20,12},{24,0},{28,4},{1,25},{... | collective-permute-start | bytes 995336 | tf_op jit(solution)/shard_map/ppermute | solution.py:23
  252.7 29.4 %collective-permute-start.31 = (s16[1296,128]{1,0:T(8,128)(2,1)S(1)}, s16[1296,128]{1,0:T(8,128)(2,1)S(1)}, u32[]{:S(2)}, u32[]{:S(2)}) collective-permute-start(s16[1296,128]{1,0:T(8,128)(2,1)S(1)} %get-tuple-element.89.refs_0_), channel_id=1, source_target_pairs={{0,16},{4,20},{8,24},{12,28},{16,0},{20,4},{24,8},{28,12},{1,17},{... | collective-permute-start | bytes 995336 | tf_op jit(solution)/shard_map/ppermute | solution.py:23
  282.2 17.9 %collective-permute-start.42 = (s16[2,1296,128]{2,1,0:T(8,128)(2,1)S(1)}, s16[2,1296,128]{2,1,0:T(8,128)(2,1)S(1)}, u32[]{:S(2)}, u32[]{:S(2)}) collective-permute-start(s16[2,1296,128]{2,1,0:T(8,128)(2,1)S(1)} %pad_add_fusion), channel_id=1, source_target_pairs={{0,4},{4,0},{8,12},{12,8},{16,20},{20,16},{24,28},{28,24},{1,5},{5... | collective-permute-start | bytes 1990664 | tf_op jit(solution)/shard_map/ppermute | solution.py:23
  283.8 29.0 %collective-permute-start.46 = (s16[2,1296,128]{2,1,0:T(8,128)(2,1)S(1)}, s16[2,1296,128]{2,1,0:T(8,128)(2,1)S(1)}, u32[]{:S(2)}, u32[]{:S(2)}) collective-permute-start(s16[2,1296,128]{2,1,0:T(8,128)(2,1)S(1)} %pad_add_fusion.1), channel_id=1, source_target_pairs={{0,4},{4,0},{8,12},{12,8},{16,20},{20,16},{24,28},{28,24},{1,5},{5... | collective-permute-start | bytes 1990664 | tf_op jit(solution)/shard_map/ppermute | solution.py:23
  (26 other events, 216.9 us)

commit v2 on v1

--- a/solution.py
+++ b/solution.py
@@ -16,6 +16,7 @@
 GROUP = 8
 LANES = 128
 VMEM_BYTES = 48 << 20
+LIGHT = pl.CostEstimate(flops=1, bytes_accessed=1, transcendentals=0)
 WHOLE = pl.BlockSpec(memory_space=pltpu.VMEM)
 
 
@@ -72,7 +73,7 @@
     def __init__(self, voxels, subjects):
         self.high = subjects // LOW
         unit = subjects * LANES
-        for top, bottom in ((5, 6), (3, 4), (2, 3), (1, 2)):
+        for top, bottom in ((2, 3), (1, 2)):
             self.cut = voxels * top // bottom
             self.pair = (voxels - self.cut) // self.high
             if self.cut % unit == 0 and voxels % unit == 0 and self.cut % self.pair == 0:
@@ -124,11 +125,7 @@
             out_specs=out_specs,
         ),
         compiler_params=params(),
-        cost_estimate=pl.CostEstimate(
-            flops=2 * time_rows * n * rank * len(ks),
-            bytes_accessed=time_rows * n * 2 * len(ks),
-            transcendentals=0,
-        ),
+        cost_estimate=LIGHT,
     )(pos, scores, *([scans] * per_step))
 
 
@@ -139,6 +136,7 @@
         in_specs=[WHOLE] * len(args),
         out_specs=jax.tree.map(lambda _: WHOLE, out_shape),
         compiler_params=params(),
+        cost_estimate=LIGHT,
     )(*args)
 
 
@@ -227,7 +225,6 @@
     rows = time_rows + rank
     shape = (rows // 2, rank) if split else (rows, rank)
     out_shape = [jax.ShapeDtypeStruct(shape, F32)] * (2 if split else 1)
-    columns = sum(layout.columns(j) for j, _ in names)
     out = pl.pallas_call(
         functools.partial(project_kernel, base is not None, split, items),
         out_shape=out_shape,
@@ -240,10 +237,7 @@
             out_specs=[full(shape)] * len(out_shape),
         ),
         compiler_params=params(),
-        cost_estimate=pl.CostEstimate(
-            flops=2 * rows * columns * rank, bytes_accessed=time_rows * columns * 2,
-            transcendentals=0,
-        ),
+        cost_estimate=LIGHT,
     )(pos, *bases, *([scans] * len(items)), *arrays)
     return out if split else out[0]
 
@@ -400,27 +394,18 @@
                     scans, layout, pos, ordered, j, ks, code, apart, per_step
                 )
 
-            def add_pieces(home, got, count):
-                piece = jax.ShapeDtypeStruct((layout.single + code.pad, rank), code.dtype)
-                return small_call(
-                    functools.partial(add_pieces_kernel, code, count), [piece] * count, home, got
-                )
-
-            away_far = part(None, 1, far, False, 1)
-            got_far = swap(away_far, mask=1)
-            second = part(away_far, None, ks[1:], True, high - 1)
+            away = part(None, 1, ks, False, high // 2)
+            got_away = swap(away, mask=1)
+            second = part(away, None, ks[1:], True, high - 1)
             got_second = [swap(second[k - 1], mask=k * LOW) for k in ks[1:]]
-            away_near = part(second[0], 1, near, False, 1)
-            got_near = swap(away_near, mask=1)
-            home_far = part(away_near, 0, far, False, 1)
-            home_near = part(home_far, 0, near, False, 1)
-            (second_own,) = part(home_near, None, ks[:1], True, 1)
-
-            first_far = add_pieces(home_far, got_far, len(far))
-            got_first = [swap(first_far[k - far[0]], mask=k * LOW) for k in far]
-            got_near, *got_second = lax.optimization_barrier((got_near, *got_second))
-            first_near = add_pieces(home_near, got_near, len(near))
-            got_first += [swap(first_near[k], mask=k * LOW) for k in near[1:]]
+            home = part(second[0], 0, ks, False, high // 2)
+            (second_own,) = part(second[0], None, ks[:1], True, 1)
+            got_away, *got_second = lax.optimization_barrier((got_away, *got_second))
+            piece = jax.ShapeDtypeStruct((layout.single + code.pad, rank), code.dtype)
+            first = small_call(
+                functools.partial(add_pieces_kernel, code, high), [piece] * high, home, got_away
+            )
+            got_first = [swap(first[k], mask=k * LOW) for k in ks[1:]]
 
             half = jax.ShapeDtypeStruct((layout.pair // 2 + code.pad, rank), code.dtype)
             keep, send = pl.pallas_call(
@@ -432,7 +417,7 @@
             )(pos, second_own, *got_second)
             got_send = swap(send, mask=1)
             return (
-                add_all(code, with_gram, [first_near[0], *got_first]),
+                add_all(code, with_gram, [first[0], *got_first]),
                 add_all(code, with_gram, [keep, got_send]),
             )
 
@@ -456,20 +441,21 @@
             if gram is not None:
                 gram = [gram] + [swap(gram, mask=k * LOW) for k in ks[1:]]
             early = [(0, [k], array) for k, array in zip(near + far, near_in + far_in)]
-            early.append((1, near, low_near))
+            late = [(1, near, low_near), (1, far, low_far)]
             pairs = [(None, [k], array) for k, array in zip(ks, seconds)]
-            return early, pairs, (1, far, low_far), gram
+            return early, late, pairs, gram
 
         partial = jnp.dot(scans, test_matrix, preferred_element_type=F32)
         summed = sum(butterfly(partial, "vox", blocks))
         scores = jnp.where(live_rows, summed, 0.0).astype(BF16)
 
         (first,), (second,) = sketch_sum(scores, Plain, False)
-        early, pairs, last, _ = gather(first, second)
+        early, late, pairs, _ = gather(first, second)
         pairs = [(j, k, array.reshape(layout.pair, rank)) for j, k, array in pairs]
         both = project(scans, layout, pos, early)
-        both = project(scans, layout, pos, pairs, both)
-        mine, send = project(scans, layout, pos, [last], both, True)
+        both = project(scans, layout, pos, late, both)
+        both = project(scans, layout, pos, pairs[: high // 2], both)
+        mine, send = project(scans, layout, pos, pairs[high // 2 :], both, True)
         mine = mine + swap_vox(send, mask=1)
         mask = 2
         while mask < blocks:
@@ -485,13 +471,13 @@
         )(length[None], pos, mine, other)
 
         (first, gram_first), (second, gram_second) = sketch_sum(scores, Fixed, True)
-        early, pairs, last, grams = gather(first, second, gram_first + gram_second)
+        early, late, pairs, grams = gather(first, second, gram_first + gram_second)
         inverse = small_call(
             functools.partial(invert_kernel, all_voxels),
             jax.ShapeDtypeStruct((rank, rank), F32), *grams,
         )
-        out = finish(layout, pos, early, inverse, voxels)
-        return finish(layout, pos, pairs + [last], inverse, voxels, out)
+        out = finish(layout, pos, early + late, inverse, voxels)
+        return finish(layout, pos, pairs, inverse, voxels, out)
 
     return on_device
 

time: 317 us -> 283 us (0.89)
  waiting for transfers between devices: 147 us -> 104 us
  starting transfers between devices: 78 us -> 92.2 us
  Pallas kernels: 77.1 us -> 70.4 us
    ppermute x47 -> x45, waiting for transfers between devices: 147 us -> 104 us  [exchange(): return lax.ppermute(value, axis, [(i, i ^ mask) for i in range(size)])]
    ppermute x47 -> x45, starting transfers between devices: 78 us -> 92.2 us  [exchange(): return lax.ppermute(value, axis, [(i, i ^ mask) for i in range(size)])]
    pallas_call x12 -> x8, Pallas kernels: 35.8 us -> 28.3 us  [sketch_part(): pl.pallas_call(functools.partial(sketch_kernel, code, apart, per_step), o...]
    pallas_call x3 -> x4, Pallas kernels: 14.6 us -> 16.3 us  [project(): pl.pallas_call(functools.partial(project_kernel, base is not None, split,...]
    pallas_call x9 -> x7, Pallas kernels: 9.8 us -> 8.61 us  [small_call(): pl.pallas_call(kernel, out_shape=out_shape, in_specs=[WHOLE] * len(args),...]
  transfers between devices with their start and end apart: 47 -> 45, of which waited for: 28 -> 23; matrix products, arithmetic and copies ran while one was open for 1% -> 1% of each run, Pallas kernels for 14% -> 17%
where the time goes in v2:
time: 283 us; the launch traced here: 282 us
  waiting for transfers between devices  104 us (37%)
  starting transfers between devices  92.2 us (33%)
  Pallas kernels  70.4 us (25%)
  matrix products  7.68 us (3%)
  other arithmetic  5.15 us (2%)
    ppermute x45, waiting for transfers between devices, exchange(): return lax.ppermute(value, axis, [(i, i ^ mask) for i in range(size)])  104 us
    ppermute x45, starting transfers between devices, exchange(): return lax.ppermute(value, axis, [(i, i ^ mask) for i in range(size)])  92.2 us
    pallas_call x8, Pallas kernels, sketch_part(): pl.pallas_call(functools.partial(sketch_kernel, code, apart, per_step), o...  28.3 us
    pallas_call x4, Pallas kernels, project(): pl.pallas_call(functools.partial(project_kernel, base is not None, split,...  16.3 us
    pallas_call x2, Pallas kernels, finish(): pl.pallas_call(functools.partial(finish_kernel, layout, items, base is no...  9.4 us
    pallas_call x7, Pallas kernels, small_call(): pl.pallas_call(kernel, out_shape=out_shape, in_specs=[WHOLE] * len(args),...  8.61 us
    dot_general x1, matrix products, on_device(): partial = jnp.dot(scans, test_matrix, preferred_element_type=F32)  7.68 us
    pallas_call x1, Pallas kernels, on_device(): pl.pallas_call(functools.partial(normalise_kernel, all_voxels), out_shape...  6.09 us
  transfers between devices with their start and end apart: 45, of which 23 were waited for; matrix products, arithmetic and copies ran while one was open for 1% of the time, Pallas kernels for 17%

profile of v2, /device:TPU:0, one launch (start us, length us, event | category | flops | bytes accessed | tf_op | source)
XLA Modules:
  0.0 282.2 jit_solution(15452157732473029891)
XLA Ops:
  1.9 7.7 %fusion.2 = f32[640,128]{1,0:T(8,128)S(1)} fusion(bf16[640,12288]{1,0:T(8,128)(2,1)} %refs_0_.17, bf16[12288,128]{1,0:T(8,128)(2,1)S(1)} %copy-done), kind=kOutput, calls=%fused_computation.17 | convolution fusion | flops 2013265920 | bytes 19202048 | tf_op jit(solution)/shard_map/dot_general | solution.py:448
  17.4 6.0 %collective-permute-done.1 = f32[640,128]{1,0:T(8,128)S(1)} collective-permute-done((f32[640,128]{1,0:T(8,128)S(1)}, f32[640,128]{1,0:T(8,128)S(1)}, u32[]{:S(2)}, u32[]{:S(2)}) %collective-permute-start.1) | collective-permute-done | bytes 327712 | tf_op jit(solution)/shard_map/ppermute | solution.py:24
  43.3 10.1 %collective-permute-done.4.refs_2_ = bf16[1024,128]{1,0:T(8,128)(2,1)S(1)} collective-permute-done((bf16[1024,128]{1,0:T(8,128)(2,1)S(1)}, bf16[1024,128]{1,0:T(8,128)(2,1)S(1)}, u32[]{:S(2)}, u32[]{:S(2)}) %collective-permute-start.4) | collective-permute-done | bytes 262176 | tf_op jit(solution)/shard_map/ppermute | solution.py:24
  54.6 5.0 %collective-permute-start.6 = (bf16[1024,128]{1,0:T(8,128)(2,1)}, bf16[1024,128]{1,0:T(8,128)(2,1)}, u32[]{:S(2)}, u32[]{:S(2)}) collective-permute-start(bf16[1024,128]{1,0:T(8,128)(2,1)} %get-tuple-element.55), channel_id=1, source_target_pairs={{0,8},{4,12},{8,0},{12,4},{16,24},{20,28},{24,16},{28,20},{1,9},{5... | collective-permute-start | bytes 786440 | tf_op jit(solution)/shard_map/ppermute | solution.py:24
  64.2 4.5 %collective-permute-done.12.refs_1_ = bf16[512,128]{1,0:T(8,128)(2,1)S(1)} collective-permute-done((bf16[512,128]{1,0:T(8,128)(2,1)S(1)}, bf16[512,128]{1,0:T(8,128)(2,1)S(1)}, u32[]{:S(2)}, u32[]{:S(2)}) %collective-permute-start.12) | collective-permute-done | bytes 131104 | tf_op jit(solution)/shard_map/ppermute | solution.py:24
  71.8 9.5 %collective-permute-done.7.refs_2_ = bf16[1024,128]{1,0:T(8,128)(2,1)} collective-permute-done((bf16[1024,128]{1,0:T(8,128)(2,1)}, bf16[1024,128]{1,0:T(8,128)(2,1)}, u32[]{:S(2)}, u32[]{:S(2)}) %collective-permute-start.7) | collective-permute-done | bytes 262176 | tf_op jit(solution)/shard_map/ppermute | solution.py:24
  85.9 12.3 %collective-permute-start.10 = (bf16[1024,128]{1,0:T(8,128)(2,1)S(1)}, bf16[1024,128]{1,0:T(8,128)(2,1)S(1)}, u32[]{:S(2)}, u32[]{:S(2)}) collective-permute-start(bf16[1024,128]{1,0:T(8,128)(2,1)S(1)} %shard_map.50.refs_4_), channel_id=1, source_target_pairs={{0,16},{4,20},{8,24},{12,28},{16,0},{20,4},{24,8},{28,12},{1,17},{... | collective-permute-start | bytes 786440 | tf_op jit(solution)/shard_map/ppermute | solution.py:24
  99.7 10.6 %collective-permute-done.10.refs_6_ = bf16[1024,128]{1,0:T(8,128)(2,1)S(1)} collective-permute-done((bf16[1024,128]{1,0:T(8,128)(2,1)S(1)}, bf16[1024,128]{1,0:T(8,128)(2,1)S(1)}, u32[]{:S(2)}, u32[]{:S(2)}) %collective-permute-start.10) | collective-permute-done | bytes 262176 | tf_op jit(solution)/shard_map/ppermute | solution.py:24
  112.6 6.7 %collective-permute-start.16 = (bf16[2,512,128]{2,1,0:T(8,128)(2,1)S(1)}, bf16[2,512,128]{2,1,0:T(8,128)(2,1)S(1)}, u32[]{:S(2)}, u32[]{:S(2)}) collective-permute-start(bf16[2,512,128]{2,1,0:T(8,128)(2,1)S(1)} %pad_maximum_fusion.2), channel_id=1, source_target_pairs={{0,8},{4,12},{8,0},{12,4},{16,24},{20,28},{24,16},{28,20},{1,9},{5... | collective-permute-start | bytes 786440 | tf_op jit(solution)/shard_map/ppermute | solution.py:24
  122.6 4.9 %shard_map.54.refs_0_ = f32[768,128]{1,0:T(8,128)S(1)} custom-call(s32[3]{0:T(128)S(1)} %pad_add_fusion.3.pos_ref, bf16[640,12288]{1,0:T(8,128)(2,1)} %refs_0_.17, bf16[640,12288]{1,0:T(8,128)(2,1)} %refs_0_.17, bf16[640,12288]{1,0:T(8,128)(2,1)} %refs_0_.17, bf16[640,12288]{1,0:T(8,128)(2,1)} %refs_0_.17, bf16[1024,128]{1,0:T(8,128)(2,1)S(1)} %shard_map.50.refs_4_, ...), custom_call_target="tpu_custom_call" | custom-call | flops 1 | bytes 1 | tf_op jit(solution)/shard_map/pallas_call | solution.py:228
  127.5 4.9 %shard_map.55.refs_0_ = f32[768,128]{1,0:T(8,128)S(1)} custom-call(s32[3]{0:T(128)S(1)} %pad_add_fusion.3.pos_ref, f32[768,128]{1,0:T(8,128)S(1)} %shard_map.54.refs_0_, bf16[640,12288]{1,0:T(8,128)(2,1)} %refs_0_.17, bf16[640,12288]{1,0:T(8,128)(2,1)} %refs_0_.17, bf16[640,12288]{1,0:T(8,128)(2,1)} %refs_0_.17, bf16[640,12288]{1,0:T(8,128)(2,1)} %refs_0_.17, ...), custom_call_target="tpu_custom_call" | custom-call | flops 1 | bytes 1 | tf_op jit(solution)/shard_map/pallas_call | solution.py:228
  142.1 5.5 %collective-permute-done.20 = f32[384,128]{1,0:T(8,128)S(1)} collective-permute-done((f32[384,128]{1,0:T(8,128)S(1)}, f32[384,128]{1,0:T(8,128)S(1)}, u32[]{:S(2)}, u32[]{:S(2)}) %collective-permute-start.20) | collective-permute-done | bytes 196640 | tf_op jit(solution)/shard_map/ppermute | solution.py:24
  149.1 6.1 %shard_map.58.scores_ref = bf16[640,128]{1,0:T(8,128)(2,1)S(1)} custom-call(s32[1]{0:T(128)} %bitcast.3.length_ref, s32[3]{0:T(128)S(1)} %pad_add_fusion.3.pos_ref, f32[384,128]{1,0:T(8,128)S(1)} %add.37.mine_ref, f32[384,128]{1,0:T(8,128)S(1)} %collective-permute-done.21.other_ref), custom_call_target="tpu_custom_call" | custom-call | tf_op jit(solution)/shard_map/pallas_call | solution.py:465
  155.2 4.1 %shard_map.59 = s16[4,1040,128]{2,1,0:T(8,128)(2,1)S(1)} custom-call(s32[3]{0:T(128)S(1)} %pad_add_fusion.3.pos_ref, bf16[640,128]{1,0:T(8,128)(2,1)S(1)} %shard_map.58.scores_ref, bf16[640,12288]{1,0:T(8,128)(2,1)} %refs_0_.17, bf16[640,12288]{1,0:T(8,128)(2,1)} %refs_0_.17), custom_call_target="tpu_custom_call" | custom-call | flops 1 | bytes 1 | tf_op jit(solution)/shard_map/pallas_call | solution.py:117
  166.1 4.9 %collective-permute-start.25 = (s16[1040,128]{1,0:T(8,128)(2,1)S(1)}, s16[1040,128]{1,0:T(8,128)(2,1)S(1)}, u32[]{:S(2)}, u32[]{:S(2)}) collective-permute-start(s16[1040,128]{1,0:T(8,128)(2,1)S(1)} %get-tuple-element.72), channel_id=1, source_target_pairs={{0,24},{4,28},{8,16},{12,20},{16,8},{20,12},{24,0},{28,4},{1,25},{... | collective-permute-start | bytes 798728 | tf_op jit(solution)/shard_map/ppermute | solution.py:24
  171.5 4.3 %shard_map.61.own_ref = s16[4,1040,128]{2,1,0:T(8,128)(2,1)S(1)} custom-call(s32[3]{0:T(128)S(1)} %pad_add_fusion.3.pos_ref, bf16[640,128]{1,0:T(8,128)(2,1)S(1)} %shard_map.58.scores_ref, bf16[640,12288]{1,0:T(8,128)(2,1)} %refs_0_.17, bf16[640,12288]{1,0:T(8,128)(2,1)} %refs_0_.17), custom_call_target="tpu_custom_call" | custom-call | flops 1 | bytes 1 | tf_op jit(solution)/shard_map/pallas_call | solution.py:117
  175.8 9.5 %collective-permute-done.24.refs_2_ = s16[1040,128]{1,0:T(8,128)(2,1)S(1)} collective-permute-done((s16[1040,128]{1,0:T(8,128)(2,1)S(1)}, s16[1040,128]{1,0:T(8,128)(2,1)S(1)}, u32[]{:S(2)}, u32[]{:S(2)}) %collective-permute-start.24) | collective-permute-done | bytes 266272 | tf_op jit(solution)/shard_map/ppermute | solution.py:24
  186.7 5.0 %collective-permute-start.26 = (s16[1040,128]{1,0:T(8,128)(2,1)S(1)}, s16[1040,128]{1,0:T(8,128)(2,1)S(1)}, u32[]{:S(2)}, u32[]{:S(2)}) collective-permute-start(s16[1040,128]{1,0:T(8,128)(2,1)S(1)} %get-tuple-element.75), channel_id=1, source_target_pairs={{0,8},{4,12},{8,0},{12,4},{16,24},{20,28},{24,16},{28,20},{1,9},{5... | collective-permute-start | bytes 798728 | tf_op jit(solution)/shard_map/ppermute | solution.py:24
  205.4 7.8 %collective-permute-done.27.refs_2_ = s16[1040,128]{1,0:T(8,128)(2,1)S(1)} collective-permute-done((s16[1040,128]{1,0:T(8,128)(2,1)S(1)}, s16[1040,128]{1,0:T(8,128)(2,1)S(1)}, u32[]{:S(2)}, u32[]{:S(2)}) %collective-permute-start.27) | collective-permute-done | bytes 266272 | tf_op jit(solution)/shard_map/ppermute | solution.py:24
  214.2 5.0 %collective-permute-start.39 = (s16[1040,128]{1,0:T(8,128)(2,1)S(1)}, s16[1040,128]{1,0:T(8,128)(2,1)S(1)}, u32[]{:S(2)}, u32[]{:S(2)}) collective-permute-start(s16[1040,128]{1,0:T(8,128)(2,1)S(1)} %get-tuple-element.78.refs_0_), channel_id=1, source_target_pairs={{0,8},{4,12},{8,0},{12,4},{16,24},{20,28},{24,16},{28,20},{1,9},{5... | collective-permute-start | bytes 798728 | tf_op jit(solution)/shard_map/ppermute | solution.py:24
  231.3 4.3 %collective-permute-done.30.refs_3_ = s16[1040,128]{1,0:T(8,128)(2,1)S(1)} collective-permute-done((s16[1040,128]{1,0:T(8,128)(2,1)S(1)}, s16[1040,128]{1,0:T(8,128)(2,1)S(1)}, u32[]{:S(2)}, u32[]{:S(2)}) %collective-permute-start.30) | collective-permute-done | bytes 266272 | tf_op jit(solution)/shard_map/ppermute | solution.py:24
  235.5 9.7 %collective-permute-done.29.refs_2_ = s16[1040,128]{1,0:T(8,128)(2,1)S(1)} collective-permute-done((s16[1040,128]{1,0:T(8,128)(2,1)S(1)}, s16[1040,128]{1,0:T(8,128)(2,1)S(1)}, u32[]{:S(2)}, u32[]{:S(2)}) %collective-permute-start.29) | collective-permute-done | bytes 266272 | tf_op jit(solution)/shard_map/ppermute | solution.py:24
  263.1 7.4 %collective-permute-done.41.refs_5_ = s16[2,1040,128]{2,1,0:T(8,128)(2,1)S(1)} collective-permute-done((s16[2,1040,128]{2,1,0:T(8,128)(2,1)S(1)}, s16[2,1040,128]{2,1,0:T(8,128)(2,1)S(1)}, u32[]{:S(2)}, u32[]{:S(2)}) %collective-permute-start.41) | collective-permute-done | bytes 532512 | tf_op jit(solution)/shard_map/ppermute | solution.py:24
  270.5 5.8 %shard_map.68.refs_0_ = f32[12288,128]{1,0:T(8,128)} custom-call(s32[3]{0:T(128)S(1)} %pad_add_fusion.3.pos_ref, f32[128,128]{1,0:T(8,128)S(1)} %shard_map.67.inverse_ref, s16[1040,128]{1,0:T(8,128)(2,1)S(1)} %get-tuple-element.78.refs_0_, s16[1040,128]{1,0:T(8,128)(2,1)S(1)} %collective-permute-done.39.refs_1_, ...), custom_call_target="tpu_custom_call" | custom-call | tf_op jit(solution)/shard_map/pallas_call | solution.py:280
  (117 shorter events, 120.4 us)
Async XLA Ops:
  27.4 26.2 %collective-permute-start.2 = (bf16[4,1024,128]{2,1,0:T(8,128)(2,1)S(1)}, bf16[4,1024,128]{2,1,0:T(8,128)(2,1)S(1)}, u32[]{:S(2)}, u32[]{:S(2)}) collective-permute-start(bf16[4,1024,128]{2,1,0:T(8,128)(2,1)S(1)} %shard_map.46), channel_id=1, source_target_pairs={{0,4},{4,0},{8,12},{12,8},{16,20},{20,16},{24,28},{28,24},{1,5},{5... | collective-permute-start | bytes 3145736 | tf_op jit(solution)/shard_map/ppermute | solution.py:24
  32.8 20.6 %collective-permute-start.4 = (bf16[1024,128]{1,0:T(8,128)(2,1)S(1)}, bf16[1024,128]{1,0:T(8,128)(2,1)S(1)}, u32[]{:S(2)}, u32[]{:S(2)}) collective-permute-start(bf16[1024,128]{1,0:T(8,128)(2,1)S(1)} %get-tuple-element.51), channel_id=1, source_target_pairs={{0,16},{4,20},{8,24},{12,28},{16,0},{20,4},{24,8},{28,12},{1,17},{... | collective-permute-start | bytes 786440 | tf_op jit(solution)/shard_map/ppermute | solution.py:24
  35.4 18.0 %collective-permute-start.5 = (bf16[1024,128]{1,0:T(8,128)(2,1)S(1)}, bf16[1024,128]{1,0:T(8,128)(2,1)S(1)}, u32[]{:S(2)}, u32[]{:S(2)}) collective-permute-start(bf16[1024,128]{1,0:T(8,128)(2,1)S(1)} %get-tuple-element.52), channel_id=1, source_target_pairs={{0,24},{4,28},{8,16},{12,20},{16,8},{20,12},{24,0},{28,4},{1,25},{... | collective-permute-start | bytes 786440 | tf_op jit(solution)/shard_map/ppermute | solution.py:24
  54.6 17.2 %collective-permute-start.6 = (bf16[1024,128]{1,0:T(8,128)(2,1)}, bf16[1024,128]{1,0:T(8,128)(2,1)}, u32[]{:S(2)}, u32[]{:S(2)}) collective-permute-start(bf16[1024,128]{1,0:T(8,128)(2,1)} %get-tuple-element.55), channel_id=1, source_target_pairs={{0,8},{4,12},{8,0},{12,4},{16,24},{20,28},{24,16},{28,20},{1,9},{5... | collective-permute-start | bytes 786440 | tf_op jit(solution)/shard_map/ppermute | solution.py:24
  59.6 21.7 %collective-permute-start.7 = (bf16[1024,128]{1,0:T(8,128)(2,1)}, bf16[1024,128]{1,0:T(8,128)(2,1)}, u32[]{:S(2)}, u32[]{:S(2)}) collective-permute-start(bf16[1024,128]{1,0:T(8,128)(2,1)} %get-tuple-element.56), channel_id=1, source_target_pairs={{0,16},{4,20},{8,24},{12,28},{16,0},{20,4},{24,8},{28,12},{1,17},{... | collective-permute-start | bytes 786440 | tf_op jit(solution)/shard_map/ppermute | solution.py:24
  61.5 19.7 %collective-permute-start.8 = (bf16[1024,128]{1,0:T(8,128)(2,1)}, bf16[1024,128]{1,0:T(8,128)(2,1)}, u32[]{:S(2)}, u32[]{:S(2)}) collective-permute-start(bf16[1024,128]{1,0:T(8,128)(2,1)} %get-tuple-element.57), channel_id=1, source_target_pairs={{0,24},{4,28},{8,16},{12,20},{16,8},{20,12},{24,0},{28,4},{1,25},{... | collective-permute-start | bytes 786440 | tf_op jit(solution)/shard_map/ppermute | solution.py:24
  68.7 30.0 %collective-permute-start.13 = (bf16[512,128]{1,0:T(8,128)(2,1)S(1)}, bf16[512,128]{1,0:T(8,128)(2,1)}, u32[]{:S(2)}, u32[]{:S(2)}) collective-permute-start(bf16[512,128]{1,0:T(8,128)(2,1)S(1)} %shard_map.53), channel_id=1, source_target_pairs={{0,4},{4,0},{8,12},{12,8},{16,20},{20,16},{24,28},{28,24},{1,5},{5... | collective-permute-start | bytes 393224 | tf_op jit(solution)/shard_map/ppermute | solution.py:24
  82.5 17.2 %collective-permute-start.11 = (bf16[1024,128]{1,0:T(8,128)(2,1)S(1)}, bf16[1024,128]{1,0:T(8,128)(2,1)S(1)}, u32[]{:S(2)}, u32[]{:S(2)}) collective-permute-start(bf16[1024,128]{1,0:T(8,128)(2,1)S(1)} %shard_map.50.refs_4_), channel_id=1, source_target_pairs={{0,24},{4,28},{8,16},{12,20},{16,8},{20,12},{24,0},{28,4},{1,25},{... | collective-permute-start | bytes 786440 | tf_op jit(solution)/shard_map/ppermute | solution.py:24
  85.9 24.4 %collective-permute-start.10 = (bf16[1024,128]{1,0:T(8,128)(2,1)S(1)}, bf16[1024,128]{1,0:T(8,128)(2,1)S(1)}, u32[]{:S(2)}, u32[]{:S(2)}) collective-permute-start(bf16[1024,128]{1,0:T(8,128)(2,1)S(1)} %shard_map.50.refs_4_), channel_id=1, source_target_pairs={{0,16},{4,20},{8,24},{12,28},{16,0},{20,4},{24,8},{28,12},{1,17},{... | collective-permute-start | bytes 786440 | tf_op jit(solution)/shard_map/ppermute | solution.py:24
  112.6 19.9 %collective-permute-start.16 = (bf16[2,512,128]{2,1,0:T(8,128)(2,1)S(1)}, bf16[2,512,128]{2,1,0:T(8,128)(2,1)S(1)}, u32[]{:S(2)}, u32[]{:S(2)}) collective-permute-start(bf16[2,512,128]{2,1,0:T(8,128)(2,1)S(1)} %pad_maximum_fusion.2), channel_id=1, source_target_pairs={{0,8},{4,12},{8,0},{12,4},{16,24},{20,28},{24,16},{28,20},{1,9},{5... | collective-permute-start | bytes 786440 | tf_op jit(solution)/shard_map/ppermute | solution.py:24
  159.3 26.4 %collective-permute-start.22 = (s16[4,1040,128]{2,1,0:T(8,128)(2,1)S(1)}, s16[4,1040,128]{2,1,0:T(8,128)(2,1)S(1)}, u32[]{:S(2)}, u32[]{:S(2)}) collective-permute-start(s16[4,1040,128]{2,1,0:T(8,128)(2,1)S(1)} %shard_map.59), channel_id=1, source_target_pairs={{0,4},{4,0},{8,12},{12,8},{16,20},{20,16},{24,28},{28,24},{1,5},{5... | collective-permute-start | bytes 3194888 | tf_op jit(solution)/shard_map/ppermute | solution.py:24
  163.7 21.6 %collective-permute-start.24 = (s16[1040,128]{1,0:T(8,128)(2,1)S(1)}, s16[1040,128]{1,0:T(8,128)(2,1)S(1)}, u32[]{:S(2)}, u32[]{:S(2)}) collective-permute-start(s16[1040,128]{1,0:T(8,128)(2,1)S(1)} %get-tuple-element.71), channel_id=1, source_target_pairs={{0,16},{4,20},{8,24},{12,28},{16,0},{20,4},{24,8},{28,12},{1,17},{... | collective-permute-start | bytes 798728 | tf_op jit(solution)/shard_map/ppermute | solution.py:24
  166.1 19.1 %collective-permute-start.25 = (s16[1040,128]{1,0:T(8,128)(2,1)S(1)}, s16[1040,128]{1,0:T(8,128)(2,1)S(1)}, u32[]{:S(2)}, u32[]{:S(2)}) collective-permute-start(s16[1040,128]{1,0:T(8,128)(2,1)S(1)} %get-tuple-element.72), channel_id=1, source_target_pairs={{0,24},{4,28},{8,16},{12,20},{16,8},{20,12},{24,0},{28,4},{1,25},{... | collective-permute-start | bytes 798728 | tf_op jit(solution)/shard_map/ppermute | solution.py:24
  186.7 18.8 %collective-permute-start.26 = (s16[1040,128]{1,0:T(8,128)(2,1)S(1)}, s16[1040,128]{1,0:T(8,128)(2,1)S(1)}, u32[]{:S(2)}, u32[]{:S(2)}) collective-permute-start(s16[1040,128]{1,0:T(8,128)(2,1)S(1)} %get-tuple-element.75), channel_id=1, source_target_pairs={{0,8},{4,12},{8,0},{12,4},{16,24},{20,28},{24,16},{28,20},{1,9},{5... | collective-permute-start | bytes 798728 | tf_op jit(solution)/shard_map/ppermute | solution.py:24
  191.6 21.6 %collective-permute-start.27 = (s16[1040,128]{1,0:T(8,128)(2,1)S(1)}, s16[1040,128]{1,0:T(8,128)(2,1)S(1)}, u32[]{:S(2)}, u32[]{:S(2)}) collective-permute-start(s16[1040,128]{1,0:T(8,128)(2,1)S(1)} %get-tuple-element.76), channel_id=1, source_target_pairs={{0,16},{4,20},{8,24},{12,28},{16,0},{20,4},{24,8},{28,12},{1,17},{... | collective-permute-start | bytes 798728 | tf_op jit(solution)/shard_map/ppermute | solution.py:24
  193.7 19.5 %collective-permute-start.28 = (s16[1040,128]{1,0:T(8,128)(2,1)S(1)}, s16[1040,128]{1,0:T(8,128)(2,1)S(1)}, u32[]{:S(2)}, u32[]{:S(2)}) collective-permute-start(s16[1040,128]{1,0:T(8,128)(2,1)S(1)} %get-tuple-element.77), channel_id=1, source_target_pairs={{0,24},{4,28},{8,16},{12,20},{16,8},{20,12},{24,0},{28,4},{1,25},{... | collective-permute-start | bytes 798728 | tf_op jit(solution)/shard_map/ppermute | solution.py:24
  203.8 20.3 %collective-permute-start.32 = (s16[528,128]{1,0:T(8,128)(2,1)S(1)}, s16[528,128]{1,0:T(8,128)(2,1)S(1)}, u32[]{:S(2)}, u32[]{:S(2)}) collective-permute-start(s16[528,128]{1,0:T(8,128)(2,1)S(1)} %get-tuple-element.84), channel_id=1, source_target_pairs={{0,4},{4,0},{8,12},{12,8},{16,20},{20,16},{24,28},{28,24},{1,5},{5... | collective-permute-start | bytes 405512 | tf_op jit(solution)/shard_map/ppermute | solution.py:24
  214.2 31.0 %collective-permute-start.39 = (s16[1040,128]{1,0:T(8,128)(2,1)S(1)}, s16[1040,128]{1,0:T(8,128)(2,1)S(1)}, u32[]{:S(2)}, u32[]{:S(2)}) collective-permute-start(s16[1040,128]{1,0:T(8,128)(2,1)S(1)} %get-tuple-element.78.refs_0_), channel_id=1, source_target_pairs={{0,8},{4,12},{8,0},{12,4},{16,24},{20,28},{24,16},{28,20},{1,9},{5... | collective-permute-start | bytes 798728 | tf_op jit(solution)/shard_map/ppermute | solution.py:24
  222.6 22.6 %collective-permute-start.29 = (s16[1040,128]{1,0:T(8,128)(2,1)S(1)}, s16[1040,128]{1,0:T(8,128)(2,1)S(1)}, u32[]{:S(2)}, u32[]{:S(2)}) collective-permute-start(s16[1040,128]{1,0:T(8,128)(2,1)S(1)} %get-tuple-element.78.refs_0_), channel_id=1, source_target_pairs={{0,16},{4,20},{8,24},{12,28},{16,0},{20,4},{24,8},{28,12},{1,17},{... | collective-permute-start | bytes 798728 | tf_op jit(solution)/shard_map/ppermute | solution.py:24
  245.3 17.8 %collective-permute-start.40 = (s16[2,1040,128]{2,1,0:T(8,128)(2,1)S(1)}, s16[2,1040,128]{2,1,0:T(8,128)(2,1)S(1)}, u32[]{:S(2)}, u32[]{:S(2)}) collective-permute-start(s16[2,1040,128]{2,1,0:T(8,128)(2,1)S(1)} %pad_add_fusion), channel_id=1, source_target_pairs={{0,4},{4,0},{8,12},{12,8},{16,20},{20,16},{24,28},{28,24},{1,5},{5... | collective-permute-start | bytes 1597448 | tf_op jit(solution)/shard_map/ppermute | solution.py:24
  246.9 23.6 %collective-permute-start.41 = (s16[2,1040,128]{2,1,0:T(8,128)(2,1)S(1)}, s16[2,1040,128]{2,1,0:T(8,128)(2,1)S(1)}, u32[]{:S(2)}, u32[]{:S(2)}) collective-permute-start(s16[2,1040,128]{2,1,0:T(8,128)(2,1)S(1)} %pad_add_fusion.1), channel_id=1, source_target_pairs={{0,4},{4,0},{8,12},{12,8},{16,20},{20,16},{24,28},{28,24},{1,5},{5... | collective-permute-start | bytes 1597448 | tf_op jit(solution)/shard_map/ppermute | solution.py:24
  253.6 22.7 %collective-permute-start.44 = (s16[2,528,128]{2,1,0:T(8,128)(2,1)S(1)}, s16[2,528,128]{2,1,0:T(8,128)(2,1)S(1)}, u32[]{:S(2)}, u32[]{:S(2)}) collective-permute-start(s16[2,528,128]{2,1,0:T(8,128)(2,1)S(1)} %pad_add_fusion.2.refs_1_), channel_id=1, source_target_pairs={{0,24},{4,28},{8,16},{12,20},{16,8},{20,12},{24,0},{28,4},{1,25},{... | collective-permute-start | bytes 811016 | tf_op jit(solution)/shard_map/ppermute | solution.py:24
  256.5 22.0 %collective-permute-start.43 = (s16[2,528,128]{2,1,0:T(8,128)(2,1)S(1)}, s16[2,528,128]{2,1,0:T(8,128)(2,1)S(1)}, u32[]{:S(2)}, u32[]{:S(2)}) collective-permute-start(s16[2,528,128]{2,1,0:T(8,128)(2,1)S(1)} %pad_add_fusion.2.refs_1_), channel_id=1, source_target_pairs={{0,16},{4,20},{8,24},{12,28},{16,0},{20,4},{24,8},{28,12},{1,17},{... | collective-permute-start | bytes 811016 | tf_op jit(solution)/shard_map/ppermute | solution.py:24
  256.5 22.0 %collective-permute-start.42 = (s16[2,528,128]{2,1,0:T(8,128)(2,1)S(1)}, s16[2,528,128]{2,1,0:T(8,128)(2,1)S(1)}, u32[]{:S(2)}, u32[]{:S(2)}) collective-permute-start(s16[2,528,128]{2,1,0:T(8,128)(2,1)S(1)} %pad_add_fusion.2.refs_1_), channel_id=1, source_target_pairs={{0,8},{4,12},{8,0},{12,4},{16,24},{20,28},{24,16},{28,20},{1,9},{5... | collective-permute-start | bytes 811016 | tf_op jit(solution)/shard_map/ppermute | solution.py:24
  (24 other events, 219.0 us)

commit v3 on v2

--- a/solution.py
+++ b/solution.py
@@ -15,21 +15,13 @@
 LOW = 2
 GROUP = 8
 LANES = 128
-VMEM_BYTES = 48 << 20
+VMEM_BYTES = 24 << 20
 LIGHT = pl.CostEstimate(flops=1, bytes_accessed=1, transcendentals=0)
 WHOLE = pl.BlockSpec(memory_space=pltpu.VMEM)
 
 
 def exchange(value, axis, size, mask):
     return lax.ppermute(value, axis, [(i, i ^ mask) for i in range(size)])
-
-
-def butterfly(value, axis, size):
-    mask = 1
-    while 2 * mask < size:
-        value = value + exchange(value, axis, size, mask)
-        mask *= 2
-    return value, exchange(value, axis, size, mask)
 
 
 class Plain:
@@ -145,18 +137,15 @@
         outs[k][...] = code.encode(code.decode(own_ref[k]) + code.decode(got_ref[k]))
 
 
-def add_all_kernel(code, with_gram, *refs):
-    outs = refs[-2:] if with_gram else refs[-1:]
-    parts = refs[: len(refs) - len(outs)]
+def add_all_kernel(code, *refs):
+    parts, outs = refs[:-2], refs[-2:]
     total = code.decode(parts[0][...])
     for part in parts[1:]:
         total = total + code.decode(part[...])
     outs[0][...] = code.encode(total)
-    if with_gram:
-        outs[1][...] = lax.dot_general(
-            total, total, (((0,), (0,)), ((), ())), precision=HIGHEST,
-            preferred_element_type=F32,
-        )
+    outs[1][...] = lax.dot_general(
+        total, total, (((0,), (0,)), ((), ())), precision=HIGHEST, preferred_element_type=F32
+    )
 
 
 def add_halves_kernel(code, pos_ref, *refs):
@@ -170,12 +159,61 @@
     send_ref[...] = code.encode(jnp.where(lower, total[half:], total[:half]))
 
 
-def add_all(code, with_gram, parts):
+def add_all(code, parts):
     rank = parts[0].shape[1]
     out = [jax.ShapeDtypeStruct(parts[0].shape, code.dtype)]
-    if with_gram:
-        out.append(jax.ShapeDtypeStruct((rank, rank), F32))
-    return small_call(functools.partial(add_all_kernel, code, with_gram), out, *parts)
+    out.append(jax.ShapeDtypeStruct((rank, rank), F32))
+    return small_call(functools.partial(add_all_kernel, code), out, *parts)
+
+
+def write_halves(pos_ref, value, outs):
+    half = value.shape[0] // 2
+    lower = pos_ref[2] == 0
+    outs[0][...] = jnp.where(lower, value[:half], value[half:])
+    outs[1][...] = jnp.where(lower, value[half:], value[:half])
+
+
+def first_kernel(count, pos_ref, panel_ref, *refs):
+    scans, outs, total = refs[:count], refs[count:-1], refs[-1]
+    n = scans[0].shape[1]
+    g = pl.program_id(0)
+
+    @pl.when(g == 0)
+    def _():
+        total[...] = jnp.zeros_like(total)
+
+    for u in range(count):
+        panel = panel_ref[u * n : (u + 1) * n]
+        total[...] += jnp.dot(scans[u][...], panel, preferred_element_type=F32)
+
+    @pl.when(g == pl.num_programs(0) - 1)
+    def _():
+        write_halves(pos_ref, total[...], outs)
+
+
+def first_project(scans, pos, panel, steps=3, count=4):
+    time_rows, voxels = scans.shape
+    rank = panel.shape[1]
+    n = voxels // (steps * count)
+    half = jax.ShapeDtypeStruct((time_rows // 2, rank), F32)
+
+    def column(u):
+        return lambda g, pos: (0, g * count + u)
+
+    return pl.pallas_call(
+        functools.partial(first_kernel, count),
+        out_shape=[half, half],
+        grid_spec=pltpu.PrefetchScalarGridSpec(
+            num_scalar_prefetch=1,
+            grid=(steps,),
+            in_specs=[pl.BlockSpec((count * n, rank), lambda g, pos: (g, 0))]
+            + [pl.BlockSpec((time_rows, n), column(u)) for u in range(count)],
+            out_specs=[pl.BlockSpec(half.shape, lambda g, pos: (0, 0))] * 2,
+            scratch_shapes=[pltpu.VMEM((time_rows, rank), F32)],
+        ),
+        compiler_params=params(),
+        cost_estimate=LIGHT,
+    )(pos, panel, *([scans] * count))
 
 
 def project_kernel(has_base, split, items, pos_ref, *refs):
@@ -186,25 +224,15 @@
     time_rows = scans[0].shape[0]
     rank = outs[0].shape[1]
     total = jnp.zeros((time_rows, rank), F32)
-    gram = jnp.zeros((rank, rank), F32)
     for scan, (source, index) in zip(scans, items):
         piece = pieces[source][...] if index is None else pieces[source][index]
         total += jnp.dot(scan[...], piece, preferred_element_type=F32)
-        gram += lax.dot_general(
-            piece, piece, (((0,), (0,)), ((), ())), preferred_element_type=F32
-        )
     if has_base:
-        total += base[:time_rows]
-        gram += base[time_rows:]
-    if not split:
-        outs[0][:time_rows] = total
-        outs[0][time_rows:] = gram
-        return
-    both = jnp.concatenate([total, gram])
-    half = both.shape[0] // 2
-    lower = pos_ref[2] == 0
-    outs[0][...] = jnp.where(lower, both[:half], both[half:])
-    outs[1][...] = jnp.where(lower, both[half:], both[:half])
+        total += base[...]
+    if split:
+        write_halves(pos_ref, total, outs)
+    else:
+        outs[0][...] = total
 
 
 def project(scans, layout, pos, groups, base=None, split=False):
@@ -222,8 +250,7 @@
     full = lambda shape: pl.BlockSpec(shape, lambda g, pos: (0,) * len(shape))
     bases = [] if base is None else [base]
     arrays = [array for _, _, array in groups]
-    rows = time_rows + rank
-    shape = (rows // 2, rank) if split else (rows, rank)
+    shape = (time_rows // 2, rank) if split else (time_rows, rank)
     out_shape = [jax.ShapeDtypeStruct(shape, F32)] * (2 if split else 1)
     out = pl.pallas_call(
         functools.partial(project_kernel, base is not None, split, items),
@@ -348,13 +375,13 @@
     )
 
 
-def normalise_kernel(all_voxels, length_ref, pos_ref, mine_ref, other_ref, out_ref):
-    time_rows = out_ref.shape[0]
+def scores_kernel(with_factor, length_ref, pos_ref, mine_ref, other_ref, *refs):
+    out_ref = refs[-1]
     mine, other = mine_ref[...], other_ref[...]
     lower = pos_ref[2] == 0
-    both = jnp.concatenate([jnp.where(lower, mine, other), jnp.where(lower, other, mine)])
-    inverse = inverse_factor(both[time_rows:] * (1.0 / all_voxels))
-    scores = times_transpose(both[:time_rows], inverse)
+    scores = jnp.concatenate([jnp.where(lower, mine, other), jnp.where(lower, other, mine)])
+    if with_factor:
+        scores = times_transpose(scores, refs[0][...])
     live = lax.broadcasted_iota(jnp.int32, scores.shape, 0) < length_ref[0]
     out_ref[...] = jnp.where(live, scores, 0.0).astype(BF16)
 
@@ -385,9 +412,8 @@
         slot_ids = jnp.arange(block_subject.shape[0], dtype=jnp.int32)
         subject = jnp.sum(jnp.where(slot_ids == me, block_subject, 0))
         length = jnp.sum(jnp.where(slot_ids == subject, lengths, 0))
-        live_rows = (jnp.arange(time_rows, dtype=jnp.int32) < length)[:, None]
-
-        def sketch_sum(scores, code, with_gram):
+
+        def sketch_sum(scores, code):
             def part(after, j, ks, apart, per_step):
                 ordered = scores if after is None else lax.optimization_barrier((scores, after))[0]
                 return sketch_part(
@@ -417,65 +443,66 @@
             )(pos, second_own, *got_second)
             got_send = swap(send, mask=1)
             return (
-                add_all(code, with_gram, [first[0], *got_first]),
-                add_all(code, with_gram, [keep, got_send]),
+                add_all(code, [first[0], *got_first]),
+                add_all(code, [keep, got_send]),
             )
 
-        def gather(first, second, gram=None):
+        def gather(first, second, gram):
             far_in = [swap(first, mask=k * LOW) for k in far]
             near_in = [first] + [swap(first, mask=k * LOW) for k in near[1:]]
             low_near = swap(jnp.stack(near_in), mask=1)
             got = swap(second, mask=1)
             lower = pos[0] == 0
             pair = jnp.stack([jnp.where(lower, second, got), jnp.where(lower, got, second)])
-            if gram is not None:
-                gram = gram + swap_vox(gram, mask=1)
-                mask = 2
-                while mask < blocks:
-                    gram = gram + swap_vox(gram, mask=mask)
-                    mask *= 2
-                gram = gram + swap(gram, mask=1)
+            mask = 1
+            while mask < blocks:
+                gram = gram + swap_vox(gram, mask=mask)
+                mask *= 2
+            gram = gram + swap(gram, mask=1)
             far_in, pair, gram = lax.optimization_barrier((far_in, pair, gram))
             low_far = swap(jnp.stack(far_in), mask=1)
             seconds = [pair] + [swap(pair, mask=k * LOW) for k in ks[1:]]
-            if gram is not None:
-                gram = [gram] + [swap(gram, mask=k * LOW) for k in ks[1:]]
+            gram = [gram] + [swap(gram, mask=k * LOW) for k in ks[1:]]
             early = [(0, [k], array) for k, array in zip(near + far, near_in + far_in)]
             late = [(1, near, low_near), (1, far, low_far)]
             pairs = [(None, [k], array) for k, array in zip(ks, seconds)]
             return early, late, pairs, gram
 
-        partial = jnp.dot(scans, test_matrix, preferred_element_type=F32)
-        summed = sum(butterfly(partial, "vox", blocks))
-        scores = jnp.where(live_rows, summed, 0.0).astype(BF16)
-
-        (first,), (second,) = sketch_sum(scores, Plain, False)
-        early, late, pairs, _ = gather(first, second)
+        def sum_scores(mine, send, *factor):
+            mine = mine + swap_vox(send, mask=1)
+            mask = 2
+            while mask < blocks:
+                mine = mine + swap_vox(mine, mask=mask)
+                mask *= 2
+            other = swap_vox(mine, mask=1)
+            return pl.pallas_call(
+                functools.partial(scores_kernel, bool(factor)),
+                out_shape=jax.ShapeDtypeStruct((time_rows, rank), BF16),
+                in_specs=[pl.BlockSpec(memory_space=pltpu.SMEM)] * 2
+                + [WHOLE] * (2 + len(factor)),
+                out_specs=WHOLE,
+                compiler_params=params(),
+                cost_estimate=LIGHT,
+            )(length[None], pos, mine, other, *factor)
+
+        def pass_over(scores, code):
+            (first, gram_first), (second, gram_second) = sketch_sum(scores, code)
+            early, late, pairs, grams = gather(first, second, gram_first + gram_second)
+            inverse = small_call(
+                functools.partial(invert_kernel, all_voxels),
+                jax.ShapeDtypeStruct((rank, rank), F32), *grams,
+            )
+            return early, late, pairs, inverse
+
+        scores = sum_scores(*first_project(scans, pos, test_matrix))
+        early, late, pairs, inverse = pass_over(scores, Plain)
         pairs = [(j, k, array.reshape(layout.pair, rank)) for j, k, array in pairs]
-        both = project(scans, layout, pos, early)
-        both = project(scans, layout, pos, late, both)
-        both = project(scans, layout, pos, pairs[: high // 2], both)
-        mine, send = project(scans, layout, pos, pairs[high // 2 :], both, True)
-        mine = mine + swap_vox(send, mask=1)
-        mask = 2
-        while mask < blocks:
-            mine = mine + swap_vox(mine, mask=mask)
-            mask *= 2
-        other = swap_vox(mine, mask=1)
-        scores = pl.pallas_call(
-            functools.partial(normalise_kernel, all_voxels),
-            out_shape=jax.ShapeDtypeStruct((time_rows, rank), BF16),
-            in_specs=[pl.BlockSpec(memory_space=pltpu.SMEM)] * 2 + [WHOLE, WHOLE],
-            out_specs=WHOLE,
-            compiler_params=params(),
-        )(length[None], pos, mine, other)
-
-        (first, gram_first), (second, gram_second) = sketch_sum(scores, Fixed, True)
-        early, late, pairs, grams = gather(first, second, gram_first + gram_second)
-        inverse = small_call(
-            functools.partial(invert_kernel, all_voxels),
-            jax.ShapeDtypeStruct((rank, rank), F32), *grams,
-        )
+        total = project(scans, layout, pos, early)
+        total = project(scans, layout, pos, late, total)
+        total = project(scans, layout, pos, pairs[: high // 2], total)
+        halves = project(scans, layout, pos, pairs[high // 2 :], total, True)
+        scores = sum_scores(*halves, inverse)
+        early, late, pairs, inverse = pass_over(scores, Fixed)
         out = finish(layout, pos, early + late, inverse, voxels)
         return finish(layout, pos, pairs, inverse, voxels, out)
 

time: 283 us -> 284 us (level)
  waiting for transfers between devices: 104 us -> 138 us
  starting transfers between devices: 92.2 us -> 75.3 us
  Pallas kernels: 70.4 us -> 54.6 us
  local copies, waits for them, and re-layouts: 1.89 us -> 12.9 us
  matrix products: 7.68 us -> 0 us
    ppermute x45 -> x52, waiting for transfers between devices: 104 us -> 138 us  [exchange(): return lax.ppermute(value, axis, [(i, i ^ mask) for i in range(size)])]
    ppermute x45 -> x52, starting transfers between devices: 92.2 us -> 75.3 us  [exchange(): return lax.ppermute(value, axis, [(i, i ^ mask) for i in range(size)])]
    pallas_call x8, Pallas kernels: 28.3 us -> 15.9 us  [sketch_part(): pl.pallas_call(functools.partial(sketch_kernel, code, apart, per_step), o...]
    unnamed x6 -> x20, local copies, waits for them, and re-layouts: 1.89 us -> 12.9 us
    pallas_call x4, Pallas kernels: 16.3 us -> 6.92 us  [project(): pl.pallas_call(functools.partial(project_kernel, base is not None, split,...]
    dot_general x1 -> x0, matrix products: 7.68 us -> none  [on_device(): partial = jnp.dot(scans, test_matrix, preferred_element_type=F32)]
    pallas_call x7 -> x8, Pallas kernels: 8.61 us -> 11.8 us  [small_call(): pl.pallas_call(kernel, out_shape=out_shape, in_specs=[WHOLE] * len(args),...]
    pallas_call x1 -> x3, Pallas kernels: 6.09 us -> 9.01 us  [the longest x1 6.32 us: first_project(): pl.pallas_call(functools.partial(first_kernel, count), out_shape=[half, h...]
  transfers between devices with their start and end apart: 45 -> 52, of which waited for: 23 -> 31; matrix products, arithmetic and copies ran while one was open for 1% -> 1% of each run, Pallas kernels for 17% -> 12%
where the time goes in v3:
time: 284 us; the launch traced here: 283 us
  waiting for transfers between devices  138 us (49%)
  starting transfers between devices  75.3 us (27%)
  Pallas kernels  54.6 us (19%)
  local copies, waits for them, and re-layouts  12.9 us (5%)
    ppermute x52, waiting for transfers between devices, exchange(): return lax.ppermute(value, axis, [(i, i ^ mask) for i in range(size)])  138 us
    ppermute x52, starting transfers between devices, exchange(): return lax.ppermute(value, axis, [(i, i ^ mask) for i in range(size)])  75.3 us
    pallas_call x8, Pallas kernels, sketch_part(): pl.pallas_call(functools.partial(sketch_kernel, code, apart, per_step), o...  15.9 us
    unnamed x20, local copies, waits for them, and re-layouts  12.9 us
    pallas_call x8, Pallas kernels, small_call(): pl.pallas_call(kernel, out_shape=out_shape, in_specs=[WHOLE] * len(args),...  11.8 us
    pallas_call x2, Pallas kernels, finish(): pl.pallas_call(functools.partial(finish_kernel, layout, items, base is no...  9.4 us
    pallas_call x4, Pallas kernels, project(): pl.pallas_call(functools.partial(project_kernel, base is not None, split,...  6.92 us
    pallas_call x1, Pallas kernels, first_project(): pl.pallas_call(functools.partial(first_kernel, count), out_shape=[half, h...  6.32 us
  transfers between devices with their start and end apart: 52, of which 31 were waited for; matrix products, arithmetic and copies ran while one was open for 1% of the time, Pallas kernels for 12%

profile of v3, /device:TPU:0, one launch (start us, length us, event | category | flops | bytes accessed | tf_op | source)
XLA Modules:
  0.0 283.5 jit_solution(9620454126994272536)
XLA Ops:
  0.1 5.5 %copy-done = bf16[640,12288]{1,0:T(8,128)(2,1)S(1)} copy-done((bf16[640,12288]{1,0:T(8,128)(2,1)S(1)}, bf16[640,12288]{1,0:T(8,128)(2,1)}, u32[]{:S(2)}) %copy-start) | copy-done | bytes 15728664
  7.4 6.3 %shard_map.46 = (f32[320,128]{1,0:T(8,128)S(1)}, f32[320,128]{1,0:T(8,128)S(1)}) custom-call(s32[3]{0:T(128)S(1)} %pad_add_fusion.3.pos_ref, bf16[12288,128]{1,0:T(8,128)(2,1)S(1)} %copy-done.3, bf16[640,12288]{1,0:T(8,128)(2,1)S(1)} %copy-done, bf16[640,12288]{1,0:T(8,128)(2,1)S(1)} %copy-done, bf16[640,12288]{1,0:T(8,128)(2,1)S(1)} %copy-done, ...), custom_call_target="tpu_custom_call" | custom-call | flops 1 | bytes 1 | tf_op jit(solution)/shard_map/pallas_call | solution.py:203
  18.3 4.5 %collective-permute-done.1 = f32[320,128]{1,0:T(8,128)S(1)} collective-permute-done((f32[320,128]{1,0:T(8,128)S(1)}, f32[320,128]{1,0:T(8,128)S(1)}, u32[]{:S(2)}, u32[]{:S(2)}) %collective-permute-start.1) | collective-permute-done | bytes 163872 | tf_op jit(solution)/shard_map/ppermute | solution.py:24
  38.3 14.6 %collective-permute-done.5.refs_2_ = bf16[1024,128]{1,0:T(8,128)(2,1)S(1)} collective-permute-done((bf16[1024,128]{1,0:T(8,128)(2,1)S(1)}, bf16[1024,128]{1,0:T(8,128)(2,1)S(1)}, u32[]{:S(2)}, u32[]{:S(2)}) %collective-permute-start.5) | collective-permute-done | bytes 262176 | tf_op jit(solution)/shard_map/ppermute | solution.py:24
  54.2 4.6 %collective-permute-start.7 = (bf16[1024,128]{1,0:T(8,128)(2,1)S(1)}, bf16[1024,128]{1,0:T(8,128)(2,1)S(1)}, u32[]{:S(2)}, u32[]{:S(2)}) collective-permute-start(bf16[1024,128]{1,0:T(8,128)(2,1)S(1)} %get-tuple-element.64), channel_id=1, source_target_pairs={{0,8},{4,12},{8,0},{12,4},{16,24},{20,28},{24,16},{28,20},{1,9},{5... | collective-permute-start | bytes 786440 | tf_op jit(solution)/shard_map/ppermute | solution.py:24
  64.5 4.5 %collective-permute-done.13.refs_1_ = bf16[512,128]{1,0:T(8,128)(2,1)S(1)} collective-permute-done((bf16[512,128]{1,0:T(8,128)(2,1)S(1)}, bf16[512,128]{1,0:T(8,128)(2,1)S(1)}, u32[]{:S(2)}, u32[]{:S(2)}) %collective-permute-start.13) | collective-permute-done | bytes 131104 | tf_op jit(solution)/shard_map/ppermute | solution.py:24
  70.8 9.4 %collective-permute-done.8.refs_2_ = bf16[1024,128]{1,0:T(8,128)(2,1)S(1)} collective-permute-done((bf16[1024,128]{1,0:T(8,128)(2,1)S(1)}, bf16[1024,128]{1,0:T(8,128)(2,1)S(1)}, u32[]{:S(2)}, u32[]{:S(2)}) %collective-permute-start.8) | collective-permute-done | bytes 262176 | tf_op jit(solution)/shard_map/ppermute | solution.py:24
  84.4 3.6 %collective-permute-start.11 = (bf16[1024,128]{1,0:T(8,128)(2,1)S(1)}, bf16[1024,128]{1,0:T(8,128)(2,1)S(1)}, u32[]{:S(2)}, u32[]{:S(2)}) collective-permute-start(bf16[1024,128]{1,0:T(8,128)(2,1)S(1)} %get-tuple-element.67.refs_4_), channel_id=1, source_target_pairs={{0,16},{4,20},{8,24},{12,28},{16,0},{20,4},{24,8},{28,12},{1,17},{... | collective-permute-start | bytes 786440 | tf_op jit(solution)/shard_map/ppermute | solution.py:24
  93.5 3.7 %collective-permute-done.17 = f32[128,128]{1,0:T(8,128)S(1)} collective-permute-done((f32[128,128]{1,0:T(8,128)S(1)}, f32[128,128]{1,0:T(8,128)S(1)}, u32[]{:S(2)}, u32[]{:S(2)}) %collective-permute-start.17) | collective-permute-done | bytes 65568 | tf_op jit(solution)/shard_map/ppermute | solution.py:24
  97.2 11.1 %collective-permute-done.11.refs_6_ = bf16[1024,128]{1,0:T(8,128)(2,1)S(1)} collective-permute-done((bf16[1024,128]{1,0:T(8,128)(2,1)S(1)}, bf16[1024,128]{1,0:T(8,128)(2,1)S(1)}, u32[]{:S(2)}, u32[]{:S(2)}) %collective-permute-start.11) | collective-permute-done | bytes 262176 | tf_op jit(solution)/shard_map/ppermute | solution.py:24
  114.5 5.5 %copy-done.2 = bf16[640,12288]{1,0:T(8,128)(2,1)S(1)} copy-done((bf16[640,12288]{1,0:T(8,128)(2,1)S(1)}, bf16[640,12288]{1,0:T(8,128)(2,1)}, u32[]{:S(2)}) %copy-start.2) | copy-done | bytes 15728664
  123.2 10.4 %collective-permute-done.18.refs_5_ = bf16[2,1024,128]{2,1,0:T(8,128)(2,1)S(1)} collective-permute-done((bf16[2,1024,128]{2,1,0:T(8,128)(2,1)S(1)}, bf16[2,1024,128]{2,1,0:T(8,128)(2,1)S(1)}, u32[]{:S(2)}, u32[]{:S(2)}) %collective-permute-start.18) | collective-permute-done | bytes 524320 | tf_op jit(solution)/shard_map/ppermute | solution.py:24
  141.6 4.7 %collective-permute-done.24 = f32[320,128]{1,0:T(8,128)S(1)} collective-permute-done((f32[320,128]{1,0:T(8,128)S(1)}, f32[320,128]{1,0:T(8,128)S(1)}, u32[]{:S(2)}, u32[]{:S(2)}) %collective-permute-start.24) | collective-permute-done | bytes 163872 | tf_op jit(solution)/shard_map/ppermute | solution.py:24
  155.7 4.1 %shard_map.60.refs_0_ = f32[128,128]{1,0:T(8,128)S(1)} custom-call(f32[128,128]{1,0:T(8,128)S(1)} %add.51.refs_0_, f32[128,128]{1,0:T(8,128)S(1)} %collective-permute-done.26.refs_1_, f32[128,128]{1,0:T(8,128)S(1)} %collective-permute-done.27.refs_2_, f32[128,128]{1,0:T(8,128)S(1)} %collective-permute-done.28.refs_3_), custom_call_target="tpu_custom_call" | custom-call | flops 1 | bytes 1 | tf_op jit(solution)/shard_map/pallas_call | solution.py:125
  173.3 14.5 %collective-permute-done.31.refs_2_ = s16[1040,128]{1,0:T(8,128)(2,1)S(1)} collective-permute-done((s16[1040,128]{1,0:T(8,128)(2,1)S(1)}, s16[1040,128]{1,0:T(8,128)(2,1)S(1)}, u32[]{:S(2)}, u32[]{:S(2)}) %collective-permute-start.31) | collective-permute-done | bytes 266272 | tf_op jit(solution)/shard_map/ppermute | solution.py:24
  190.7 3.7 %collective-permute-start.33 = (s16[1040,128]{1,0:T(8,128)(2,1)S(1)}, s16[1040,128]{1,0:T(8,128)(2,1)S(1)}, u32[]{:S(2)}, u32[]{:S(2)}) collective-permute-start(s16[1040,128]{1,0:T(8,128)(2,1)S(1)} %get-tuple-element.89), channel_id=1, source_target_pairs={{0,8},{4,12},{8,0},{12,4},{16,24},{20,28},{24,16},{28,20},{1,9},{5... | collective-permute-start | bytes 798728 | tf_op jit(solution)/shard_map/ppermute | solution.py:24
  206.0 10.0 %collective-permute-done.34.refs_2_ = s16[1040,128]{1,0:T(8,128)(2,1)S(1)} collective-permute-done((s16[1040,128]{1,0:T(8,128)(2,1)S(1)}, s16[1040,128]{1,0:T(8,128)(2,1)S(1)}, u32[]{:S(2)}, u32[]{:S(2)}) %collective-permute-start.34) | collective-permute-done | bytes 266272 | tf_op jit(solution)/shard_map/ppermute | solution.py:24
  217.0 4.4 %collective-permute-start.46 = (s16[1040,128]{1,0:T(8,128)(2,1)S(1)}, s16[1040,128]{1,0:T(8,128)(2,1)S(1)}, u32[]{:S(2)}, u32[]{:S(2)}) collective-permute-start(s16[1040,128]{1,0:T(8,128)(2,1)S(1)} %get-tuple-element.92.refs_0_), channel_id=1, source_target_pairs={{0,8},{4,12},{8,0},{12,4},{16,24},{20,28},{24,16},{28,20},{1,9},{5... | collective-permute-start | bytes 798728 | tf_op jit(solution)/shard_map/ppermute | solution.py:24
  232.4 4.3 %collective-permute-done.37.refs_3_ = s16[1040,128]{1,0:T(8,128)(2,1)S(1)} collective-permute-done((s16[1040,128]{1,0:T(8,128)(2,1)S(1)}, s16[1040,128]{1,0:T(8,128)(2,1)S(1)}, u32[]{:S(2)}, u32[]{:S(2)}) %collective-permute-start.37) | collective-permute-done | bytes 266272 | tf_op jit(solution)/shard_map/ppermute | solution.py:24
  236.6 10.0 %collective-permute-done.36.refs_2_ = s16[1040,128]{1,0:T(8,128)(2,1)S(1)} collective-permute-done((s16[1040,128]{1,0:T(8,128)(2,1)S(1)}, s16[1040,128]{1,0:T(8,128)(2,1)S(1)}, u32[]{:S(2)}, u32[]{:S(2)}) %collective-permute-start.36) | collective-permute-done | bytes 266272 | tf_op jit(solution)/shard_map/ppermute | solution.py:24
  260.3 4.1 %shard_map.70.inverse_ref = f32[128,128]{1,0:T(8,128)S(1)} custom-call(f32[128,128]{1,0:T(8,128)S(1)} %add.57.refs_0_, f32[128,128]{1,0:T(8,128)S(1)} %collective-permute-done.43.refs_1_, f32[128,128]{1,0:T(8,128)S(1)} %collective-permute-done.44.refs_2_, f32[128,128]{1,0:T(8,128)S(1)} %collective-permute-done.45.refs_3_), custom_call_target="tpu_custom_call" | custom-call | flops 1 | bytes 1 | tf_op jit(solution)/shard_map/pallas_call | solution.py:125
  264.4 7.4 %collective-permute-done.48.refs_5_ = s16[2,1040,128]{2,1,0:T(8,128)(2,1)S(1)} collective-permute-done((s16[2,1040,128]{2,1,0:T(8,128)(2,1)S(1)}, s16[2,1040,128]{2,1,0:T(8,128)(2,1)S(1)}, u32[]{:S(2)}, u32[]{:S(2)}) %collective-permute-start.48) | collective-permute-done | bytes 532512 | tf_op jit(solution)/shard_map/ppermute | solution.py:24
  271.7 5.8 %shard_map.71.refs_0_ = f32[12288,128]{1,0:T(8,128)} custom-call(s32[3]{0:T(128)S(1)} %pad_add_fusion.3.pos_ref, f32[128,128]{1,0:T(8,128)S(1)} %shard_map.70.inverse_ref, s16[1040,128]{1,0:T(8,128)(2,1)S(1)} %get-tuple-element.92.refs_0_, s16[1040,128]{1,0:T(8,128)(2,1)S(1)} %collective-permute-done.46.refs_1_, ...), custom_call_target="tpu_custom_call" | custom-call | tf_op jit(solution)/shard_map/pallas_call | solution.py:307
  279.7 3.6 %shard_map.72 = f32[12288,128]{1,0:T(8,128)} custom-call(s32[3]{0:T(128)S(1)} %pad_add_fusion.3.pos_ref, f32[128,128]{1,0:T(8,128)S(1)} %shard_map.70.inverse_ref, f32[12288,128]{1,0:T(8,128)} %shard_map.71.refs_0_, s16[2,528,128]{2,1,0:T(8,128)(2,1)S(1)} %pad_add_fusion.2.refs_1_, ...), custom_call_target="tpu_custom_call", output_to_operand_aliasing={{}: (2, {})} | custom-call | tf_op jit(solution)/shard_map/pallas_call | solution.py:307
  (151 shorter events, 122.6 us)
Async XLA Ops:
  28.3 25.6 %collective-permute-start.3 = (bf16[4,1024,128]{2,1,0:T(8,128)(2,1)S(1)}, bf16[4,1024,128]{2,1,0:T(8,128)(2,1)S(1)}, u32[]{:S(2)}, u32[]{:S(2)}) collective-permute-start(bf16[4,1024,128]{2,1,0:T(8,128)(2,1)S(1)} %shard_map.48), channel_id=1, source_target_pairs={{0,4},{4,0},{8,12},{12,8},{16,20},{20,16},{24,28},{28,24},{1,5},{5... | collective-permute-start | bytes 3145736 | tf_op jit(solution)/shard_map/ppermute | solution.py:24
  31.6 21.4 %collective-permute-start.5 = (bf16[1024,128]{1,0:T(8,128)(2,1)S(1)}, bf16[1024,128]{1,0:T(8,128)(2,1)S(1)}, u32[]{:S(2)}, u32[]{:S(2)}) collective-permute-start(bf16[1024,128]{1,0:T(8,128)(2,1)S(1)} %get-tuple-element.60), channel_id=1, source_target_pairs={{0,16},{4,20},{8,24},{12,28},{16,0},{20,4},{24,8},{28,12},{1,17},{... | collective-permute-start | bytes 786440 | tf_op jit(solution)/shard_map/ppermute | solution.py:24
  34.2 18.7 %collective-permute-start.6 = (bf16[1024,128]{1,0:T(8,128)(2,1)S(1)}, bf16[1024,128]{1,0:T(8,128)(2,1)S(1)}, u32[]{:S(2)}, u32[]{:S(2)}) collective-permute-start(bf16[1024,128]{1,0:T(8,128)(2,1)S(1)} %get-tuple-element.61), channel_id=1, source_target_pairs={{0,24},{4,28},{8,16},{12,20},{16,8},{20,12},{24,0},{28,4},{1,25},{... | collective-permute-start | bytes 786440 | tf_op jit(solution)/shard_map/ppermute | solution.py:24
  58.8 21.3 %collective-permute-start.8 = (bf16[1024,128]{1,0:T(8,128)(2,1)S(1)}, bf16[1024,128]{1,0:T(8,128)(2,1)S(1)}, u32[]{:S(2)}, u32[]{:S(2)}) collective-permute-start(bf16[1024,128]{1,0:T(8,128)(2,1)S(1)} %get-tuple-element.65), channel_id=1, source_target_pairs={{0,16},{4,20},{8,24},{12,28},{16,0},{20,4},{24,8},{28,12},{1,17},{... | collective-permute-start | bytes 786440 | tf_op jit(solution)/shard_map/ppermute | solution.py:24
  60.8 19.3 %collective-permute-start.9 = (bf16[1024,128]{1,0:T(8,128)(2,1)S(1)}, bf16[1024,128]{1,0:T(8,128)(2,1)S(1)}, u32[]{:S(2)}, u32[]{:S(2)}) collective-permute-start(bf16[1024,128]{1,0:T(8,128)(2,1)S(1)} %get-tuple-element.66), channel_id=1, source_target_pairs={{0,24},{4,28},{8,16},{12,20},{16,8},{20,12},{24,0},{28,4},{1,25},{... | collective-permute-start | bytes 786440 | tf_op jit(solution)/shard_map/ppermute | solution.py:24
  69.4 20.7 %collective-permute-start.14 = (bf16[512,128]{1,0:T(8,128)(2,1)S(1)}, bf16[512,128]{1,0:T(8,128)(2,1)S(1)}, u32[]{:S(2)}, u32[]{:S(2)}) collective-permute-start(bf16[512,128]{1,0:T(8,128)(2,1)S(1)} %get-tuple-element.73), channel_id=1, source_target_pairs={{0,4},{4,0},{8,12},{12,8},{16,20},{20,16},{24,28},{28,24},{1,5},{5... | collective-permute-start | bytes 393224 | tf_op jit(solution)/shard_map/ppermute | solution.py:24
  84.4 23.9 %collective-permute-start.11 = (bf16[1024,128]{1,0:T(8,128)(2,1)S(1)}, bf16[1024,128]{1,0:T(8,128)(2,1)S(1)}, u32[]{:S(2)}, u32[]{:S(2)}) collective-permute-start(bf16[1024,128]{1,0:T(8,128)(2,1)S(1)} %get-tuple-element.67.refs_4_), channel_id=1, source_target_pairs={{0,16},{4,20},{8,24},{12,28},{16,0},{20,4},{24,8},{28,12},{1,17},{... | collective-permute-start | bytes 786440 | tf_op jit(solution)/shard_map/ppermute | solution.py:24
  88.0 21.0 %collective-permute-start.10 = (bf16[1024,128]{1,0:T(8,128)(2,1)S(1)}, bf16[1024,128]{1,0:T(8,128)(2,1)S(1)}, u32[]{:S(2)}, u32[]{:S(2)}) collective-permute-start(bf16[1024,128]{1,0:T(8,128)(2,1)S(1)} %get-tuple-element.67.refs_4_), channel_id=1, source_target_pairs={{0,8},{4,12},{8,0},{12,4},{16,24},{20,28},{24,16},{28,20},{1,9},{5... | collective-permute-start | bytes 786440 | tf_op jit(solution)/shard_map/ppermute | solution.py:24
  109.0 24.6 %collective-permute-start.18 = (bf16[2,1024,128]{2,1,0:T(8,128)(2,1)S(1)}, bf16[2,1024,128]{2,1,0:T(8,128)(2,1)S(1)}, u32[]{:S(2)}, u32[]{:S(2)}) collective-permute-start(bf16[2,1024,128]{2,1,0:T(8,128)(2,1)S(1)} %pad_maximum_fusion), channel_id=1, source_target_pairs={{0,4},{4,0},{8,12},{12,8},{16,20},{20,16},{24,28},{28,24},{1,5},{5... | collective-permute-start | bytes 1572872 | tf_op jit(solution)/shard_map/ppermute | solution.py:24
  110.6 25.1 %collective-permute-start.20 = (bf16[2,512,128]{2,1,0:T(8,128)(2,1)S(1)}, bf16[2,512,128]{2,1,0:T(8,128)(2,1)S(1)}, u32[]{:S(2)}, u32[]{:S(2)}) collective-permute-start(bf16[2,512,128]{2,1,0:T(8,128)(2,1)S(1)} %pad_maximum_fusion.2), channel_id=1, source_target_pairs={{0,8},{4,12},{8,0},{12,4},{16,24},{20,28},{24,16},{28,20},{1,9},{5... | collective-permute-start | bytes 786440 | tf_op jit(solution)/shard_map/ppermute | solution.py:24
  111.2 25.9 %collective-permute-start.22 = (bf16[2,512,128]{2,1,0:T(8,128)(2,1)S(1)}, bf16[2,512,128]{2,1,0:T(8,128)(2,1)S(1)}, u32[]{:S(2)}, u32[]{:S(2)}) collective-permute-start(bf16[2,512,128]{2,1,0:T(8,128)(2,1)S(1)} %pad_maximum_fusion.2), channel_id=1, source_target_pairs={{0,24},{4,28},{8,16},{12,20},{16,8},{20,12},{24,0},{28,4},{1,25},{... | collective-permute-start | bytes 786440 | tf_op jit(solution)/shard_map/ppermute | solution.py:24
  114.0 23.1 %collective-permute-start.21 = (bf16[2,512,128]{2,1,0:T(8,128)(2,1)S(1)}, bf16[2,512,128]{2,1,0:T(8,128)(2,1)S(1)}, u32[]{:S(2)}, u32[]{:S(2)}) collective-permute-start(bf16[2,512,128]{2,1,0:T(8,128)(2,1)S(1)} %pad_maximum_fusion.2), channel_id=1, source_target_pairs={{0,16},{4,20},{8,24},{12,28},{16,0},{20,4},{24,8},{28,12},{1,17},{... | collective-permute-start | bytes 786440 | tf_op jit(solution)/shard_map/ppermute | solution.py:24
  164.4 25.3 %collective-permute-start.29 = (s16[4,1040,128]{2,1,0:T(8,128)(2,1)S(1)}, s16[4,1040,128]{2,1,0:T(8,128)(2,1)S(1)}, u32[]{:S(2)}, u32[]{:S(2)}) collective-permute-start(s16[4,1040,128]{2,1,0:T(8,128)(2,1)S(1)} %shard_map.62), channel_id=1, source_target_pairs={{0,4},{4,0},{8,12},{12,8},{16,20},{20,16},{24,28},{28,24},{1,5},{5... | collective-permute-start | bytes 3194888 | tf_op jit(solution)/shard_map/ppermute | solution.py:24
  166.7 21.1 %collective-permute-start.31 = (s16[1040,128]{1,0:T(8,128)(2,1)S(1)}, s16[1040,128]{1,0:T(8,128)(2,1)S(1)}, u32[]{:S(2)}, u32[]{:S(2)}) collective-permute-start(s16[1040,128]{1,0:T(8,128)(2,1)S(1)} %get-tuple-element.85), channel_id=1, source_target_pairs={{0,16},{4,20},{8,24},{12,28},{16,0},{20,4},{24,8},{28,12},{1,17},{... | collective-permute-start | bytes 798728 | tf_op jit(solution)/shard_map/ppermute | solution.py:24
  168.2 19.7 %collective-permute-start.32 = (s16[1040,128]{1,0:T(8,128)(2,1)S(1)}, s16[1040,128]{1,0:T(8,128)(2,1)S(1)}, u32[]{:S(2)}, u32[]{:S(2)}) collective-permute-start(s16[1040,128]{1,0:T(8,128)(2,1)S(1)} %get-tuple-element.86), channel_id=1, source_target_pairs={{0,24},{4,28},{8,16},{12,20},{16,8},{20,12},{24,0},{28,4},{1,25},{... | collective-permute-start | bytes 798728 | tf_op jit(solution)/shard_map/ppermute | solution.py:24
  194.4 21.6 %collective-permute-start.34 = (s16[1040,128]{1,0:T(8,128)(2,1)S(1)}, s16[1040,128]{1,0:T(8,128)(2,1)S(1)}, u32[]{:S(2)}, u32[]{:S(2)}) collective-permute-start(s16[1040,128]{1,0:T(8,128)(2,1)S(1)} %get-tuple-element.90), channel_id=1, source_target_pairs={{0,16},{4,20},{8,24},{12,28},{16,0},{20,4},{24,8},{28,12},{1,17},{... | collective-permute-start | bytes 798728 | tf_op jit(solution)/shard_map/ppermute | solution.py:24
  194.6 21.4 %collective-permute-start.35 = (s16[1040,128]{1,0:T(8,128)(2,1)S(1)}, s16[1040,128]{1,0:T(8,128)(2,1)S(1)}, u32[]{:S(2)}, u32[]{:S(2)}) collective-permute-start(s16[1040,128]{1,0:T(8,128)(2,1)S(1)} %get-tuple-element.91), channel_id=1, source_target_pairs={{0,24},{4,28},{8,16},{12,20},{16,8},{20,12},{24,0},{28,4},{1,25},{... | collective-permute-start | bytes 798728 | tf_op jit(solution)/shard_map/ppermute | solution.py:24
  204.4 20.8 %collective-permute-start.39 = (s16[528,128]{1,0:T(8,128)(2,1)S(1)}, s16[528,128]{1,0:T(8,128)(2,1)S(1)}, u32[]{:S(2)}, u32[]{:S(2)}) collective-permute-start(s16[528,128]{1,0:T(8,128)(2,1)S(1)} %get-tuple-element.98), channel_id=1, source_target_pairs={{0,4},{4,0},{8,12},{12,8},{16,20},{20,16},{24,28},{28,24},{1,5},{5... | collective-permute-start | bytes 405512 | tf_op jit(solution)/shard_map/ppermute | solution.py:24
  217.0 29.7 %collective-permute-start.46 = (s16[1040,128]{1,0:T(8,128)(2,1)S(1)}, s16[1040,128]{1,0:T(8,128)(2,1)S(1)}, u32[]{:S(2)}, u32[]{:S(2)}) collective-permute-start(s16[1040,128]{1,0:T(8,128)(2,1)S(1)} %get-tuple-element.92.refs_0_), channel_id=1, source_target_pairs={{0,8},{4,12},{8,0},{12,4},{16,24},{20,28},{24,16},{28,20},{1,9},{5... | collective-permute-start | bytes 798728 | tf_op jit(solution)/shard_map/ppermute | solution.py:24
  223.7 23.0 %collective-permute-start.36 = (s16[1040,128]{1,0:T(8,128)(2,1)S(1)}, s16[1040,128]{1,0:T(8,128)(2,1)S(1)}, u32[]{:S(2)}, u32[]{:S(2)}) collective-permute-start(s16[1040,128]{1,0:T(8,128)(2,1)S(1)} %get-tuple-element.92.refs_0_), channel_id=1, source_target_pairs={{0,16},{4,20},{8,24},{12,28},{16,0},{20,4},{24,8},{28,12},{1,17},{... | collective-permute-start | bytes 798728 | tf_op jit(solution)/shard_map/ppermute | solution.py:24
  248.3 23.5 %collective-permute-start.48 = (s16[2,1040,128]{2,1,0:T(8,128)(2,1)S(1)}, s16[2,1040,128]{2,1,0:T(8,128)(2,1)S(1)}, u32[]{:S(2)}, u32[]{:S(2)}) collective-permute-start(s16[2,1040,128]{2,1,0:T(8,128)(2,1)S(1)} %pad_add_fusion.1), channel_id=1, source_target_pairs={{0,4},{4,0},{8,12},{12,8},{16,20},{20,16},{24,28},{28,24},{1,5},{5... | collective-permute-start | bytes 1597448 | tf_op jit(solution)/shard_map/ppermute | solution.py:24
  255.3 22.2 %collective-permute-start.51 = (s16[2,528,128]{2,1,0:T(8,128)(2,1)S(1)}, s16[2,528,128]{2,1,0:T(8,128)(2,1)S(1)}, u32[]{:S(2)}, u32[]{:S(2)}) collective-permute-start(s16[2,528,128]{2,1,0:T(8,128)(2,1)S(1)} %pad_add_fusion.2.refs_1_), channel_id=1, source_target_pairs={{0,24},{4,28},{8,16},{12,20},{16,8},{20,12},{24,0},{28,4},{1,25},{... | collective-permute-start | bytes 811016 | tf_op jit(solution)/shard_map/ppermute | solution.py:24
  258.1 21.6 %collective-permute-start.50 = (s16[2,528,128]{2,1,0:T(8,128)(2,1)S(1)}, s16[2,528,128]{2,1,0:T(8,128)(2,1)S(1)}, u32[]{:S(2)}, u32[]{:S(2)}) collective-permute-start(s16[2,528,128]{2,1,0:T(8,128)(2,1)S(1)} %pad_add_fusion.2.refs_1_), channel_id=1, source_target_pairs={{0,16},{4,20},{8,24},{12,28},{16,0},{20,4},{24,8},{28,12},{1,17},{... | collective-permute-start | bytes 811016 | tf_op jit(solution)/shard_map/ppermute | solution.py:24
  258.1 21.6 %collective-permute-start.49 = (s16[2,528,128]{2,1,0:T(8,128)(2,1)S(1)}, s16[2,528,128]{2,1,0:T(8,128)(2,1)S(1)}, u32[]{:S(2)}, u32[]{:S(2)}) collective-permute-start(s16[2,528,128]{2,1,0:T(8,128)(2,1)S(1)} %pad_add_fusion.2.refs_1_), channel_id=1, source_target_pairs={{0,8},{4,12},{8,0},{12,4},{16,24},{20,28},{24,16},{28,20},{1,9},{5... | collective-permute-start | bytes 811016 | tf_op jit(solution)/shard_map/ppermute | solution.py:24
  (38 other events, 404.2 us)

commit v4 on v3

--- a/solution.py
+++ b/solution.py
@@ -15,7 +15,8 @@
 LOW = 2
 GROUP = 8
 LANES = 128
-VMEM_BYTES = 24 << 20
+VMEM_BYTES = 20 << 20
+VMEM_FIRST = 56 << 20
 LIGHT = pl.CostEstimate(flops=1, bytes_accessed=1, transcendentals=0)
 WHOLE = pl.BlockSpec(memory_space=pltpu.VMEM)
 
@@ -57,8 +58,8 @@
         return wide[:rows] * jnp.exp2(wide[rows : rows + 1] * (1.0 / STEPS))
 
 
-def params():
-    return pltpu.CompilerParams(vmem_limit_bytes=VMEM_BYTES)
+def params(limit=VMEM_BYTES):
+    return pltpu.CompilerParams(vmem_limit_bytes=limit)
 
 
 class Layout:
@@ -211,7 +212,7 @@
             out_specs=[pl.BlockSpec(half.shape, lambda g, pos: (0, 0))] * 2,
             scratch_shapes=[pltpu.VMEM((time_rows, rank), F32)],
         ),
-        compiler_params=params(),
+        compiler_params=params(VMEM_FIRST),
         cost_estimate=LIGHT,
     )(pos, panel, *([scans] * count))
 
@@ -375,14 +376,15 @@
     )
 
 
-def scores_kernel(with_factor, length_ref, pos_ref, mine_ref, other_ref, *refs):
+def scores_kernel(with_factor, lengths_ref, subjects_ref, pos_ref, mine_ref, other_ref, *refs):
     out_ref = refs[-1]
+    length = lengths_ref[subjects_ref[pos_ref[1] * LOW + pos_ref[0]]]
     mine, other = mine_ref[...], other_ref[...]
     lower = pos_ref[2] == 0
     scores = jnp.concatenate([jnp.where(lower, mine, other), jnp.where(lower, other, mine)])
     if with_factor:
         scores = times_transpose(scores, refs[0][...])
-    live = lax.broadcasted_iota(jnp.int32, scores.shape, 0) < length_ref[0]
+    live = lax.broadcasted_iota(jnp.int32, scores.shape, 0) < length
     out_ref[...] = jnp.where(live, scores, 0.0).astype(BF16)
 
 
@@ -409,9 +411,6 @@
         me = lax.axis_index("subj")
         core = lax.axis_index("vox") % 2
         pos = jnp.stack([me % LOW, me // LOW, core]).astype(jnp.int32)
-        slot_ids = jnp.arange(block_subject.shape[0], dtype=jnp.int32)
-        subject = jnp.sum(jnp.where(slot_ids == me, block_subject, 0))
-        length = jnp.sum(jnp.where(slot_ids == subject, lengths, 0))
 
         def sketch_sum(scores, code):
             def part(after, j, ks, apart, per_step):
@@ -450,7 +449,6 @@
         def gather(first, second, gram):
             far_in = [swap(first, mask=k * LOW) for k in far]
             near_in = [first] + [swap(first, mask=k * LOW) for k in near[1:]]
-            low_near = swap(jnp.stack(near_in), mask=1)
             got = swap(second, mask=1)
             lower = pos[0] == 0
             pair = jnp.stack([jnp.where(lower, second, got), jnp.where(lower, got, second)])
@@ -458,6 +456,8 @@
             while mask < blocks:
                 gram = gram + swap_vox(gram, mask=mask)
                 mask *= 2
+            near_in, gram = lax.optimization_barrier((near_in, gram))
+            low_near = swap(jnp.stack(near_in), mask=1)
             gram = gram + swap(gram, mask=1)
             far_in, pair, gram = lax.optimization_barrier((far_in, pair, gram))
             low_far = swap(jnp.stack(far_in), mask=1)
@@ -478,12 +478,12 @@
             return pl.pallas_call(
                 functools.partial(scores_kernel, bool(factor)),
                 out_shape=jax.ShapeDtypeStruct((time_rows, rank), BF16),
-                in_specs=[pl.BlockSpec(memory_space=pltpu.SMEM)] * 2
+                in_specs=[pl.BlockSpec(memory_space=pltpu.SMEM)] * 3
                 + [WHOLE] * (2 + len(factor)),
                 out_specs=WHOLE,
                 compiler_params=params(),
                 cost_estimate=LIGHT,
-            )(length[None], pos, mine, other, *factor)
+            )(lengths, block_subject, pos, mine, other, *factor)
 
         def pass_over(scores, code):
             (first, gram_first), (second, gram_second) = sketch_sum(scores, code)
@@ -500,6 +500,7 @@
         total = project(scans, layout, pos, early)
         total = project(scans, layout, pos, late, total)
         total = project(scans, layout, pos, pairs[: high // 2], total)
+        total, inverse = lax.optimization_barrier((total, inverse))
         halves = project(scans, layout, pos, pairs[high // 2 :], total, True)
         scores = sum_scores(*halves, inverse)
         early, late, pairs, inverse = pass_over(scores, Fixed)

time: 284 us -> 279 us (0.982)
  waiting for transfers between devices: 138 us -> 121 us
  starting transfers between devices: 75.3 us -> 87 us
    ppermute x52, waiting for transfers between devices: 138 us -> 121 us  [exchange(): return lax.ppermute(value, axis, [(i, i ^ mask) for i in range(size)])]
    ppermute x52, starting transfers between devices: 75.3 us -> 87 us  [exchange(): return lax.ppermute(value, axis, [(i, i ^ mask) for i in range(size)])]
    pallas_call x1, Pallas kernels: 6.32 us -> 10.3 us  [first_project(): pl.pallas_call(functools.partial(first_kernel, count), out_shape=[half, h...]
  transfers between devices with their start and end apart: 52 -> 52, of which waited for: 31 -> 33; matrix products, arithmetic and copies ran while one was open for 1% -> 0% of each run, Pallas kernels for 12% -> 12%
where the time goes in v4:
time: 279 us
  waiting for transfers between devices  121 us (43%)
  starting transfers between devices  87 us (31%)
  Pallas kernels  57.2 us (21%)
  local copies, waits for them, and re-layouts  11 us (4%)
    ppermute x52, waiting for transfers between devices, exchange(): return lax.ppermute(value, axis, [(i, i ^ mask) for i in range(size)])  121 us
    ppermute x52, starting transfers between devices, exchange(): return lax.ppermute(value, axis, [(i, i ^ mask) for i in range(size)])  87 us
    pallas_call x8, Pallas kernels, sketch_part(): pl.pallas_call(functools.partial(sketch_kernel, code, apart, per_step), o...  15.9 us
    pallas_call x8, Pallas kernels, small_call(): pl.pallas_call(kernel, out_shape=out_shape, in_specs=[WHOLE] * len(args),...  11.8 us
    unnamed x20, local copies, waits for them, and re-layouts  11 us
    pallas_call x1, Pallas kernels, first_project(): pl.pallas_call(functools.partial(first_kernel, count), out_shape=[half, h...  10.3 us
    pallas_call x2, Pallas kernels, finish(): pl.pallas_call(functools.partial(finish_kernel, layout, items, base is no...  9.12 us
    pallas_call x4, Pallas kernels, project(): pl.pallas_call(functools.partial(project_kernel, base is not None, split,...  6.91 us
  transfers between devices with their start and end apart: 52, of which 33 were waited for; matrix products, arithmetic and copies ran while one was open for 0% of the time, Pallas kernels for 12%

profile of v4, /device:TPU:0, one launch (start us, length us, event | category | flops | bytes accessed | tf_op | source)
XLA Modules:
  0.0 278.6 jit_solution(1525502647052971308)
XLA Ops:
  0.7 10.3 %shard_map.46 = (f32[320,128]{1,0:T(8,128)}, f32[320,128]{1,0:T(8,128)}) custom-call(s32[3]{0:T(128)} %pad_add_fusion.3.pos_ref, bf16[12288,128]{1,0:T(8,128)(2,1)} %panel_ref.1, bf16[640,12288]{1,0:T(8,128)(2,1)} %refs_0_.19, bf16[640,12288]{1,0:T(8,128)(2,1)} %refs_0_.19, bf16[640,12288]{1,0:T(8,128)(2,1)} %refs_0_.19, bf16[640,12288]{1,0:T(8,128)(2,1)} %refs_0_.19), custom_call_target="tpu_custom_call" | custom-call | flops 1 | bytes 1 | tf_op jit(solution)/shard_map/pallas_call | solution.py:204
  16.5 4.5 %collective-permute-done.1 = f32[320,128]{1,0:T(8,128)S(1)} collective-permute-done((f32[320,128]{1,0:T(8,128)S(1)}, f32[320,128]{1,0:T(8,128)S(1)}, u32[]{:S(2)}, u32[]{:S(2)}) %collective-permute-start.1) | collective-permute-done | bytes 163872 | tf_op jit(solution)/shard_map/ppermute | solution.py:25
  23.2 5.5 %copy-done = bf16[640,12288]{1,0:T(8,128)(2,1)S(1)} copy-done((bf16[640,12288]{1,0:T(8,128)(2,1)S(1)}, bf16[640,12288]{1,0:T(8,128)(2,1)}, u32[]{:S(2)}) %copy-start) | copy-done | bytes 15728664
  41.1 14.6 %collective-permute-done.5.refs_2_ = bf16[1024,128]{1,0:T(8,128)(2,1)S(1)} collective-permute-done((bf16[1024,128]{1,0:T(8,128)(2,1)S(1)}, bf16[1024,128]{1,0:T(8,128)(2,1)S(1)}, u32[]{:S(2)}, u32[]{:S(2)}) %collective-permute-start.5) | collective-permute-done | bytes 262176 | tf_op jit(solution)/shard_map/ppermute | solution.py:25
  56.5 4.6 %collective-permute-start.7 = (bf16[1024,128]{1,0:T(8,128)(2,1)S(1)}, bf16[1024,128]{1,0:T(8,128)(2,1)S(1)}, u32[]{:S(2)}, u32[]{:S(2)}) collective-permute-start(bf16[1024,128]{1,0:T(8,128)(2,1)S(1)} %get-tuple-element.72), channel_id=1, source_target_pairs={{0,8},{4,12},{8,0},{12,4},{16,24},{20,28},{24,16},{28,20},{1,9},{5... | collective-permute-start | bytes 786440 | tf_op jit(solution)/shard_map/ppermute | solution.py:25
  66.8 4.5 %collective-permute-done.11.refs_1_ = bf16[512,128]{1,0:T(8,128)(2,1)S(1)} collective-permute-done((bf16[512,128]{1,0:T(8,128)(2,1)S(1)}, bf16[512,128]{1,0:T(8,128)(2,1)S(1)}, u32[]{:S(2)}, u32[]{:S(2)}) %collective-permute-start.11) | collective-permute-done | bytes 131104 | tf_op jit(solution)/shard_map/ppermute | solution.py:25
  73.1 9.5 %collective-permute-done.8.refs_2_ = bf16[1024,128]{1,0:T(8,128)(2,1)S(1)} collective-permute-done((bf16[1024,128]{1,0:T(8,128)(2,1)S(1)}, bf16[1024,128]{1,0:T(8,128)(2,1)S(1)}, u32[]{:S(2)}, u32[]{:S(2)}) %collective-permute-start.8) | collective-permute-done | bytes 262176 | tf_op jit(solution)/shard_map/ppermute | solution.py:25
  83.2 3.4 %collective-permute-start.15 = (bf16[1024,128]{1,0:T(8,128)(2,1)S(1)}, bf16[1024,128]{1,0:T(8,128)(2,1)S(1)}, u32[]{:S(2)}, u32[]{:S(2)}) collective-permute-start(bf16[1024,128]{1,0:T(8,128)(2,1)S(1)} %get-tuple-element.83.refs_4_), channel_id=1, source_target_pairs={{0,24},{4,28},{8,16},{12,20},{16,8},{20,12},{24,0},{28,4},{1,25},{... | collective-permute-start | bytes 786440 | tf_op jit(solution)/shard_map/ppermute | solution.py:25
  86.6 12.5 %collective-permute-start.14 = (bf16[1024,128]{1,0:T(8,128)(2,1)S(1)}, bf16[1024,128]{1,0:T(8,128)(2,1)S(1)}, u32[]{:S(2)}, u32[]{:S(2)}) collective-permute-start(bf16[1024,128]{1,0:T(8,128)(2,1)S(1)} %get-tuple-element.83.refs_4_), channel_id=1, source_target_pairs={{0,16},{4,20},{8,24},{12,28},{16,0},{20,4},{24,8},{28,12},{1,17},{... | collective-permute-start | bytes 786440 | tf_op jit(solution)/shard_map/ppermute | solution.py:25
  120.7 6.3 %collective-permute-start.25 = (bf16[2,512,128]{2,1,0:T(8,128)(2,1)S(1)}, bf16[2,512,128]{2,1,0:T(8,128)(2,1)S(1)}, u32[]{:S(2)}, u32[]{:S(2)}) collective-permute-start(bf16[2,512,128]{2,1,0:T(8,128)(2,1)S(1)} %pad_maximum_fusion.2), channel_id=1, source_target_pairs={{0,24},{4,28},{8,16},{12,20},{16,8},{20,12},{24,0},{28,4},{1,25},{... | collective-permute-start | bytes 786440 | tf_op jit(solution)/shard_map/ppermute | solution.py:25
  127.0 5.5 %copy-done.1 = bf16[640,12288]{1,0:T(8,128)(2,1)S(1)} copy-done((bf16[640,12288]{1,0:T(8,128)(2,1)S(1)}, bf16[640,12288]{1,0:T(8,128)(2,1)}, u32[]{:S(2)}) %copy-start.1) | copy-done | bytes 15728664
  134.5 4.1 %shard_map.59.refs_0_ = f32[128,128]{1,0:T(8,128)S(1)} custom-call(f32[128,128]{1,0:T(8,128)S(1)} %add.51.refs_0_, f32[128,128]{1,0:T(8,128)S(1)} %collective-permute-done.21.refs_1_, f32[128,128]{1,0:T(8,128)S(1)} %collective-permute-done.22.refs_2_, f32[128,128]{1,0:T(8,128)S(1)} %collective-permute-done.23.refs_3_), custom_call_target="tpu_custom_call" | custom-call | flops 1 | bytes 1 | tf_op jit(solution)/shard_map/pallas_call | solution.py:126
  146.7 4.8 %collective-permute-done.27 = f32[320,128]{1,0:T(8,128)S(1)} collective-permute-done((f32[320,128]{1,0:T(8,128)S(1)}, f32[320,128]{1,0:T(8,128)S(1)}, u32[]{:S(2)}, u32[]{:S(2)}) %collective-permute-start.27) | collective-permute-done | bytes 163872 | tf_op jit(solution)/shard_map/ppermute | solution.py:25
  165.0 15.9 %collective-permute-done.31.refs_2_ = s16[1040,128]{1,0:T(8,128)(2,1)S(1)} collective-permute-done((s16[1040,128]{1,0:T(8,128)(2,1)S(1)}, s16[1040,128]{1,0:T(8,128)(2,1)S(1)}, u32[]{:S(2)}, u32[]{:S(2)}) %collective-permute-start.31) | collective-permute-done | bytes 266272 | tf_op jit(solution)/shard_map/ppermute | solution.py:25
  188.8 3.6 %collective-permute-start.33 = (s16[1040,128]{1,0:T(8,128)(2,1)S(1)}, s16[1040,128]{1,0:T(8,128)(2,1)S(1)}, u32[]{:S(2)}, u32[]{:S(2)}) collective-permute-start(s16[1040,128]{1,0:T(8,128)(2,1)S(1)} %get-tuple-element.102), channel_id=1, source_target_pairs={{0,8},{4,12},{8,0},{12,4},{16,24},{20,28},{24,16},{28,20},{1,9},{5... | collective-permute-start | bytes 798728 | tf_op jit(solution)/shard_map/ppermute | solution.py:25
  197.1 6.1 %collective-permute-done.33.refs_1_ = s16[1040,128]{1,0:T(8,128)(2,1)S(1)} collective-permute-done((s16[1040,128]{1,0:T(8,128)(2,1)S(1)}, s16[1040,128]{1,0:T(8,128)(2,1)S(1)}, u32[]{:S(2)}, u32[]{:S(2)}) %collective-permute-start.33) | collective-permute-done | bytes 266272 | tf_op jit(solution)/shard_map/ppermute | solution.py:25
  203.2 10.9 %collective-permute-done.34.refs_2_ = s16[1040,128]{1,0:T(8,128)(2,1)S(1)} collective-permute-done((s16[1040,128]{1,0:T(8,128)(2,1)S(1)}, s16[1040,128]{1,0:T(8,128)(2,1)S(1)}, u32[]{:S(2)}, u32[]{:S(2)}) %collective-permute-start.34) | collective-permute-done | bytes 266272 | tf_op jit(solution)/shard_map/ppermute | solution.py:25
  214.9 4.8 %collective-permute-start.40 = (s16[1040,128]{1,0:T(8,128)(2,1)S(1)}, s16[1040,128]{1,0:T(8,128)(2,1)S(1)}, u32[]{:S(2)}, u32[]{:S(2)}) collective-permute-start(s16[1040,128]{1,0:T(8,128)(2,1)S(1)} %get-tuple-element.116.refs_0_), channel_id=1, source_target_pairs={{0,8},{4,12},{8,0},{12,4},{16,24},{20,28},{24,16},{28,20},{1,9},{5... | collective-permute-start | bytes 798728 | tf_op jit(solution)/shard_map/ppermute | solution.py:25
  233.9 9.7 %collective-permute-done.36.refs_2_ = s16[1040,128]{1,0:T(8,128)(2,1)S(1)} collective-permute-done((s16[1040,128]{1,0:T(8,128)(2,1)S(1)}, s16[1040,128]{1,0:T(8,128)(2,1)S(1)}, u32[]{:S(2)}, u32[]{:S(2)}) %collective-permute-start.36) | collective-permute-done | bytes 266272 | tf_op jit(solution)/shard_map/ppermute | solution.py:25
  246.1 3.9 %collective-permute-start.44 = (f32[128,128]{1,0:T(8,128)S(1)}, f32[128,128]{1,0:T(8,128)S(1)}, u32[]{:S(2)}, u32[]{:S(2)}) collective-permute-start(f32[128,128]{1,0:T(8,128)S(1)} %add.57.refs_0_), channel_id=1, source_target_pairs={{0,8},{4,12},{8,0},{12,4},{16,24},{20,28},{24,16},{28,20},{1,9},{5... | collective-permute-start | bytes 196616 | tf_op jit(solution)/shard_map/ppermute | solution.py:25
  252.3 9.0 %collective-permute-done.45.refs_2_ = f32[128,128]{1,0:T(8,128)S(1)} collective-permute-done((f32[128,128]{1,0:T(8,128)S(1)}, f32[128,128]{1,0:T(8,128)S(1)}, u32[]{:S(2)}, u32[]{:S(2)}) %collective-permute-start.45) | collective-permute-done | bytes 65568 | tf_op jit(solution)/shard_map/ppermute | solution.py:25
  263.4 4.1 %shard_map.70.inverse_ref = f32[128,128]{1,0:T(8,128)S(1)} custom-call(f32[128,128]{1,0:T(8,128)S(1)} %add.57.refs_0_, f32[128,128]{1,0:T(8,128)S(1)} %collective-permute-done.44.refs_1_, f32[128,128]{1,0:T(8,128)S(1)} %collective-permute-done.45.refs_2_, f32[128,128]{1,0:T(8,128)S(1)} %collective-permute-done.46.refs_3_), custom_call_target="tpu_custom_call" | custom-call | flops 1 | bytes 1 | tf_op jit(solution)/shard_map/pallas_call | solution.py:126
  267.5 5.5 %shard_map.71.refs_0_ = f32[12288,128]{1,0:T(8,128)} custom-call(s32[3]{0:T(128)S(1)} %copy-done.3, f32[128,128]{1,0:T(8,128)S(1)} %shard_map.70.inverse_ref, s16[1040,128]{1,0:T(8,128)(2,1)S(1)} %get-tuple-element.116.refs_0_, s16[1040,128]{1,0:T(8,128)(2,1)S(1)} %collective-permute-done.40.refs_1_, s16[1040,128]{1,0:T(8,128)(2,1)S(1)} %collective-permute-done.36.refs_2_, ...), custom_call_target="tpu_custom_call" | custom-call | tf_op jit(solution)/shard_map/pallas_call | solution.py:308
  274.8 3.6 %shard_map.72 = f32[12288,128]{1,0:T(8,128)} custom-call(s32[3]{0:T(128)S(1)} %copy-done.3, f32[128,128]{1,0:T(8,128)S(1)} %shard_map.70.inverse_ref, f32[12288,128]{1,0:T(8,128)} %shard_map.71.refs_0_, s16[2,528,128]{2,1,0:T(8,128)(2,1)S(1)} %pad_add_fusion.2.refs_1_, ...), custom_call_target="tpu_custom_call", output_to_operand_aliasing={{}: (2, {})} | custom-call | tf_op jit(solution)/shard_map/pallas_call | solution.py:308
  (149 shorter events, 110.8 us)
Async XLA Ops:
  31.0 25.3 %collective-permute-start.3 = (bf16[4,1024,128]{2,1,0:T(8,128)(2,1)S(1)}, bf16[4,1024,128]{2,1,0:T(8,128)(2,1)S(1)}, u32[]{:S(2)}, u32[]{:S(2)}) collective-permute-start(bf16[4,1024,128]{2,1,0:T(8,128)(2,1)S(1)} %shard_map.48), channel_id=1, source_target_pairs={{0,4},{4,0},{8,12},{12,8},{16,20},{20,16},{24,28},{28,24},{1,5},{5... | collective-permute-start | bytes 3145736 | tf_op jit(solution)/shard_map/ppermute | solution.py:25
  34.2 21.4 %collective-permute-start.5 = (bf16[1024,128]{1,0:T(8,128)(2,1)S(1)}, bf16[1024,128]{1,0:T(8,128)(2,1)S(1)}, u32[]{:S(2)}, u32[]{:S(2)}) collective-permute-start(bf16[1024,128]{1,0:T(8,128)(2,1)S(1)} %get-tuple-element.68), channel_id=1, source_target_pairs={{0,16},{4,20},{8,24},{12,28},{16,0},{20,4},{24,8},{28,12},{1,17},{... | collective-permute-start | bytes 786440 | tf_op jit(solution)/shard_map/ppermute | solution.py:25
  36.9 18.8 %collective-permute-start.6 = (bf16[1024,128]{1,0:T(8,128)(2,1)S(1)}, bf16[1024,128]{1,0:T(8,128)(2,1)S(1)}, u32[]{:S(2)}, u32[]{:S(2)}) collective-permute-start(bf16[1024,128]{1,0:T(8,128)(2,1)S(1)} %get-tuple-element.69), channel_id=1, source_target_pairs={{0,24},{4,28},{8,16},{12,20},{16,8},{20,12},{24,0},{28,4},{1,25},{... | collective-permute-start | bytes 786440 | tf_op jit(solution)/shard_map/ppermute | solution.py:25
  38.3 17.7 %collective-permute-start.4 = (bf16[1024,128]{1,0:T(8,128)(2,1)S(1)}, bf16[1024,128]{1,0:T(8,128)(2,1)S(1)}, u32[]{:S(2)}, u32[]{:S(2)}) collective-permute-start(bf16[1024,128]{1,0:T(8,128)(2,1)S(1)} %get-tuple-element.66), channel_id=1, source_target_pairs={{0,8},{4,12},{8,0},{12,4},{16,24},{20,28},{24,16},{28,20},{1,9},{5... | collective-permute-start | bytes 786440 | tf_op jit(solution)/shard_map/ppermute | solution.py:25
  61.2 21.3 %collective-permute-start.8 = (bf16[1024,128]{1,0:T(8,128)(2,1)S(1)}, bf16[1024,128]{1,0:T(8,128)(2,1)S(1)}, u32[]{:S(2)}, u32[]{:S(2)}) collective-permute-start(bf16[1024,128]{1,0:T(8,128)(2,1)S(1)} %get-tuple-element.73), channel_id=1, source_target_pairs={{0,16},{4,20},{8,24},{12,28},{16,0},{20,4},{24,8},{28,12},{1,17},{... | collective-permute-start | bytes 786440 | tf_op jit(solution)/shard_map/ppermute | solution.py:25
  63.2 19.3 %collective-permute-start.9 = (bf16[1024,128]{1,0:T(8,128)(2,1)S(1)}, bf16[1024,128]{1,0:T(8,128)(2,1)S(1)}, u32[]{:S(2)}, u32[]{:S(2)}) collective-permute-start(bf16[1024,128]{1,0:T(8,128)(2,1)S(1)} %get-tuple-element.74), channel_id=1, source_target_pairs={{0,24},{4,28},{8,16},{12,20},{16,8},{20,12},{24,0},{28,4},{1,25},{... | collective-permute-start | bytes 786440 | tf_op jit(solution)/shard_map/ppermute | solution.py:25
  71.7 28.0 %collective-permute-start.16 = (bf16[512,128]{1,0:T(8,128)(2,1)S(1)}, bf16[512,128]{1,0:T(8,128)(2,1)S(1)}, u32[]{:S(2)}, u32[]{:S(2)}) collective-permute-start(bf16[512,128]{1,0:T(8,128)(2,1)S(1)} %get-tuple-element.85), channel_id=1, source_target_pairs={{0,4},{4,0},{8,12},{12,8},{16,20},{20,16},{24,28},{28,24},{1,5},{5... | collective-permute-start | bytes 393224 | tf_op jit(solution)/shard_map/ppermute | solution.py:25
  83.2 27.8 %collective-permute-start.15 = (bf16[1024,128]{1,0:T(8,128)(2,1)S(1)}, bf16[1024,128]{1,0:T(8,128)(2,1)S(1)}, u32[]{:S(2)}, u32[]{:S(2)}) collective-permute-start(bf16[1024,128]{1,0:T(8,128)(2,1)S(1)} %get-tuple-element.83.refs_4_), channel_id=1, source_target_pairs={{0,24},{4,28},{8,16},{12,20},{16,8},{20,12},{24,0},{28,4},{1,25},{... | collective-permute-start | bytes 786440 | tf_op jit(solution)/shard_map/ppermute | solution.py:25
  86.6 24.3 %collective-permute-start.14 = (bf16[1024,128]{1,0:T(8,128)(2,1)S(1)}, bf16[1024,128]{1,0:T(8,128)(2,1)S(1)}, u32[]{:S(2)}, u32[]{:S(2)}) collective-permute-start(bf16[1024,128]{1,0:T(8,128)(2,1)S(1)} %get-tuple-element.83.refs_4_), channel_id=1, source_target_pairs={{0,16},{4,20},{8,24},{12,28},{16,0},{20,4},{24,8},{28,12},{1,17},{... | collective-permute-start | bytes 786440 | tf_op jit(solution)/shard_map/ppermute | solution.py:25
  106.5 32.1 %collective-permute-start.18 = (bf16[2,1024,128]{2,1,0:T(8,128)(2,1)S(1)}, bf16[2,1024,128]{2,1,0:T(8,128)(2,1)S(1)}, u32[]{:S(2)}, u32[]{:S(2)}) collective-permute-start(bf16[2,1024,128]{2,1,0:T(8,128)(2,1)S(1)} %pad_maximum_fusion), channel_id=1, source_target_pairs={{0,4},{4,0},{8,12},{12,8},{16,20},{20,16},{24,28},{28,24},{1,5},{5... | collective-permute-start | bytes 1572872 | tf_op jit(solution)/shard_map/ppermute | solution.py:25
  111.0 27.6 %collective-permute-start.19 = (bf16[2,1024,128]{2,1,0:T(8,128)(2,1)S(1)}, bf16[2,1024,128]{2,1,0:T(8,128)(2,1)S(1)}, u32[]{:S(2)}, u32[]{:S(2)}) collective-permute-start(bf16[2,1024,128]{2,1,0:T(8,128)(2,1)S(1)} %pad_maximum_fusion.1), channel_id=1, source_target_pairs={{0,4},{4,0},{8,12},{12,8},{16,20},{20,16},{24,28},{28,24},{1,5},{5... | collective-permute-start | bytes 1572872 | tf_op jit(solution)/shard_map/ppermute | solution.py:25
  118.3 22.4 %collective-permute-start.20 = (bf16[2,512,128]{2,1,0:T(8,128)(2,1)S(1)}, bf16[2,512,128]{2,1,0:T(8,128)(2,1)S(1)}, u32[]{:S(2)}, u32[]{:S(2)}) collective-permute-start(bf16[2,512,128]{2,1,0:T(8,128)(2,1)S(1)} %pad_maximum_fusion.2), channel_id=1, source_target_pairs={{0,8},{4,12},{8,0},{12,4},{16,24},{20,28},{24,16},{28,20},{1,9},{5... | collective-permute-start | bytes 786440 | tf_op jit(solution)/shard_map/ppermute | solution.py:25
  120.7 21.5 %collective-permute-start.25 = (bf16[2,512,128]{2,1,0:T(8,128)(2,1)S(1)}, bf16[2,512,128]{2,1,0:T(8,128)(2,1)S(1)}, u32[]{:S(2)}, u32[]{:S(2)}) collective-permute-start(bf16[2,512,128]{2,1,0:T(8,128)(2,1)S(1)} %pad_maximum_fusion.2), channel_id=1, source_target_pairs={{0,24},{4,28},{8,16},{12,20},{16,8},{20,12},{24,0},{28,4},{1,25},{... | collective-permute-start | bytes 786440 | tf_op jit(solution)/shard_map/ppermute | solution.py:25
  156.9 25.6 %collective-permute-start.29 = (s16[4,1040,128]{2,1,0:T(8,128)(2,1)S(1)}, s16[4,1040,128]{2,1,0:T(8,128)(2,1)S(1)}, u32[]{:S(2)}, u32[]{:S(2)}) collective-permute-start(s16[4,1040,128]{2,1,0:T(8,128)(2,1)S(1)} %shard_map.62), channel_id=1, source_target_pairs={{0,4},{4,0},{8,12},{12,8},{16,20},{20,16},{24,28},{28,24},{1,5},{5... | collective-permute-start | bytes 3194888 | tf_op jit(solution)/shard_map/ppermute | solution.py:25
  160.3 20.7 %collective-permute-start.31 = (s16[1040,128]{1,0:T(8,128)(2,1)S(1)}, s16[1040,128]{1,0:T(8,128)(2,1)S(1)}, u32[]{:S(2)}, u32[]{:S(2)}) collective-permute-start(s16[1040,128]{1,0:T(8,128)(2,1)S(1)} %get-tuple-element.98), channel_id=1, source_target_pairs={{0,16},{4,20},{8,24},{12,28},{16,0},{20,4},{24,8},{28,12},{1,17},{... | collective-permute-start | bytes 798728 | tf_op jit(solution)/shard_map/ppermute | solution.py:25
  163.1 17.8 %collective-permute-start.32 = (s16[1040,128]{1,0:T(8,128)(2,1)S(1)}, s16[1040,128]{1,0:T(8,128)(2,1)S(1)}, u32[]{:S(2)}, u32[]{:S(2)}) collective-permute-start(s16[1040,128]{1,0:T(8,128)(2,1)S(1)} %get-tuple-element.99), channel_id=1, source_target_pairs={{0,24},{4,28},{8,16},{12,20},{16,8},{20,12},{24,0},{28,4},{1,25},{... | collective-permute-start | bytes 798728 | tf_op jit(solution)/shard_map/ppermute | solution.py:25
  163.1 19.2 %collective-permute-start.30 = (s16[1040,128]{1,0:T(8,128)(2,1)S(1)}, s16[1040,128]{1,0:T(8,128)(2,1)S(1)}, u32[]{:S(2)}, u32[]{:S(2)}) collective-permute-start(s16[1040,128]{1,0:T(8,128)(2,1)S(1)} %get-tuple-element.96), channel_id=1, source_target_pairs={{0,8},{4,12},{8,0},{12,4},{16,24},{20,28},{24,16},{28,20},{1,9},{5... | collective-permute-start | bytes 798728 | tf_op jit(solution)/shard_map/ppermute | solution.py:25
  192.4 21.6 %collective-permute-start.34 = (s16[1040,128]{1,0:T(8,128)(2,1)S(1)}, s16[1040,128]{1,0:T(8,128)(2,1)S(1)}, u32[]{:S(2)}, u32[]{:S(2)}) collective-permute-start(s16[1040,128]{1,0:T(8,128)(2,1)S(1)} %get-tuple-element.103), channel_id=1, source_target_pairs={{0,16},{4,20},{8,24},{12,28},{16,0},{20,4},{24,8},{28,12},{1,17},{... | collective-permute-start | bytes 798728 | tf_op jit(solution)/shard_map/ppermute | solution.py:25
  193.7 20.4 %collective-permute-start.35 = (s16[1040,128]{1,0:T(8,128)(2,1)S(1)}, s16[1040,128]{1,0:T(8,128)(2,1)S(1)}, u32[]{:S(2)}, u32[]{:S(2)}) collective-permute-start(s16[1040,128]{1,0:T(8,128)(2,1)S(1)} %get-tuple-element.104), channel_id=1, source_target_pairs={{0,24},{4,28},{8,16},{12,20},{16,8},{20,12},{24,0},{28,4},{1,25},{... | collective-permute-start | bytes 798728 | tf_op jit(solution)/shard_map/ppermute | solution.py:25
  195.5 25.9 %collective-permute-start.39 = (s16[528,128]{1,0:T(8,128)(2,1)S(1)}, s16[528,128]{1,0:T(8,128)(2,1)S(1)}, u32[]{:S(2)}, u32[]{:S(2)}) collective-permute-start(s16[528,128]{1,0:T(8,128)(2,1)S(1)} %get-tuple-element.111), channel_id=1, source_target_pairs={{0,4},{4,0},{8,12},{12,8},{16,20},{20,16},{24,28},{28,24},{1,5},{5... | collective-permute-start | bytes 405512 | tf_op jit(solution)/shard_map/ppermute | solution.py:25
  221.4 22.2 %collective-permute-start.36 = (s16[1040,128]{1,0:T(8,128)(2,1)S(1)}, s16[1040,128]{1,0:T(8,128)(2,1)S(1)}, u32[]{:S(2)}, u32[]{:S(2)}) collective-permute-start(s16[1040,128]{1,0:T(8,128)(2,1)S(1)} %get-tuple-element.116.refs_0_), channel_id=1, source_target_pairs={{0,16},{4,20},{8,24},{12,28},{16,0},{20,4},{24,8},{28,12},{1,17},{... | collective-permute-start | bytes 798728 | tf_op jit(solution)/shard_map/ppermute | solution.py:25
  230.0 37.5 %collective-permute-start.47 = (s16[2,1040,128]{2,1,0:T(8,128)(2,1)S(1)}, s16[2,1040,128]{2,1,0:T(8,128)(2,1)S(1)}, u32[]{:S(2)}, u32[]{:S(2)}) collective-permute-start(s16[2,1040,128]{2,1,0:T(8,128)(2,1)S(1)} %pad_add_fusion), channel_id=1, source_target_pairs={{0,4},{4,0},{8,12},{12,8},{16,20},{20,16},{24,28},{28,24},{1,5},{5... | collective-permute-start | bytes 1597448 | tf_op jit(solution)/shard_map/ppermute | solution.py:25
  243.6 23.8 %collective-permute-start.48 = (s16[2,1040,128]{2,1,0:T(8,128)(2,1)S(1)}, s16[2,1040,128]{2,1,0:T(8,128)(2,1)S(1)}, u32[]{:S(2)}, u32[]{:S(2)}) collective-permute-start(s16[2,1040,128]{2,1,0:T(8,128)(2,1)S(1)} %pad_add_fusion.1), channel_id=1, source_target_pairs={{0,4},{4,0},{8,12},{12,8},{16,20},{20,16},{24,28},{28,24},{1,5},{5... | collective-permute-start | bytes 1597448 | tf_op jit(solution)/shard_map/ppermute | solution.py:25
  251.8 21.2 %collective-permute-start.51 = (s16[2,528,128]{2,1,0:T(8,128)(2,1)S(1)}, s16[2,528,128]{2,1,0:T(8,128)(2,1)S(1)}, u32[]{:S(2)}, u32[]{:S(2)}) collective-permute-start(s16[2,528,128]{2,1,0:T(8,128)(2,1)S(1)} %pad_add_fusion.2.refs_1_), channel_id=1, source_target_pairs={{0,24},{4,28},{8,16},{12,20},{16,8},{20,12},{24,0},{28,4},{1,25},{... | collective-permute-start | bytes 811016 | tf_op jit(solution)/shard_map/ppermute | solution.py:25
  (38 other events, 414.4 us)

commit v5 on v4

--- a/solution.py
+++ b/solution.py
@@ -15,8 +15,7 @@
 LOW = 2
 GROUP = 8
 LANES = 128
-VMEM_BYTES = 20 << 20
-VMEM_FIRST = 56 << 20
+VMEM_BYTES = 48 << 20
 LIGHT = pl.CostEstimate(flops=1, bytes_accessed=1, transcendentals=0)
 WHOLE = pl.BlockSpec(memory_space=pltpu.VMEM)
 
@@ -58,8 +57,8 @@
         return wide[:rows] * jnp.exp2(wide[rows : rows + 1] * (1.0 / STEPS))
 
 
-def params(limit=VMEM_BYTES):
-    return pltpu.CompilerParams(vmem_limit_bytes=limit)
+def params():
+    return pltpu.CompilerParams(vmem_limit_bytes=VMEM_BYTES)
 
 
 class Layout:
@@ -212,7 +211,7 @@
             out_specs=[pl.BlockSpec(half.shape, lambda g, pos: (0, 0))] * 2,
             scratch_shapes=[pltpu.VMEM((time_rows, rank), F32)],
         ),
-        compiler_params=params(VMEM_FIRST),
+        compiler_params=params(),
         cost_estimate=LIGHT,
     )(pos, panel, *([scans] * count))
 
@@ -318,6 +317,7 @@
         ],
         input_output_aliases={2: 0} if bases else {},
         compiler_params=params(),
+        cost_estimate=LIGHT,
     )(pos, inverse, *bases, *arrays)
 
 
@@ -425,7 +425,9 @@
             got_second = [swap(second[k - 1], mask=k * LOW) for k in ks[1:]]
             home = part(second[0], 0, ks, False, high // 2)
             (second_own,) = part(second[0], None, ks[:1], True, 1)
-            got_away, *got_second = lax.optimization_barrier((got_away, *got_second))
+            got_away, got_second, home, second_own = lax.optimization_barrier(
+                (got_away, got_second, home, second_own)
+            )
             piece = jax.ShapeDtypeStruct((layout.single + code.pad, rank), code.dtype)
             first = small_call(
                 functools.partial(add_pieces_kernel, code, high), [piece] * high, home, got_away
@@ -439,6 +441,7 @@
                 in_specs=[pl.BlockSpec(memory_space=pltpu.SMEM)] + [WHOLE] * high,
                 out_specs=[WHOLE, WHOLE],
                 compiler_params=params(),
+                cost_estimate=LIGHT,
             )(pos, second_own, *got_second)
             got_send = swap(send, mask=1)
             return (
@@ -447,12 +450,14 @@
             )
 
         def gather(first, second, gram):
+            gram = gram + swap_vox(gram, mask=1)
+            first, second, gram = lax.optimization_barrier((first, second, gram))
             far_in = [swap(first, mask=k * LOW) for k in far]
             near_in = [first] + [swap(first, mask=k * LOW) for k in near[1:]]
             got = swap(second, mask=1)
             lower = pos[0] == 0
             pair = jnp.stack([jnp.where(lower, second, got), jnp.where(lower, got, second)])
-            mask = 1
+            mask = 2
             while mask < blocks:
                 gram = gram + swap_vox(gram, mask=mask)
                 mask *= 2

time: 279 us -> 283 us (1.014)
  Pallas kernels: 57.2 us -> 76.6 us
  starting transfers between devices: 87 us -> 74.6 us
  local copies, waits for them, and re-layouts: 11 us -> 1.9 us
  waiting for transfers between devices: 121 us -> 129 us
    pallas_call x8, Pallas kernels: 15.9 us -> 28.4 us  [sketch_part(): pl.pallas_call(functools.partial(sketch_kernel, code, apart, per_step), o...]
    ppermute x52, starting transfers between devices: 87 us -> 74.6 us  [exchange(): return lax.ppermute(value, axis, [(i, i ^ mask) for i in range(size)])]
    unnamed x20 -> x6, local copies, waits for them, and re-layouts: 11 us -> 1.9 us
    pallas_call x4, Pallas kernels: 6.91 us -> 15.4 us  [project(): pl.pallas_call(functools.partial(project_kernel, base is not None, split,...]
    ppermute x52, waiting for transfers between devices: 121 us -> 129 us  [exchange(): return lax.ppermute(value, axis, [(i, i ^ mask) for i in range(size)])]
  transfers between devices with their start and end apart: 52 -> 52, of which waited for: 33 -> 31; matrix products, arithmetic and copies ran while one was open for 0% -> 0% of each run, Pallas kernels for 12% -> 17%
where the time goes in v5:
time: 283 us
  waiting for transfers between devices  129 us (46%)
  Pallas kernels  76.6 us (27%)
  starting transfers between devices  74.6 us (26%)
    ppermute x52, waiting for transfers between devices, exchange(): return lax.ppermute(value, axis, [(i, i ^ mask) for i in range(size)])  129 us
    ppermute x52, starting transfers between devices, exchange(): return lax.ppermute(value, axis, [(i, i ^ mask) for i in range(size)])  74.6 us
    pallas_call x8, Pallas kernels, sketch_part(): pl.pallas_call(functools.partial(sketch_kernel, code, apart, per_step), o...  28.4 us
    pallas_call x4, Pallas kernels, project(): pl.pallas_call(functools.partial(project_kernel, base is not None, split,...  15.4 us
    pallas_call x8, Pallas kernels, small_call(): pl.pallas_call(kernel, out_shape=out_shape, in_specs=[WHOLE] * len(args),...  11.7 us
    pallas_call x2, Pallas kernels, finish(): pl.pallas_call(functools.partial(finish_kernel, layout, items, base is no...  9.12 us
    pallas_call x1, Pallas kernels, first_project(): pl.pallas_call(functools.partial(first_kernel, count), out_shape=[half, h...  8.72 us
  transfers between devices with their start and end apart: 52, of which 31 were waited for; matrix products, arithmetic and copies ran while one was open for 0% of the time, Pallas kernels for 17%

profile of v5, /device:TPU:0, one launch (start us, length us, event | category | flops | bytes accessed | tf_op | source)
XLA Modules:
  0.0 282.7 jit_solution(11144349236547829226)
XLA Ops:
  2.0 8.7 %shard_map.46 = (f32[320,128]{1,0:T(8,128)S(1)}, f32[320,128]{1,0:T(8,128)S(1)}) custom-call(s32[3]{0:T(128)S(1)} %pad_add_fusion.3.pos_ref, bf16[12288,128]{1,0:T(8,128)(2,1)S(1)} %copy-done, bf16[640,12288]{1,0:T(8,128)(2,1)} %refs_0_.19, bf16[640,12288]{1,0:T(8,128)(2,1)} %refs_0_.19, bf16[640,12288]{1,0:T(8,128)(2,1)} %refs_0_.19, ...), custom_call_target="tpu_custom_call" | custom-call | flops 1 | bytes 1 | tf_op jit(solution)/shard_map/pallas_call | solution.py:203
  15.2 4.5 %collective-permute-done.1 = f32[320,128]{1,0:T(8,128)S(1)} collective-permute-done((f32[320,128]{1,0:T(8,128)S(1)}, f32[320,128]{1,0:T(8,128)S(1)}, u32[]{:S(2)}, u32[]{:S(2)}) %collective-permute-start.1) | collective-permute-done | bytes 163872 | tf_op jit(solution)/shard_map/ppermute | solution.py:24
  37.5 4.0 %shard_map.50.own_ref = bf16[4,1024,128]{2,1,0:T(8,128)(2,1)S(1)} custom-call(s32[3]{0:T(128)S(1)} %pad_add_fusion.3.pos_ref, bf16[640,128]{1,0:T(8,128)(2,1)S(1)} %shard_map.47.scores_ref, bf16[640,12288]{1,0:T(8,128)(2,1)} %refs_0_.19, bf16[640,12288]{1,0:T(8,128)(2,1)} %refs_0_.19), custom_call_target="tpu_custom_call" | custom-call | flops 1 | bytes 1 | tf_op jit(solution)/shard_map/pallas_call | solution.py:109
  41.5 10.9 %collective-permute-done.5.refs_2_ = bf16[1024,128]{1,0:T(8,128)(2,1)S(1)} collective-permute-done((bf16[1024,128]{1,0:T(8,128)(2,1)S(1)}, bf16[1024,128]{1,0:T(8,128)(2,1)S(1)}, u32[]{:S(2)}, u32[]{:S(2)}) %collective-permute-start.5) | collective-permute-done | bytes 262176 | tf_op jit(solution)/shard_map/ppermute | solution.py:24
  52.9 5.0 %collective-permute-start.7 = (bf16[1024,128]{1,0:T(8,128)(2,1)S(1)}, bf16[1024,128]{1,0:T(8,128)(2,1)S(1)}, u32[]{:S(2)}, u32[]{:S(2)}) collective-permute-start(bf16[1024,128]{1,0:T(8,128)(2,1)S(1)} %get-tuple-element.83), channel_id=1, source_target_pairs={{0,8},{4,12},{8,0},{12,4},{16,24},{20,28},{24,16},{28,20},{1,9},{5... | collective-permute-start | bytes 786440 | tf_op jit(solution)/shard_map/ppermute | solution.py:24
  62.6 4.5 %collective-permute-done.10.refs_1_ = bf16[512,128]{1,0:T(8,128)(2,1)S(1)} collective-permute-done((bf16[512,128]{1,0:T(8,128)(2,1)S(1)}, bf16[512,128]{1,0:T(8,128)(2,1)S(1)}, u32[]{:S(2)}, u32[]{:S(2)}) %collective-permute-start.10) | collective-permute-done | bytes 131104 | tf_op jit(solution)/shard_map/ppermute | solution.py:24
  69.8 9.5 %collective-permute-done.8.refs_2_ = bf16[1024,128]{1,0:T(8,128)(2,1)S(1)} collective-permute-done((bf16[1024,128]{1,0:T(8,128)(2,1)S(1)}, bf16[1024,128]{1,0:T(8,128)(2,1)S(1)}, u32[]{:S(2)}, u32[]{:S(2)}) %collective-permute-start.8) | collective-permute-done | bytes 262176 | tf_op jit(solution)/shard_map/ppermute | solution.py:24
  90.9 12.4 %collective-permute-done.12.refs_5_ = bf16[1024,128]{1,0:T(8,128)(2,1)S(1)} collective-permute-done((bf16[1024,128]{1,0:T(8,128)(2,1)S(1)}, bf16[1024,128]{1,0:T(8,128)(2,1)S(1)}, u32[]{:S(2)}, u32[]{:S(2)}) %collective-permute-start.12) | collective-permute-done | bytes 262176 | tf_op jit(solution)/shard_map/ppermute | solution.py:24
  122.6 4.6 %shard_map.56.refs_0_ = f32[640,128]{1,0:T(8,128)S(1)} custom-call(s32[3]{0:T(128)S(1)} %pad_add_fusion.3.pos_ref, bf16[640,12288]{1,0:T(8,128)(2,1)} %refs_0_.19, bf16[640,12288]{1,0:T(8,128)(2,1)} %refs_0_.19, bf16[640,12288]{1,0:T(8,128)(2,1)} %refs_0_.19, bf16[640,12288]{1,0:T(8,128)(2,1)} %refs_0_.19, bf16[1024,128]{1,0:T(8,128)(2,1)S(1)} %get-tuple-element.98.refs_4_, ...), custom_call_target="tpu_custom_call" | custom-call | flops 1 | bytes 1 | tf_op jit(solution)/shard_map/pallas_call | solution.py:255
  127.2 4.1 %shard_map.59.refs_0_ = f32[128,128]{1,0:T(8,128)S(1)} custom-call(f32[128,128]{1,0:T(8,128)S(1)} %add.51.refs_0_, f32[128,128]{1,0:T(8,128)S(1)} %collective-permute-done.21.refs_1_, f32[128,128]{1,0:T(8,128)S(1)} %collective-permute-done.22.refs_2_, f32[128,128]{1,0:T(8,128)S(1)} %collective-permute-done.23.refs_3_), custom_call_target="tpu_custom_call" | custom-call | flops 1 | bytes 1 | tf_op jit(solution)/shard_map/pallas_call | solution.py:125
  131.3 4.6 %shard_map.57.refs_0_ = f32[640,128]{1,0:T(8,128)S(1)} custom-call(s32[3]{0:T(128)S(1)} %pad_add_fusion.3.pos_ref, f32[640,128]{1,0:T(8,128)S(1)} %shard_map.56.refs_0_, bf16[640,12288]{1,0:T(8,128)(2,1)} %refs_0_.19, bf16[640,12288]{1,0:T(8,128)(2,1)} %refs_0_.19, bf16[640,12288]{1,0:T(8,128)(2,1)} %refs_0_.19, bf16[640,12288]{1,0:T(8,128)(2,1)} %refs_0_.19, ...), custom_call_target="tpu_custom_call" | custom-call | flops 1 | bytes 1 | tf_op jit(solution)/shard_map/pallas_call | solution.py:255
  139.0 4.1 %collective-permute-done.24 = bf16[2,512,128]{2,1,0:T(8,128)(2,1)S(1)} collective-permute-done((bf16[2,512,128]{2,1,0:T(8,128)(2,1)S(1)}, bf16[2,512,128]{2,1,0:T(8,128)(2,1)S(1)}, u32[]{:S(2)}, u32[]{:S(2)}) %collective-permute-start.24) | collective-permute-done | bytes 262176 | tf_op jit(solution)/shard_map/ppermute | solution.py:24
  148.4 5.7 %collective-permute-done.27 = f32[320,128]{1,0:T(8,128)S(1)} collective-permute-done((f32[320,128]{1,0:T(8,128)S(1)}, f32[320,128]{1,0:T(8,128)S(1)}, u32[]{:S(2)}, u32[]{:S(2)}) %collective-permute-start.27) | collective-permute-done | bytes 163872 | tf_op jit(solution)/shard_map/ppermute | solution.py:24
  156.5 4.3 %shard_map.62 = s16[4,1040,128]{2,1,0:T(8,128)(2,1)S(1)} custom-call(s32[3]{0:T(128)S(1)} %pad_add_fusion.3.pos_ref, bf16[640,128]{1,0:T(8,128)(2,1)S(1)} %shard_map.61.scores_ref, bf16[640,12288]{1,0:T(8,128)(2,1)} %refs_0_.19, bf16[640,12288]{1,0:T(8,128)(2,1)} %refs_0_.19), custom_call_target="tpu_custom_call" | custom-call | flops 1 | bytes 1 | tf_op jit(solution)/shard_map/pallas_call | solution.py:109
  171.5 4.1 %shard_map.64.own_ref = s16[4,1040,128]{2,1,0:T(8,128)(2,1)S(1)} custom-call(s32[3]{0:T(128)S(1)} %pad_add_fusion.3.pos_ref, bf16[640,128]{1,0:T(8,128)(2,1)S(1)} %shard_map.61.scores_ref, bf16[640,12288]{1,0:T(8,128)(2,1)} %refs_0_.19, bf16[640,12288]{1,0:T(8,128)(2,1)} %refs_0_.19), custom_call_target="tpu_custom_call" | custom-call | flops 1 | bytes 1 | tf_op jit(solution)/shard_map/pallas_call | solution.py:109
  175.6 10.8 %collective-permute-done.31.refs_2_ = s16[1040,128]{1,0:T(8,128)(2,1)S(1)} collective-permute-done((s16[1040,128]{1,0:T(8,128)(2,1)S(1)}, s16[1040,128]{1,0:T(8,128)(2,1)S(1)}, u32[]{:S(2)}, u32[]{:S(2)}) %collective-permute-start.31) | collective-permute-done | bytes 266272 | tf_op jit(solution)/shard_map/ppermute | solution.py:24
  188.3 4.9 %collective-permute-start.33 = (s16[1040,128]{1,0:T(8,128)(2,1)S(1)}, s16[1040,128]{1,0:T(8,128)(2,1)S(1)}, u32[]{:S(2)}, u32[]{:S(2)}) collective-permute-start(s16[1040,128]{1,0:T(8,128)(2,1)S(1)} %get-tuple-element.118), channel_id=1, source_target_pairs={{0,8},{4,12},{8,0},{12,4},{16,24},{20,28},{24,16},{28,20},{1,9},{5... | collective-permute-start | bytes 798728 | tf_op jit(solution)/shard_map/ppermute | solution.py:24
  203.6 11.2 %collective-permute-done.34.refs_2_ = s16[1040,128]{1,0:T(8,128)(2,1)S(1)} collective-permute-done((s16[1040,128]{1,0:T(8,128)(2,1)S(1)}, s16[1040,128]{1,0:T(8,128)(2,1)S(1)}, u32[]{:S(2)}, u32[]{:S(2)}) %collective-permute-start.34) | collective-permute-done | bytes 266272 | tf_op jit(solution)/shard_map/ppermute | solution.py:24
  219.2 4.6 %collective-permute-start.41 = (s16[1040,128]{1,0:T(8,128)(2,1)S(1)}, s16[1040,128]{1,0:T(8,128)(2,1)S(1)}, u32[]{:S(2)}, u32[]{:S(2)}) collective-permute-start(s16[1040,128]{1,0:T(8,128)(2,1)S(1)} %get-tuple-element.136.refs_0_), channel_id=1, source_target_pairs={{0,8},{4,12},{8,0},{12,4},{16,24},{20,28},{24,16},{28,20},{1,9},{5... | collective-permute-start | bytes 798728 | tf_op jit(solution)/shard_map/ppermute | solution.py:24
  225.5 5.1 %collective-permute-done.41.refs_1_ = s16[1040,128]{1,0:T(8,128)(2,1)S(1)} collective-permute-done((s16[1040,128]{1,0:T(8,128)(2,1)S(1)}, s16[1040,128]{1,0:T(8,128)(2,1)S(1)}, u32[]{:S(2)}, u32[]{:S(2)}) %collective-permute-start.41) | collective-permute-done | bytes 266272 | tf_op jit(solution)/shard_map/ppermute | solution.py:24
  238.5 9.9 %collective-permute-done.38.refs_2_ = s16[1040,128]{1,0:T(8,128)(2,1)S(1)} collective-permute-done((s16[1040,128]{1,0:T(8,128)(2,1)S(1)}, s16[1040,128]{1,0:T(8,128)(2,1)S(1)}, u32[]{:S(2)}, u32[]{:S(2)}) %collective-permute-start.38) | collective-permute-done | bytes 266272 | tf_op jit(solution)/shard_map/ppermute | solution.py:24
  260.4 4.1 %shard_map.70.inverse_ref = f32[128,128]{1,0:T(8,128)S(1)} custom-call(f32[128,128]{1,0:T(8,128)S(1)} %add.57.refs_0_, f32[128,128]{1,0:T(8,128)S(1)} %collective-permute-done.44.refs_1_, f32[128,128]{1,0:T(8,128)S(1)} %collective-permute-done.45.refs_2_, f32[128,128]{1,0:T(8,128)S(1)} %collective-permute-done.46.refs_3_), custom_call_target="tpu_custom_call" | custom-call | flops 1 | bytes 1 | tf_op jit(solution)/shard_map/pallas_call | solution.py:125
  264.5 5.5 %shard_map.71.refs_0_ = f32[12288,128]{1,0:T(8,128)} custom-call(s32[3]{0:T(128)S(1)} %pad_add_fusion.3.pos_ref, f32[128,128]{1,0:T(8,128)S(1)} %shard_map.70.inverse_ref, s16[1040,128]{1,0:T(8,128)(2,1)S(1)} %get-tuple-element.136.refs_0_, s16[1040,128]{1,0:T(8,128)(2,1)S(1)} %collective-permute-done.41.refs_1_, ...), custom_call_target="tpu_custom_call" | custom-call | flops 1 | bytes 1 | tf_op jit(solution)/shard_map/pallas_call | solution.py:307
  270.1 8.9 %collective-permute-done.50.refs_3_ = s16[2,528,128]{2,1,0:T(8,128)(2,1)S(1)} collective-permute-done((s16[2,528,128]{2,1,0:T(8,128)(2,1)S(1)}, s16[2,528,128]{2,1,0:T(8,128)(2,1)S(1)}, u32[]{:S(2)}, u32[]{:S(2)}) %collective-permute-start.50) | collective-permute-done | bytes 270368 | tf_op jit(solution)/shard_map/ppermute | solution.py:24
  (134 shorter events, 126.1 us)
Async XLA Ops:
  25.6 27.1 %collective-permute-start.3 = (bf16[4,1024,128]{2,1,0:T(8,128)(2,1)S(1)}, bf16[4,1024,128]{2,1,0:T(8,128)(2,1)S(1)}, u32[]{:S(2)}, u32[]{:S(2)}) collective-permute-start(bf16[4,1024,128]{2,1,0:T(8,128)(2,1)S(1)} %shard_map.48), channel_id=1, source_target_pairs={{0,4},{4,0},{8,12},{12,8},{16,20},{20,16},{24,28},{28,24},{1,5},{5... | collective-permute-start | bytes 3145736 | tf_op jit(solution)/shard_map/ppermute | solution.py:24
  31.0 21.4 %collective-permute-start.5 = (bf16[1024,128]{1,0:T(8,128)(2,1)S(1)}, bf16[1024,128]{1,0:T(8,128)(2,1)S(1)}, u32[]{:S(2)}, u32[]{:S(2)}) collective-permute-start(bf16[1024,128]{1,0:T(8,128)(2,1)S(1)} %get-tuple-element.77), channel_id=1, source_target_pairs={{0,16},{4,20},{8,24},{12,28},{16,0},{20,4},{24,8},{28,12},{1,17},{... | collective-permute-start | bytes 786440 | tf_op jit(solution)/shard_map/ppermute | solution.py:24
  33.7 18.8 %collective-permute-start.6 = (bf16[1024,128]{1,0:T(8,128)(2,1)S(1)}, bf16[1024,128]{1,0:T(8,128)(2,1)S(1)}, u32[]{:S(2)}, u32[]{:S(2)}) collective-permute-start(bf16[1024,128]{1,0:T(8,128)(2,1)S(1)} %get-tuple-element.78), channel_id=1, source_target_pairs={{0,24},{4,28},{8,16},{12,20},{16,8},{20,12},{24,0},{28,4},{1,25},{... | collective-permute-start | bytes 786440 | tf_op jit(solution)/shard_map/ppermute | solution.py:24
  35.0 17.6 %collective-permute-start.4 = (bf16[1024,128]{1,0:T(8,128)(2,1)S(1)}, bf16[1024,128]{1,0:T(8,128)(2,1)S(1)}, u32[]{:S(2)}, u32[]{:S(2)}) collective-permute-start(bf16[1024,128]{1,0:T(8,128)(2,1)S(1)} %get-tuple-element.76), channel_id=1, source_target_pairs={{0,8},{4,12},{8,0},{12,4},{16,24},{20,28},{24,16},{28,20},{1,9},{5... | collective-permute-start | bytes 786440 | tf_op jit(solution)/shard_map/ppermute | solution.py:24
  52.9 16.9 %collective-permute-start.7 = (bf16[1024,128]{1,0:T(8,128)(2,1)S(1)}, bf16[1024,128]{1,0:T(8,128)(2,1)S(1)}, u32[]{:S(2)}, u32[]{:S(2)}) collective-permute-start(bf16[1024,128]{1,0:T(8,128)(2,1)S(1)} %get-tuple-element.83), channel_id=1, source_target_pairs={{0,8},{4,12},{8,0},{12,4},{16,24},{20,28},{24,16},{28,20},{1,9},{5... | collective-permute-start | bytes 786440 | tf_op jit(solution)/shard_map/ppermute | solution.py:24
  57.9 21.3 %collective-permute-start.8 = (bf16[1024,128]{1,0:T(8,128)(2,1)S(1)}, bf16[1024,128]{1,0:T(8,128)(2,1)S(1)}, u32[]{:S(2)}, u32[]{:S(2)}) collective-permute-start(bf16[1024,128]{1,0:T(8,128)(2,1)S(1)} %get-tuple-element.84), channel_id=1, source_target_pairs={{0,16},{4,20},{8,24},{12,28},{16,0},{20,4},{24,8},{28,12},{1,17},{... | collective-permute-start | bytes 786440 | tf_op jit(solution)/shard_map/ppermute | solution.py:24
  59.9 19.3 %collective-permute-start.9 = (bf16[1024,128]{1,0:T(8,128)(2,1)S(1)}, bf16[1024,128]{1,0:T(8,128)(2,1)S(1)}, u32[]{:S(2)}, u32[]{:S(2)}) collective-permute-start(bf16[1024,128]{1,0:T(8,128)(2,1)S(1)} %get-tuple-element.85), channel_id=1, source_target_pairs={{0,24},{4,28},{8,16},{12,20},{16,8},{20,12},{24,0},{28,4},{1,25},{... | collective-permute-start | bytes 786440 | tf_op jit(solution)/shard_map/ppermute | solution.py:24
  83.3 25.0 %collective-permute-start.15 = (bf16[1024,128]{1,0:T(8,128)(2,1)S(1)}, bf16[1024,128]{1,0:T(8,128)(2,1)S(1)}, u32[]{:S(2)}, u32[]{:S(2)}) collective-permute-start(bf16[1024,128]{1,0:T(8,128)(2,1)S(1)} %get-tuple-element.98.refs_4_), channel_id=1, source_target_pairs={{0,24},{4,28},{8,16},{12,20},{16,8},{20,12},{24,0},{28,4},{1,25},{... | collective-permute-start | bytes 786440 | tf_op jit(solution)/shard_map/ppermute | solution.py:24
  86.7 23.1 %collective-permute-start.14 = (bf16[1024,128]{1,0:T(8,128)(2,1)S(1)}, bf16[1024,128]{1,0:T(8,128)(2,1)S(1)}, u32[]{:S(2)}, u32[]{:S(2)}) collective-permute-start(bf16[1024,128]{1,0:T(8,128)(2,1)S(1)} %get-tuple-element.98.refs_4_), channel_id=1, source_target_pairs={{0,16},{4,20},{8,24},{12,28},{16,0},{20,4},{24,8},{28,12},{1,17},{... | collective-permute-start | bytes 786440 | tf_op jit(solution)/shard_map/ppermute | solution.py:24
  104.9 26.4 %collective-permute-start.18 = (bf16[2,1024,128]{2,1,0:T(8,128)(2,1)S(1)}, bf16[2,1024,128]{2,1,0:T(8,128)(2,1)S(1)}, u32[]{:S(2)}, u32[]{:S(2)}) collective-permute-start(bf16[2,1024,128]{2,1,0:T(8,128)(2,1)S(1)} %pad_maximum_fusion), channel_id=1, source_target_pairs={{0,4},{4,0},{8,12},{12,8},{16,20},{20,16},{24,28},{28,24},{1,5},{5... | collective-permute-start | bytes 1572872 | tf_op jit(solution)/shard_map/ppermute | solution.py:24
  109.8 21.4 %collective-permute-start.19 = (bf16[2,1024,128]{2,1,0:T(8,128)(2,1)S(1)}, bf16[2,1024,128]{2,1,0:T(8,128)(2,1)S(1)}, u32[]{:S(2)}, u32[]{:S(2)}) collective-permute-start(bf16[2,1024,128]{2,1,0:T(8,128)(2,1)S(1)} %pad_maximum_fusion.1), channel_id=1, source_target_pairs={{0,4},{4,0},{8,12},{12,8},{16,20},{20,16},{24,28},{28,24},{1,5},{5... | collective-permute-start | bytes 1572872 | tf_op jit(solution)/shard_map/ppermute | solution.py:24
  117.9 18.0 %collective-permute-start.20 = (bf16[2,512,128]{2,1,0:T(8,128)(2,1)S(1)}, bf16[2,512,128]{2,1,0:T(8,128)(2,1)S(1)}, u32[]{:S(2)}, u32[]{:S(2)}) collective-permute-start(bf16[2,512,128]{2,1,0:T(8,128)(2,1)S(1)} %pad_maximum_fusion.2), channel_id=1, source_target_pairs={{0,8},{4,12},{8,0},{12,4},{16,24},{20,28},{24,16},{28,20},{1,9},{5... | collective-permute-start | bytes 786440 | tf_op jit(solution)/shard_map/ppermute | solution.py:24
  120.5 18.5 %collective-permute-start.25 = (bf16[2,512,128]{2,1,0:T(8,128)(2,1)S(1)}, bf16[2,512,128]{2,1,0:T(8,128)(2,1)S(1)}, u32[]{:S(2)}, u32[]{:S(2)}) collective-permute-start(bf16[2,512,128]{2,1,0:T(8,128)(2,1)S(1)} %pad_maximum_fusion.2), channel_id=1, source_target_pairs={{0,24},{4,28},{8,16},{12,20},{16,8},{20,12},{24,0},{28,4},{1,25},{... | collective-permute-start | bytes 786440 | tf_op jit(solution)/shard_map/ppermute | solution.py:24
  121.9 21.3 %collective-permute-start.24 = (bf16[2,512,128]{2,1,0:T(8,128)(2,1)S(1)}, bf16[2,512,128]{2,1,0:T(8,128)(2,1)S(1)}, u32[]{:S(2)}, u32[]{:S(2)}) collective-permute-start(bf16[2,512,128]{2,1,0:T(8,128)(2,1)S(1)} %pad_maximum_fusion.2), channel_id=1, source_target_pairs={{0,16},{4,20},{8,24},{12,28},{16,0},{20,4},{24,8},{28,12},{1,17},{... | collective-permute-start | bytes 786440 | tf_op jit(solution)/shard_map/ppermute | solution.py:24
  160.8 26.4 %collective-permute-start.29 = (s16[4,1040,128]{2,1,0:T(8,128)(2,1)S(1)}, s16[4,1040,128]{2,1,0:T(8,128)(2,1)S(1)}, u32[]{:S(2)}, u32[]{:S(2)}) collective-permute-start(s16[4,1040,128]{2,1,0:T(8,128)(2,1)S(1)} %shard_map.62), channel_id=1, source_target_pairs={{0,4},{4,0},{8,12},{12,8},{16,20},{20,16},{24,28},{28,24},{1,5},{5... | collective-permute-start | bytes 3194888 | tf_op jit(solution)/shard_map/ppermute | solution.py:24
  165.3 21.2 %collective-permute-start.31 = (s16[1040,128]{1,0:T(8,128)(2,1)S(1)}, s16[1040,128]{1,0:T(8,128)(2,1)S(1)}, u32[]{:S(2)}, u32[]{:S(2)}) collective-permute-start(s16[1040,128]{1,0:T(8,128)(2,1)S(1)} %get-tuple-element.112), channel_id=1, source_target_pairs={{0,16},{4,20},{8,24},{12,28},{16,0},{20,4},{24,8},{28,12},{1,17},{... | collective-permute-start | bytes 798728 | tf_op jit(solution)/shard_map/ppermute | solution.py:24
  165.4 21.1 %collective-permute-start.32 = (s16[1040,128]{1,0:T(8,128)(2,1)S(1)}, s16[1040,128]{1,0:T(8,128)(2,1)S(1)}, u32[]{:S(2)}, u32[]{:S(2)}) collective-permute-start(s16[1040,128]{1,0:T(8,128)(2,1)S(1)} %get-tuple-element.113), channel_id=1, source_target_pairs={{0,24},{4,28},{8,16},{12,20},{16,8},{20,12},{24,0},{28,4},{1,25},{... | collective-permute-start | bytes 798728 | tf_op jit(solution)/shard_map/ppermute | solution.py:24
  168.6 18.7 %collective-permute-start.30 = (s16[1040,128]{1,0:T(8,128)(2,1)S(1)}, s16[1040,128]{1,0:T(8,128)(2,1)S(1)}, u32[]{:S(2)}, u32[]{:S(2)}) collective-permute-start(s16[1040,128]{1,0:T(8,128)(2,1)S(1)} %get-tuple-element.111), channel_id=1, source_target_pairs={{0,8},{4,12},{8,0},{12,4},{16,24},{20,28},{24,16},{28,20},{1,9},{5... | collective-permute-start | bytes 798728 | tf_op jit(solution)/shard_map/ppermute | solution.py:24
  193.2 21.6 %collective-permute-start.34 = (s16[1040,128]{1,0:T(8,128)(2,1)S(1)}, s16[1040,128]{1,0:T(8,128)(2,1)S(1)}, u32[]{:S(2)}, u32[]{:S(2)}) collective-permute-start(s16[1040,128]{1,0:T(8,128)(2,1)S(1)} %get-tuple-element.119), channel_id=1, source_target_pairs={{0,16},{4,20},{8,24},{12,28},{16,0},{20,4},{24,8},{28,12},{1,17},{... | collective-permute-start | bytes 798728 | tf_op jit(solution)/shard_map/ppermute | solution.py:24
  193.2 21.6 %collective-permute-start.35 = (s16[1040,128]{1,0:T(8,128)(2,1)S(1)}, s16[1040,128]{1,0:T(8,128)(2,1)S(1)}, u32[]{:S(2)}, u32[]{:S(2)}) collective-permute-start(s16[1040,128]{1,0:T(8,128)(2,1)S(1)} %get-tuple-element.120), channel_id=1, source_target_pairs={{0,24},{4,28},{8,16},{12,20},{16,8},{20,12},{24,0},{28,4},{1,25},{... | collective-permute-start | bytes 798728 | tf_op jit(solution)/shard_map/ppermute | solution.py:24
  225.4 23.0 %collective-permute-start.38 = (s16[1040,128]{1,0:T(8,128)(2,1)S(1)}, s16[1040,128]{1,0:T(8,128)(2,1)S(1)}, u32[]{:S(2)}, u32[]{:S(2)}) collective-permute-start(s16[1040,128]{1,0:T(8,128)(2,1)S(1)} %get-tuple-element.136.refs_0_), channel_id=1, source_target_pairs={{0,16},{4,20},{8,24},{12,28},{16,0},{20,4},{24,8},{28,12},{1,17},{... | collective-permute-start | bytes 798728 | tf_op jit(solution)/shard_map/ppermute | solution.py:24
  231.1 33.4 %collective-permute-start.47 = (s16[2,1040,128]{2,1,0:T(8,128)(2,1)S(1)}, s16[2,1040,128]{2,1,0:T(8,128)(2,1)S(1)}, u32[]{:S(2)}, u32[]{:S(2)}) collective-permute-start(s16[2,1040,128]{2,1,0:T(8,128)(2,1)S(1)} %pad_add_fusion), channel_id=1, source_target_pairs={{0,4},{4,0},{8,12},{12,8},{16,20},{20,16},{24,28},{28,24},{1,5},{5... | collective-permute-start | bytes 1597448 | tf_op jit(solution)/shard_map/ppermute | solution.py:24
  257.6 21.3 %collective-permute-start.50 = (s16[2,528,128]{2,1,0:T(8,128)(2,1)S(1)}, s16[2,528,128]{2,1,0:T(8,128)(2,1)S(1)}, u32[]{:S(2)}, u32[]{:S(2)}) collective-permute-start(s16[2,528,128]{2,1,0:T(8,128)(2,1)S(1)} %pad_add_fusion.2.refs_1_), channel_id=1, source_target_pairs={{0,16},{4,20},{8,24},{12,28},{16,0},{20,4},{24,8},{28,12},{1,17},{... | collective-permute-start | bytes 811016 | tf_op jit(solution)/shard_map/ppermute | solution.py:24
  257.6 21.3 %collective-permute-start.49 = (s16[2,528,128]{2,1,0:T(8,128)(2,1)S(1)}, s16[2,528,128]{2,1,0:T(8,128)(2,1)S(1)}, u32[]{:S(2)}, u32[]{:S(2)}) collective-permute-start(s16[2,528,128]{2,1,0:T(8,128)(2,1)S(1)} %pad_add_fusion.2.refs_1_), channel_id=1, source_target_pairs={{0,8},{4,12},{8,0},{12,4},{16,24},{20,28},{24,16},{28,20},{1,9},{5... | collective-permute-start | bytes 811016 | tf_op jit(solution)/shard_map/ppermute | solution.py:24
  (31 other events, 242.0 us)

commit v6 on v5

--- a/solution.py
+++ b/solution.py
@@ -15,7 +15,8 @@
 LOW = 2
 GROUP = 8
 LANES = 128
-VMEM_BYTES = 48 << 20
+VMEM_BYTES = 20 << 20
+VMEM_FIRST = 48 << 20
 LIGHT = pl.CostEstimate(flops=1, bytes_accessed=1, transcendentals=0)
 WHOLE = pl.BlockSpec(memory_space=pltpu.VMEM)
 
@@ -27,6 +28,7 @@
 class Plain:
     pad = 0
     dtype = BF16
+    limit = VMEM_FIRST
 
     @staticmethod
     def encode(value):
@@ -40,6 +42,7 @@
 class Fixed:
     pad = 16
     dtype = I16
+    limit = VMEM_BYTES
 
     @staticmethod
     def encode(value):
@@ -57,8 +60,8 @@
         return wide[:rows] * jnp.exp2(wide[rows : rows + 1] * (1.0 / STEPS))
 
 
-def params():
-    return pltpu.CompilerParams(vmem_limit_bytes=VMEM_BYTES)
+def params(limit=VMEM_BYTES):
+    return pltpu.CompilerParams(vmem_limit_bytes=limit)
 
 
 class Layout:
@@ -116,7 +119,7 @@
             + [pl.BlockSpec((time_rows, n), column(u)) for u in range(per_step)],
             out_specs=out_specs,
         ),
-        compiler_params=params(),
+        compiler_params=params(code.limit),
         cost_estimate=LIGHT,
     )(pos, scores, *([scans] * per_step))
 
@@ -211,7 +214,7 @@
             out_specs=[pl.BlockSpec(half.shape, lambda g, pos: (0, 0))] * 2,
             scratch_shapes=[pltpu.VMEM((time_rows, rank), F32)],
         ),
-        compiler_params=params(),
+        compiler_params=params(VMEM_FIRST),
         cost_estimate=LIGHT,
     )(pos, panel, *([scans] * count))
 
@@ -407,7 +410,6 @@
         layout = Layout(voxels, subjects)
         high = layout.high
         ks = list(range(high))
-        near, far = ks[: high // 2], ks[high // 2 :]
         me = lax.axis_index("subj")
         core = lax.axis_index("vox") % 2
         pos = jnp.stack([me % LOW, me // LOW, core]).astype(jnp.int32)
@@ -452,8 +454,8 @@
         def gather(first, second, gram):
             gram = gram + swap_vox(gram, mask=1)
             first, second, gram = lax.optimization_barrier((first, second, gram))
-            far_in = [swap(first, mask=k * LOW) for k in far]
-            near_in = [first] + [swap(first, mask=k * LOW) for k in near[1:]]
+            low_own = swap(first, mask=1)
+            pieces = [swap(first, mask=k * LOW) for k in ks[1:]]
             got = swap(second, mask=1)
             lower = pos[0] == 0
             pair = jnp.stack([jnp.where(lower, second, got), jnp.where(lower, got, second)])
@@ -461,17 +463,15 @@
             while mask < blocks:
                 gram = gram + swap_vox(gram, mask=mask)
                 mask *= 2
-            near_in, gram = lax.optimization_barrier((near_in, gram))
-            low_near = swap(jnp.stack(near_in), mask=1)
             gram = gram + swap(gram, mask=1)
-            far_in, pair, gram = lax.optimization_barrier((far_in, pair, gram))
-            low_far = swap(jnp.stack(far_in), mask=1)
+            grams = [gram] + [swap(gram, mask=k * LOW) for k in ks[1:]]
+            pieces, pair, grams = lax.optimization_barrier((pieces, pair, grams))
+            low_rest = swap(jnp.stack(pieces), mask=1)
             seconds = [pair] + [swap(pair, mask=k * LOW) for k in ks[1:]]
-            gram = [gram] + [swap(gram, mask=k * LOW) for k in ks[1:]]
-            early = [(0, [k], array) for k, array in zip(near + far, near_in + far_in)]
-            late = [(1, near, low_near), (1, far, low_far)]
+            early = [(0, [k], array) for k, array in zip(ks, [first] + pieces)]
+            late = [(1, ks[:1], low_own), (1, ks[1:], low_rest)]
             pairs = [(None, [k], array) for k, array in zip(ks, seconds)]
-            return early, late, pairs, gram
+            return early, late, pairs, grams
 
         def sum_scores(mine, send, *factor):
             mine = mine + swap_vox(send, mask=1)

time: 283 us -> 291 us (1.028)
  starting transfers between devices: 74.6 us -> 91.9 us
  Pallas kernels: 76.6 us -> 61.9 us
  local copies, waits for them, and re-layouts: 1.9 us -> 7.37 us
    ppermute x52, starting transfers between devices: 74.6 us -> 91.9 us  [exchange(): return lax.ppermute(value, axis, [(i, i ^ mask) for i in range(size)])]
    pallas_call x4, Pallas kernels: 15.4 us -> 6.92 us  [project(): pl.pallas_call(functools.partial(project_kernel, base is not None, split,...]
    pallas_call x8, Pallas kernels: 28.4 us -> 22.2 us  [sketch_part(): pl.pallas_call(functools.partial(sketch_kernel, code, apart, per_step), o...]
    unnamed x6 -> x10, local copies, waits for them, and re-layouts: 1.9 us -> 7.37 us
  transfers between devices with their start and end apart: 52 -> 52, of which waited for: 31 -> 28; matrix products, arithmetic and copies ran while one was open for 0% -> 0% of each run, Pallas kernels for 17% -> 13%
where the time goes in v6:
time: 291 us
  waiting for transfers between devices  129 us (44%)
  starting transfers between devices  91.9 us (32%)
  Pallas kernels  61.9 us (21%)
  local copies, waits for them, and re-layouts  7.37 us (3%)
    ppermute x52, waiting for transfers between devices, exchange(): return lax.ppermute(value, axis, [(i, i ^ mask) for i in range(size)])  129 us
    ppermute x52, starting transfers between devices, exchange(): return lax.ppermute(value, axis, [(i, i ^ mask) for i in range(size)])  91.9 us
    pallas_call x8, Pallas kernels, sketch_part(): pl.pallas_call(functools.partial(sketch_kernel, code, apart, per_step), o...  22.2 us
    pallas_call x8, Pallas kernels, small_call(): pl.pallas_call(kernel, out_shape=out_shape, in_specs=[WHOLE] * len(args),...  11.8 us
    pallas_call x2, Pallas kernels, finish(): pl.pallas_call(functools.partial(finish_kernel, layout, items, base is no...  9.12 us
    pallas_call x1, Pallas kernels, first_project(): pl.pallas_call(functools.partial(first_kernel, count), out_shape=[half, h...  8.72 us
    unnamed x10, local copies, waits for them, and re-layouts  7.37 us
    pallas_call x4, Pallas kernels, project(): pl.pallas_call(functools.partial(project_kernel, base is not None, split,...  6.92 us
  transfers between devices with their start and end apart: 52, of which 28 were waited for; matrix products, arithmetic and copies ran while one was open for 0% of the time, Pallas kernels for 13%

profile of v6, /device:TPU:0, one launch (start us, length us, event | category | flops | bytes accessed | tf_op | source)
XLA Modules:
  0.0 290.9 jit_solution(13468595621847204026)
XLA Ops:
  2.0 8.7 %shard_map.46 = (f32[320,128]{1,0:T(8,128)S(1)}, f32[320,128]{1,0:T(8,128)S(1)}) custom-call(s32[3]{0:T(128)S(1)} %pad_add_fusion.2.pos_ref, bf16[12288,128]{1,0:T(8,128)(2,1)S(1)} %copy-done.2, bf16[640,12288]{1,0:T(8,128)(2,1)} %refs_0_.19, bf16[640,12288]{1,0:T(8,128)(2,1)} %refs_0_.19, bf16[640,12288]{1,0:T(8,128)(2,1)} %refs_0_.19, ...), custom_call_target="tpu_custom_call" | custom-call | flops 1 | bytes 1 | tf_op jit(solution)/shard_map/pallas_call | solution.py:206
  15.2 4.5 %collective-permute-done.1 = f32[320,128]{1,0:T(8,128)S(1)} collective-permute-done((f32[320,128]{1,0:T(8,128)S(1)}, f32[320,128]{1,0:T(8,128)S(1)}, u32[]{:S(2)}, u32[]{:S(2)}) %collective-permute-start.1) | collective-permute-done | bytes 163872 | tf_op jit(solution)/shard_map/ppermute | solution.py:25
  21.8 3.8 %shard_map.48 = bf16[4,1024,128]{2,1,0:T(8,128)(2,1)S(1)} custom-call(s32[3]{0:T(128)S(1)} %pad_add_fusion.2.pos_ref, bf16[640,128]{1,0:T(8,128)(2,1)S(1)} %shard_map.47.scores_ref, bf16[640,12288]{1,0:T(8,128)(2,1)} %refs_0_.19, bf16[640,12288]{1,0:T(8,128)(2,1)} %refs_0_.19), custom_call_target="tpu_custom_call" | custom-call | flops 1 | bytes 1 | tf_op jit(solution)/shard_map/pallas_call | solution.py:112
  37.6 4.0 %shard_map.50.own_ref = bf16[4,1024,128]{2,1,0:T(8,128)(2,1)S(1)} custom-call(s32[3]{0:T(128)S(1)} %pad_add_fusion.2.pos_ref, bf16[640,128]{1,0:T(8,128)(2,1)S(1)} %shard_map.47.scores_ref, bf16[640,12288]{1,0:T(8,128)(2,1)} %refs_0_.19, bf16[640,12288]{1,0:T(8,128)(2,1)} %refs_0_.19), custom_call_target="tpu_custom_call" | custom-call | flops 1 | bytes 1 | tf_op jit(solution)/shard_map/pallas_call | solution.py:112
  41.5 10.9 %collective-permute-done.5.refs_2_ = bf16[1024,128]{1,0:T(8,128)(2,1)S(1)} collective-permute-done((bf16[1024,128]{1,0:T(8,128)(2,1)S(1)}, bf16[1024,128]{1,0:T(8,128)(2,1)S(1)}, u32[]{:S(2)}, u32[]{:S(2)}) %collective-permute-start.5) | collective-permute-done | bytes 262176 | tf_op jit(solution)/shard_map/ppermute | solution.py:25
  52.9 5.0 %collective-permute-start.7 = (bf16[1024,128]{1,0:T(8,128)(2,1)S(1)}, bf16[1024,128]{1,0:T(8,128)(2,1)S(1)}, u32[]{:S(2)}, u32[]{:S(2)}) collective-permute-start(bf16[1024,128]{1,0:T(8,128)(2,1)S(1)} %get-tuple-element.85), channel_id=1, source_target_pairs={{0,8},{4,12},{8,0},{12,4},{16,24},{20,28},{24,16},{28,20},{1,9},{5... | collective-permute-start | bytes 786440 | tf_op jit(solution)/shard_map/ppermute | solution.py:25
  62.6 4.5 %collective-permute-done.10.refs_1_ = bf16[512,128]{1,0:T(8,128)(2,1)S(1)} collective-permute-done((bf16[512,128]{1,0:T(8,128)(2,1)S(1)}, bf16[512,128]{1,0:T(8,128)(2,1)S(1)}, u32[]{:S(2)}, u32[]{:S(2)}) %collective-permute-start.10) | collective-permute-done | bytes 131104 | tf_op jit(solution)/shard_map/ppermute | solution.py:25
  69.8 9.5 %collective-permute-done.8.refs_2_ = bf16[1024,128]{1,0:T(8,128)(2,1)S(1)} collective-permute-done((bf16[1024,128]{1,0:T(8,128)(2,1)S(1)}, bf16[1024,128]{1,0:T(8,128)(2,1)S(1)}, u32[]{:S(2)}, u32[]{:S(2)}) %collective-permute-start.8) | collective-permute-done | bytes 262176 | tf_op jit(solution)/shard_map/ppermute | solution.py:25
  97.0 11.4 %collective-permute-done.20.refs_3_ = f32[128,128]{1,0:T(8,128)S(1)} collective-permute-done((f32[128,128]{1,0:T(8,128)S(1)}, f32[128,128]{1,0:T(8,128)S(1)}, u32[]{:S(2)}, u32[]{:S(2)}) %collective-permute-start.20) | collective-permute-done | bytes 65568 | tf_op jit(solution)/shard_map/ppermute | solution.py:25
  108.5 8.2 %collective-permute-start.18 = (f32[128,128]{1,0:T(8,128)S(1)}, f32[128,128]{1,0:T(8,128)S(1)}, u32[]{:S(2)}, u32[]{:S(2)}) collective-permute-start(f32[128,128]{1,0:T(8,128)S(1)} %add.51.refs_0_), channel_id=1, source_target_pairs={{0,8},{4,12},{8,0},{12,4},{16,24},{20,28},{24,16},{28,20},{1,9},{5... | collective-permute-start | bytes 196616 | tf_op jit(solution)/shard_map/ppermute | solution.py:25
  126.5 5.5 %copy-done = bf16[640,12288]{1,0:T(8,128)(2,1)S(1)} copy-done((bf16[640,12288]{1,0:T(8,128)(2,1)S(1)}, bf16[640,12288]{1,0:T(8,128)(2,1)}, u32[]{:S(2)}) %copy-start) | copy-done | bytes 15728664
  134.0 4.1 %shard_map.59.refs_0_ = f32[128,128]{1,0:T(8,128)S(1)} custom-call(f32[128,128]{1,0:T(8,128)S(1)} %add.51.refs_0_, f32[128,128]{1,0:T(8,128)S(1)} %collective-permute-done.18.refs_1_, f32[128,128]{1,0:T(8,128)S(1)} %collective-permute-done.19.refs_2_, f32[128,128]{1,0:T(8,128)S(1)} %collective-permute-done.20.refs_3_), custom_call_target="tpu_custom_call" | custom-call | flops 1 | bytes 1 | tf_op jit(solution)/shard_map/pallas_call | solution.py:128
  138.1 5.1 %collective-permute-done.21.refs_5_ = bf16[1024,128]{1,0:T(8,128)(2,1)S(1)} collective-permute-done((bf16[1024,128]{1,0:T(8,128)(2,1)S(1)}, bf16[1024,128]{1,0:T(8,128)(2,1)S(1)}, u32[]{:S(2)}, u32[]{:S(2)}) %collective-permute-start.21) | collective-permute-done | bytes 262176 | tf_op jit(solution)/shard_map/ppermute | solution.py:25
  151.2 4.7 %collective-permute-done.27 = f32[320,128]{1,0:T(8,128)S(1)} collective-permute-done((f32[320,128]{1,0:T(8,128)S(1)}, f32[320,128]{1,0:T(8,128)S(1)}, u32[]{:S(2)}, u32[]{:S(2)}) %collective-permute-start.27) | collective-permute-done | bytes 163872 | tf_op jit(solution)/shard_map/ppermute | solution.py:25
  172.9 13.6 %collective-permute-done.31.refs_2_ = s16[1040,128]{1,0:T(8,128)(2,1)S(1)} collective-permute-done((s16[1040,128]{1,0:T(8,128)(2,1)S(1)}, s16[1040,128]{1,0:T(8,128)(2,1)S(1)}, u32[]{:S(2)}, u32[]{:S(2)}) %collective-permute-start.31) | collective-permute-done | bytes 266272 | tf_op jit(solution)/shard_map/ppermute | solution.py:25
  188.6 5.0 %collective-permute-start.33 = (s16[1040,128]{1,0:T(8,128)(2,1)S(1)}, s16[1040,128]{1,0:T(8,128)(2,1)S(1)}, u32[]{:S(2)}, u32[]{:S(2)}) collective-permute-start(s16[1040,128]{1,0:T(8,128)(2,1)S(1)} %get-tuple-element.121), channel_id=1, source_target_pairs={{0,8},{4,12},{8,0},{12,4},{16,24},{20,28},{24,16},{28,20},{1,9},{5... | collective-permute-start | bytes 798728 | tf_op jit(solution)/shard_map/ppermute | solution.py:25
  197.6 4.5 %collective-permute-done.36.refs_1_ = s16[528,128]{1,0:T(8,128)(2,1)S(1)} collective-permute-done((s16[528,128]{1,0:T(8,128)(2,1)S(1)}, s16[528,128]{1,0:T(8,128)(2,1)S(1)}, u32[]{:S(2)}, u32[]{:S(2)}) %collective-permute-start.36) | collective-permute-done | bytes 135200 | tf_op jit(solution)/shard_map/ppermute | solution.py:25
  204.5 10.8 %collective-permute-done.34.refs_2_ = s16[1040,128]{1,0:T(8,128)(2,1)S(1)} collective-permute-done((s16[1040,128]{1,0:T(8,128)(2,1)S(1)}, s16[1040,128]{1,0:T(8,128)(2,1)S(1)}, u32[]{:S(2)}, u32[]{:S(2)}) %collective-permute-start.34) | collective-permute-done | bytes 266272 | tf_op jit(solution)/shard_map/ppermute | solution.py:25
  226.3 3.9 %collective-permute-start.39 = (s16[1040,128]{1,0:T(8,128)(2,1)S(1)}, s16[1040,128]{1,0:T(8,128)(2,1)S(1)}, u32[]{:S(2)}, u32[]{:S(2)}) collective-permute-start(s16[1040,128]{1,0:T(8,128)(2,1)S(1)} %get-tuple-element.134.refs_0_), channel_id=1, source_target_pairs={{0,16},{4,20},{8,24},{12,28},{16,0},{20,4},{24,8},{28,12},{1,17},{... | collective-permute-start | bytes 798728 | tf_op jit(solution)/shard_map/ppermute | solution.py:25
  233.9 12.5 %collective-permute-done.46.refs_3_ = f32[128,128]{1,0:T(8,128)S(1)} collective-permute-done((f32[128,128]{1,0:T(8,128)S(1)}, f32[128,128]{1,0:T(8,128)S(1)}, u32[]{:S(2)}, u32[]{:S(2)}) %collective-permute-start.46) | collective-permute-done | bytes 65568 | tf_op jit(solution)/shard_map/ppermute | solution.py:25
  246.4 8.3 %collective-permute-start.44 = (f32[128,128]{1,0:T(8,128)S(1)}, f32[128,128]{1,0:T(8,128)S(1)}, u32[]{:S(2)}, u32[]{:S(2)}) collective-permute-start(f32[128,128]{1,0:T(8,128)S(1)} %add.57.refs_0_), channel_id=1, source_target_pairs={{0,8},{4,12},{8,0},{12,4},{16,24},{20,28},{24,16},{28,20},{1,9},{5... | collective-permute-start | bytes 196616 | tf_op jit(solution)/shard_map/ppermute | solution.py:25
  263.5 4.1 %shard_map.70.inverse_ref = f32[128,128]{1,0:T(8,128)S(1)} custom-call(f32[128,128]{1,0:T(8,128)S(1)} %add.57.refs_0_, f32[128,128]{1,0:T(8,128)S(1)} %collective-permute-done.44.refs_1_, f32[128,128]{1,0:T(8,128)S(1)} %collective-permute-done.45.refs_2_, f32[128,128]{1,0:T(8,128)S(1)} %collective-permute-done.46.refs_3_), custom_call_target="tpu_custom_call" | custom-call | flops 1 | bytes 1 | tf_op jit(solution)/shard_map/pallas_call | solution.py:128
  267.6 14.0 %collective-permute-done.47.refs_4_ = s16[1040,128]{1,0:T(8,128)(2,1)S(1)} collective-permute-done((s16[1040,128]{1,0:T(8,128)(2,1)S(1)}, s16[1040,128]{1,0:T(8,128)(2,1)S(1)}, u32[]{:S(2)}, u32[]{:S(2)}) %collective-permute-start.47) | collective-permute-done | bytes 266272 | tf_op jit(solution)/shard_map/ppermute | solution.py:25
  281.6 5.5 %shard_map.71.refs_0_ = f32[12288,128]{1,0:T(8,128)} custom-call(s32[3]{0:T(128)S(1)} %pad_add_fusion.2.pos_ref, f32[128,128]{1,0:T(8,128)S(1)} %shard_map.70.inverse_ref, s16[1040,128]{1,0:T(8,128)(2,1)S(1)} %get-tuple-element.134.refs_0_, s16[1040,128]{1,0:T(8,128)(2,1)S(1)} %collective-permute-done.38.refs_1_, ...), custom_call_target="tpu_custom_call" | custom-call | flops 1 | bytes 1 | tf_op jit(solution)/shard_map/pallas_call | solution.py:310
  (136 shorter events, 118.3 us)
Async XLA Ops:
  25.6 27.0 %collective-permute-start.3 = (bf16[4,1024,128]{2,1,0:T(8,128)(2,1)S(1)}, bf16[4,1024,128]{2,1,0:T(8,128)(2,1)S(1)}, u32[]{:S(2)}, u32[]{:S(2)}) collective-permute-start(bf16[4,1024,128]{2,1,0:T(8,128)(2,1)S(1)} %shard_map.48), channel_id=1, source_target_pairs={{0,4},{4,0},{8,12},{12,8},{16,20},{20,16},{24,28},{28,24},{1,5},{5... | collective-permute-start | bytes 3145736 | tf_op jit(solution)/shard_map/ppermute | solution.py:25
  31.0 21.4 %collective-permute-start.5 = (bf16[1024,128]{1,0:T(8,128)(2,1)S(1)}, bf16[1024,128]{1,0:T(8,128)(2,1)S(1)}, u32[]{:S(2)}, u32[]{:S(2)}) collective-permute-start(bf16[1024,128]{1,0:T(8,128)(2,1)S(1)} %get-tuple-element.79), channel_id=1, source_target_pairs={{0,16},{4,20},{8,24},{12,28},{16,0},{20,4},{24,8},{28,12},{1,17},{... | collective-permute-start | bytes 786440 | tf_op jit(solution)/shard_map/ppermute | solution.py:25
  57.9 21.3 %collective-permute-start.8 = (bf16[1024,128]{1,0:T(8,128)(2,1)S(1)}, bf16[1024,128]{1,0:T(8,128)(2,1)S(1)}, u32[]{:S(2)}, u32[]{:S(2)}) collective-permute-start(bf16[1024,128]{1,0:T(8,128)(2,1)S(1)} %get-tuple-element.86), channel_id=1, source_target_pairs={{0,16},{4,20},{8,24},{12,28},{16,0},{20,4},{24,8},{28,12},{1,17},{... | collective-permute-start | bytes 786440 | tf_op jit(solution)/shard_map/ppermute | solution.py:25
  86.2 32.7 %collective-permute-start.14 = (bf16[1024,128]{1,0:T(8,128)(2,1)S(1)}, bf16[1024,128]{1,0:T(8,128)(2,1)S(1)}, u32[]{:S(2)}, u32[]{:S(2)}) collective-permute-start(bf16[1024,128]{1,0:T(8,128)(2,1)S(1)} %get-tuple-element.98.refs_4_), channel_id=1, source_target_pairs={{0,24},{4,28},{8,16},{12,20},{16,8},{20,12},{24,0},{28,4},{1,25},{... | collective-permute-start | bytes 786440 | tf_op jit(solution)/shard_map/ppermute | solution.py:25
  89.6 29.3 %collective-permute-start.13 = (bf16[1024,128]{1,0:T(8,128)(2,1)S(1)}, bf16[1024,128]{1,0:T(8,128)(2,1)S(1)}, u32[]{:S(2)}, u32[]{:S(2)}) collective-permute-start(bf16[1024,128]{1,0:T(8,128)(2,1)S(1)} %get-tuple-element.98.refs_4_), channel_id=1, source_target_pairs={{0,16},{4,20},{8,24},{12,28},{16,0},{20,4},{24,8},{28,12},{1,17},{... | collective-permute-start | bytes 786440 | tf_op jit(solution)/shard_map/ppermute | solution.py:25
  93.1 25.8 %collective-permute-start.12 = (bf16[1024,128]{1,0:T(8,128)(2,1)S(1)}, bf16[1024,128]{1,0:T(8,128)(2,1)S(1)}, u32[]{:S(2)}, u32[]{:S(2)}) collective-permute-start(bf16[1024,128]{1,0:T(8,128)(2,1)S(1)} %get-tuple-element.98.refs_4_), channel_id=1, source_target_pairs={{0,8},{4,12},{8,0},{12,4},{16,24},{20,28},{24,16},{28,20},{1,9},{5... | collective-permute-start | bytes 786440 | tf_op jit(solution)/shard_map/ppermute | solution.py:25
  96.1 21.3 %collective-permute-start.19 = (f32[128,128]{1,0:T(8,128)S(1)}, f32[128,128]{1,0:T(8,128)S(1)}, u32[]{:S(2)}, u32[]{:S(2)}) collective-permute-start(f32[128,128]{1,0:T(8,128)S(1)} %add.51.refs_0_), channel_id=1, source_target_pairs={{0,16},{4,20},{8,24},{12,28},{16,0},{20,4},{24,8},{28,12},{1,17},{... | collective-permute-start | bytes 196616 | tf_op jit(solution)/shard_map/ppermute | solution.py:25
  119.0 24.2 %collective-permute-start.22 = (bf16[3,1024,128]{2,1,0:T(8,128)(2,1)S(1)}, bf16[3,1024,128]{2,1,0:T(8,128)(2,1)S(1)}, u32[]{:S(2)}, u32[]{:S(2)}) collective-permute-start(bf16[3,1024,128]{2,1,0:T(8,128)(2,1)S(1)} %pad_maximum_fusion), channel_id=1, source_target_pairs={{0,4},{4,0},{8,12},{12,8},{16,20},{20,16},{24,28},{28,24},{1,5},{5... | collective-permute-start | bytes 2359304 | tf_op jit(solution)/shard_map/ppermute | solution.py:25
  120.6 22.6 %collective-permute-start.21 = (bf16[1024,128]{1,0:T(8,128)(2,1)S(1)}, bf16[1024,128]{1,0:T(8,128)(2,1)S(1)}, u32[]{:S(2)}, u32[]{:S(2)}) collective-permute-start(bf16[1024,128]{1,0:T(8,128)(2,1)S(1)} %get-tuple-element.98.refs_4_), channel_id=1, source_target_pairs={{0,4},{4,0},{8,12},{12,8},{16,20},{20,16},{24,28},{28,24},{1,5},{5... | collective-permute-start | bytes 786440 | tf_op jit(solution)/shard_map/ppermute | solution.py:25
  121.1 24.2 %collective-permute-start.23 = (bf16[2,512,128]{2,1,0:T(8,128)(2,1)S(1)}, bf16[2,512,128]{2,1,0:T(8,128)(2,1)S(1)}, u32[]{:S(2)}, u32[]{:S(2)}) collective-permute-start(bf16[2,512,128]{2,1,0:T(8,128)(2,1)S(1)} %pad_maximum_fusion.1), channel_id=1, source_target_pairs={{0,8},{4,12},{8,0},{12,4},{16,24},{20,28},{24,16},{28,20},{1,9},{5... | collective-permute-start | bytes 786440 | tf_op jit(solution)/shard_map/ppermute | solution.py:25
  123.1 23.6 %collective-permute-start.25 = (bf16[2,512,128]{2,1,0:T(8,128)(2,1)S(1)}, bf16[2,512,128]{2,1,0:T(8,128)(2,1)S(1)}, u32[]{:S(2)}, u32[]{:S(2)}) collective-permute-start(bf16[2,512,128]{2,1,0:T(8,128)(2,1)S(1)} %pad_maximum_fusion.1), channel_id=1, source_target_pairs={{0,24},{4,28},{8,16},{12,20},{16,8},{20,12},{24,0},{28,4},{1,25},{... | collective-permute-start | bytes 786440 | tf_op jit(solution)/shard_map/ppermute | solution.py:25
  126.5 20.2 %collective-permute-start.24 = (bf16[2,512,128]{2,1,0:T(8,128)(2,1)S(1)}, bf16[2,512,128]{2,1,0:T(8,128)(2,1)S(1)}, u32[]{:S(2)}, u32[]{:S(2)}) collective-permute-start(bf16[2,512,128]{2,1,0:T(8,128)(2,1)S(1)} %pad_maximum_fusion.1), channel_id=1, source_target_pairs={{0,16},{4,20},{8,24},{12,28},{16,0},{20,4},{24,8},{28,12},{1,17},{... | collective-permute-start | bytes 786440 | tf_op jit(solution)/shard_map/ppermute | solution.py:25
  161.3 26.3 %collective-permute-start.29 = (s16[4,1040,128]{2,1,0:T(8,128)(2,1)S(1)}, s16[4,1040,128]{2,1,0:T(8,128)(2,1)S(1)}, u32[]{:S(2)}, u32[]{:S(2)}) collective-permute-start(s16[4,1040,128]{2,1,0:T(8,128)(2,1)S(1)} %shard_map.62), channel_id=1, source_target_pairs={{0,4},{4,0},{8,12},{12,8},{16,20},{20,16},{24,28},{28,24},{1,5},{5... | collective-permute-start | bytes 3194888 | tf_op jit(solution)/shard_map/ppermute | solution.py:25
  164.7 21.9 %collective-permute-start.31 = (s16[1040,128]{1,0:T(8,128)(2,1)S(1)}, s16[1040,128]{1,0:T(8,128)(2,1)S(1)}, u32[]{:S(2)}, u32[]{:S(2)}) collective-permute-start(s16[1040,128]{1,0:T(8,128)(2,1)S(1)} %get-tuple-element.115), channel_id=1, source_target_pairs={{0,16},{4,20},{8,24},{12,28},{16,0},{20,4},{24,8},{28,12},{1,17},{... | collective-permute-start | bytes 798728 | tf_op jit(solution)/shard_map/ppermute | solution.py:25
  193.6 21.6 %collective-permute-start.34 = (s16[1040,128]{1,0:T(8,128)(2,1)S(1)}, s16[1040,128]{1,0:T(8,128)(2,1)S(1)}, u32[]{:S(2)}, u32[]{:S(2)}) collective-permute-start(s16[1040,128]{1,0:T(8,128)(2,1)S(1)} %get-tuple-element.122), channel_id=1, source_target_pairs={{0,16},{4,20},{8,24},{12,28},{16,0},{20,4},{24,8},{28,12},{1,17},{... | collective-permute-start | bytes 798728 | tf_op jit(solution)/shard_map/ppermute | solution.py:25
  194.6 20.7 %collective-permute-start.35 = (s16[1040,128]{1,0:T(8,128)(2,1)S(1)}, s16[1040,128]{1,0:T(8,128)(2,1)S(1)}, u32[]{:S(2)}, u32[]{:S(2)}) collective-permute-start(s16[1040,128]{1,0:T(8,128)(2,1)S(1)} %get-tuple-element.123), channel_id=1, source_target_pairs={{0,24},{4,28},{8,16},{12,20},{16,8},{20,12},{24,0},{28,4},{1,25},{... | collective-permute-start | bytes 798728 | tf_op jit(solution)/shard_map/ppermute | solution.py:25
  223.9 33.1 %collective-permute-start.40 = (s16[1040,128]{1,0:T(8,128)(2,1)S(1)}, s16[1040,128]{1,0:T(8,128)(2,1)S(1)}, u32[]{:S(2)}, u32[]{:S(2)}) collective-permute-start(s16[1040,128]{1,0:T(8,128)(2,1)S(1)} %get-tuple-element.134.refs_0_), channel_id=1, source_target_pairs={{0,24},{4,28},{8,16},{12,20},{16,8},{20,12},{24,0},{28,4},{1,25},{... | collective-permute-start | bytes 798728 | tf_op jit(solution)/shard_map/ppermute | solution.py:25
  226.3 30.7 %collective-permute-start.39 = (s16[1040,128]{1,0:T(8,128)(2,1)S(1)}, s16[1040,128]{1,0:T(8,128)(2,1)S(1)}, u32[]{:S(2)}, u32[]{:S(2)}) collective-permute-start(s16[1040,128]{1,0:T(8,128)(2,1)S(1)} %get-tuple-element.134.refs_0_), channel_id=1, source_target_pairs={{0,16},{4,20},{8,24},{12,28},{16,0},{20,4},{24,8},{28,12},{1,17},{... | collective-permute-start | bytes 798728 | tf_op jit(solution)/shard_map/ppermute | solution.py:25
  230.2 26.8 %collective-permute-start.38 = (s16[1040,128]{1,0:T(8,128)(2,1)S(1)}, s16[1040,128]{1,0:T(8,128)(2,1)S(1)}, u32[]{:S(2)}, u32[]{:S(2)}) collective-permute-start(s16[1040,128]{1,0:T(8,128)(2,1)S(1)} %get-tuple-element.134.refs_0_), channel_id=1, source_target_pairs={{0,8},{4,12},{8,0},{12,4},{16,24},{20,28},{24,16},{28,20},{1,9},{5... | collective-permute-start | bytes 798728 | tf_op jit(solution)/shard_map/ppermute | solution.py:25
  231.8 23.7 %collective-permute-start.45 = (f32[128,128]{1,0:T(8,128)S(1)}, f32[128,128]{1,0:T(8,128)S(1)}, u32[]{:S(2)}, u32[]{:S(2)}) collective-permute-start(f32[128,128]{1,0:T(8,128)S(1)} %add.57.refs_0_), channel_id=1, source_target_pairs={{0,16},{4,20},{8,24},{12,28},{16,0},{20,4},{24,8},{28,12},{1,17},{... | collective-permute-start | bytes 196616 | tf_op jit(solution)/shard_map/ppermute | solution.py:25
  257.1 24.5 %collective-permute-start.48 = (s16[3,1040,128]{2,1,0:T(8,128)(2,1)S(1)}, s16[3,1040,128]{2,1,0:T(8,128)(2,1)S(1)}, u32[]{:S(2)}, u32[]{:S(2)}) collective-permute-start(s16[3,1040,128]{2,1,0:T(8,128)(2,1)S(1)} %pad_add_fusion), channel_id=1, source_target_pairs={{0,4},{4,0},{8,12},{12,8},{16,20},{20,16},{24,28},{28,24},{1,5},{5... | collective-permute-start | bytes 2396168 | tf_op jit(solution)/shard_map/ppermute | solution.py:25
  257.6 29.5 %collective-permute-start.51 = (s16[2,528,128]{2,1,0:T(8,128)(2,1)S(1)}, s16[2,528,128]{2,1,0:T(8,128)(2,1)S(1)}, u32[]{:S(2)}, u32[]{:S(2)}) collective-permute-start(s16[2,528,128]{2,1,0:T(8,128)(2,1)S(1)} %pad_add_fusion.1.refs_1_), channel_id=1, source_target_pairs={{0,24},{4,28},{8,16},{12,20},{16,8},{20,12},{24,0},{28,4},{1,25},{... | collective-permute-start | bytes 811016 | tf_op jit(solution)/shard_map/ppermute | solution.py:25
  260.0 27.1 %collective-permute-start.50 = (s16[2,528,128]{2,1,0:T(8,128)(2,1)S(1)}, s16[2,528,128]{2,1,0:T(8,128)(2,1)S(1)}, u32[]{:S(2)}, u32[]{:S(2)}) collective-permute-start(s16[2,528,128]{2,1,0:T(8,128)(2,1)S(1)} %pad_add_fusion.1.refs_1_), channel_id=1, source_target_pairs={{0,16},{4,20},{8,24},{12,28},{16,0},{20,4},{24,8},{28,12},{1,17},{... | collective-permute-start | bytes 811016 | tf_op jit(solution)/shard_map/ppermute | solution.py:25
  261.1 26.0 %collective-permute-start.49 = (s16[2,528,128]{2,1,0:T(8,128)(2,1)S(1)}, s16[2,528,128]{2,1,0:T(8,128)(2,1)S(1)}, u32[]{:S(2)}, u32[]{:S(2)}) collective-permute-start(s16[2,528,128]{2,1,0:T(8,128)(2,1)S(1)} %pad_add_fusion.1.refs_1_), channel_id=1, source_target_pairs={{0,8},{4,12},{8,0},{12,4},{16,24},{20,28},{24,16},{28,20},{1,9},{5... | collective-permute-start | bytes 811016 | tf_op jit(solution)/shard_map/ppermute | solution.py:25
  (33 other events, 338.5 us)

commit v7 on v6

--- a/solution.py
+++ b/solution.py
@@ -454,7 +454,6 @@
         def gather(first, second, gram):
             gram = gram + swap_vox(gram, mask=1)
             first, second, gram = lax.optimization_barrier((first, second, gram))
-            low_own = swap(first, mask=1)
             pieces = [swap(first, mask=k * LOW) for k in ks[1:]]
             got = swap(second, mask=1)
             lower = pos[0] == 0
@@ -464,12 +463,17 @@
                 gram = gram + swap_vox(gram, mask=mask)
                 mask *= 2
             gram = gram + swap(gram, mask=1)
-            grams = [gram] + [swap(gram, mask=k * LOW) for k in ks[1:]]
-            pieces, pair, grams = lax.optimization_barrier((pieces, pair, grams))
-            low_rest = swap(jnp.stack(pieces), mask=1)
+            gram = gram + swap(gram, mask=LOW)
+            pieces, pair, gram = lax.optimization_barrier((pieces, pair, gram))
+            low_got = swap(jnp.stack([first] + pieces), mask=1)
             seconds = [pair] + [swap(pair, mask=k * LOW) for k in ks[1:]]
+            mask = 2
+            while 2 * mask < high:
+                gram = gram + swap(gram, mask=mask * LOW)
+                mask *= 2
+            grams = [gram, swap(gram, mask=mask * LOW)]
             early = [(0, [k], array) for k, array in zip(ks, [first] + pieces)]
-            late = [(1, ks[:1], low_own), (1, ks[1:], low_rest)]
+            late = [(1, ks, low_got)]
             pairs = [(None, [k], array) for k, array in zip(ks, seconds)]
             return early, late, pairs, grams
 

time: 291 us -> 293 us (level)
  waiting for transfers between devices: 129 us -> 152 us
  starting transfers between devices: 91.9 us -> 70.2 us
    ppermute x52 -> x48, waiting for transfers between devices: 129 us -> 152 us  [exchange(): return lax.ppermute(value, axis, [(i, i ^ mask) for i in range(size)])]
    ppermute x52 -> x48, starting transfers between devices: 91.9 us -> 70.2 us  [exchange(): return lax.ppermute(value, axis, [(i, i ^ mask) for i in range(size)])]
  transfers between devices with their start and end apart: 52 -> 48, of which waited for: 28 -> 27; matrix products, arithmetic and copies ran while one was open for 0% -> 0% of each run, Pallas kernels for 13% -> 13%
where the time goes in v7:
time: 293 us
  waiting for transfers between devices  152 us (52%)
  starting transfers between devices  70.2 us (24%)
  Pallas kernels  62 us (21%)
  local copies, waits for them, and re-layouts  7.37 us (3%)
    ppermute x48, waiting for transfers between devices, exchange(): return lax.ppermute(value, axis, [(i, i ^ mask) for i in range(size)])  152 us
    ppermute x48, starting transfers between devices, exchange(): return lax.ppermute(value, axis, [(i, i ^ mask) for i in range(size)])  70.2 us
    pallas_call x8, Pallas kernels, sketch_part(): pl.pallas_call(functools.partial(sketch_kernel, code, apart, per_step), o...  22.2 us
    pallas_call x8, Pallas kernels, small_call(): pl.pallas_call(kernel, out_shape=out_shape, in_specs=[WHOLE] * len(args),...  11.8 us
    pallas_call x2, Pallas kernels, finish(): pl.pallas_call(functools.partial(finish_kernel, layout, items, base is no...  9.13 us
    pallas_call x1, Pallas kernels, first_project(): pl.pallas_call(functools.partial(first_kernel, count), out_shape=[half, h...  8.72 us
    unnamed x10, local copies, waits for them, and re-layouts  7.37 us
    pallas_call x4, Pallas kernels, project(): pl.pallas_call(functools.partial(project_kernel, base is not None, split,...  6.92 us
  transfers between devices with their start and end apart: 48, of which 27 were waited for; matrix products, arithmetic and copies ran while one was open for 0% of the time, Pallas kernels for 13%

profile of v7, /device:TPU:0, one launch (start us, length us, event | category | flops | bytes accessed | tf_op | source)
XLA Modules:
  0.0 293.0 jit_solution(9551838112640875980)
XLA Ops:
  2.0 8.7 %shard_map.46 = (f32[320,128]{1,0:T(8,128)S(1)}, f32[320,128]{1,0:T(8,128)S(1)}) custom-call(s32[3]{0:T(128)S(1)} %pad_add_fusion.2.pos_ref, bf16[12288,128]{1,0:T(8,128)(2,1)S(1)} %copy-done.2, bf16[640,12288]{1,0:T(8,128)(2,1)} %refs_0_.19, bf16[640,12288]{1,0:T(8,128)(2,1)} %refs_0_.19, bf16[640,12288]{1,0:T(8,128)(2,1)} %refs_0_.19, ...), custom_call_target="tpu_custom_call" | custom-call | flops 1 | bytes 1 | tf_op jit(solution)/shard_map/pallas_call | solution.py:206
  15.2 4.5 %collective-permute-done.1 = f32[320,128]{1,0:T(8,128)S(1)} collective-permute-done((f32[320,128]{1,0:T(8,128)S(1)}, f32[320,128]{1,0:T(8,128)S(1)}, u32[]{:S(2)}, u32[]{:S(2)}) %collective-permute-start.1) | collective-permute-done | bytes 163872 | tf_op jit(solution)/shard_map/ppermute | solution.py:25
  21.8 3.8 %shard_map.48 = bf16[4,1024,128]{2,1,0:T(8,128)(2,1)S(1)} custom-call(s32[3]{0:T(128)S(1)} %pad_add_fusion.2.pos_ref, bf16[640,128]{1,0:T(8,128)(2,1)S(1)} %shard_map.47.scores_ref, bf16[640,12288]{1,0:T(8,128)(2,1)} %refs_0_.19, bf16[640,12288]{1,0:T(8,128)(2,1)} %refs_0_.19), custom_call_target="tpu_custom_call" | custom-call | flops 1 | bytes 1 | tf_op jit(solution)/shard_map/pallas_call | solution.py:112
  37.6 4.0 %shard_map.50.own_ref = bf16[4,1024,128]{2,1,0:T(8,128)(2,1)S(1)} custom-call(s32[3]{0:T(128)S(1)} %pad_add_fusion.2.pos_ref, bf16[640,128]{1,0:T(8,128)(2,1)S(1)} %shard_map.47.scores_ref, bf16[640,12288]{1,0:T(8,128)(2,1)} %refs_0_.19, bf16[640,12288]{1,0:T(8,128)(2,1)} %refs_0_.19), custom_call_target="tpu_custom_call" | custom-call | flops 1 | bytes 1 | tf_op jit(solution)/shard_map/pallas_call | solution.py:112
  41.5 10.9 %collective-permute-done.5.refs_2_ = bf16[1024,128]{1,0:T(8,128)(2,1)S(1)} collective-permute-done((bf16[1024,128]{1,0:T(8,128)(2,1)S(1)}, bf16[1024,128]{1,0:T(8,128)(2,1)S(1)}, u32[]{:S(2)}, u32[]{:S(2)}) %collective-permute-start.5) | collective-permute-done | bytes 262176 | tf_op jit(solution)/shard_map/ppermute | solution.py:25
  52.9 5.0 %collective-permute-start.7 = (bf16[1024,128]{1,0:T(8,128)(2,1)S(1)}, bf16[1024,128]{1,0:T(8,128)(2,1)S(1)}, u32[]{:S(2)}, u32[]{:S(2)}) collective-permute-start(bf16[1024,128]{1,0:T(8,128)(2,1)S(1)} %get-tuple-element.79), channel_id=1, source_target_pairs={{0,8},{4,12},{8,0},{12,4},{16,24},{20,28},{24,16},{28,20},{1,9},{5... | collective-permute-start | bytes 786440 | tf_op jit(solution)/shard_map/ppermute | solution.py:25
  62.6 4.5 %collective-permute-done.10.refs_1_ = bf16[512,128]{1,0:T(8,128)(2,1)S(1)} collective-permute-done((bf16[512,128]{1,0:T(8,128)(2,1)S(1)}, bf16[512,128]{1,0:T(8,128)(2,1)S(1)}, u32[]{:S(2)}, u32[]{:S(2)}) %collective-permute-start.10) | collective-permute-done | bytes 131104 | tf_op jit(solution)/shard_map/ppermute | solution.py:25
  69.8 9.5 %collective-permute-done.8.refs_2_ = bf16[1024,128]{1,0:T(8,128)(2,1)S(1)} collective-permute-done((bf16[1024,128]{1,0:T(8,128)(2,1)S(1)}, bf16[1024,128]{1,0:T(8,128)(2,1)S(1)}, u32[]{:S(2)}, u32[]{:S(2)}) %collective-permute-start.8) | collective-permute-done | bytes 262176 | tf_op jit(solution)/shard_map/ppermute | solution.py:25
  95.3 11.5 %collective-permute-done.18 = f32[128,128]{1,0:T(8,128)S(1)} collective-permute-done((f32[128,128]{1,0:T(8,128)S(1)}, f32[128,128]{1,0:T(8,128)S(1)}, u32[]{:S(2)}, u32[]{:S(2)}) %collective-permute-start.18) | collective-permute-done | bytes 65568 | tf_op jit(solution)/shard_map/ppermute | solution.py:25
  106.7 5.0 %collective-permute-done.13.refs_6_ = bf16[1024,128]{1,0:T(8,128)(2,1)S(1)} collective-permute-done((bf16[1024,128]{1,0:T(8,128)(2,1)S(1)}, bf16[1024,128]{1,0:T(8,128)(2,1)S(1)}, u32[]{:S(2)}, u32[]{:S(2)}) %collective-permute-start.13) | collective-permute-done | bytes 262176 | tf_op jit(solution)/shard_map/ppermute | solution.py:25
  119.8 5.5 %copy-done = bf16[640,12288]{1,0:T(8,128)(2,1)S(1)} copy-done((bf16[640,12288]{1,0:T(8,128)(2,1)S(1)}, bf16[640,12288]{1,0:T(8,128)(2,1)}, u32[]{:S(2)}) %copy-start) | copy-done | bytes 15728664
  127.3 15.7 %collective-permute-done.21.refs_1_ = f32[128,128]{1,0:T(8,128)S(1)} collective-permute-done((f32[128,128]{1,0:T(8,128)S(1)}, f32[128,128]{1,0:T(8,128)S(1)}, u32[]{:S(2)}, u32[]{:S(2)}) %collective-permute-start.21) | collective-permute-done | bytes 65568 | tf_op jit(solution)/shard_map/ppermute | solution.py:25
  143.0 4.1 %shard_map.59.refs_0_ = f32[128,128]{1,0:T(8,128)S(1)} custom-call(f32[128,128]{1,0:T(8,128)S(1)} %add.58.refs_0_, f32[128,128]{1,0:T(8,128)S(1)} %collective-permute-done.21.refs_1_), custom_call_target="tpu_custom_call" | custom-call | flops 1 | bytes 1 | tf_op jit(solution)/shard_map/pallas_call | solution.py:128
  155.1 4.8 %collective-permute-done.25 = f32[320,128]{1,0:T(8,128)S(1)} collective-permute-done((f32[320,128]{1,0:T(8,128)S(1)}, f32[320,128]{1,0:T(8,128)S(1)}, u32[]{:S(2)}, u32[]{:S(2)}) %collective-permute-start.25) | collective-permute-done | bytes 163872 | tf_op jit(solution)/shard_map/ppermute | solution.py:25
  175.1 13.2 %collective-permute-done.29.refs_2_ = s16[1040,128]{1,0:T(8,128)(2,1)S(1)} collective-permute-done((s16[1040,128]{1,0:T(8,128)(2,1)S(1)}, s16[1040,128]{1,0:T(8,128)(2,1)S(1)}, u32[]{:S(2)}, u32[]{:S(2)}) %collective-permute-start.29) | collective-permute-done | bytes 266272 | tf_op jit(solution)/shard_map/ppermute | solution.py:25
  191.9 3.6 %collective-permute-start.31 = (s16[1040,128]{1,0:T(8,128)(2,1)S(1)}, s16[1040,128]{1,0:T(8,128)(2,1)S(1)}, u32[]{:S(2)}, u32[]{:S(2)}) collective-permute-start(s16[1040,128]{1,0:T(8,128)(2,1)S(1)} %get-tuple-element.112), channel_id=1, source_target_pairs={{0,8},{4,12},{8,0},{12,4},{16,24},{20,28},{24,16},{28,20},{1,9},{5... | collective-permute-start | bytes 798728 | tf_op jit(solution)/shard_map/ppermute | solution.py:25
  206.4 10.7 %collective-permute-done.32.refs_2_ = s16[1040,128]{1,0:T(8,128)(2,1)S(1)} collective-permute-done((s16[1040,128]{1,0:T(8,128)(2,1)S(1)}, s16[1040,128]{1,0:T(8,128)(2,1)S(1)}, u32[]{:S(2)}, u32[]{:S(2)}) %collective-permute-start.32) | collective-permute-done | bytes 266272 | tf_op jit(solution)/shard_map/ppermute | solution.py:25
  227.0 5.3 %collective-permute-start.37 = (s16[1040,128]{1,0:T(8,128)(2,1)S(1)}, s16[1040,128]{1,0:T(8,128)(2,1)S(1)}, u32[]{:S(2)}, u32[]{:S(2)}) collective-permute-start(s16[1040,128]{1,0:T(8,128)(2,1)S(1)} %get-tuple-element.125.refs_0_), channel_id=1, source_target_pairs={{0,16},{4,20},{8,24},{12,28},{16,0},{20,4},{24,8},{28,12},{1,17},{... | collective-permute-start | bytes 798728 | tf_op jit(solution)/shard_map/ppermute | solution.py:25
  234.8 9.6 %collective-permute-done.42 = f32[128,128]{1,0:T(8,128)S(1)} collective-permute-done((f32[128,128]{1,0:T(8,128)S(1)}, f32[128,128]{1,0:T(8,128)S(1)}, u32[]{:S(2)}, u32[]{:S(2)}) %collective-permute-start.42) | collective-permute-done | bytes 65568 | tf_op jit(solution)/shard_map/ppermute | solution.py:25
  244.4 7.3 %collective-permute-done.37.refs_2_ = s16[1040,128]{1,0:T(8,128)(2,1)S(1)} collective-permute-done((s16[1040,128]{1,0:T(8,128)(2,1)S(1)}, s16[1040,128]{1,0:T(8,128)(2,1)S(1)}, u32[]{:S(2)}, u32[]{:S(2)}) %collective-permute-start.37) | collective-permute-done | bytes 266272 | tf_op jit(solution)/shard_map/ppermute | solution.py:25
  257.8 21.7 %collective-permute-done.43.refs_1_ = f32[128,128]{1,0:T(8,128)S(1)} collective-permute-done((f32[128,128]{1,0:T(8,128)S(1)}, f32[128,128]{1,0:T(8,128)S(1)}, u32[]{:S(2)}, u32[]{:S(2)}) %collective-permute-start.43) | collective-permute-done | bytes 65568 | tf_op jit(solution)/shard_map/ppermute | solution.py:25
  279.5 4.1 %shard_map.70.inverse_ref = f32[128,128]{1,0:T(8,128)S(1)} custom-call(f32[128,128]{1,0:T(8,128)S(1)} %add.65.refs_0_, f32[128,128]{1,0:T(8,128)S(1)} %collective-permute-done.43.refs_1_), custom_call_target="tpu_custom_call" | custom-call | flops 1 | bytes 1 | tf_op jit(solution)/shard_map/pallas_call | solution.py:128
  283.6 5.5 %shard_map.71.refs_0_ = f32[12288,128]{1,0:T(8,128)} custom-call(s32[3]{0:T(128)S(1)} %pad_add_fusion.2.pos_ref, f32[128,128]{1,0:T(8,128)S(1)} %shard_map.70.inverse_ref, s16[1040,128]{1,0:T(8,128)(2,1)S(1)} %get-tuple-element.125.refs_0_, s16[1040,128]{1,0:T(8,128)(2,1)S(1)} %collective-permute-done.36.refs_1_, ...), custom_call_target="tpu_custom_call" | custom-call | flops 1 | bytes 1 | tf_op jit(solution)/shard_map/pallas_call | solution.py:310
  289.2 3.6 %shard_map.72 = f32[12288,128]{1,0:T(8,128)} custom-call(s32[3]{0:T(128)S(1)} %pad_add_fusion.2.pos_ref, f32[128,128]{1,0:T(8,128)S(1)} %shard_map.70.inverse_ref, f32[12288,128]{1,0:T(8,128)} %shard_map.71.refs_0_, s16[2,528,128]{2,1,0:T(8,128)(2,1)S(1)} %pad_add_fusion.1.refs_1_, ...), custom_call_target="tpu_custom_call", output_to_operand_aliasing={{}: (2, {})} | custom-call | flops 1 | bytes 1 | tf_op jit(solution)/shard_map/pallas_call | solution.py:310
  (130 shorter events, 110.3 us)
Async XLA Ops:
  25.6 27.0 %collective-permute-start.3 = (bf16[4,1024,128]{2,1,0:T(8,128)(2,1)S(1)}, bf16[4,1024,128]{2,1,0:T(8,128)(2,1)S(1)}, u32[]{:S(2)}, u32[]{:S(2)}) collective-permute-start(bf16[4,1024,128]{2,1,0:T(8,128)(2,1)S(1)} %shard_map.48), channel_id=1, source_target_pairs={{0,4},{4,0},{8,12},{12,8},{16,20},{20,16},{24,28},{28,24},{1,5},{5... | collective-permute-start | bytes 3145736 | tf_op jit(solution)/shard_map/ppermute | solution.py:25
  31.0 21.4 %collective-permute-start.5 = (bf16[1024,128]{1,0:T(8,128)(2,1)S(1)}, bf16[1024,128]{1,0:T(8,128)(2,1)S(1)}, u32[]{:S(2)}, u32[]{:S(2)}) collective-permute-start(bf16[1024,128]{1,0:T(8,128)(2,1)S(1)} %get-tuple-element.73), channel_id=1, source_target_pairs={{0,16},{4,20},{8,24},{12,28},{16,0},{20,4},{24,8},{28,12},{1,17},{... | collective-permute-start | bytes 786440 | tf_op jit(solution)/shard_map/ppermute | solution.py:25
  57.9 21.3 %collective-permute-start.8 = (bf16[1024,128]{1,0:T(8,128)(2,1)S(1)}, bf16[1024,128]{1,0:T(8,128)(2,1)S(1)}, u32[]{:S(2)}, u32[]{:S(2)}) collective-permute-start(bf16[1024,128]{1,0:T(8,128)(2,1)S(1)} %get-tuple-element.80), channel_id=1, source_target_pairs={{0,16},{4,20},{8,24},{12,28},{16,0},{20,4},{24,8},{28,12},{1,17},{... | collective-permute-start | bytes 786440 | tf_op jit(solution)/shard_map/ppermute | solution.py:25
  59.9 19.3 %collective-permute-start.9 = (bf16[1024,128]{1,0:T(8,128)(2,1)S(1)}, bf16[1024,128]{1,0:T(8,128)(2,1)S(1)}, u32[]{:S(2)}, u32[]{:S(2)}) collective-permute-start(bf16[1024,128]{1,0:T(8,128)(2,1)S(1)} %get-tuple-element.81), channel_id=1, source_target_pairs={{0,24},{4,28},{8,16},{12,20},{16,8},{20,12},{24,0},{28,4},{1,25},{... | collective-permute-start | bytes 786440 | tf_op jit(solution)/shard_map/ppermute | solution.py:25
  86.2 20.5 %collective-permute-start.14 = (bf16[1024,128]{1,0:T(8,128)(2,1)S(1)}, bf16[1024,128]{1,0:T(8,128)(2,1)S(1)}, u32[]{:S(2)}, u32[]{:S(2)}) collective-permute-start(bf16[1024,128]{1,0:T(8,128)(2,1)S(1)} %get-tuple-element.92.refs_4_), channel_id=1, source_target_pairs={{0,24},{4,28},{8,16},{12,20},{16,8},{20,12},{24,0},{28,4},{1,25},{... | collective-permute-start | bytes 786440 | tf_op jit(solution)/shard_map/ppermute | solution.py:25
  89.6 22.2 %collective-permute-start.13 = (bf16[1024,128]{1,0:T(8,128)(2,1)S(1)}, bf16[1024,128]{1,0:T(8,128)(2,1)S(1)}, u32[]{:S(2)}, u32[]{:S(2)}) collective-permute-start(bf16[1024,128]{1,0:T(8,128)(2,1)S(1)} %get-tuple-element.92.refs_4_), channel_id=1, source_target_pairs={{0,16},{4,20},{8,24},{12,28},{16,0},{20,4},{24,8},{28,12},{1,17},{... | collective-permute-start | bytes 786440 | tf_op jit(solution)/shard_map/ppermute | solution.py:25
  111.9 35.2 %collective-permute-start.19 = (bf16[4,1024,128]{2,1,0:T(8,128)(2,1)S(1)}, bf16[4,1024,128]{2,1,0:T(8,128)(2,1)S(1)}, u32[]{:S(2)}, u32[]{:S(2)}) collective-permute-start(bf16[4,1024,128]{2,1,0:T(8,128)(2,1)S(1)} %pad_maximum_fusion), channel_id=1, source_target_pairs={{0,4},{4,0},{8,12},{12,8},{16,20},{20,16},{24,28},{28,24},{1,5},{5... | collective-permute-start | bytes 3145736 | tf_op jit(solution)/shard_map/ppermute | solution.py:25
  113.5 35.7 %collective-permute-start.20 = (bf16[2,512,128]{2,1,0:T(8,128)(2,1)S(1)}, bf16[2,512,128]{2,1,0:T(8,128)(2,1)S(1)}, u32[]{:S(2)}, u32[]{:S(2)}) collective-permute-start(bf16[2,512,128]{2,1,0:T(8,128)(2,1)S(1)} %pad_maximum_fusion.1), channel_id=1, source_target_pairs={{0,8},{4,12},{8,0},{12,4},{16,24},{20,28},{24,16},{28,20},{1,9},{5... | collective-permute-start | bytes 786440 | tf_op jit(solution)/shard_map/ppermute | solution.py:25
  114.1 36.6 %collective-permute-start.23 = (bf16[2,512,128]{2,1,0:T(8,128)(2,1)S(1)}, bf16[2,512,128]{2,1,0:T(8,128)(2,1)S(1)}, u32[]{:S(2)}, u32[]{:S(2)}) collective-permute-start(bf16[2,512,128]{2,1,0:T(8,128)(2,1)S(1)} %pad_maximum_fusion.1), channel_id=1, source_target_pairs={{0,24},{4,28},{8,16},{12,20},{16,8},{20,12},{24,0},{28,4},{1,25},{... | collective-permute-start | bytes 786440 | tf_op jit(solution)/shard_map/ppermute | solution.py:25
  116.9 33.8 %collective-permute-start.22 = (bf16[2,512,128]{2,1,0:T(8,128)(2,1)S(1)}, bf16[2,512,128]{2,1,0:T(8,128)(2,1)S(1)}, u32[]{:S(2)}, u32[]{:S(2)}) collective-permute-start(bf16[2,512,128]{2,1,0:T(8,128)(2,1)S(1)} %pad_maximum_fusion.1), channel_id=1, source_target_pairs={{0,16},{4,20},{8,24},{12,28},{16,0},{20,4},{24,8},{28,12},{1,17},{... | collective-permute-start | bytes 786440 | tf_op jit(solution)/shard_map/ppermute | solution.py:25
  117.5 25.6 %collective-permute-start.21 = (f32[128,128]{1,0:T(8,128)S(1)}, f32[128,128]{1,0:T(8,128)S(1)}, u32[]{:S(2)}, u32[]{:S(2)}) collective-permute-start(f32[128,128]{1,0:T(8,128)S(1)} %add.58.refs_0_), channel_id=1, source_target_pairs={{0,16},{4,20},{8,24},{12,28},{16,0},{20,4},{24,8},{28,12},{1,17},{... | collective-permute-start | bytes 196616 | tf_op jit(solution)/shard_map/ppermute | solution.py:25
  165.3 25.6 %collective-permute-start.27 = (s16[4,1040,128]{2,1,0:T(8,128)(2,1)S(1)}, s16[4,1040,128]{2,1,0:T(8,128)(2,1)S(1)}, u32[]{:S(2)}, u32[]{:S(2)}) collective-permute-start(s16[4,1040,128]{2,1,0:T(8,128)(2,1)S(1)} %shard_map.62), channel_id=1, source_target_pairs={{0,4},{4,0},{8,12},{12,8},{16,20},{20,16},{24,28},{28,24},{1,5},{5... | collective-permute-start | bytes 3194888 | tf_op jit(solution)/shard_map/ppermute | solution.py:25
  167.6 20.7 %collective-permute-start.29 = (s16[1040,128]{1,0:T(8,128)(2,1)S(1)}, s16[1040,128]{1,0:T(8,128)(2,1)S(1)}, u32[]{:S(2)}, u32[]{:S(2)}) collective-permute-start(s16[1040,128]{1,0:T(8,128)(2,1)S(1)} %get-tuple-element.106), channel_id=1, source_target_pairs={{0,16},{4,20},{8,24},{12,28},{16,0},{20,4},{24,8},{28,12},{1,17},{... | collective-permute-start | bytes 798728 | tf_op jit(solution)/shard_map/ppermute | solution.py:25
  167.7 20.6 %collective-permute-start.30 = (s16[1040,128]{1,0:T(8,128)(2,1)S(1)}, s16[1040,128]{1,0:T(8,128)(2,1)S(1)}, u32[]{:S(2)}, u32[]{:S(2)}) collective-permute-start(s16[1040,128]{1,0:T(8,128)(2,1)S(1)} %get-tuple-element.107), channel_id=1, source_target_pairs={{0,24},{4,28},{8,16},{12,20},{16,8},{20,12},{24,0},{28,4},{1,25},{... | collective-permute-start | bytes 798728 | tf_op jit(solution)/shard_map/ppermute | solution.py:25
  170.4 19.2 %collective-permute-start.28 = (s16[1040,128]{1,0:T(8,128)(2,1)S(1)}, s16[1040,128]{1,0:T(8,128)(2,1)S(1)}, u32[]{:S(2)}, u32[]{:S(2)}) collective-permute-start(s16[1040,128]{1,0:T(8,128)(2,1)S(1)} %get-tuple-element.105), channel_id=1, source_target_pairs={{0,8},{4,12},{8,0},{12,4},{16,24},{20,28},{24,16},{28,20},{1,9},{5... | collective-permute-start | bytes 798728 | tf_op jit(solution)/shard_map/ppermute | solution.py:25
  195.5 21.6 %collective-permute-start.32 = (s16[1040,128]{1,0:T(8,128)(2,1)S(1)}, s16[1040,128]{1,0:T(8,128)(2,1)S(1)}, u32[]{:S(2)}, u32[]{:S(2)}) collective-permute-start(s16[1040,128]{1,0:T(8,128)(2,1)S(1)} %get-tuple-element.113), channel_id=1, source_target_pairs={{0,16},{4,20},{8,24},{12,28},{16,0},{20,4},{24,8},{28,12},{1,17},{... | collective-permute-start | bytes 798728 | tf_op jit(solution)/shard_map/ppermute | solution.py:25
  195.5 21.6 %collective-permute-start.33 = (s16[1040,128]{1,0:T(8,128)(2,1)S(1)}, s16[1040,128]{1,0:T(8,128)(2,1)S(1)}, u32[]{:S(2)}, u32[]{:S(2)}) collective-permute-start(s16[1040,128]{1,0:T(8,128)(2,1)S(1)} %get-tuple-element.114), channel_id=1, source_target_pairs={{0,24},{4,28},{8,16},{12,20},{16,8},{20,12},{24,0},{28,4},{1,25},{... | collective-permute-start | bytes 798728 | tf_op jit(solution)/shard_map/ppermute | solution.py:25
  227.0 24.8 %collective-permute-start.37 = (s16[1040,128]{1,0:T(8,128)(2,1)S(1)}, s16[1040,128]{1,0:T(8,128)(2,1)S(1)}, u32[]{:S(2)}, u32[]{:S(2)}) collective-permute-start(s16[1040,128]{1,0:T(8,128)(2,1)S(1)} %get-tuple-element.125.refs_0_), channel_id=1, source_target_pairs={{0,16},{4,20},{8,24},{12,28},{16,0},{20,4},{24,8},{28,12},{1,17},{... | collective-permute-start | bytes 798728 | tf_op jit(solution)/shard_map/ppermute | solution.py:25
  232.3 19.4 %collective-permute-start.36 = (s16[1040,128]{1,0:T(8,128)(2,1)S(1)}, s16[1040,128]{1,0:T(8,128)(2,1)S(1)}, u32[]{:S(2)}, u32[]{:S(2)}) collective-permute-start(s16[1040,128]{1,0:T(8,128)(2,1)S(1)} %get-tuple-element.125.refs_0_), channel_id=1, source_target_pairs={{0,8},{4,12},{8,0},{12,4},{16,24},{20,28},{24,16},{28,20},{1,9},{5... | collective-permute-start | bytes 798728 | tf_op jit(solution)/shard_map/ppermute | solution.py:25
  251.8 31.8 %collective-permute-start.44 = (s16[4,1040,128]{2,1,0:T(8,128)(2,1)S(1)}, s16[4,1040,128]{2,1,0:T(8,128)(2,1)S(1)}, u32[]{:S(2)}, u32[]{:S(2)}) collective-permute-start(s16[4,1040,128]{2,1,0:T(8,128)(2,1)S(1)} %pad_add_fusion), channel_id=1, source_target_pairs={{0,4},{4,0},{8,12},{12,8},{16,20},{20,16},{24,28},{28,24},{1,5},{5... | collective-permute-start | bytes 3194888 | tf_op jit(solution)/shard_map/ppermute | solution.py:25
  253.4 35.8 %collective-permute-start.47 = (s16[2,528,128]{2,1,0:T(8,128)(2,1)S(1)}, s16[2,528,128]{2,1,0:T(8,128)(2,1)S(1)}, u32[]{:S(2)}, u32[]{:S(2)}) collective-permute-start(s16[2,528,128]{2,1,0:T(8,128)(2,1)S(1)} %pad_add_fusion.1.refs_1_), channel_id=1, source_target_pairs={{0,24},{4,28},{8,16},{12,20},{16,8},{20,12},{24,0},{28,4},{1,25},{... | collective-permute-start | bytes 811016 | tf_op jit(solution)/shard_map/ppermute | solution.py:25
  254.6 34.6 %collective-permute-start.46 = (s16[2,528,128]{2,1,0:T(8,128)(2,1)S(1)}, s16[2,528,128]{2,1,0:T(8,128)(2,1)S(1)}, u32[]{:S(2)}, u32[]{:S(2)}) collective-permute-start(s16[2,528,128]{2,1,0:T(8,128)(2,1)S(1)} %pad_add_fusion.1.refs_1_), channel_id=1, source_target_pairs={{0,16},{4,20},{8,24},{12,28},{16,0},{20,4},{24,8},{28,12},{1,17},{... | collective-permute-start | bytes 811016 | tf_op jit(solution)/shard_map/ppermute | solution.py:25
  254.6 34.6 %collective-permute-start.45 = (s16[2,528,128]{2,1,0:T(8,128)(2,1)S(1)}, s16[2,528,128]{2,1,0:T(8,128)(2,1)S(1)}, u32[]{:S(2)}, u32[]{:S(2)}) collective-permute-start(s16[2,528,128]{2,1,0:T(8,128)(2,1)S(1)} %pad_add_fusion.1.refs_1_), channel_id=1, source_target_pairs={{0,8},{4,12},{8,0},{12,4},{16,24},{20,28},{24,16},{28,20},{1,9},{5... | collective-permute-start | bytes 811016 | tf_op jit(solution)/shard_map/ppermute | solution.py:25
  257.8 21.7 %collective-permute-start.43 = (f32[128,128]{1,0:T(8,128)S(1)}, f32[128,128]{1,0:T(8,128)S(1)}, u32[]{:S(2)}, u32[]{:S(2)}) collective-permute-start(f32[128,128]{1,0:T(8,128)S(1)} %add.65.refs_0_), channel_id=1, source_target_pairs={{0,16},{4,20},{8,24},{12,28},{16,0},{20,4},{24,8},{28,12},{1,17},{... | collective-permute-start | bytes 196616 | tf_op jit(solution)/shard_map/ppermute | solution.py:25
  (29 other events, 281.8 us)

commit v8 on v6

--- a/solution.py
+++ b/solution.py
@@ -68,7 +68,7 @@
     def __init__(self, voxels, subjects):
         self.high = subjects // LOW
         unit = subjects * LANES
-        for top, bottom in ((2, 3), (1, 2)):
+        for top, bottom in ((3, 4), (2, 3), (1, 2)):
             self.cut = voxels * top // bottom
             self.pair = (voxels - self.cut) // self.high
             if self.cut % unit == 0 and voxels % unit == 0 and self.cut % self.pair == 0:
@@ -454,7 +454,6 @@
         def gather(first, second, gram):
             gram = gram + swap_vox(gram, mask=1)
             first, second, gram = lax.optimization_barrier((first, second, gram))
-            low_own = swap(first, mask=1)
             pieces = [swap(first, mask=k * LOW) for k in ks[1:]]
             got = swap(second, mask=1)
             lower = pos[0] == 0
@@ -464,14 +463,16 @@
                 gram = gram + swap_vox(gram, mask=mask)
                 mask *= 2
             gram = gram + swap(gram, mask=1)
+            pieces, pair, gram = lax.optimization_barrier((pieces, pair, gram))
+            near, far = ks[: high // 2], ks[high // 2 :]
+            low_near = swap(jnp.stack([first] + pieces[: len(near) - 1]), mask=1)
+            low_far = swap(jnp.stack(pieces[len(near) - 1 :]), mask=1)
             grams = [gram] + [swap(gram, mask=k * LOW) for k in ks[1:]]
-            pieces, pair, grams = lax.optimization_barrier((pieces, pair, grams))
-            low_rest = swap(jnp.stack(pieces), mask=1)
+            pair, grams = lax.optimization_barrier((pair, grams))
             seconds = [pair] + [swap(pair, mask=k * LOW) for k in ks[1:]]
             early = [(0, [k], array) for k, array in zip(ks, [first] + pieces)]
-            late = [(1, ks[:1], low_own), (1, ks[1:], low_rest)]
             pairs = [(None, [k], array) for k, array in zip(ks, seconds)]
-            return early, late, pairs, grams
+            return early, (1, near, low_near), (1, far, low_far), pairs, grams
 
         def sum_scores(mine, send, *factor):
             mine = mine + swap_vox(send, mask=1)
@@ -492,25 +493,23 @@
 
         def pass_over(scores, code):
             (first, gram_first), (second, gram_second) = sketch_sum(scores, code)
-            early, late, pairs, grams = gather(first, second, gram_first + gram_second)
+            early, near, far, pairs, grams = gather(first, second, gram_first + gram_second)
             inverse = small_call(
                 functools.partial(invert_kernel, all_voxels),
                 jax.ShapeDtypeStruct((rank, rank), F32), *grams,
             )
-            return early, late, pairs, inverse
+            return early, near, [far] + pairs, inverse
 
         scores = sum_scores(*first_project(scans, pos, test_matrix))
-        early, late, pairs, inverse = pass_over(scores, Plain)
-        pairs = [(j, k, array.reshape(layout.pair, rank)) for j, k, array in pairs]
+        early, near, last, inverse = pass_over(scores, Plain)
+        last = last[:1] + [(j, k, array.reshape(-1, rank)) for j, k, array in last[1:]]
         total = project(scans, layout, pos, early)
-        total = project(scans, layout, pos, late, total)
-        total = project(scans, layout, pos, pairs[: high // 2], total)
+        total = project(scans, layout, pos, [near], total)
         total, inverse = lax.optimization_barrier((total, inverse))
-        halves = project(scans, layout, pos, pairs[high // 2 :], total, True)
-        scores = sum_scores(*halves, inverse)
-        early, late, pairs, inverse = pass_over(scores, Fixed)
-        out = finish(layout, pos, early + late, inverse, voxels)
-        return finish(layout, pos, pairs, inverse, voxels, out)
+        scores = sum_scores(*project(scans, layout, pos, last, total, True), inverse)
+        early, near, last, inverse = pass_over(scores, Fixed)
+        out = finish(layout, pos, early + [near], inverse, voxels)
+        return finish(layout, pos, last, inverse, voxels, out)
 
     return on_device
 

time: 291 us -> 281 us (0.966)
  starting transfers between devices: 91.9 us -> 67.4 us
  waiting for transfers between devices: 129 us -> 140 us
    ppermute x52, starting transfers between devices: 91.9 us -> 67.4 us  [exchange(): return lax.ppermute(value, axis, [(i, i ^ mask) for i in range(size)])]
    ppermute x52, waiting for transfers between devices: 129 us -> 140 us  [exchange(): return lax.ppermute(value, axis, [(i, i ^ mask) for i in range(size)])]
    pallas_call x4 -> x3, Pallas kernels: 6.92 us -> 8.42 us  [project(): pl.pallas_call(functools.partial(project_kernel, base is not None, split,...]
  transfers between devices with their start and end apart: 52 -> 52, of which waited for: 28 -> 31; matrix products, arithmetic and copies ran while one was open for 0% -> 0% of each run, Pallas kernels for 13% -> 13%
where the time goes in v8:
time: 281 us
  waiting for transfers between devices  140 us (50%)
  starting transfers between devices  67.4 us (24%)
  Pallas kernels  64.6 us (23%)
  local copies, waits for them, and re-layouts  7.37 us (3%)
    ppermute x52, waiting for transfers between devices, exchange(): return lax.ppermute(value, axis, [(i, i ^ mask) for i in range(size)])  140 us
    ppermute x52, starting transfers between devices, exchange(): return lax.ppermute(value, axis, [(i, i ^ mask) for i in range(size)])  67.4 us
    pallas_call x8, Pallas kernels, sketch_part(): pl.pallas_call(functools.partial(sketch_kernel, code, apart, per_step), o...  23.3 us
    pallas_call x8, Pallas kernels, small_call(): pl.pallas_call(kernel, out_shape=out_shape, in_specs=[WHOLE] * len(args),...  12 us
    pallas_call x2, Pallas kernels, finish(): pl.pallas_call(functools.partial(finish_kernel, layout, items, base is no...  9.07 us
    pallas_call x1, Pallas kernels, first_project(): pl.pallas_call(functools.partial(first_kernel, count), out_shape=[half, h...  8.72 us
    pallas_call x3, Pallas kernels, project(): pl.pallas_call(functools.partial(project_kernel, base is not None, split,...  8.42 us
    unnamed x10, local copies, waits for them, and re-layouts  7.37 us
  transfers between devices with their start and end apart: 52, of which 31 were waited for; matrix products, arithmetic and copies ran while one was open for 0% of the time, Pallas kernels for 13%

profile of v8, /device:TPU:0, one launch (start us, length us, event | category | flops | bytes accessed | tf_op | source)
XLA Modules:
  0.0 280.8 jit_solution(15936384420127772374)
XLA Ops:
  2.0 8.7 %shard_map.46 = (f32[320,128]{1,0:T(8,128)S(1)}, f32[320,128]{1,0:T(8,128)S(1)}) custom-call(s32[3]{0:T(128)S(1)} %pad_add_fusion.3.pos_ref, bf16[12288,128]{1,0:T(8,128)(2,1)S(1)} %copy-done.2, bf16[640,12288]{1,0:T(8,128)(2,1)} %refs_0_.19, bf16[640,12288]{1,0:T(8,128)(2,1)} %refs_0_.19, bf16[640,12288]{1,0:T(8,128)(2,1)} %refs_0_.19, ...), custom_call_target="tpu_custom_call" | custom-call | flops 1 | bytes 1 | tf_op jit(solution)/shard_map/pallas_call | solution.py:206
  15.2 4.5 %collective-permute-done.1 = f32[320,128]{1,0:T(8,128)S(1)} collective-permute-done((f32[320,128]{1,0:T(8,128)S(1)}, f32[320,128]{1,0:T(8,128)S(1)}, u32[]{:S(2)}, u32[]{:S(2)}) %collective-permute-start.1) | collective-permute-done | bytes 163872 | tf_op jit(solution)/shard_map/ppermute | solution.py:25
  21.8 4.1 %shard_map.48 = bf16[4,1152,128]{2,1,0:T(8,128)(2,1)S(1)} custom-call(s32[3]{0:T(128)S(1)} %pad_add_fusion.3.pos_ref, bf16[640,128]{1,0:T(8,128)(2,1)S(1)} %shard_map.47.scores_ref, bf16[640,12288]{1,0:T(8,128)(2,1)} %refs_0_.19, bf16[640,12288]{1,0:T(8,128)(2,1)} %refs_0_.19), custom_call_target="tpu_custom_call" | custom-call | flops 1 | bytes 1 | tf_op jit(solution)/shard_map/pallas_call | solution.py:112
  37.3 4.1 %shard_map.50.own_ref = bf16[4,1152,128]{2,1,0:T(8,128)(2,1)S(1)} custom-call(s32[3]{0:T(128)S(1)} %pad_add_fusion.3.pos_ref, bf16[640,128]{1,0:T(8,128)(2,1)S(1)} %shard_map.47.scores_ref, bf16[640,12288]{1,0:T(8,128)(2,1)} %refs_0_.19, bf16[640,12288]{1,0:T(8,128)(2,1)} %refs_0_.19), custom_call_target="tpu_custom_call" | custom-call | flops 1 | bytes 1 | tf_op jit(solution)/shard_map/pallas_call | solution.py:112
  41.4 6.7 %collective-permute-done.5.refs_2_ = bf16[768,128]{1,0:T(8,128)(2,1)S(1)} collective-permute-done((bf16[768,128]{1,0:T(8,128)(2,1)S(1)}, bf16[768,128]{1,0:T(8,128)(2,1)S(1)}, u32[]{:S(2)}, u32[]{:S(2)}) %collective-permute-start.5) | collective-permute-done | bytes 196640 | tf_op jit(solution)/shard_map/ppermute | solution.py:25
  48.3 5.7 %collective-permute-done.3.got_ref = bf16[4,1152,128]{2,1,0:T(8,128)(2,1)S(1)} collective-permute-done((bf16[4,1152,128]{2,1,0:T(8,128)(2,1)S(1)}, bf16[4,1152,128]{2,1,0:T(8,128)(2,1)S(1)}, u32[]{:S(2)}, u32[]{:S(2)}) %collective-permute-start.3) | collective-permute-done | bytes 1179680 | tf_op jit(solution)/shard_map/ppermute | solution.py:25
  67.9 11.7 %collective-permute-done.8.refs_2_ = bf16[1152,128]{1,0:T(8,128)(2,1)S(1)} collective-permute-done((bf16[1152,128]{1,0:T(8,128)(2,1)S(1)}, bf16[1152,128]{1,0:T(8,128)(2,1)S(1)}, u32[]{:S(2)}, u32[]{:S(2)}) %collective-permute-start.8) | collective-permute-done | bytes 294944 | tf_op jit(solution)/shard_map/ppermute | solution.py:25
  87.3 3.9 %collective-permute-start.13 = (bf16[1152,128]{1,0:T(8,128)(2,1)S(1)}, bf16[1152,128]{1,0:T(8,128)(2,1)S(1)}, u32[]{:S(2)}, u32[]{:S(2)}) collective-permute-start(bf16[1152,128]{1,0:T(8,128)(2,1)S(1)} %get-tuple-element.102.refs_4_), channel_id=1, source_target_pairs={{0,16},{4,20},{8,24},{12,28},{16,0},{20,4},{24,8},{28,12},{1,17},{... | collective-permute-start | bytes 884744 | tf_op jit(solution)/shard_map/ppermute | solution.py:25
  92.0 3.7 %collective-permute-done.17 = f32[128,128]{1,0:T(8,128)S(1)} collective-permute-done((f32[128,128]{1,0:T(8,128)S(1)}, f32[128,128]{1,0:T(8,128)S(1)}, u32[]{:S(2)}, u32[]{:S(2)}) %collective-permute-start.17) | collective-permute-done | bytes 65568 | tf_op jit(solution)/shard_map/ppermute | solution.py:25
  96.7 17.4 %collective-permute-done.13.refs_6_ = bf16[1152,128]{1,0:T(8,128)(2,1)S(1)} collective-permute-done((bf16[1152,128]{1,0:T(8,128)(2,1)S(1)}, bf16[1152,128]{1,0:T(8,128)(2,1)S(1)}, u32[]{:S(2)}, u32[]{:S(2)}) %collective-permute-start.13) | collective-permute-done | bytes 294944 | tf_op jit(solution)/shard_map/ppermute | solution.py:25
  128.8 5.5 %copy-done = bf16[640,12288]{1,0:T(8,128)(2,1)S(1)} copy-done((bf16[640,12288]{1,0:T(8,128)(2,1)S(1)}, bf16[640,12288]{1,0:T(8,128)(2,1)}, u32[]{:S(2)}) %copy-start) | copy-done | bytes 15728664
  137.7 4.1 %shard_map.58.refs_0_ = f32[128,128]{1,0:T(8,128)S(1)} custom-call(f32[128,128]{1,0:T(8,128)S(1)} %add.51.refs_0_, f32[128,128]{1,0:T(8,128)S(1)} %collective-permute-done.19.refs_1_, f32[128,128]{1,0:T(8,128)S(1)} %collective-permute-done.20.refs_2_, f32[128,128]{1,0:T(8,128)S(1)} %collective-permute-done.21.refs_3_), custom_call_target="tpu_custom_call" | custom-call | flops 1 | bytes 1 | tf_op jit(solution)/shard_map/pallas_call | solution.py:128
  149.0 5.7 %collective-permute-done.27 = f32[320,128]{1,0:T(8,128)S(1)} collective-permute-done((f32[320,128]{1,0:T(8,128)S(1)}, f32[320,128]{1,0:T(8,128)S(1)}, u32[]{:S(2)}, u32[]{:S(2)}) %collective-permute-start.27) | collective-permute-done | bytes 163872 | tf_op jit(solution)/shard_map/ppermute | solution.py:25
  167.4 3.8 %shard_map.63.own_ref = s16[4,1168,128]{2,1,0:T(8,128)(2,1)S(1)} custom-call(s32[3]{0:T(128)S(1)} %pad_add_fusion.3.pos_ref, bf16[640,128]{1,0:T(8,128)(2,1)S(1)} %shard_map.60.scores_ref, bf16[640,12288]{1,0:T(8,128)(2,1)S(1)} %copy-done.1, bf16[640,12288]{1,0:T(8,128)(2,1)S(1)} %copy-done.1), custom_call_target="tpu_custom_call" | custom-call | flops 1 | bytes 1 | tf_op jit(solution)/shard_map/pallas_call | solution.py:112
  171.2 7.9 %collective-permute-done.31.refs_2_ = s16[784,128]{1,0:T(8,128)(2,1)S(1)} collective-permute-done((s16[784,128]{1,0:T(8,128)(2,1)S(1)}, s16[784,128]{1,0:T(8,128)(2,1)S(1)}, u32[]{:S(2)}, u32[]{:S(2)}) %collective-permute-start.31) | collective-permute-done | bytes 200736 | tf_op jit(solution)/shard_map/ppermute | solution.py:25
  180.4 8.7 %collective-permute-done.29.got_ref = s16[4,1168,128]{2,1,0:T(8,128)(2,1)S(1)} collective-permute-done((s16[4,1168,128]{2,1,0:T(8,128)(2,1)S(1)}, s16[4,1168,128]{2,1,0:T(8,128)(2,1)S(1)}, u32[]{:S(2)}, u32[]{:S(2)}) %collective-permute-start.29) | collective-permute-done | bytes 1196064 | tf_op jit(solution)/shard_map/ppermute | solution.py:25
  196.1 4.1 %collective-permute-done.36.refs_1_ = s16[400,128]{1,0:T(8,128)(2,1)S(1)} collective-permute-done((s16[400,128]{1,0:T(8,128)(2,1)S(1)}, s16[400,128]{1,0:T(8,128)(2,1)S(1)}, u32[]{:S(2)}, u32[]{:S(2)}) %collective-permute-start.36) | collective-permute-done | bytes 102432 | tf_op jit(solution)/shard_map/ppermute | solution.py:25
  204.1 10.1 %collective-permute-done.34.refs_2_ = s16[1168,128]{1,0:T(8,128)(2,1)S(1)} collective-permute-done((s16[1168,128]{1,0:T(8,128)(2,1)S(1)}, s16[1168,128]{1,0:T(8,128)(2,1)S(1)}, u32[]{:S(2)}, u32[]{:S(2)}) %collective-permute-start.34) | collective-permute-done | bytes 299040 | tf_op jit(solution)/shard_map/ppermute | solution.py:25
  220.0 4.3 %collective-permute-start.39 = (s16[1168,128]{1,0:T(8,128)(2,1)S(1)}, s16[1168,128]{1,0:T(8,128)(2,1)S(1)}, u32[]{:S(2)}, u32[]{:S(2)}) collective-permute-start(s16[1168,128]{1,0:T(8,128)(2,1)S(1)} %get-tuple-element.140.refs_0_), channel_id=1, source_target_pairs={{0,16},{4,20},{8,24},{12,28},{16,0},{20,4},{24,8},{28,12},{1,17},{... | collective-permute-start | bytes 897032 | tf_op jit(solution)/shard_map/ppermute | solution.py:25
  229.4 17.8 %collective-permute-done.39.refs_2_ = s16[1168,128]{1,0:T(8,128)(2,1)S(1)} collective-permute-done((s16[1168,128]{1,0:T(8,128)(2,1)S(1)}, s16[1168,128]{1,0:T(8,128)(2,1)S(1)}, u32[]{:S(2)}, u32[]{:S(2)}) %collective-permute-start.39) | collective-permute-done | bytes 299040 | tf_op jit(solution)/shard_map/ppermute | solution.py:25
  261.9 4.1 %shard_map.69.inverse_ref = f32[128,128]{1,0:T(8,128)S(1)} custom-call(f32[128,128]{1,0:T(8,128)S(1)} %add.57.refs_0_, f32[128,128]{1,0:T(8,128)S(1)} %collective-permute-done.44.refs_1_, f32[128,128]{1,0:T(8,128)S(1)} %collective-permute-done.45.refs_2_, f32[128,128]{1,0:T(8,128)S(1)} %collective-permute-done.46.refs_3_), custom_call_target="tpu_custom_call" | custom-call | flops 1 | bytes 1 | tf_op jit(solution)/shard_map/pallas_call | solution.py:128
  266.0 5.0 %shard_map.70.refs_0_ = f32[12288,128]{1,0:T(8,128)} custom-call(s32[3]{0:T(128)S(1)} %pad_add_fusion.3.pos_ref, f32[128,128]{1,0:T(8,128)S(1)} %shard_map.69.inverse_ref, s16[1168,128]{1,0:T(8,128)(2,1)S(1)} %get-tuple-element.140.refs_0_, s16[1168,128]{1,0:T(8,128)(2,1)S(1)} %collective-permute-done.38.refs_1_, ...), custom_call_target="tpu_custom_call" | custom-call | flops 1 | bytes 1 | tf_op jit(solution)/shard_map/pallas_call | solution.py:310
  271.0 5.5 %collective-permute-done.50.refs_4_ = s16[2,400,128]{2,1,0:T(8,128)(2,1)S(1)} collective-permute-done((s16[2,400,128]{2,1,0:T(8,128)(2,1)S(1)}, s16[2,400,128]{2,1,0:T(8,128)(2,1)S(1)}, u32[]{:S(2)}, u32[]{:S(2)}) %collective-permute-start.50) | collective-permute-done | bytes 204832 | tf_op jit(solution)/shard_map/ppermute | solution.py:25
  276.5 4.1 %shard_map.71 = f32[12288,128]{1,0:T(8,128)} custom-call(s32[3]{0:T(128)S(1)} %pad_add_fusion.3.pos_ref, f32[128,128]{1,0:T(8,128)S(1)} %shard_map.69.inverse_ref, f32[12288,128]{1,0:T(8,128)} %shard_map.70.refs_0_, s16[2,1168,128]{2,1,0:T(8,128)(2,1)S(1)} %collective-permute-done.48.refs_1_, ...), custom_call_target="tpu_custom_call", output_to_operand_aliasing={{}: (2, {})} | custom-call | flops 1 | bytes 1 | tf_op jit(solution)/shard_map/pallas_call | solution.py:310
  (137 shorter events, 118.8 us)
Async XLA Ops:
  25.9 28.1 %collective-permute-start.3 = (bf16[4,1152,128]{2,1,0:T(8,128)(2,1)S(1)}, bf16[4,1152,128]{2,1,0:T(8,128)(2,1)S(1)}, u32[]{:S(2)}, u32[]{:S(2)}) collective-permute-start(bf16[4,1152,128]{2,1,0:T(8,128)(2,1)S(1)} %shard_map.48), channel_id=1, source_target_pairs={{0,4},{4,0},{8,12},{12,8},{16,20},{20,16},{24,28},{28,24},{1,5},{5... | collective-permute-start | bytes 3538952 | tf_op jit(solution)/shard_map/ppermute | solution.py:25
  30.9 17.2 %collective-permute-start.5 = (bf16[768,128]{1,0:T(8,128)(2,1)S(1)}, bf16[768,128]{1,0:T(8,128)(2,1)S(1)}, u32[]{:S(2)}, u32[]{:S(2)}) collective-permute-start(bf16[768,128]{1,0:T(8,128)(2,1)S(1)} %get-tuple-element.83), channel_id=1, source_target_pairs={{0,16},{4,20},{8,24},{12,28},{16,0},{20,4},{24,8},{28,12},{1,17},{... | collective-permute-start | bytes 589832 | tf_op jit(solution)/shard_map/ppermute | solution.py:25
  33.5 14.6 %collective-permute-start.6 = (bf16[768,128]{1,0:T(8,128)(2,1)S(1)}, bf16[768,128]{1,0:T(8,128)(2,1)S(1)}, u32[]{:S(2)}, u32[]{:S(2)}) collective-permute-start(bf16[768,128]{1,0:T(8,128)(2,1)S(1)} %get-tuple-element.84), channel_id=1, source_target_pairs={{0,24},{4,28},{8,16},{12,20},{16,8},{20,12},{24,0},{28,4},{1,25},{... | collective-permute-start | bytes 589832 | tf_op jit(solution)/shard_map/ppermute | solution.py:25
  56.2 23.5 %collective-permute-start.8 = (bf16[1152,128]{1,0:T(8,128)(2,1)S(1)}, bf16[1152,128]{1,0:T(8,128)(2,1)S(1)}, u32[]{:S(2)}, u32[]{:S(2)}) collective-permute-start(bf16[1152,128]{1,0:T(8,128)(2,1)S(1)} %get-tuple-element.90), channel_id=1, source_target_pairs={{0,16},{4,20},{8,24},{12,28},{16,0},{20,4},{24,8},{28,12},{1,17},{... | collective-permute-start | bytes 884744 | tf_op jit(solution)/shard_map/ppermute | solution.py:25
  58.8 20.9 %collective-permute-start.9 = (bf16[1152,128]{1,0:T(8,128)(2,1)S(1)}, bf16[1152,128]{1,0:T(8,128)(2,1)S(1)}, u32[]{:S(2)}, u32[]{:S(2)}) collective-permute-start(bf16[1152,128]{1,0:T(8,128)(2,1)S(1)} %get-tuple-element.91), channel_id=1, source_target_pairs={{0,24},{4,28},{8,16},{12,20},{16,8},{20,12},{24,0},{28,4},{1,25},{... | collective-permute-start | bytes 884744 | tf_op jit(solution)/shard_map/ppermute | solution.py:25
  87.3 26.8 %collective-permute-start.13 = (bf16[1152,128]{1,0:T(8,128)(2,1)S(1)}, bf16[1152,128]{1,0:T(8,128)(2,1)S(1)}, u32[]{:S(2)}, u32[]{:S(2)}) collective-permute-start(bf16[1152,128]{1,0:T(8,128)(2,1)S(1)} %get-tuple-element.102.refs_4_), channel_id=1, source_target_pairs={{0,16},{4,20},{8,24},{12,28},{16,0},{20,4},{24,8},{28,12},{1,17},{... | collective-permute-start | bytes 884744 | tf_op jit(solution)/shard_map/ppermute | solution.py:25
  91.2 22.9 %collective-permute-start.12 = (bf16[1152,128]{1,0:T(8,128)(2,1)S(1)}, bf16[1152,128]{1,0:T(8,128)(2,1)S(1)}, u32[]{:S(2)}, u32[]{:S(2)}) collective-permute-start(bf16[1152,128]{1,0:T(8,128)(2,1)S(1)} %get-tuple-element.102.refs_4_), channel_id=1, source_target_pairs={{0,8},{4,12},{8,0},{12,4},{16,24},{20,28},{24,16},{28,20},{1,9},{5... | collective-permute-start | bytes 884744 | tf_op jit(solution)/shard_map/ppermute | solution.py:25
  114.2 27.7 %collective-permute-start.18 = (bf16[2,1152,128]{2,1,0:T(8,128)(2,1)S(1)}, bf16[2,1152,128]{2,1,0:T(8,128)(2,1)S(1)}, u32[]{:S(2)}, u32[]{:S(2)}) collective-permute-start(bf16[2,1152,128]{2,1,0:T(8,128)(2,1)S(1)} %pad_maximum_fusion), channel_id=1, source_target_pairs={{0,4},{4,0},{8,12},{12,8},{16,20},{20,16},{24,28},{28,24},{1,5},{5... | collective-permute-start | bytes 1769480 | tf_op jit(solution)/shard_map/ppermute | solution.py:25
  114.8 29.0 %collective-permute-start.22 = (bf16[2,1152,128]{2,1,0:T(8,128)(2,1)S(1)}, bf16[2,1152,128]{2,1,0:T(8,128)(2,1)S(1)}, u32[]{:S(2)}, u32[]{:S(2)}) collective-permute-start(bf16[2,1152,128]{2,1,0:T(8,128)(2,1)S(1)} %pad_maximum_fusion.1), channel_id=1, source_target_pairs={{0,4},{4,0},{8,12},{12,8},{16,20},{20,16},{24,28},{28,24},{1,5},{5... | collective-permute-start | bytes 1769480 | tf_op jit(solution)/shard_map/ppermute | solution.py:25
  124.4 19.4 %collective-permute-start.25 = (bf16[2,384,128]{2,1,0:T(8,128)(2,1)S(1)}, bf16[2,384,128]{2,1,0:T(8,128)(2,1)S(1)}, u32[]{:S(2)}, u32[]{:S(2)}) collective-permute-start(bf16[2,384,128]{2,1,0:T(8,128)(2,1)S(1)} %pad_maximum_fusion.2), channel_id=1, source_target_pairs={{0,24},{4,28},{8,16},{12,20},{16,8},{20,12},{24,0},{28,4},{1,25},{... | collective-permute-start | bytes 589832 | tf_op jit(solution)/shard_map/ppermute | solution.py:25
  126.9 16.9 %collective-permute-start.24 = (bf16[2,384,128]{2,1,0:T(8,128)(2,1)S(1)}, bf16[2,384,128]{2,1,0:T(8,128)(2,1)S(1)}, u32[]{:S(2)}, u32[]{:S(2)}) collective-permute-start(bf16[2,384,128]{2,1,0:T(8,128)(2,1)S(1)} %pad_maximum_fusion.2), channel_id=1, source_target_pairs={{0,16},{4,20},{8,24},{12,28},{16,0},{20,4},{24,8},{28,12},{1,17},{... | collective-permute-start | bytes 589832 | tf_op jit(solution)/shard_map/ppermute | solution.py:25
  126.9 16.9 %collective-permute-start.23 = (bf16[2,384,128]{2,1,0:T(8,128)(2,1)S(1)}, bf16[2,384,128]{2,1,0:T(8,128)(2,1)S(1)}, u32[]{:S(2)}, u32[]{:S(2)}) collective-permute-start(bf16[2,384,128]{2,1,0:T(8,128)(2,1)S(1)} %pad_maximum_fusion.2), channel_id=1, source_target_pairs={{0,8},{4,12},{8,0},{12,4},{16,24},{20,28},{24,16},{28,20},{1,9},{5... | collective-permute-start | bytes 589832 | tf_op jit(solution)/shard_map/ppermute | solution.py:25
  160.7 28.4 %collective-permute-start.29 = (s16[4,1168,128]{2,1,0:T(8,128)(2,1)S(1)}, s16[4,1168,128]{2,1,0:T(8,128)(2,1)S(1)}, u32[]{:S(2)}, u32[]{:S(2)}) collective-permute-start(s16[4,1168,128]{2,1,0:T(8,128)(2,1)S(1)} %shard_map.61), channel_id=1, source_target_pairs={{0,4},{4,0},{8,12},{12,8},{16,20},{20,16},{24,28},{28,24},{1,5},{5... | collective-permute-start | bytes 3588104 | tf_op jit(solution)/shard_map/ppermute | solution.py:25
  162.8 16.3 %collective-permute-start.31 = (s16[784,128]{1,0:T(8,128)(2,1)S(1)}, s16[784,128]{1,0:T(8,128)(2,1)S(1)}, u32[]{:S(2)}, u32[]{:S(2)}) collective-permute-start(s16[784,128]{1,0:T(8,128)(2,1)S(1)} %get-tuple-element.121), channel_id=1, source_target_pairs={{0,16},{4,20},{8,24},{12,28},{16,0},{20,4},{24,8},{28,12},{1,17},{... | collective-permute-start | bytes 602120 | tf_op jit(solution)/shard_map/ppermute | solution.py:25
  163.8 15.2 %collective-permute-start.32 = (s16[784,128]{1,0:T(8,128)(2,1)S(1)}, s16[784,128]{1,0:T(8,128)(2,1)S(1)}, u32[]{:S(2)}, u32[]{:S(2)}) collective-permute-start(s16[784,128]{1,0:T(8,128)(2,1)S(1)} %get-tuple-element.122), channel_id=1, source_target_pairs={{0,24},{4,28},{8,16},{12,20},{16,8},{20,12},{24,0},{28,4},{1,25},{... | collective-permute-start | bytes 602120 | tf_op jit(solution)/shard_map/ppermute | solution.py:25
  165.4 15.0 %collective-permute-start.30 = (s16[784,128]{1,0:T(8,128)(2,1)S(1)}, s16[784,128]{1,0:T(8,128)(2,1)S(1)}, u32[]{:S(2)}, u32[]{:S(2)}) collective-permute-start(s16[784,128]{1,0:T(8,128)(2,1)S(1)} %get-tuple-element.120), channel_id=1, source_target_pairs={{0,8},{4,12},{8,0},{12,4},{16,24},{20,28},{24,16},{28,20},{1,9},{5... | collective-permute-start | bytes 602120 | tf_op jit(solution)/shard_map/ppermute | solution.py:25
  190.4 23.8 %collective-permute-start.34 = (s16[1168,128]{1,0:T(8,128)(2,1)S(1)}, s16[1168,128]{1,0:T(8,128)(2,1)S(1)}, u32[]{:S(2)}, u32[]{:S(2)}) collective-permute-start(s16[1168,128]{1,0:T(8,128)(2,1)S(1)} %get-tuple-element.128), channel_id=1, source_target_pairs={{0,16},{4,20},{8,24},{12,28},{16,0},{20,4},{24,8},{28,12},{1,17},{... | collective-permute-start | bytes 897032 | tf_op jit(solution)/shard_map/ppermute | solution.py:25
  193.4 20.8 %collective-permute-start.35 = (s16[1168,128]{1,0:T(8,128)(2,1)S(1)}, s16[1168,128]{1,0:T(8,128)(2,1)S(1)}, u32[]{:S(2)}, u32[]{:S(2)}) collective-permute-start(s16[1168,128]{1,0:T(8,128)(2,1)S(1)} %get-tuple-element.129), channel_id=1, source_target_pairs={{0,24},{4,28},{8,16},{12,20},{16,8},{20,12},{24,0},{28,4},{1,25},{... | collective-permute-start | bytes 897032 | tf_op jit(solution)/shard_map/ppermute | solution.py:25
  220.0 27.2 %collective-permute-start.39 = (s16[1168,128]{1,0:T(8,128)(2,1)S(1)}, s16[1168,128]{1,0:T(8,128)(2,1)S(1)}, u32[]{:S(2)}, u32[]{:S(2)}) collective-permute-start(s16[1168,128]{1,0:T(8,128)(2,1)S(1)} %get-tuple-element.140.refs_0_), channel_id=1, source_target_pairs={{0,16},{4,20},{8,24},{12,28},{16,0},{20,4},{24,8},{28,12},{1,17},{... | collective-permute-start | bytes 897032 | tf_op jit(solution)/shard_map/ppermute | solution.py:25
  224.3 22.9 %collective-permute-start.38 = (s16[1168,128]{1,0:T(8,128)(2,1)S(1)}, s16[1168,128]{1,0:T(8,128)(2,1)S(1)}, u32[]{:S(2)}, u32[]{:S(2)}) collective-permute-start(s16[1168,128]{1,0:T(8,128)(2,1)S(1)} %get-tuple-element.140.refs_0_), channel_id=1, source_target_pairs={{0,8},{4,12},{8,0},{12,4},{16,24},{20,28},{24,16},{28,20},{1,9},{5... | collective-permute-start | bytes 897032 | tf_op jit(solution)/shard_map/ppermute | solution.py:25
  247.3 18.7 %collective-permute-start.47 = (s16[2,1168,128]{2,1,0:T(8,128)(2,1)S(1)}, s16[2,1168,128]{2,1,0:T(8,128)(2,1)S(1)}, u32[]{:S(2)}, u32[]{:S(2)}) collective-permute-start(s16[2,1168,128]{2,1,0:T(8,128)(2,1)S(1)} %pad_add_fusion), channel_id=1, source_target_pairs={{0,4},{4,0},{8,12},{12,8},{16,20},{20,16},{24,28},{28,24},{1,5},{5... | collective-permute-start | bytes 1794056 | tf_op jit(solution)/shard_map/ppermute | solution.py:25
  248.9 27.6 %collective-permute-start.48 = (s16[2,1168,128]{2,1,0:T(8,128)(2,1)S(1)}, s16[2,1168,128]{2,1,0:T(8,128)(2,1)S(1)}, u32[]{:S(2)}, u32[]{:S(2)}) collective-permute-start(s16[2,1168,128]{2,1,0:T(8,128)(2,1)S(1)} %pad_add_fusion.1), channel_id=1, source_target_pairs={{0,4},{4,0},{8,12},{12,8},{16,20},{20,16},{24,28},{28,24},{1,5},{5... | collective-permute-start | bytes 1794056 | tf_op jit(solution)/shard_map/ppermute | solution.py:25
  260.0 16.6 %collective-permute-start.50 = (s16[2,400,128]{2,1,0:T(8,128)(2,1)S(1)}, s16[2,400,128]{2,1,0:T(8,128)(2,1)S(1)}, u32[]{:S(2)}, u32[]{:S(2)}) collective-permute-start(s16[2,400,128]{2,1,0:T(8,128)(2,1)S(1)} %pad_add_fusion.2.refs_2_), channel_id=1, source_target_pairs={{0,16},{4,20},{8,24},{12,28},{16,0},{20,4},{24,8},{28,12},{1,17},{... | collective-permute-start | bytes 614408 | tf_op jit(solution)/shard_map/ppermute | solution.py:25
  260.0 16.6 %collective-permute-start.49 = (s16[2,400,128]{2,1,0:T(8,128)(2,1)S(1)}, s16[2,400,128]{2,1,0:T(8,128)(2,1)S(1)}, u32[]{:S(2)}, u32[]{:S(2)}) collective-permute-start(s16[2,400,128]{2,1,0:T(8,128)(2,1)S(1)} %pad_add_fusion.2.refs_2_), channel_id=1, source_target_pairs={{0,8},{4,12},{8,0},{12,4},{16,24},{20,28},{24,16},{28,20},{1,9},{5... | collective-permute-start | bytes 614408 | tf_op jit(solution)/shard_map/ppermute | solution.py:25
  (33 other events, 241.2 us)

commit v9 on v8

--- a/solution.py
+++ b/solution.py
@@ -15,8 +15,7 @@
 LOW = 2
 GROUP = 8
 LANES = 128
-VMEM_BYTES = 20 << 20
-VMEM_FIRST = 48 << 20
+VMEM_BYTES = 48 << 20
 LIGHT = pl.CostEstimate(flops=1, bytes_accessed=1, transcendentals=0)
 WHOLE = pl.BlockSpec(memory_space=pltpu.VMEM)
 
@@ -28,7 +27,6 @@
 class Plain:
     pad = 0
     dtype = BF16
-    limit = VMEM_FIRST
 
     @staticmethod
     def encode(value):
@@ -42,7 +40,6 @@
 class Fixed:
     pad = 16
     dtype = I16
-    limit = VMEM_BYTES
 
     @staticmethod
     def encode(value):
@@ -60,15 +57,15 @@
         return wide[:rows] * jnp.exp2(wide[rows : rows + 1] * (1.0 / STEPS))
 
 
-def params(limit=VMEM_BYTES):
-    return pltpu.CompilerParams(vmem_limit_bytes=limit)
+def params():
+    return pltpu.CompilerParams(vmem_limit_bytes=VMEM_BYTES)
 
 
 class Layout:
     def __init__(self, voxels, subjects):
         self.high = subjects // LOW
         unit = subjects * LANES
-        for top, bottom in ((3, 4), (2, 3), (1, 2)):
+        for top, bottom in ((2, 3), (1, 2)):
             self.cut = voxels * top // bottom
             self.pair = (voxels - self.cut) // self.high
             if self.cut % unit == 0 and voxels % unit == 0 and self.cut % self.pair == 0:
@@ -119,7 +116,7 @@
             + [pl.BlockSpec((time_rows, n), column(u)) for u in range(per_step)],
             out_specs=out_specs,
         ),
-        compiler_params=params(code.limit),
+        compiler_params=params(),
         cost_estimate=LIGHT,
     )(pos, scores, *([scans] * per_step))
 
@@ -214,7 +211,7 @@
             out_specs=[pl.BlockSpec(half.shape, lambda g, pos: (0, 0))] * 2,
             scratch_shapes=[pltpu.VMEM((time_rows, rank), F32)],
         ),
-        compiler_params=params(VMEM_FIRST),
+        compiler_params=params(),
         cost_estimate=LIGHT,
     )(pos, panel, *([scans] * count))
 
@@ -451,7 +448,7 @@
                 add_all(code, [keep, got_send]),
             )
 
-        def gather(first, second, gram):
+        def gather(first, second, gram, gram_last):
             gram = gram + swap_vox(gram, mask=1)
             first, second, gram = lax.optimization_barrier((first, second, gram))
             pieces = [swap(first, mask=k * LOW) for k in ks[1:]]
@@ -467,15 +464,29 @@
             near, far = ks[: high // 2], ks[high // 2 :]
             low_near = swap(jnp.stack([first] + pieces[: len(near) - 1]), mask=1)
             low_far = swap(jnp.stack(pieces[len(near) - 1 :]), mask=1)
-            grams = [gram] + [swap(gram, mask=k * LOW) for k in ks[1:]]
-            pair, grams = lax.optimization_barrier((pair, grams))
+            if not gram_last:
+                grams = [gram] + [swap(gram, mask=k * LOW) for k in ks[1:]]
+                pair, grams = lax.optimization_barrier((pair, grams))
             seconds = [pair] + [swap(pair, mask=k * LOW) for k in ks[1:]]
+            if gram_last:
+                seconds, gram = lax.optimization_barrier((seconds, gram))
+                grams = [gram] + [swap(gram, mask=k * LOW) for k in ks[1:]]
             early = [(0, [k], array) for k, array in zip(ks, [first] + pieces)]
             pairs = [(None, [k], array) for k, array in zip(ks, seconds)]
             return early, (1, near, low_near), (1, far, low_far), pairs, grams
 
-        def sum_scores(mine, send, *factor):
+        def invert(grams):
+            return small_call(
+                functools.partial(invert_kernel, all_voxels),
+                jax.ShapeDtypeStruct((rank, rank), F32), *grams,
+            )
+
+        def sum_scores(mine, send, grams=None):
             mine = mine + swap_vox(send, mask=1)
+            factor = []
+            if grams is not None:
+                mine, grams = lax.optimization_barrier((mine, grams))
+                factor = [invert(grams)]
             mask = 2
             while mask < blocks:
                 mine = mine + swap_vox(mine, mask=mask)
@@ -491,25 +502,21 @@
                 cost_estimate=LIGHT,
             )(lengths, block_subject, pos, mine, other, *factor)
 
-        def pass_over(scores, code):
+        def pass_over(scores, code, gram_last):
             (first, gram_first), (second, gram_second) = sketch_sum(scores, code)
-            early, near, far, pairs, grams = gather(first, second, gram_first + gram_second)
-            inverse = small_call(
-                functools.partial(invert_kernel, all_voxels),
-                jax.ShapeDtypeStruct((rank, rank), F32), *grams,
-            )
-            return early, near, [far] + pairs, inverse
+            return gather(first, second, gram_first + gram_second, gram_last)
 
         scores = sum_scores(*first_project(scans, pos, test_matrix))
-        early, near, last, inverse = pass_over(scores, Plain)
-        last = last[:1] + [(j, k, array.reshape(-1, rank)) for j, k, array in last[1:]]
+        early, near, far, pairs, grams = pass_over(scores, Plain, True)
+        pairs = [(j, k, array.reshape(-1, rank)) for j, k, array in pairs]
         total = project(scans, layout, pos, early)
         total = project(scans, layout, pos, [near], total)
-        total, inverse = lax.optimization_barrier((total, inverse))
-        scores = sum_scores(*project(scans, layout, pos, last, total, True), inverse)
-        early, near, last, inverse = pass_over(scores, Fixed)
+        total = project(scans, layout, pos, [far], total)
+        scores = sum_scores(*project(scans, layout, pos, pairs, total, True), grams)
+        early, near, far, pairs, grams = pass_over(scores, Fixed, False)
+        inverse = invert(grams)
         out = finish(layout, pos, early + [near], inverse, voxels)
-        return finish(layout, pos, last, inverse, voxels, out)
+        return finish(layout, pos, [far] + pairs, inverse, voxels, out)
 
     return on_device
 

time: 281 us -> 303 us (1.078)
  Pallas kernels: 64.6 us -> 76.6 us
  starting transfers between devices: 67.4 us -> 75.8 us
  waiting for transfers between devices: 140 us -> 147 us
  local copies, waits for them, and re-layouts: 7.37 us -> 1.9 us
    ppermute x52, starting transfers between devices: 67.4 us -> 75.8 us  [exchange(): return lax.ppermute(value, axis, [(i, i ^ mask) for i in range(size)])]
    pallas_call x3 -> x4, Pallas kernels: 8.42 us -> 15.4 us  [project(): pl.pallas_call(functools.partial(project_kernel, base is not None, split,...]
    ppermute x52, waiting for transfers between devices: 140 us -> 147 us  [exchange(): return lax.ppermute(value, axis, [(i, i ^ mask) for i in range(size)])]
    unnamed x10 -> x6, local copies, waits for them, and re-layouts: 7.37 us -> 1.9 us
    pallas_call x8, Pallas kernels: 23.3 us -> 28.4 us  [sketch_part(): pl.pallas_call(functools.partial(sketch_kernel, code, apart, per_step), o...]
  transfers between devices with their start and end apart: 52 -> 52, of which waited for: 31 -> 29; matrix products, arithmetic and copies ran while one was open for 0% -> 0% of each run, Pallas kernels for 13% -> 14%
where the time goes in v9:
time: 303 us
  waiting for transfers between devices  147 us (49%)
  Pallas kernels  76.6 us (25%)
  starting transfers between devices  75.8 us (25%)
    ppermute x52, waiting for transfers between devices, exchange(): return lax.ppermute(value, axis, [(i, i ^ mask) for i in range(size)])  147 us
    ppermute x52, starting transfers between devices, exchange(): return lax.ppermute(value, axis, [(i, i ^ mask) for i in range(size)])  75.8 us
    pallas_call x8, Pallas kernels, sketch_part(): pl.pallas_call(functools.partial(sketch_kernel, code, apart, per_step), o...  28.4 us
    pallas_call x4, Pallas kernels, project(): pl.pallas_call(functools.partial(project_kernel, base is not None, split,...  15.4 us
    pallas_call x8, Pallas kernels, small_call(): pl.pallas_call(kernel, out_shape=out_shape, in_specs=[WHOLE] * len(args),...  11.8 us
    pallas_call x2, Pallas kernels, finish(): pl.pallas_call(functools.partial(finish_kernel, layout, items, base is no...  9.12 us
    pallas_call x1, Pallas kernels, first_project(): pl.pallas_call(functools.partial(first_kernel, count), out_shape=[half, h...  8.72 us
  transfers between devices with their start and end apart: 52, of which 29 were waited for; matrix products, arithmetic and copies ran while one was open for 0% of the time, Pallas kernels for 14%

profile of v9, /device:TPU:0, one launch (start us, length us, event | category | flops | bytes accessed | tf_op | source)
XLA Modules:
  0.0 302.5 jit_solution(14441028838229505414)
XLA Ops:
  2.0 8.7 %shard_map.46 = (f32[320,128]{1,0:T(8,128)S(1)}, f32[320,128]{1,0:T(8,128)S(1)}) custom-call(s32[3]{0:T(128)S(1)} %pad_add_fusion.3.pos_ref, bf16[12288,128]{1,0:T(8,128)(2,1)S(1)} %copy-done, bf16[640,12288]{1,0:T(8,128)(2,1)} %refs_0_.19, bf16[640,12288]{1,0:T(8,128)(2,1)} %refs_0_.19, bf16[640,12288]{1,0:T(8,128)(2,1)} %refs_0_.19, ...), custom_call_target="tpu_custom_call" | custom-call | flops 1 | bytes 1 | tf_op jit(solution)/shard_map/pallas_call | solution.py:203
  15.2 4.5 %collective-permute-done.1 = f32[320,128]{1,0:T(8,128)S(1)} collective-permute-done((f32[320,128]{1,0:T(8,128)S(1)}, f32[320,128]{1,0:T(8,128)S(1)}, u32[]{:S(2)}, u32[]{:S(2)}) %collective-permute-start.1) | collective-permute-done | bytes 163872 | tf_op jit(solution)/shard_map/ppermute | solution.py:24
  37.5 4.0 %shard_map.50.own_ref = bf16[4,1024,128]{2,1,0:T(8,128)(2,1)S(1)} custom-call(s32[3]{0:T(128)S(1)} %pad_add_fusion.3.pos_ref, bf16[640,128]{1,0:T(8,128)(2,1)S(1)} %shard_map.47.scores_ref, bf16[640,12288]{1,0:T(8,128)(2,1)} %refs_0_.19, bf16[640,12288]{1,0:T(8,128)(2,1)} %refs_0_.19), custom_call_target="tpu_custom_call" | custom-call | flops 1 | bytes 1 | tf_op jit(solution)/shard_map/pallas_call | solution.py:109
  41.5 10.9 %collective-permute-done.5.refs_2_ = bf16[1024,128]{1,0:T(8,128)(2,1)S(1)} collective-permute-done((bf16[1024,128]{1,0:T(8,128)(2,1)S(1)}, bf16[1024,128]{1,0:T(8,128)(2,1)S(1)}, u32[]{:S(2)}, u32[]{:S(2)}) %collective-permute-start.5) | collective-permute-done | bytes 262176 | tf_op jit(solution)/shard_map/ppermute | solution.py:24
  52.9 5.0 %collective-permute-start.7 = (bf16[1024,128]{1,0:T(8,128)(2,1)S(1)}, bf16[1024,128]{1,0:T(8,128)(2,1)S(1)}, u32[]{:S(2)}, u32[]{:S(2)}) collective-permute-start(bf16[1024,128]{1,0:T(8,128)(2,1)S(1)} %get-tuple-element.92), channel_id=1, source_target_pairs={{0,8},{4,12},{8,0},{12,4},{16,24},{20,28},{24,16},{28,20},{1,9},{5... | collective-permute-start | bytes 786440 | tf_op jit(solution)/shard_map/ppermute | solution.py:24
  62.6 4.5 %collective-permute-done.10.refs_1_ = bf16[512,128]{1,0:T(8,128)(2,1)S(1)} collective-permute-done((bf16[512,128]{1,0:T(8,128)(2,1)S(1)}, bf16[512,128]{1,0:T(8,128)(2,1)S(1)}, u32[]{:S(2)}, u32[]{:S(2)}) %collective-permute-start.10) | collective-permute-done | bytes 131104 | tf_op jit(solution)/shard_map/ppermute | solution.py:24
  69.8 9.5 %collective-permute-done.8.refs_2_ = bf16[1024,128]{1,0:T(8,128)(2,1)S(1)} collective-permute-done((bf16[1024,128]{1,0:T(8,128)(2,1)S(1)}, bf16[1024,128]{1,0:T(8,128)(2,1)S(1)}, u32[]{:S(2)}, u32[]{:S(2)}) %collective-permute-start.8) | collective-permute-done | bytes 262176 | tf_op jit(solution)/shard_map/ppermute | solution.py:24
  96.2 15.6 %collective-permute-done.13.refs_6_ = bf16[1024,128]{1,0:T(8,128)(2,1)S(1)} collective-permute-done((bf16[1024,128]{1,0:T(8,128)(2,1)S(1)}, bf16[1024,128]{1,0:T(8,128)(2,1)S(1)}, u32[]{:S(2)}, u32[]{:S(2)}) %collective-permute-start.13) | collective-permute-done | bytes 262176 | tf_op jit(solution)/shard_map/ppermute | solution.py:24
  118.4 4.6 %shard_map.56.refs_0_ = f32[640,128]{1,0:T(8,128)S(1)} custom-call(s32[3]{0:T(128)S(1)} %pad_add_fusion.3.pos_ref, bf16[640,12288]{1,0:T(8,128)(2,1)} %refs_0_.19, bf16[640,12288]{1,0:T(8,128)(2,1)} %refs_0_.19, bf16[640,12288]{1,0:T(8,128)(2,1)} %refs_0_.19, bf16[640,12288]{1,0:T(8,128)(2,1)} %refs_0_.19, bf16[1024,128]{1,0:T(8,128)(2,1)S(1)} %get-tuple-element.105.refs_4_, ...), custom_call_target="tpu_custom_call" | custom-call | flops 1 | bytes 1 | tf_op jit(solution)/shard_map/pallas_call | solution.py:255
  125.2 13.4 %collective-permute-done.21 = bf16[2,512,128]{2,1,0:T(8,128)(2,1)S(1)} collective-permute-done((bf16[2,512,128]{2,1,0:T(8,128)(2,1)S(1)}, bf16[2,512,128]{2,1,0:T(8,128)(2,1)S(1)}, u32[]{:S(2)}, u32[]{:S(2)}) %collective-permute-start.21) | collective-permute-done | bytes 262176 | tf_op jit(solution)/shard_map/ppermute | solution.py:24
  144.8 4.6 %shard_map.59 = (f32[320,128]{1,0:T(8,128)S(1)}, f32[320,128]{1,0:T(8,128)S(1)}) custom-call(s32[3]{0:T(128)S(1)} %pad_add_fusion.3.pos_ref, f32[640,128]{1,0:T(8,128)S(1)} %shard_map.58.refs_0_, bf16[640,12288]{1,0:T(8,128)(2,1)} %refs_0_.19, bf16[640,12288]{1,0:T(8,128)(2,1)} %refs_0_.19, bf16[640,12288]{1,0:T(8,128)(2,1)} %refs_0_.19, ...), custom_call_target="tpu_custom_call" | custom-call | flops 1 | bytes 1 | tf_op jit(solution)/shard_map/pallas_call | solution.py:255
  160.1 4.7 %collective-permute-done.27 = f32[320,128]{1,0:T(8,128)S(1)} collective-permute-done((f32[320,128]{1,0:T(8,128)S(1)}, f32[320,128]{1,0:T(8,128)S(1)}, u32[]{:S(2)}, u32[]{:S(2)}) %collective-permute-start.27) | collective-permute-done | bytes 163872 | tf_op jit(solution)/shard_map/ppermute | solution.py:24
  164.9 4.1 %shard_map.60.refs_0_ = f32[128,128]{1,0:T(8,128)S(1)} custom-call(f32[128,128]{1,0:T(8,128)S(1)} %add.51.refs_0_, f32[128,128]{1,0:T(8,128)S(1)} %collective-permute-done.24.refs_1_, f32[128,128]{1,0:T(8,128)S(1)} %collective-permute-done.25.refs_2_, f32[128,128]{1,0:T(8,128)S(1)} %collective-permute-done.26.refs_3_), custom_call_target="tpu_custom_call" | custom-call | flops 1 | bytes 1 | tf_op jit(solution)/shard_map/pallas_call | solution.py:125
  170.0 4.3 %shard_map.62 = s16[4,1040,128]{2,1,0:T(8,128)(2,1)S(1)} custom-call(s32[3]{0:T(128)S(1)} %pad_add_fusion.3.pos_ref, bf16[640,128]{1,0:T(8,128)(2,1)S(1)} %shard_map.61.scores_ref, bf16[640,12288]{1,0:T(8,128)(2,1)} %refs_0_.19, bf16[640,12288]{1,0:T(8,128)(2,1)} %refs_0_.19), custom_call_target="tpu_custom_call" | custom-call | flops 1 | bytes 1 | tf_op jit(solution)/shard_map/pallas_call | solution.py:109
  185.8 4.1 %shard_map.64.own_ref = s16[4,1040,128]{2,1,0:T(8,128)(2,1)S(1)} custom-call(s32[3]{0:T(128)S(1)} %pad_add_fusion.3.pos_ref, bf16[640,128]{1,0:T(8,128)(2,1)S(1)} %shard_map.61.scores_ref, bf16[640,12288]{1,0:T(8,128)(2,1)} %refs_0_.19, bf16[640,12288]{1,0:T(8,128)(2,1)} %refs_0_.19), custom_call_target="tpu_custom_call" | custom-call | flops 1 | bytes 1 | tf_op jit(solution)/shard_map/pallas_call | solution.py:109
  189.9 9.4 %collective-permute-done.31.refs_2_ = s16[1040,128]{1,0:T(8,128)(2,1)S(1)} collective-permute-done((s16[1040,128]{1,0:T(8,128)(2,1)S(1)}, s16[1040,128]{1,0:T(8,128)(2,1)S(1)}, u32[]{:S(2)}, u32[]{:S(2)}) %collective-permute-start.31) | collective-permute-done | bytes 266272 | tf_op jit(solution)/shard_map/ppermute | solution.py:24
  201.9 4.7 %collective-permute-start.33 = (s16[1040,128]{1,0:T(8,128)(2,1)S(1)}, s16[1040,128]{1,0:T(8,128)(2,1)S(1)}, u32[]{:S(2)}, u32[]{:S(2)}) collective-permute-start(s16[1040,128]{1,0:T(8,128)(2,1)S(1)} %get-tuple-element.133), channel_id=1, source_target_pairs={{0,8},{4,12},{8,0},{12,4},{16,24},{20,28},{24,16},{28,20},{1,9},{5... | collective-permute-start | bytes 798728 | tf_op jit(solution)/shard_map/ppermute | solution.py:24
  210.7 4.5 %collective-permute-done.36.refs_1_ = s16[528,128]{1,0:T(8,128)(2,1)S(1)} collective-permute-done((s16[528,128]{1,0:T(8,128)(2,1)S(1)}, s16[528,128]{1,0:T(8,128)(2,1)S(1)}, u32[]{:S(2)}, u32[]{:S(2)}) %collective-permute-start.36) | collective-permute-done | bytes 135200 | tf_op jit(solution)/shard_map/ppermute | solution.py:24
  218.3 9.9 %collective-permute-done.34.refs_2_ = s16[1040,128]{1,0:T(8,128)(2,1)S(1)} collective-permute-done((s16[1040,128]{1,0:T(8,128)(2,1)S(1)}, s16[1040,128]{1,0:T(8,128)(2,1)S(1)}, u32[]{:S(2)}, u32[]{:S(2)}) %collective-permute-start.34) | collective-permute-done | bytes 266272 | tf_op jit(solution)/shard_map/ppermute | solution.py:24
  246.4 16.4 %collective-permute-done.39.refs_2_ = s16[1040,128]{1,0:T(8,128)(2,1)S(1)} collective-permute-done((s16[1040,128]{1,0:T(8,128)(2,1)S(1)}, s16[1040,128]{1,0:T(8,128)(2,1)S(1)}, u32[]{:S(2)}, u32[]{:S(2)}) %collective-permute-start.39) | collective-permute-done | bytes 266272 | tf_op jit(solution)/shard_map/ppermute | solution.py:24
  277.6 4.1 %shard_map.70.inverse_ref = f32[128,128]{1,0:T(8,128)S(1)} custom-call(f32[128,128]{1,0:T(8,128)S(1)} %add.57.refs_0_, f32[128,128]{1,0:T(8,128)S(1)} %collective-permute-done.44.refs_1_, f32[128,128]{1,0:T(8,128)S(1)} %collective-permute-done.45.refs_2_, f32[128,128]{1,0:T(8,128)S(1)} %collective-permute-done.46.refs_3_), custom_call_target="tpu_custom_call" | custom-call | flops 1 | bytes 1 | tf_op jit(solution)/shard_map/pallas_call | solution.py:125
  281.6 4.6 %shard_map.71.refs_0_ = f32[12288,128]{1,0:T(8,128)} custom-call(s32[3]{0:T(128)S(1)} %pad_add_fusion.3.pos_ref, f32[128,128]{1,0:T(8,128)S(1)} %shard_map.70.inverse_ref, s16[1040,128]{1,0:T(8,128)(2,1)S(1)} %get-tuple-element.146.refs_0_, s16[1040,128]{1,0:T(8,128)(2,1)S(1)} %collective-permute-done.38.refs_1_, ...), custom_call_target="tpu_custom_call" | custom-call | flops 1 | bytes 1 | tf_op jit(solution)/shard_map/pallas_call | solution.py:307
  286.2 11.5 %collective-permute-done.50.refs_4_ = s16[2,528,128]{2,1,0:T(8,128)(2,1)S(1)} collective-permute-done((s16[2,528,128]{2,1,0:T(8,128)(2,1)S(1)}, s16[2,528,128]{2,1,0:T(8,128)(2,1)S(1)}, u32[]{:S(2)}, u32[]{:S(2)}) %collective-permute-start.50) | collective-permute-done | bytes 270368 | tf_op jit(solution)/shard_map/ppermute | solution.py:24
  297.8 4.6 %shard_map.72 = f32[12288,128]{1,0:T(8,128)} custom-call(s32[3]{0:T(128)S(1)} %pad_add_fusion.3.pos_ref, f32[128,128]{1,0:T(8,128)S(1)} %shard_map.70.inverse_ref, f32[12288,128]{1,0:T(8,128)} %shard_map.71.refs_0_, s16[2,1040,128]{2,1,0:T(8,128)(2,1)S(1)} %collective-permute-done.48.refs_1_, ...), custom_call_target="tpu_custom_call", output_to_operand_aliasing={{}: (2, {})} | custom-call | flops 1 | bytes 1 | tf_op jit(solution)/shard_map/pallas_call | solution.py:307
  (134 shorter events, 130.0 us)
Async XLA Ops:
  25.6 27.1 %collective-permute-start.3 = (bf16[4,1024,128]{2,1,0:T(8,128)(2,1)S(1)}, bf16[4,1024,128]{2,1,0:T(8,128)(2,1)S(1)}, u32[]{:S(2)}, u32[]{:S(2)}) collective-permute-start(bf16[4,1024,128]{2,1,0:T(8,128)(2,1)S(1)} %shard_map.48), channel_id=1, source_target_pairs={{0,4},{4,0},{8,12},{12,8},{16,20},{20,16},{24,28},{28,24},{1,5},{5... | collective-permute-start | bytes 3145736 | tf_op jit(solution)/shard_map/ppermute | solution.py:24
  31.0 21.4 %collective-permute-start.5 = (bf16[1024,128]{1,0:T(8,128)(2,1)S(1)}, bf16[1024,128]{1,0:T(8,128)(2,1)S(1)}, u32[]{:S(2)}, u32[]{:S(2)}) collective-permute-start(bf16[1024,128]{1,0:T(8,128)(2,1)S(1)} %get-tuple-element.86), channel_id=1, source_target_pairs={{0,16},{4,20},{8,24},{12,28},{16,0},{20,4},{24,8},{28,12},{1,17},{... | collective-permute-start | bytes 786440 | tf_op jit(solution)/shard_map/ppermute | solution.py:24
  33.7 18.8 %collective-permute-start.6 = (bf16[1024,128]{1,0:T(8,128)(2,1)S(1)}, bf16[1024,128]{1,0:T(8,128)(2,1)S(1)}, u32[]{:S(2)}, u32[]{:S(2)}) collective-permute-start(bf16[1024,128]{1,0:T(8,128)(2,1)S(1)} %get-tuple-element.87), channel_id=1, source_target_pairs={{0,24},{4,28},{8,16},{12,20},{16,8},{20,12},{24,0},{28,4},{1,25},{... | collective-permute-start | bytes 786440 | tf_op jit(solution)/shard_map/ppermute | solution.py:24
  35.0 17.6 %collective-permute-start.4 = (bf16[1024,128]{1,0:T(8,128)(2,1)S(1)}, bf16[1024,128]{1,0:T(8,128)(2,1)S(1)}, u32[]{:S(2)}, u32[]{:S(2)}) collective-permute-start(bf16[1024,128]{1,0:T(8,128)(2,1)S(1)} %get-tuple-element.85), channel_id=1, source_target_pairs={{0,8},{4,12},{8,0},{12,4},{16,24},{20,28},{24,16},{28,20},{1,9},{5... | collective-permute-start | bytes 786440 | tf_op jit(solution)/shard_map/ppermute | solution.py:24
  57.9 21.3 %collective-permute-start.8 = (bf16[1024,128]{1,0:T(8,128)(2,1)S(1)}, bf16[1024,128]{1,0:T(8,128)(2,1)S(1)}, u32[]{:S(2)}, u32[]{:S(2)}) collective-permute-start(bf16[1024,128]{1,0:T(8,128)(2,1)S(1)} %get-tuple-element.93), channel_id=1, source_target_pairs={{0,16},{4,20},{8,24},{12,28},{16,0},{20,4},{24,8},{28,12},{1,17},{... | collective-permute-start | bytes 786440 | tf_op jit(solution)/shard_map/ppermute | solution.py:24
  59.9 19.3 %collective-permute-start.9 = (bf16[1024,128]{1,0:T(8,128)(2,1)S(1)}, bf16[1024,128]{1,0:T(8,128)(2,1)S(1)}, u32[]{:S(2)}, u32[]{:S(2)}) collective-permute-start(bf16[1024,128]{1,0:T(8,128)(2,1)S(1)} %get-tuple-element.94), channel_id=1, source_target_pairs={{0,24},{4,28},{8,16},{12,20},{16,8},{20,12},{24,0},{28,4},{1,25},{... | collective-permute-start | bytes 786440 | tf_op jit(solution)/shard_map/ppermute | solution.py:24
  89.6 22.2 %collective-permute-start.13 = (bf16[1024,128]{1,0:T(8,128)(2,1)S(1)}, bf16[1024,128]{1,0:T(8,128)(2,1)S(1)}, u32[]{:S(2)}, u32[]{:S(2)}) collective-permute-start(bf16[1024,128]{1,0:T(8,128)(2,1)S(1)} %get-tuple-element.105.refs_4_), channel_id=1, source_target_pairs={{0,16},{4,20},{8,24},{12,28},{16,0},{20,4},{24,8},{28,12},{1,17},{... | collective-permute-start | bytes 786440 | tf_op jit(solution)/shard_map/ppermute | solution.py:24
  93.1 18.7 %collective-permute-start.12 = (bf16[1024,128]{1,0:T(8,128)(2,1)S(1)}, bf16[1024,128]{1,0:T(8,128)(2,1)S(1)}, u32[]{:S(2)}, u32[]{:S(2)}) collective-permute-start(bf16[1024,128]{1,0:T(8,128)(2,1)S(1)} %get-tuple-element.105.refs_4_), channel_id=1, source_target_pairs={{0,8},{4,12},{8,0},{12,4},{16,24},{20,28},{24,16},{28,20},{1,9},{5... | collective-permute-start | bytes 786440 | tf_op jit(solution)/shard_map/ppermute | solution.py:24
  111.8 26.7 %collective-permute-start.18 = (bf16[2,1024,128]{2,1,0:T(8,128)(2,1)S(1)}, bf16[2,1024,128]{2,1,0:T(8,128)(2,1)S(1)}, u32[]{:S(2)}, u32[]{:S(2)}) collective-permute-start(bf16[2,1024,128]{2,1,0:T(8,128)(2,1)S(1)} %pad_maximum_fusion), channel_id=1, source_target_pairs={{0,4},{4,0},{8,12},{12,8},{16,20},{20,16},{24,28},{28,24},{1,5},{5... | collective-permute-start | bytes 1572872 | tf_op jit(solution)/shard_map/ppermute | solution.py:24
  113.5 28.2 %collective-permute-start.19 = (bf16[2,1024,128]{2,1,0:T(8,128)(2,1)S(1)}, bf16[2,1024,128]{2,1,0:T(8,128)(2,1)S(1)}, u32[]{:S(2)}, u32[]{:S(2)}) collective-permute-start(bf16[2,1024,128]{2,1,0:T(8,128)(2,1)S(1)} %pad_maximum_fusion.1), channel_id=1, source_target_pairs={{0,4},{4,0},{8,12},{12,8},{16,20},{20,16},{24,28},{28,24},{1,5},{5... | collective-permute-start | bytes 1572872 | tf_op jit(solution)/shard_map/ppermute | solution.py:24
  117.4 21.1 %collective-permute-start.21 = (bf16[2,512,128]{2,1,0:T(8,128)(2,1)S(1)}, bf16[2,512,128]{2,1,0:T(8,128)(2,1)S(1)}, u32[]{:S(2)}, u32[]{:S(2)}) collective-permute-start(bf16[2,512,128]{2,1,0:T(8,128)(2,1)S(1)} %pad_maximum_fusion.2), channel_id=1, source_target_pairs={{0,16},{4,20},{8,24},{12,28},{16,0},{20,4},{24,8},{28,12},{1,17},{... | collective-permute-start | bytes 786440 | tf_op jit(solution)/shard_map/ppermute | solution.py:24
  117.4 21.1 %collective-permute-start.20 = (bf16[2,512,128]{2,1,0:T(8,128)(2,1)S(1)}, bf16[2,512,128]{2,1,0:T(8,128)(2,1)S(1)}, u32[]{:S(2)}, u32[]{:S(2)}) collective-permute-start(bf16[2,512,128]{2,1,0:T(8,128)(2,1)S(1)} %pad_maximum_fusion.2), channel_id=1, source_target_pairs={{0,8},{4,12},{8,0},{12,4},{16,24},{20,28},{24,16},{28,20},{1,9},{5... | collective-permute-start | bytes 786440 | tf_op jit(solution)/shard_map/ppermute | solution.py:24
  174.3 26.6 %collective-permute-start.29 = (s16[4,1040,128]{2,1,0:T(8,128)(2,1)S(1)}, s16[4,1040,128]{2,1,0:T(8,128)(2,1)S(1)}, u32[]{:S(2)}, u32[]{:S(2)}) collective-permute-start(s16[4,1040,128]{2,1,0:T(8,128)(2,1)S(1)} %shard_map.62), channel_id=1, source_target_pairs={{0,4},{4,0},{8,12},{12,8},{16,20},{20,16},{24,28},{28,24},{1,5},{5... | collective-permute-start | bytes 3194888 | tf_op jit(solution)/shard_map/ppermute | solution.py:24
  179.7 19.5 %collective-permute-start.31 = (s16[1040,128]{1,0:T(8,128)(2,1)S(1)}, s16[1040,128]{1,0:T(8,128)(2,1)S(1)}, u32[]{:S(2)}, u32[]{:S(2)}) collective-permute-start(s16[1040,128]{1,0:T(8,128)(2,1)S(1)} %get-tuple-element.127), channel_id=1, source_target_pairs={{0,16},{4,20},{8,24},{12,28},{16,0},{20,4},{24,8},{28,12},{1,17},{... | collective-permute-start | bytes 798728 | tf_op jit(solution)/shard_map/ppermute | solution.py:24
  180.0 19.2 %collective-permute-start.32 = (s16[1040,128]{1,0:T(8,128)(2,1)S(1)}, s16[1040,128]{1,0:T(8,128)(2,1)S(1)}, u32[]{:S(2)}, u32[]{:S(2)}) collective-permute-start(s16[1040,128]{1,0:T(8,128)(2,1)S(1)} %get-tuple-element.128), channel_id=1, source_target_pairs={{0,24},{4,28},{8,16},{12,20},{16,8},{20,12},{24,0},{28,4},{1,25},{... | collective-permute-start | bytes 798728 | tf_op jit(solution)/shard_map/ppermute | solution.py:24
  181.0 19.8 %collective-permute-start.30 = (s16[1040,128]{1,0:T(8,128)(2,1)S(1)}, s16[1040,128]{1,0:T(8,128)(2,1)S(1)}, u32[]{:S(2)}, u32[]{:S(2)}) collective-permute-start(s16[1040,128]{1,0:T(8,128)(2,1)S(1)} %get-tuple-element.126), channel_id=1, source_target_pairs={{0,8},{4,12},{8,0},{12,4},{16,24},{20,28},{24,16},{28,20},{1,9},{5... | collective-permute-start | bytes 798728 | tf_op jit(solution)/shard_map/ppermute | solution.py:24
  206.5 21.6 %collective-permute-start.34 = (s16[1040,128]{1,0:T(8,128)(2,1)S(1)}, s16[1040,128]{1,0:T(8,128)(2,1)S(1)}, u32[]{:S(2)}, u32[]{:S(2)}) collective-permute-start(s16[1040,128]{1,0:T(8,128)(2,1)S(1)} %get-tuple-element.134), channel_id=1, source_target_pairs={{0,16},{4,20},{8,24},{12,28},{16,0},{20,4},{24,8},{28,12},{1,17},{... | collective-permute-start | bytes 798728 | tf_op jit(solution)/shard_map/ppermute | solution.py:24
  207.8 20.4 %collective-permute-start.35 = (s16[1040,128]{1,0:T(8,128)(2,1)S(1)}, s16[1040,128]{1,0:T(8,128)(2,1)S(1)}, u32[]{:S(2)}, u32[]{:S(2)}) collective-permute-start(s16[1040,128]{1,0:T(8,128)(2,1)S(1)} %get-tuple-element.135), channel_id=1, source_target_pairs={{0,24},{4,28},{8,16},{12,20},{16,8},{20,12},{24,0},{28,4},{1,25},{... | collective-permute-start | bytes 798728 | tf_op jit(solution)/shard_map/ppermute | solution.py:24
  239.4 23.3 %collective-permute-start.39 = (s16[1040,128]{1,0:T(8,128)(2,1)S(1)}, s16[1040,128]{1,0:T(8,128)(2,1)S(1)}, u32[]{:S(2)}, u32[]{:S(2)}) collective-permute-start(s16[1040,128]{1,0:T(8,128)(2,1)S(1)} %get-tuple-element.146.refs_0_), channel_id=1, source_target_pairs={{0,16},{4,20},{8,24},{12,28},{16,0},{20,4},{24,8},{28,12},{1,17},{... | collective-permute-start | bytes 798728 | tf_op jit(solution)/shard_map/ppermute | solution.py:24
  243.3 19.4 %collective-permute-start.38 = (s16[1040,128]{1,0:T(8,128)(2,1)S(1)}, s16[1040,128]{1,0:T(8,128)(2,1)S(1)}, u32[]{:S(2)}, u32[]{:S(2)}) collective-permute-start(s16[1040,128]{1,0:T(8,128)(2,1)S(1)} %get-tuple-element.146.refs_0_), channel_id=1, source_target_pairs={{0,8},{4,12},{8,0},{12,4},{16,24},{20,28},{24,16},{28,20},{1,9},{5... | collective-permute-start | bytes 798728 | tf_op jit(solution)/shard_map/ppermute | solution.py:24
  262.8 18.8 %collective-permute-start.47 = (s16[2,1040,128]{2,1,0:T(8,128)(2,1)S(1)}, s16[2,1040,128]{2,1,0:T(8,128)(2,1)S(1)}, u32[]{:S(2)}, u32[]{:S(2)}) collective-permute-start(s16[2,1040,128]{2,1,0:T(8,128)(2,1)S(1)} %pad_add_fusion), channel_id=1, source_target_pairs={{0,4},{4,0},{8,12},{12,8},{16,20},{20,16},{24,28},{28,24},{1,5},{5... | collective-permute-start | bytes 1597448 | tf_op jit(solution)/shard_map/ppermute | solution.py:24
  263.4 34.4 %collective-permute-start.48 = (s16[2,1040,128]{2,1,0:T(8,128)(2,1)S(1)}, s16[2,1040,128]{2,1,0:T(8,128)(2,1)S(1)}, u32[]{:S(2)}, u32[]{:S(2)}) collective-permute-start(s16[2,1040,128]{2,1,0:T(8,128)(2,1)S(1)} %pad_add_fusion.1), channel_id=1, source_target_pairs={{0,4},{4,0},{8,12},{12,8},{16,20},{20,16},{24,28},{28,24},{1,5},{5... | collective-permute-start | bytes 1597448 | tf_op jit(solution)/shard_map/ppermute | solution.py:24
  275.7 22.1 %collective-permute-start.50 = (s16[2,528,128]{2,1,0:T(8,128)(2,1)S(1)}, s16[2,528,128]{2,1,0:T(8,128)(2,1)S(1)}, u32[]{:S(2)}, u32[]{:S(2)}) collective-permute-start(s16[2,528,128]{2,1,0:T(8,128)(2,1)S(1)} %pad_add_fusion.2.refs_2_), channel_id=1, source_target_pairs={{0,16},{4,20},{8,24},{12,28},{16,0},{20,4},{24,8},{28,12},{1,17},{... | collective-permute-start | bytes 811016 | tf_op jit(solution)/shard_map/ppermute | solution.py:24
  275.7 22.1 %collective-permute-start.49 = (s16[2,528,128]{2,1,0:T(8,128)(2,1)S(1)}, s16[2,528,128]{2,1,0:T(8,128)(2,1)S(1)}, u32[]{:S(2)}, u32[]{:S(2)}) collective-permute-start(s16[2,528,128]{2,1,0:T(8,128)(2,1)S(1)} %pad_add_fusion.2.refs_2_), channel_id=1, source_target_pairs={{0,8},{4,12},{8,0},{12,4},{16,24},{20,28},{24,16},{28,20},{1,9},{5... | collective-permute-start | bytes 811016 | tf_op jit(solution)/shard_map/ppermute | solution.py:24
  (31 other events, 244.3 us)

commit v10 on v5

--- a/solution.py
+++ b/solution.py
@@ -14,6 +14,7 @@
 STEPS = 64.0
 LOW = 2
 GROUP = 8
+SYNC_ROWS = 16
 LANES = 128
 VMEM_BYTES = 48 << 20
 LIGHT = pl.CostEstimate(flops=1, bytes_accessed=1, transcendentals=0)
@@ -216,26 +217,34 @@
     )(pos, panel, *([scans] * count))
 
 
-def project_kernel(has_base, split, items, pos_ref, *refs):
+def project_kernel(has_base, has_after, split, items, pos_ref, *refs):
     refs = list(refs)
     base = refs.pop(0) if has_base else None
+    if has_after:
+        refs.pop(0)
     outs = [refs.pop() for _ in range(2 if split else 1)][::-1]
     scans, pieces = refs[: len(items)], refs[len(items) :]
     time_rows = scans[0].shape[0]
     rank = outs[0].shape[1]
     total = jnp.zeros((time_rows, rank), F32)
+    gram = jnp.zeros((rank, rank), F32)
     for scan, (source, index) in zip(scans, items):
         piece = pieces[source][...] if index is None else pieces[source][index]
         total += jnp.dot(scan[...], piece, preferred_element_type=F32)
+        gram += lax.dot_general(
+            piece, piece, (((0,), (0,)), ((), ())), preferred_element_type=F32
+        )
     if has_base:
-        total += base[...]
+        total += base[:time_rows]
+        gram += base[time_rows:]
     if split:
-        write_halves(pos_ref, total, outs)
+        write_halves(pos_ref, jnp.concatenate([total, gram]), outs)
     else:
-        outs[0][...] = total
-
-
-def project(scans, layout, pos, groups, base=None, split=False):
+        outs[0][:time_rows] = total
+        outs[0][time_rows:] = gram
+
+
+def project(scans, layout, pos, groups, base=None, split=False, after=None):
     time_rows = scans.shape[0]
     rank = groups[0][2].shape[-1]
     items, names = [], []
@@ -249,23 +258,26 @@
 
     full = lambda shape: pl.BlockSpec(shape, lambda g, pos: (0,) * len(shape))
     bases = [] if base is None else [base]
+    afters = [] if after is None else [after]
     arrays = [array for _, _, array in groups]
-    shape = (time_rows // 2, rank) if split else (time_rows, rank)
+    rows = time_rows + rank
+    shape = (rows // 2, rank) if split else (rows, rank)
     out_shape = [jax.ShapeDtypeStruct(shape, F32)] * (2 if split else 1)
     out = pl.pallas_call(
-        functools.partial(project_kernel, base is not None, split, items),
+        functools.partial(project_kernel, base is not None, after is not None, split, items),
         out_shape=out_shape,
         grid_spec=pltpu.PrefetchScalarGridSpec(
             num_scalar_prefetch=1,
             grid=(1,),
             in_specs=[full(b.shape) for b in bases]
+            + [pl.BlockSpec(memory_space=pl.ANY)] * len(afters)
             + [pl.BlockSpec((time_rows, layout.columns(j)), column(j, k)) for j, k in names]
             + [full(p.shape) for p in arrays],
             out_specs=[full(shape)] * len(out_shape),
         ),
         compiler_params=params(),
         cost_estimate=LIGHT,
-    )(pos, *bases, *([scans] * len(items)), *arrays)
+    )(pos, *bases, *afters, *([scans] * len(items)), *arrays)
     return out if split else out[0]
 
 
@@ -376,14 +388,16 @@
     )
 
 
-def scores_kernel(with_factor, lengths_ref, subjects_ref, pos_ref, mine_ref, other_ref, *refs):
-    out_ref = refs[-1]
+def scores_kernel(all_voxels, lengths_ref, subjects_ref, pos_ref, mine_ref, other_ref, out_ref):
     length = lengths_ref[subjects_ref[pos_ref[1] * LOW + pos_ref[0]]]
+    time_rows = out_ref.shape[0]
     mine, other = mine_ref[...], other_ref[...]
     lower = pos_ref[2] == 0
-    scores = jnp.concatenate([jnp.where(lower, mine, other), jnp.where(lower, other, mine)])
-    if with_factor:
-        scores = times_transpose(scores, refs[0][...])
+    both = jnp.concatenate([jnp.where(lower, mine, other), jnp.where(lower, other, mine)])
+    scores = both[:time_rows]
+    if both.shape[0] > time_rows:
+        inverse = inverse_factor(both[time_rows:] * (1.0 / all_voxels))
+        scores = times_transpose(scores, inverse)
     live = lax.broadcasted_iota(jnp.int32, scores.shape, 0) < length
     out_ref[...] = jnp.where(live, scores, 0.0).astype(BF16)
 
@@ -449,31 +463,33 @@
                 add_all(code, [keep, got_send]),
             )
 
-        def gather(first, second, gram):
-            gram = gram + swap_vox(gram, mask=1)
-            first, second, gram = lax.optimization_barrier((first, second, gram))
+        def gather(first, second, gram=None):
+            meet = swap_vox(first[:SYNC_ROWS] if gram is None else gram, mask=1)
+            first, second, meet = lax.optimization_barrier((first, second, meet))
             far_in = [swap(first, mask=k * LOW) for k in far]
             near_in = [first] + [swap(first, mask=k * LOW) for k in near[1:]]
             got = swap(second, mask=1)
             lower = pos[0] == 0
             pair = jnp.stack([jnp.where(lower, second, got), jnp.where(lower, got, second)])
-            mask = 2
-            while mask < blocks:
-                gram = gram + swap_vox(gram, mask=mask)
-                mask *= 2
-            near_in, gram = lax.optimization_barrier((near_in, gram))
+            if gram is not None:
+                gram = gram + meet
+                mask = 2
+                while mask < blocks:
+                    gram = gram + swap_vox(gram, mask=mask)
+                    mask *= 2
+                gram = gram + swap(gram, mask=1)
+            far_in, near_in, pair, gram = lax.optimization_barrier((far_in, near_in, pair, gram))
             low_near = swap(jnp.stack(near_in), mask=1)
-            gram = gram + swap(gram, mask=1)
-            far_in, pair, gram = lax.optimization_barrier((far_in, pair, gram))
             low_far = swap(jnp.stack(far_in), mask=1)
+            if gram is not None:
+                gram = [gram] + [swap(gram, mask=k * LOW) for k in ks[1:]]
             seconds = [pair] + [swap(pair, mask=k * LOW) for k in ks[1:]]
-            gram = [gram] + [swap(gram, mask=k * LOW) for k in ks[1:]]
             early = [(0, [k], array) for k, array in zip(near + far, near_in + far_in)]
             late = [(1, near, low_near), (1, far, low_far)]
             pairs = [(None, [k], array) for k, array in zip(ks, seconds)]
-            return early, late, pairs, gram
-
-        def sum_scores(mine, send, *factor):
+            return early, late, pairs, meet if gram is None else gram
+
+        def sum_scores(mine, send):
             mine = mine + swap_vox(send, mask=1)
             mask = 2
             while mask < blocks:
@@ -481,34 +497,30 @@
                 mask *= 2
             other = swap_vox(mine, mask=1)
             return pl.pallas_call(
-                functools.partial(scores_kernel, bool(factor)),
+                functools.partial(scores_kernel, all_voxels),
                 out_shape=jax.ShapeDtypeStruct((time_rows, rank), BF16),
-                in_specs=[pl.BlockSpec(memory_space=pltpu.SMEM)] * 3
-                + [WHOLE] * (2 + len(factor)),
+                in_specs=[pl.BlockSpec(memory_space=pltpu.SMEM)] * 3 + [WHOLE] * 2,
                 out_specs=WHOLE,
                 compiler_params=params(),
                 cost_estimate=LIGHT,
-            )(lengths, block_subject, pos, mine, other, *factor)
-
-        def pass_over(scores, code):
-            (first, gram_first), (second, gram_second) = sketch_sum(scores, code)
-            early, late, pairs, grams = gather(first, second, gram_first + gram_second)
-            inverse = small_call(
-                functools.partial(invert_kernel, all_voxels),
-                jax.ShapeDtypeStruct((rank, rank), F32), *grams,
-            )
-            return early, late, pairs, inverse
+            )(lengths, block_subject, pos, mine, other)
 
         scores = sum_scores(*first_project(scans, pos, test_matrix))
-        early, late, pairs, inverse = pass_over(scores, Plain)
+        (first, _), (second, _) = sketch_sum(scores, Plain)
+        early, late, pairs, meet = gather(first, second)
         pairs = [(j, k, array.reshape(layout.pair, rank)) for j, k, array in pairs]
-        total = project(scans, layout, pos, early)
+        total = project(scans, layout, pos, early, after=meet)
         total = project(scans, layout, pos, late, total)
         total = project(scans, layout, pos, pairs[: high // 2], total)
-        total, inverse = lax.optimization_barrier((total, inverse))
         halves = project(scans, layout, pos, pairs[high // 2 :], total, True)
-        scores = sum_scores(*halves, inverse)
-        early, late, pairs, inverse = pass_over(scores, Fixed)
+        scores = sum_scores(*halves)
+
+        (first, gram_first), (second, gram_second) = sketch_sum(scores, Fixed)
+        early, late, pairs, grams = gather(first, second, gram_first + gram_second)
+        inverse = small_call(
+            functools.partial(invert_kernel, all_voxels),
+            jax.ShapeDtypeStruct((rank, rank), F32), *grams,
+        )
         out = finish(layout, pos, early + late, inverse, voxels)
         return finish(layout, pos, pairs, inverse, voxels, out)
 

time: 283 us -> 297 us (1.049)
  waiting for transfers between devices: 129 us -> 146 us
  starting transfers between devices: 74.6 us -> 68.5 us
    ppermute x52 -> x47, waiting for transfers between devices: 129 us -> 146 us  [exchange(): return lax.ppermute(value, axis, [(i, i ^ mask) for i in range(size)])]
    ppermute x52 -> x47, starting transfers between devices: 74.6 us -> 68.5 us  [exchange(): return lax.ppermute(value, axis, [(i, i ^ mask) for i in range(size)])]
    pallas_call x6, Pallas kernels: 17 us -> 22.5 us  [the longest x4 16.3 us: project(): pl.pallas_call(functools.partial(project_kernel, base is not None, after...]
    pallas_call x8 -> x7, Pallas kernels: 11.7 us -> 8.94 us  [small_call(): pl.pallas_call(kernel, out_shape=out_shape, in_specs=[WHOLE] * len(args),...]
  transfers between devices with their start and end apart: 52 -> 47, of which waited for: 31 -> 29; matrix products, arithmetic and copies ran while one was open for 0% -> 0% of each run, Pallas kernels for 17% -> 16%
where the time goes in v10:
time: 297 us; the launch traced here: 296 us
  waiting for transfers between devices  146 us (49%)
  Pallas kernels  79.1 us (27%)
  starting transfers between devices  68.5 us (23%)
    ppermute x47, waiting for transfers between devices, exchange(): return lax.ppermute(value, axis, [(i, i ^ mask) for i in range(size)])  146 us
    ppermute x47, starting transfers between devices, exchange(): return lax.ppermute(value, axis, [(i, i ^ mask) for i in range(size)])  68.5 us
    pallas_call x8, Pallas kernels, sketch_part(): pl.pallas_call(functools.partial(sketch_kernel, code, apart, per_step), o...  28.1 us
    pallas_call x4, Pallas kernels, project(): pl.pallas_call(functools.partial(project_kernel, base is not None, after...  16.3 us
    pallas_call x2, Pallas kernels, finish(): pl.pallas_call(functools.partial(finish_kernel, layout, items, base is no...  9.12 us
    pallas_call x7, Pallas kernels, small_call(): pl.pallas_call(kernel, out_shape=out_shape, in_specs=[WHOLE] * len(args),...  8.94 us
    pallas_call x1, Pallas kernels, first_project(): pl.pallas_call(functools.partial(first_kernel, count), out_shape=[half, h...  8.72 us
    pallas_call x2, Pallas kernels, sum_scores(): pl.pallas_call(functools.partial(scores_kernel, all_voxels), out_shape=ja...  6.24 us
  transfers between devices with their start and end apart: 47, of which 29 were waited for; matrix products, arithmetic and copies ran while one was open for 0% of the time, Pallas kernels for 16%

profile of v10, /device:TPU:0, one launch (start us, length us, event | category | flops | bytes accessed | tf_op | source)
XLA Modules:
  0.0 296.4 jit_solution(17723843539924355625)
XLA Ops:
  2.0 8.7 %shard_map.46 = (f32[320,128]{1,0:T(8,128)S(1)}, f32[320,128]{1,0:T(8,128)S(1)}) custom-call(s32[3]{0:T(128)S(1)} %pad_add_fusion.3.pos_ref, bf16[12288,128]{1,0:T(8,128)(2,1)S(1)} %copy-done, bf16[640,12288]{1,0:T(8,128)(2,1)} %refs_0_.17, bf16[640,12288]{1,0:T(8,128)(2,1)} %refs_0_.17, bf16[640,12288]{1,0:T(8,128)(2,1)} %refs_0_.17, ...), custom_call_target="tpu_custom_call" | custom-call | flops 1 | bytes 1 | tf_op jit(solution)/shard_map/pallas_call | solution.py:204
  15.2 4.5 %collective-permute-done.1 = f32[320,128]{1,0:T(8,128)S(1)} collective-permute-done((f32[320,128]{1,0:T(8,128)S(1)}, f32[320,128]{1,0:T(8,128)S(1)}, u32[]{:S(2)}, u32[]{:S(2)}) %collective-permute-start.1) | collective-permute-done | bytes 163872 | tf_op jit(solution)/shard_map/ppermute | solution.py:25
  41.5 10.9 %collective-permute-done.5.refs_2_ = bf16[1024,128]{1,0:T(8,128)(2,1)S(1)} collective-permute-done((bf16[1024,128]{1,0:T(8,128)(2,1)S(1)}, bf16[1024,128]{1,0:T(8,128)(2,1)S(1)}, u32[]{:S(2)}, u32[]{:S(2)}) %collective-permute-start.5) | collective-permute-done | bytes 262176 | tf_op jit(solution)/shard_map/ppermute | solution.py:25
  52.9 5.0 %collective-permute-start.7 = (bf16[1024,128]{1,0:T(8,128)(2,1)S(1)}, bf16[1024,128]{1,0:T(8,128)(2,1)S(1)}, u32[]{:S(2)}, u32[]{:S(2)}) collective-permute-start(bf16[1024,128]{1,0:T(8,128)(2,1)S(1)} %get-tuple-element.76), channel_id=1, source_target_pairs={{0,8},{4,12},{8,0},{12,4},{16,24},{20,28},{24,16},{28,20},{1,9},{5... | collective-permute-start | bytes 786440 | tf_op jit(solution)/shard_map/ppermute | solution.py:25
  62.6 7.2 %collective-permute-done.7.refs_1_ = bf16[1024,128]{1,0:T(8,128)(2,1)S(1)} collective-permute-done((bf16[1024,128]{1,0:T(8,128)(2,1)S(1)}, bf16[1024,128]{1,0:T(8,128)(2,1)S(1)}, u32[]{:S(2)}, u32[]{:S(2)}) %collective-permute-start.7) | collective-permute-done | bytes 262176 | tf_op jit(solution)/shard_map/ppermute | solution.py:25
  69.8 9.5 %collective-permute-done.8.refs_2_ = bf16[1024,128]{1,0:T(8,128)(2,1)S(1)} collective-permute-done((bf16[1024,128]{1,0:T(8,128)(2,1)S(1)}, bf16[1024,128]{1,0:T(8,128)(2,1)S(1)}, u32[]{:S(2)}, u32[]{:S(2)}) %collective-permute-start.8) | collective-permute-done | bytes 262176 | tf_op jit(solution)/shard_map/ppermute | solution.py:25
  82.2 5.0 %collective-permute-start.14 = (bf16[1024,128]{1,0:T(8,128)(2,1)S(1)}, bf16[1024,128]{1,0:T(8,128)(2,1)S(1)}, u32[]{:S(2)}, u32[]{:S(2)}) collective-permute-start(bf16[1024,128]{1,0:T(8,128)(2,1)S(1)} %get-tuple-element.90.refs_5_), channel_id=1, source_target_pairs={{0,8},{4,12},{8,0},{12,4},{16,24},{20,28},{24,16},{28,20},{1,9},{5... | collective-permute-start | bytes 786440 | tf_op jit(solution)/shard_map/ppermute | solution.py:25
  93.9 9.6 %collective-permute-done.13.refs_8_ = bf16[1024,128]{1,0:T(8,128)(2,1)S(1)} collective-permute-done((bf16[1024,128]{1,0:T(8,128)(2,1)S(1)}, bf16[1024,128]{1,0:T(8,128)(2,1)S(1)}, u32[]{:S(2)}, u32[]{:S(2)}) %collective-permute-start.13) | collective-permute-done | bytes 262176 | tf_op jit(solution)/shard_map/ppermute | solution.py:25
  103.5 9.1 %collective-permute-done.12.refs_7_ = bf16[1024,128]{1,0:T(8,128)(2,1)S(1)} collective-permute-done((bf16[1024,128]{1,0:T(8,128)(2,1)S(1)}, bf16[1024,128]{1,0:T(8,128)(2,1)S(1)}, u32[]{:S(2)}, u32[]{:S(2)}) %collective-permute-start.12) | collective-permute-done | bytes 262176 | tf_op jit(solution)/shard_map/ppermute | solution.py:25
  118.3 4.9 %shard_map.56.refs_0_ = f32[768,128]{1,0:T(8,128)S(1)} custom-call(s32[3]{0:T(128)S(1)} %pad_add_fusion.3.pos_ref, bf16[16,128]{1,0:T(8,128)(2,1)S(1)} %collective-permute-done.11.refs_0_, bf16[640,12288]{1,0:T(8,128)(2,1)} %refs_0_.17, bf16[640,12288]{1,0:T(8,128)(2,1)} %refs_0_.17, bf16[640,12288]{1,0:T(8,128)(2,1)} %refs_0_.17, ...), custom_call_target="tpu_custom_call" | custom-call | flops 1 | bytes 1 | tf_op jit(solution)/shard_map/pallas_call | solution.py:266
  127.5 9.8 %collective-permute-done.17.refs_6_ = bf16[2,1024,128]{2,1,0:T(8,128)(2,1)S(1)} collective-permute-done((bf16[2,1024,128]{2,1,0:T(8,128)(2,1)S(1)}, bf16[2,1024,128]{2,1,0:T(8,128)(2,1)S(1)}, u32[]{:S(2)}, u32[]{:S(2)}) %collective-permute-start.17) | collective-permute-done | bytes 524320 | tf_op jit(solution)/shard_map/ppermute | solution.py:25
  137.3 4.9 %shard_map.57.refs_0_ = f32[768,128]{1,0:T(8,128)S(1)} custom-call(s32[3]{0:T(128)S(1)} %pad_add_fusion.3.pos_ref, f32[768,128]{1,0:T(8,128)S(1)} %shard_map.56.refs_0_, bf16[640,12288]{1,0:T(8,128)(2,1)} %refs_0_.17, bf16[640,12288]{1,0:T(8,128)(2,1)} %refs_0_.17, bf16[640,12288]{1,0:T(8,128)(2,1)} %refs_0_.17, bf16[640,12288]{1,0:T(8,128)(2,1)} %refs_0_.17, ...), custom_call_target="tpu_custom_call" | custom-call | flops 1 | bytes 1 | tf_op jit(solution)/shard_map/pallas_call | solution.py:266
  152.0 5.3 %collective-permute-done.22 = f32[384,128]{1,0:T(8,128)S(1)} collective-permute-done((f32[384,128]{1,0:T(8,128)S(1)}, f32[384,128]{1,0:T(8,128)S(1)}, u32[]{:S(2)}, u32[]{:S(2)}) %collective-permute-start.22) | collective-permute-done | bytes 196640 | tf_op jit(solution)/shard_map/ppermute | solution.py:25
  158.9 5.6 %shard_map.60.scores_ref = bf16[640,128]{1,0:T(8,128)(2,1)S(1)} custom-call(s32[8]{0:T(128)S(1)} %copy-done.1, s32[8]{0:T(128)S(1)} %copy-done.2, s32[3]{0:T(128)S(1)} %pad_add_fusion.3.pos_ref, f32[384,128]{1,0:T(8,128)S(1)} %add.37.mine_ref, f32[384,128]{1,0:T(8,128)S(1)} %collective-permute-done.23.other_ref), custom_call_target="tpu_custom_call" | custom-call | flops 1 | bytes 1 | tf_op jit(solution)/shard_map/pallas_call | solution.py:499
  184.3 10.2 %collective-permute-done.26.refs_2_ = s16[1040,128]{1,0:T(8,128)(2,1)S(1)} collective-permute-done((s16[1040,128]{1,0:T(8,128)(2,1)S(1)}, s16[1040,128]{1,0:T(8,128)(2,1)S(1)}, u32[]{:S(2)}, u32[]{:S(2)}) %collective-permute-start.26) | collective-permute-done | bytes 266272 | tf_op jit(solution)/shard_map/ppermute | solution.py:25
  196.8 4.9 %collective-permute-start.28 = (s16[1040,128]{1,0:T(8,128)(2,1)S(1)}, s16[1040,128]{1,0:T(8,128)(2,1)S(1)}, u32[]{:S(2)}, u32[]{:S(2)}) collective-permute-start(s16[1040,128]{1,0:T(8,128)(2,1)S(1)} %get-tuple-element.105), channel_id=1, source_target_pairs={{0,8},{4,12},{8,0},{12,4},{16,24},{20,28},{24,16},{28,20},{1,9},{5... | collective-permute-start | bytes 798728 | tf_op jit(solution)/shard_map/ppermute | solution.py:25
  205.6 4.6 %collective-permute-done.31.refs_1_ = s16[528,128]{1,0:T(8,128)(2,1)S(1)} collective-permute-done((s16[528,128]{1,0:T(8,128)(2,1)S(1)}, s16[528,128]{1,0:T(8,128)(2,1)S(1)}, u32[]{:S(2)}, u32[]{:S(2)}) %collective-permute-start.31) | collective-permute-done | bytes 135200 | tf_op jit(solution)/shard_map/ppermute | solution.py:25
  212.9 10.5 %collective-permute-done.29.refs_2_ = s16[1040,128]{1,0:T(8,128)(2,1)S(1)} collective-permute-done((s16[1040,128]{1,0:T(8,128)(2,1)S(1)}, s16[1040,128]{1,0:T(8,128)(2,1)S(1)}, u32[]{:S(2)}, u32[]{:S(2)}) %collective-permute-start.29) | collective-permute-done | bytes 266272 | tf_op jit(solution)/shard_map/ppermute | solution.py:25
  232.0 5.0 %collective-permute-start.35 = (s16[1040,128]{1,0:T(8,128)(2,1)S(1)}, s16[1040,128]{1,0:T(8,128)(2,1)S(1)}, u32[]{:S(2)}, u32[]{:S(2)}) collective-permute-start(s16[1040,128]{1,0:T(8,128)(2,1)S(1)} %get-tuple-element.122.refs_0_), channel_id=1, source_target_pairs={{0,8},{4,12},{8,0},{12,4},{16,24},{20,28},{24,16},{28,20},{1,9},{5... | collective-permute-start | bytes 798728 | tf_op jit(solution)/shard_map/ppermute | solution.py:25
  238.7 6.9 %collective-permute-done.35.refs_1_ = s16[1040,128]{1,0:T(8,128)(2,1)S(1)} collective-permute-done((s16[1040,128]{1,0:T(8,128)(2,1)S(1)}, s16[1040,128]{1,0:T(8,128)(2,1)S(1)}, u32[]{:S(2)}, u32[]{:S(2)}) %collective-permute-start.35) | collective-permute-done | bytes 266272 | tf_op jit(solution)/shard_map/ppermute | solution.py:25
  245.6 6.1 %collective-permute-done.34.refs_3_ = s16[1040,128]{1,0:T(8,128)(2,1)S(1)} collective-permute-done((s16[1040,128]{1,0:T(8,128)(2,1)S(1)}, s16[1040,128]{1,0:T(8,128)(2,1)S(1)}, u32[]{:S(2)}, u32[]{:S(2)}) %collective-permute-start.34) | collective-permute-done | bytes 266272 | tf_op jit(solution)/shard_map/ppermute | solution.py:25
  251.7 9.0 %collective-permute-done.33.refs_2_ = s16[1040,128]{1,0:T(8,128)(2,1)S(1)} collective-permute-done((s16[1040,128]{1,0:T(8,128)(2,1)S(1)}, s16[1040,128]{1,0:T(8,128)(2,1)S(1)}, u32[]{:S(2)}, u32[]{:S(2)}) %collective-permute-start.33) | collective-permute-done | bytes 266272 | tf_op jit(solution)/shard_map/ppermute | solution.py:25
  270.6 8.9 %collective-permute-done.40.refs_2_ = f32[128,128]{1,0:T(8,128)S(1)} collective-permute-done((f32[128,128]{1,0:T(8,128)S(1)}, f32[128,128]{1,0:T(8,128)S(1)}, u32[]{:S(2)}, u32[]{:S(2)}) %collective-permute-start.40) | collective-permute-done | bytes 65568 | tf_op jit(solution)/shard_map/ppermute | solution.py:25
  285.7 5.5 %shard_map.70.refs_0_ = f32[12288,128]{1,0:T(8,128)} custom-call(s32[3]{0:T(128)S(1)} %pad_add_fusion.3.pos_ref, f32[128,128]{1,0:T(8,128)S(1)} %shard_map.69.inverse_ref, s16[1040,128]{1,0:T(8,128)(2,1)S(1)} %get-tuple-element.122.refs_0_, s16[1040,128]{1,0:T(8,128)(2,1)S(1)} %collective-permute-done.35.refs_1_, ...), custom_call_target="tpu_custom_call" | custom-call | flops 1 | bytes 1 | tf_op jit(solution)/shard_map/pallas_call | solution.py:319
  (120 shorter events, 124.2 us)
Async XLA Ops:
  25.6 27.1 %collective-permute-start.3 = (bf16[4,1024,128]{2,1,0:T(8,128)(2,1)S(1)}, bf16[4,1024,128]{2,1,0:T(8,128)(2,1)S(1)}, u32[]{:S(2)}, u32[]{:S(2)}) collective-permute-start(bf16[4,1024,128]{2,1,0:T(8,128)(2,1)S(1)} %shard_map.48), channel_id=1, source_target_pairs={{0,4},{4,0},{8,12},{12,8},{16,20},{20,16},{24,28},{28,24},{1,5},{5... | collective-permute-start | bytes 3145736 | tf_op jit(solution)/shard_map/ppermute | solution.py:25
  31.0 21.4 %collective-permute-start.5 = (bf16[1024,128]{1,0:T(8,128)(2,1)S(1)}, bf16[1024,128]{1,0:T(8,128)(2,1)S(1)}, u32[]{:S(2)}, u32[]{:S(2)}) collective-permute-start(bf16[1024,128]{1,0:T(8,128)(2,1)S(1)} %get-tuple-element.70), channel_id=1, source_target_pairs={{0,16},{4,20},{8,24},{12,28},{16,0},{20,4},{24,8},{28,12},{1,17},{... | collective-permute-start | bytes 786440 | tf_op jit(solution)/shard_map/ppermute | solution.py:25
  33.7 18.8 %collective-permute-start.6 = (bf16[1024,128]{1,0:T(8,128)(2,1)S(1)}, bf16[1024,128]{1,0:T(8,128)(2,1)S(1)}, u32[]{:S(2)}, u32[]{:S(2)}) collective-permute-start(bf16[1024,128]{1,0:T(8,128)(2,1)S(1)} %get-tuple-element.71), channel_id=1, source_target_pairs={{0,24},{4,28},{8,16},{12,20},{16,8},{20,12},{24,0},{28,4},{1,25},{... | collective-permute-start | bytes 786440 | tf_op jit(solution)/shard_map/ppermute | solution.py:25
  35.0 17.6 %collective-permute-start.4 = (bf16[1024,128]{1,0:T(8,128)(2,1)S(1)}, bf16[1024,128]{1,0:T(8,128)(2,1)S(1)}, u32[]{:S(2)}, u32[]{:S(2)}) collective-permute-start(bf16[1024,128]{1,0:T(8,128)(2,1)S(1)} %get-tuple-element.69), channel_id=1, source_target_pairs={{0,8},{4,12},{8,0},{12,4},{16,24},{20,28},{24,16},{28,20},{1,9},{5... | collective-permute-start | bytes 786440 | tf_op jit(solution)/shard_map/ppermute | solution.py:25
  52.9 16.9 %collective-permute-start.7 = (bf16[1024,128]{1,0:T(8,128)(2,1)S(1)}, bf16[1024,128]{1,0:T(8,128)(2,1)S(1)}, u32[]{:S(2)}, u32[]{:S(2)}) collective-permute-start(bf16[1024,128]{1,0:T(8,128)(2,1)S(1)} %get-tuple-element.76), channel_id=1, source_target_pairs={{0,8},{4,12},{8,0},{12,4},{16,24},{20,28},{24,16},{28,20},{1,9},{5... | collective-permute-start | bytes 786440 | tf_op jit(solution)/shard_map/ppermute | solution.py:25
  57.9 21.3 %collective-permute-start.8 = (bf16[1024,128]{1,0:T(8,128)(2,1)S(1)}, bf16[1024,128]{1,0:T(8,128)(2,1)S(1)}, u32[]{:S(2)}, u32[]{:S(2)}) collective-permute-start(bf16[1024,128]{1,0:T(8,128)(2,1)S(1)} %get-tuple-element.77), channel_id=1, source_target_pairs={{0,16},{4,20},{8,24},{12,28},{16,0},{20,4},{24,8},{28,12},{1,17},{... | collective-permute-start | bytes 786440 | tf_op jit(solution)/shard_map/ppermute | solution.py:25
  59.9 19.3 %collective-permute-start.9 = (bf16[1024,128]{1,0:T(8,128)(2,1)S(1)}, bf16[1024,128]{1,0:T(8,128)(2,1)S(1)}, u32[]{:S(2)}, u32[]{:S(2)}) collective-permute-start(bf16[1024,128]{1,0:T(8,128)(2,1)S(1)} %get-tuple-element.78), channel_id=1, source_target_pairs={{0,24},{4,28},{8,16},{12,20},{16,8},{20,12},{24,0},{28,4},{1,25},{... | collective-permute-start | bytes 786440 | tf_op jit(solution)/shard_map/ppermute | solution.py:25
  62.0 18.6 %collective-permute-start.10 = (bf16[512,128]{1,0:T(8,128)(2,1)S(1)}, bf16[512,128]{1,0:T(8,128)(2,1)S(1)}, u32[]{:S(2)}, u32[]{:S(2)}) collective-permute-start(bf16[512,128]{1,0:T(8,128)(2,1)S(1)} %get-tuple-element.85), channel_id=1, source_target_pairs={{0,4},{4,0},{8,12},{12,8},{16,20},{20,16},{24,28},{28,24},{1,5},{5... | collective-permute-start | bytes 393224 | tf_op jit(solution)/shard_map/ppermute | solution.py:25
  87.2 16.3 %collective-permute-start.13 = (bf16[1024,128]{1,0:T(8,128)(2,1)S(1)}, bf16[1024,128]{1,0:T(8,128)(2,1)S(1)}, u32[]{:S(2)}, u32[]{:S(2)}) collective-permute-start(bf16[1024,128]{1,0:T(8,128)(2,1)S(1)} %get-tuple-element.90.refs_5_), channel_id=1, source_target_pairs={{0,24},{4,28},{8,16},{12,20},{16,8},{20,12},{24,0},{28,4},{1,25},{... | collective-permute-start | bytes 786440 | tf_op jit(solution)/shard_map/ppermute | solution.py:25
  90.6 21.9 %collective-permute-start.12 = (bf16[1024,128]{1,0:T(8,128)(2,1)S(1)}, bf16[1024,128]{1,0:T(8,128)(2,1)S(1)}, u32[]{:S(2)}, u32[]{:S(2)}) collective-permute-start(bf16[1024,128]{1,0:T(8,128)(2,1)S(1)} %get-tuple-element.90.refs_5_), channel_id=1, source_target_pairs={{0,16},{4,20},{8,24},{12,28},{16,0},{20,4},{24,8},{28,12},{1,17},{... | collective-permute-start | bytes 786440 | tf_op jit(solution)/shard_map/ppermute | solution.py:25
  114.3 23.0 %collective-permute-start.17 = (bf16[2,1024,128]{2,1,0:T(8,128)(2,1)S(1)}, bf16[2,1024,128]{2,1,0:T(8,128)(2,1)S(1)}, u32[]{:S(2)}, u32[]{:S(2)}) collective-permute-start(bf16[2,1024,128]{2,1,0:T(8,128)(2,1)S(1)} %pad_maximum_fusion.1), channel_id=1, source_target_pairs={{0,4},{4,0},{8,12},{12,8},{16,20},{20,16},{24,28},{28,24},{1,5},{5... | collective-permute-start | bytes 1572872 | tf_op jit(solution)/shard_map/ppermute | solution.py:25
  114.8 27.4 %collective-permute-start.18 = (bf16[2,512,128]{2,1,0:T(8,128)(2,1)S(1)}, bf16[2,512,128]{2,1,0:T(8,128)(2,1)S(1)}, u32[]{:S(2)}, u32[]{:S(2)}) collective-permute-start(bf16[2,512,128]{2,1,0:T(8,128)(2,1)S(1)} %pad_maximum_fusion.2), channel_id=1, source_target_pairs={{0,8},{4,12},{8,0},{12,4},{16,24},{20,28},{24,16},{28,20},{1,9},{5... | collective-permute-start | bytes 786440 | tf_op jit(solution)/shard_map/ppermute | solution.py:25
  114.8 30.7 %collective-permute-start.20 = (bf16[2,512,128]{2,1,0:T(8,128)(2,1)S(1)}, bf16[2,512,128]{2,1,0:T(8,128)(2,1)S(1)}, u32[]{:S(2)}, u32[]{:S(2)}) collective-permute-start(bf16[2,512,128]{2,1,0:T(8,128)(2,1)S(1)} %pad_maximum_fusion.2), channel_id=1, source_target_pairs={{0,24},{4,28},{8,16},{12,20},{16,8},{20,12},{24,0},{28,4},{1,25},{... | collective-permute-start | bytes 786440 | tf_op jit(solution)/shard_map/ppermute | solution.py:25
  117.5 28.0 %collective-permute-start.19 = (bf16[2,512,128]{2,1,0:T(8,128)(2,1)S(1)}, bf16[2,512,128]{2,1,0:T(8,128)(2,1)S(1)}, u32[]{:S(2)}, u32[]{:S(2)}) collective-permute-start(bf16[2,512,128]{2,1,0:T(8,128)(2,1)S(1)} %pad_maximum_fusion.2), channel_id=1, source_target_pairs={{0,16},{4,20},{8,24},{12,28},{16,0},{20,4},{24,8},{28,12},{1,17},{... | collective-permute-start | bytes 786440 | tf_op jit(solution)/shard_map/ppermute | solution.py:25
  168.6 27.2 %collective-permute-start.24 = (s16[4,1040,128]{2,1,0:T(8,128)(2,1)S(1)}, s16[4,1040,128]{2,1,0:T(8,128)(2,1)S(1)}, u32[]{:S(2)}, u32[]{:S(2)}) collective-permute-start(s16[4,1040,128]{2,1,0:T(8,128)(2,1)S(1)} %shard_map.61), channel_id=1, source_target_pairs={{0,4},{4,0},{8,12},{12,8},{16,20},{20,16},{24,28},{28,24},{1,5},{5... | collective-permute-start | bytes 3194888 | tf_op jit(solution)/shard_map/ppermute | solution.py:25
  174.2 20.3 %collective-permute-start.26 = (s16[1040,128]{1,0:T(8,128)(2,1)S(1)}, s16[1040,128]{1,0:T(8,128)(2,1)S(1)}, u32[]{:S(2)}, u32[]{:S(2)}) collective-permute-start(s16[1040,128]{1,0:T(8,128)(2,1)S(1)} %get-tuple-element.99), channel_id=1, source_target_pairs={{0,16},{4,20},{8,24},{12,28},{16,0},{20,4},{24,8},{28,12},{1,17},{... | collective-permute-start | bytes 798728 | tf_op jit(solution)/shard_map/ppermute | solution.py:25
  174.2 20.3 %collective-permute-start.27 = (s16[1040,128]{1,0:T(8,128)(2,1)S(1)}, s16[1040,128]{1,0:T(8,128)(2,1)S(1)}, u32[]{:S(2)}, u32[]{:S(2)}) collective-permute-start(s16[1040,128]{1,0:T(8,128)(2,1)S(1)} %get-tuple-element.100), channel_id=1, source_target_pairs={{0,24},{4,28},{8,16},{12,20},{16,8},{20,12},{24,0},{28,4},{1,25},{... | collective-permute-start | bytes 798728 | tf_op jit(solution)/shard_map/ppermute | solution.py:25
  176.6 19.2 %collective-permute-start.25 = (s16[1040,128]{1,0:T(8,128)(2,1)S(1)}, s16[1040,128]{1,0:T(8,128)(2,1)S(1)}, u32[]{:S(2)}, u32[]{:S(2)}) collective-permute-start(s16[1040,128]{1,0:T(8,128)(2,1)S(1)} %get-tuple-element.98), channel_id=1, source_target_pairs={{0,8},{4,12},{8,0},{12,4},{16,24},{20,28},{24,16},{28,20},{1,9},{5... | collective-permute-start | bytes 798728 | tf_op jit(solution)/shard_map/ppermute | solution.py:25
  201.7 21.6 %collective-permute-start.29 = (s16[1040,128]{1,0:T(8,128)(2,1)S(1)}, s16[1040,128]{1,0:T(8,128)(2,1)S(1)}, u32[]{:S(2)}, u32[]{:S(2)}) collective-permute-start(s16[1040,128]{1,0:T(8,128)(2,1)S(1)} %get-tuple-element.106), channel_id=1, source_target_pairs={{0,16},{4,20},{8,24},{12,28},{16,0},{20,4},{24,8},{28,12},{1,17},{... | collective-permute-start | bytes 798728 | tf_op jit(solution)/shard_map/ppermute | solution.py:25
  201.9 21.5 %collective-permute-start.30 = (s16[1040,128]{1,0:T(8,128)(2,1)S(1)}, s16[1040,128]{1,0:T(8,128)(2,1)S(1)}, u32[]{:S(2)}, u32[]{:S(2)}) collective-permute-start(s16[1040,128]{1,0:T(8,128)(2,1)S(1)} %get-tuple-element.107), channel_id=1, source_target_pairs={{0,24},{4,28},{8,16},{12,20},{16,8},{20,12},{24,0},{28,4},{1,25},{... | collective-permute-start | bytes 798728 | tf_op jit(solution)/shard_map/ppermute | solution.py:25
  238.6 22.1 %collective-permute-start.33 = (s16[1040,128]{1,0:T(8,128)(2,1)S(1)}, s16[1040,128]{1,0:T(8,128)(2,1)S(1)}, u32[]{:S(2)}, u32[]{:S(2)}) collective-permute-start(s16[1040,128]{1,0:T(8,128)(2,1)S(1)} %get-tuple-element.122.refs_0_), channel_id=1, source_target_pairs={{0,16},{4,20},{8,24},{12,28},{16,0},{20,4},{24,8},{28,12},{1,17},{... | collective-permute-start | bytes 798728 | tf_op jit(solution)/shard_map/ppermute | solution.py:25
  260.7 25.0 %collective-permute-start.42 = (s16[2,1040,128]{2,1,0:T(8,128)(2,1)S(1)}, s16[2,1040,128]{2,1,0:T(8,128)(2,1)S(1)}, u32[]{:S(2)}, u32[]{:S(2)}) collective-permute-start(s16[2,1040,128]{2,1,0:T(8,128)(2,1)S(1)} %pad_add_fusion), channel_id=1, source_target_pairs={{0,4},{4,0},{8,12},{12,8},{16,20},{20,16},{24,28},{28,24},{1,5},{5... | collective-permute-start | bytes 1597448 | tf_op jit(solution)/shard_map/ppermute | solution.py:25
  261.2 24.5 %collective-permute-start.43 = (s16[2,1040,128]{2,1,0:T(8,128)(2,1)S(1)}, s16[2,1040,128]{2,1,0:T(8,128)(2,1)S(1)}, u32[]{:S(2)}, u32[]{:S(2)}) collective-permute-start(s16[2,1040,128]{2,1,0:T(8,128)(2,1)S(1)} %pad_add_fusion.1), channel_id=1, source_target_pairs={{0,4},{4,0},{8,12},{12,8},{16,20},{20,16},{24,28},{28,24},{1,5},{5... | collective-permute-start | bytes 1597448 | tf_op jit(solution)/shard_map/ppermute | solution.py:25
  269.1 22.2 %collective-permute-start.46 = (s16[2,528,128]{2,1,0:T(8,128)(2,1)S(1)}, s16[2,528,128]{2,1,0:T(8,128)(2,1)S(1)}, u32[]{:S(2)}, u32[]{:S(2)}) collective-permute-start(s16[2,528,128]{2,1,0:T(8,128)(2,1)S(1)} %pad_add_fusion.2.refs_1_), channel_id=1, source_target_pairs={{0,24},{4,28},{8,16},{12,20},{16,8},{20,12},{24,0},{28,4},{1,25},{... | collective-permute-start | bytes 811016 | tf_op jit(solution)/shard_map/ppermute | solution.py:25
  (26 other events, 236.3 us)

commit v11 on v4

--- a/solution.py
+++ b/solution.py
@@ -16,7 +16,7 @@
 GROUP = 8
 LANES = 128
 VMEM_BYTES = 20 << 20
-VMEM_FIRST = 56 << 20
+VMEM_FIRST = 48 << 20
 LIGHT = pl.CostEstimate(flops=1, bytes_accessed=1, transcendentals=0)
 WHOLE = pl.BlockSpec(memory_space=pltpu.VMEM)
 
@@ -28,6 +28,7 @@
 class Plain:
     pad = 0
     dtype = BF16
+    limit = VMEM_FIRST
 
     @staticmethod
     def encode(value):
@@ -41,6 +42,7 @@
 class Fixed:
     pad = 16
     dtype = I16
+    limit = VMEM_BYTES
 
     @staticmethod
     def encode(value):
@@ -117,7 +119,7 @@
             + [pl.BlockSpec((time_rows, n), column(u)) for u in range(per_step)],
             out_specs=out_specs,
         ),
-        compiler_params=params(),
+        compiler_params=params(code.limit),
         cost_estimate=LIGHT,
     )(pos, scores, *([scans] * per_step))
 
@@ -425,7 +427,9 @@
             got_second = [swap(second[k - 1], mask=k * LOW) for k in ks[1:]]
             home = part(second[0], 0, ks, False, high // 2)
             (second_own,) = part(second[0], None, ks[:1], True, 1)
-            got_away, *got_second = lax.optimization_barrier((got_away, *got_second))
+            got_away, got_second, home, second_own = lax.optimization_barrier(
+                (got_away, got_second, home, second_own)
+            )
             piece = jax.ShapeDtypeStruct((layout.single + code.pad, rank), code.dtype)
             first = small_call(
                 functools.partial(add_pieces_kernel, code, high), [piece] * high, home, got_away

time: 279 us -> 273 us (0.978)
  waiting for transfers between devices: 121 us -> 115 us
  Pallas kernels: 57.2 us -> 62 us
  local copies, waits for them, and re-layouts: 11 us -> 7.37 us
    pallas_call x8, Pallas kernels: 15.9 us -> 22.2 us  [sketch_part(): pl.pallas_call(functools.partial(sketch_kernel, code, apart, per_step), o...]
    ppermute x52, waiting for transfers between devices: 121 us -> 115 us  [exchange(): return lax.ppermute(value, axis, [(i, i ^ mask) for i in range(size)])]
    unnamed x20 -> x10, local copies, waits for them, and re-layouts: 11 us -> 7.37 us
  transfers between devices with their start and end apart: 52 -> 52, of which waited for: 33 -> 32; matrix products, arithmetic and copies ran while one was open for 0% -> 0% of each run, Pallas kernels for 12% -> 14%
where the time goes in v11:
time: 273 us
  waiting for transfers between devices  115 us (42%)
  starting transfers between devices  87.4 us (32%)
  Pallas kernels  62 us (23%)
  local copies, waits for them, and re-layouts  7.37 us (3%)
    ppermute x52, waiting for transfers between devices, exchange(): return lax.ppermute(value, axis, [(i, i ^ mask) for i in range(size)])  115 us
    ppermute x52, starting transfers between devices, exchange(): return lax.ppermute(value, axis, [(i, i ^ mask) for i in range(size)])  87.4 us
    pallas_call x8, Pallas kernels, sketch_part(): pl.pallas_call(functools.partial(sketch_kernel, code, apart, per_step), o...  22.2 us
    pallas_call x8, Pallas kernels, small_call(): pl.pallas_call(kernel, out_shape=out_shape, in_specs=[WHOLE] * len(args),...  11.8 us
    pallas_call x2, Pallas kernels, finish(): pl.pallas_call(functools.partial(finish_kernel, layout, items, base is no...  9.12 us
    pallas_call x1, Pallas kernels, first_project(): pl.pallas_call(functools.partial(first_kernel, count), out_shape=[half, h...  8.72 us
    unnamed x10, local copies, waits for them, and re-layouts  7.37 us
    pallas_call x4, Pallas kernels, project(): pl.pallas_call(functools.partial(project_kernel, base is not None, split,...  6.92 us
  transfers between devices with their start and end apart: 52, of which 32 were waited for; matrix products, arithmetic and copies ran while one was open for 0% of the time, Pallas kernels for 14%

profile of v11, /device:TPU:0, one launch (start us, length us, event | category | flops | bytes accessed | tf_op | source)
XLA Modules:
  0.0 272.6 jit_solution(8275533332984319744)
XLA Ops:
  2.0 8.7 %shard_map.46 = (f32[320,128]{1,0:T(8,128)S(1)}, f32[320,128]{1,0:T(8,128)S(1)}) custom-call(s32[3]{0:T(128)S(1)} %pad_add_fusion.3.pos_ref, bf16[12288,128]{1,0:T(8,128)(2,1)S(1)} %copy-done.2, bf16[640,12288]{1,0:T(8,128)(2,1)} %refs_0_.19, bf16[640,12288]{1,0:T(8,128)(2,1)} %refs_0_.19, bf16[640,12288]{1,0:T(8,128)(2,1)} %refs_0_.19, ...), custom_call_target="tpu_custom_call" | custom-call | flops 1 | bytes 1 | tf_op jit(solution)/shard_map/pallas_call | solution.py:206
  15.2 4.5 %collective-permute-done.1 = f32[320,128]{1,0:T(8,128)S(1)} collective-permute-done((f32[320,128]{1,0:T(8,128)S(1)}, f32[320,128]{1,0:T(8,128)S(1)}, u32[]{:S(2)}, u32[]{:S(2)}) %collective-permute-start.1) | collective-permute-done | bytes 163872 | tf_op jit(solution)/shard_map/ppermute | solution.py:25
  21.8 3.8 %shard_map.48 = bf16[4,1024,128]{2,1,0:T(8,128)(2,1)S(1)} custom-call(s32[3]{0:T(128)S(1)} %pad_add_fusion.3.pos_ref, bf16[640,128]{1,0:T(8,128)(2,1)S(1)} %shard_map.47.scores_ref, bf16[640,12288]{1,0:T(8,128)(2,1)} %refs_0_.19, bf16[640,12288]{1,0:T(8,128)(2,1)} %refs_0_.19), custom_call_target="tpu_custom_call" | custom-call | flops 1 | bytes 1 | tf_op jit(solution)/shard_map/pallas_call | solution.py:112
  37.6 4.0 %shard_map.50.own_ref = bf16[4,1024,128]{2,1,0:T(8,128)(2,1)S(1)} custom-call(s32[3]{0:T(128)S(1)} %pad_add_fusion.3.pos_ref, bf16[640,128]{1,0:T(8,128)(2,1)S(1)} %shard_map.47.scores_ref, bf16[640,12288]{1,0:T(8,128)(2,1)} %refs_0_.19, bf16[640,12288]{1,0:T(8,128)(2,1)} %refs_0_.19), custom_call_target="tpu_custom_call" | custom-call | flops 1 | bytes 1 | tf_op jit(solution)/shard_map/pallas_call | solution.py:112
  41.5 10.9 %collective-permute-done.5.refs_2_ = bf16[1024,128]{1,0:T(8,128)(2,1)S(1)} collective-permute-done((bf16[1024,128]{1,0:T(8,128)(2,1)S(1)}, bf16[1024,128]{1,0:T(8,128)(2,1)S(1)}, u32[]{:S(2)}, u32[]{:S(2)}) %collective-permute-start.5) | collective-permute-done | bytes 262176 | tf_op jit(solution)/shard_map/ppermute | solution.py:25
  52.9 5.0 %collective-permute-start.7 = (bf16[1024,128]{1,0:T(8,128)(2,1)S(1)}, bf16[1024,128]{1,0:T(8,128)(2,1)S(1)}, u32[]{:S(2)}, u32[]{:S(2)}) collective-permute-start(bf16[1024,128]{1,0:T(8,128)(2,1)S(1)} %get-tuple-element.77), channel_id=1, source_target_pairs={{0,8},{4,12},{8,0},{12,4},{16,24},{20,28},{24,16},{28,20},{1,9},{5... | collective-permute-start | bytes 786440 | tf_op jit(solution)/shard_map/ppermute | solution.py:25
  62.6 4.5 %collective-permute-done.11.refs_1_ = bf16[512,128]{1,0:T(8,128)(2,1)S(1)} collective-permute-done((bf16[512,128]{1,0:T(8,128)(2,1)S(1)}, bf16[512,128]{1,0:T(8,128)(2,1)S(1)}, u32[]{:S(2)}, u32[]{:S(2)}) %collective-permute-start.11) | collective-permute-done | bytes 131104 | tf_op jit(solution)/shard_map/ppermute | solution.py:25
  69.8 9.5 %collective-permute-done.8.refs_2_ = bf16[1024,128]{1,0:T(8,128)(2,1)S(1)} collective-permute-done((bf16[1024,128]{1,0:T(8,128)(2,1)S(1)}, bf16[1024,128]{1,0:T(8,128)(2,1)S(1)}, u32[]{:S(2)}, u32[]{:S(2)}) %collective-permute-start.8) | collective-permute-done | bytes 262176 | tf_op jit(solution)/shard_map/ppermute | solution.py:25
  83.4 12.5 %collective-permute-start.14 = (bf16[1024,128]{1,0:T(8,128)(2,1)S(1)}, bf16[1024,128]{1,0:T(8,128)(2,1)S(1)}, u32[]{:S(2)}, u32[]{:S(2)}) collective-permute-start(bf16[1024,128]{1,0:T(8,128)(2,1)S(1)} %get-tuple-element.89.refs_4_), channel_id=1, source_target_pairs={{0,16},{4,20},{8,24},{12,28},{16,0},{20,4},{24,8},{28,12},{1,17},{... | collective-permute-start | bytes 786440 | tf_op jit(solution)/shard_map/ppermute | solution.py:25
  117.3 6.4 %collective-permute-start.25 = (bf16[2,512,128]{2,1,0:T(8,128)(2,1)S(1)}, bf16[2,512,128]{2,1,0:T(8,128)(2,1)S(1)}, u32[]{:S(2)}, u32[]{:S(2)}) collective-permute-start(bf16[2,512,128]{2,1,0:T(8,128)(2,1)S(1)} %pad_maximum_fusion.2), channel_id=1, source_target_pairs={{0,24},{4,28},{8,16},{12,20},{16,8},{20,12},{24,0},{28,4},{1,25},{... | collective-permute-start | bytes 786440 | tf_op jit(solution)/shard_map/ppermute | solution.py:25
  123.7 5.5 %copy-done = bf16[640,12288]{1,0:T(8,128)(2,1)S(1)} copy-done((bf16[640,12288]{1,0:T(8,128)(2,1)S(1)}, bf16[640,12288]{1,0:T(8,128)(2,1)}, u32[]{:S(2)}) %copy-start) | copy-done | bytes 15728664
  131.2 4.1 %shard_map.59.refs_0_ = f32[128,128]{1,0:T(8,128)S(1)} custom-call(f32[128,128]{1,0:T(8,128)S(1)} %add.51.refs_0_, f32[128,128]{1,0:T(8,128)S(1)} %collective-permute-done.21.refs_1_, f32[128,128]{1,0:T(8,128)S(1)} %collective-permute-done.22.refs_2_, f32[128,128]{1,0:T(8,128)S(1)} %collective-permute-done.23.refs_3_), custom_call_target="tpu_custom_call" | custom-call | flops 1 | bytes 1 | tf_op jit(solution)/shard_map/pallas_call | solution.py:128
  143.4 4.7 %collective-permute-done.27 = f32[320,128]{1,0:T(8,128)S(1)} collective-permute-done((f32[320,128]{1,0:T(8,128)S(1)}, f32[320,128]{1,0:T(8,128)S(1)}, u32[]{:S(2)}, u32[]{:S(2)}) %collective-permute-start.27) | collective-permute-done | bytes 163872 | tf_op jit(solution)/shard_map/ppermute | solution.py:25
  164.5 13.2 %collective-permute-done.31.refs_2_ = s16[1040,128]{1,0:T(8,128)(2,1)S(1)} collective-permute-done((s16[1040,128]{1,0:T(8,128)(2,1)S(1)}, s16[1040,128]{1,0:T(8,128)(2,1)S(1)}, u32[]{:S(2)}, u32[]{:S(2)}) %collective-permute-start.31) | collective-permute-done | bytes 266272 | tf_op jit(solution)/shard_map/ppermute | solution.py:25
  182.8 3.6 %collective-permute-start.33 = (s16[1040,128]{1,0:T(8,128)(2,1)S(1)}, s16[1040,128]{1,0:T(8,128)(2,1)S(1)}, u32[]{:S(2)}, u32[]{:S(2)}) collective-permute-start(s16[1040,128]{1,0:T(8,128)(2,1)S(1)} %get-tuple-element.109), channel_id=1, source_target_pairs={{0,8},{4,12},{8,0},{12,4},{16,24},{20,28},{24,16},{28,20},{1,9},{5... | collective-permute-start | bytes 798728 | tf_op jit(solution)/shard_map/ppermute | solution.py:25
  191.1 6.1 %collective-permute-done.33.refs_1_ = s16[1040,128]{1,0:T(8,128)(2,1)S(1)} collective-permute-done((s16[1040,128]{1,0:T(8,128)(2,1)S(1)}, s16[1040,128]{1,0:T(8,128)(2,1)S(1)}, u32[]{:S(2)}, u32[]{:S(2)}) %collective-permute-start.33) | collective-permute-done | bytes 266272 | tf_op jit(solution)/shard_map/ppermute | solution.py:25
  197.2 10.9 %collective-permute-done.34.refs_2_ = s16[1040,128]{1,0:T(8,128)(2,1)S(1)} collective-permute-done((s16[1040,128]{1,0:T(8,128)(2,1)S(1)}, s16[1040,128]{1,0:T(8,128)(2,1)S(1)}, u32[]{:S(2)}, u32[]{:S(2)}) %collective-permute-start.34) | collective-permute-done | bytes 266272 | tf_op jit(solution)/shard_map/ppermute | solution.py:25
  209.0 4.8 %collective-permute-start.40 = (s16[1040,128]{1,0:T(8,128)(2,1)S(1)}, s16[1040,128]{1,0:T(8,128)(2,1)S(1)}, u32[]{:S(2)}, u32[]{:S(2)}) collective-permute-start(s16[1040,128]{1,0:T(8,128)(2,1)S(1)} %get-tuple-element.124.refs_0_), channel_id=1, source_target_pairs={{0,8},{4,12},{8,0},{12,4},{16,24},{20,28},{24,16},{28,20},{1,9},{5... | collective-permute-start | bytes 798728 | tf_op jit(solution)/shard_map/ppermute | solution.py:25
  227.9 9.6 %collective-permute-done.36.refs_2_ = s16[1040,128]{1,0:T(8,128)(2,1)S(1)} collective-permute-done((s16[1040,128]{1,0:T(8,128)(2,1)S(1)}, s16[1040,128]{1,0:T(8,128)(2,1)S(1)}, u32[]{:S(2)}, u32[]{:S(2)}) %collective-permute-start.36) | collective-permute-done | bytes 266272 | tf_op jit(solution)/shard_map/ppermute | solution.py:25
  240.1 3.9 %collective-permute-start.44 = (f32[128,128]{1,0:T(8,128)S(1)}, f32[128,128]{1,0:T(8,128)S(1)}, u32[]{:S(2)}, u32[]{:S(2)}) collective-permute-start(f32[128,128]{1,0:T(8,128)S(1)} %add.57.refs_0_), channel_id=1, source_target_pairs={{0,8},{4,12},{8,0},{12,4},{16,24},{20,28},{24,16},{28,20},{1,9},{5... | collective-permute-start | bytes 196616 | tf_op jit(solution)/shard_map/ppermute | solution.py:25
  246.3 9.0 %collective-permute-done.45.refs_2_ = f32[128,128]{1,0:T(8,128)S(1)} collective-permute-done((f32[128,128]{1,0:T(8,128)S(1)}, f32[128,128]{1,0:T(8,128)S(1)}, u32[]{:S(2)}, u32[]{:S(2)}) %collective-permute-start.45) | collective-permute-done | bytes 65568 | tf_op jit(solution)/shard_map/ppermute | solution.py:25
  257.4 4.1 %shard_map.70.inverse_ref = f32[128,128]{1,0:T(8,128)S(1)} custom-call(f32[128,128]{1,0:T(8,128)S(1)} %add.57.refs_0_, f32[128,128]{1,0:T(8,128)S(1)} %collective-permute-done.44.refs_1_, f32[128,128]{1,0:T(8,128)S(1)} %collective-permute-done.45.refs_2_, f32[128,128]{1,0:T(8,128)S(1)} %collective-permute-done.46.refs_3_), custom_call_target="tpu_custom_call" | custom-call | flops 1 | bytes 1 | tf_op jit(solution)/shard_map/pallas_call | solution.py:128
  261.5 5.5 %shard_map.71.refs_0_ = f32[12288,128]{1,0:T(8,128)} custom-call(s32[3]{0:T(128)S(1)} %pad_add_fusion.3.pos_ref, f32[128,128]{1,0:T(8,128)S(1)} %shard_map.70.inverse_ref, s16[1040,128]{1,0:T(8,128)(2,1)S(1)} %get-tuple-element.124.refs_0_, s16[1040,128]{1,0:T(8,128)(2,1)S(1)} %collective-permute-done.40.refs_1_, ...), custom_call_target="tpu_custom_call" | custom-call | tf_op jit(solution)/shard_map/pallas_call | solution.py:310
  268.8 3.6 %shard_map.72 = f32[12288,128]{1,0:T(8,128)} custom-call(s32[3]{0:T(128)S(1)} %pad_add_fusion.3.pos_ref, f32[128,128]{1,0:T(8,128)S(1)} %shard_map.70.inverse_ref, f32[12288,128]{1,0:T(8,128)} %shard_map.71.refs_0_, s16[2,528,128]{2,1,0:T(8,128)(2,1)S(1)} %pad_add_fusion.2.refs_1_, ...), custom_call_target="tpu_custom_call", output_to_operand_aliasing={{}: (2, {})} | custom-call | tf_op jit(solution)/shard_map/pallas_call | solution.py:310
  (138 shorter events, 113.6 us)
Async XLA Ops:
  25.6 27.0 %collective-permute-start.3 = (bf16[4,1024,128]{2,1,0:T(8,128)(2,1)S(1)}, bf16[4,1024,128]{2,1,0:T(8,128)(2,1)S(1)}, u32[]{:S(2)}, u32[]{:S(2)}) collective-permute-start(bf16[4,1024,128]{2,1,0:T(8,128)(2,1)S(1)} %shard_map.48), channel_id=1, source_target_pairs={{0,4},{4,0},{8,12},{12,8},{16,20},{20,16},{24,28},{28,24},{1,5},{5... | collective-permute-start | bytes 3145736 | tf_op jit(solution)/shard_map/ppermute | solution.py:25
  31.0 21.4 %collective-permute-start.5 = (bf16[1024,128]{1,0:T(8,128)(2,1)S(1)}, bf16[1024,128]{1,0:T(8,128)(2,1)S(1)}, u32[]{:S(2)}, u32[]{:S(2)}) collective-permute-start(bf16[1024,128]{1,0:T(8,128)(2,1)S(1)} %get-tuple-element.71), channel_id=1, source_target_pairs={{0,16},{4,20},{8,24},{12,28},{16,0},{20,4},{24,8},{28,12},{1,17},{... | collective-permute-start | bytes 786440 | tf_op jit(solution)/shard_map/ppermute | solution.py:25
  33.6 18.8 %collective-permute-start.6 = (bf16[1024,128]{1,0:T(8,128)(2,1)S(1)}, bf16[1024,128]{1,0:T(8,128)(2,1)S(1)}, u32[]{:S(2)}, u32[]{:S(2)}) collective-permute-start(bf16[1024,128]{1,0:T(8,128)(2,1)S(1)} %get-tuple-element.72), channel_id=1, source_target_pairs={{0,24},{4,28},{8,16},{12,20},{16,8},{20,12},{24,0},{28,4},{1,25},{... | collective-permute-start | bytes 786440 | tf_op jit(solution)/shard_map/ppermute | solution.py:25
  35.0 17.6 %collective-permute-start.4 = (bf16[1024,128]{1,0:T(8,128)(2,1)S(1)}, bf16[1024,128]{1,0:T(8,128)(2,1)S(1)}, u32[]{:S(2)}, u32[]{:S(2)}) collective-permute-start(bf16[1024,128]{1,0:T(8,128)(2,1)S(1)} %get-tuple-element.70), channel_id=1, source_target_pairs={{0,8},{4,12},{8,0},{12,4},{16,24},{20,28},{24,16},{28,20},{1,9},{5... | collective-permute-start | bytes 786440 | tf_op jit(solution)/shard_map/ppermute | solution.py:25
  57.9 21.3 %collective-permute-start.8 = (bf16[1024,128]{1,0:T(8,128)(2,1)S(1)}, bf16[1024,128]{1,0:T(8,128)(2,1)S(1)}, u32[]{:S(2)}, u32[]{:S(2)}) collective-permute-start(bf16[1024,128]{1,0:T(8,128)(2,1)S(1)} %get-tuple-element.78), channel_id=1, source_target_pairs={{0,16},{4,20},{8,24},{12,28},{16,0},{20,4},{24,8},{28,12},{1,17},{... | collective-permute-start | bytes 786440 | tf_op jit(solution)/shard_map/ppermute | solution.py:25
  59.9 19.3 %collective-permute-start.9 = (bf16[1024,128]{1,0:T(8,128)(2,1)S(1)}, bf16[1024,128]{1,0:T(8,128)(2,1)S(1)}, u32[]{:S(2)}, u32[]{:S(2)}) collective-permute-start(bf16[1024,128]{1,0:T(8,128)(2,1)S(1)} %get-tuple-element.79), channel_id=1, source_target_pairs={{0,24},{4,28},{8,16},{12,20},{16,8},{20,12},{24,0},{28,4},{1,25},{... | collective-permute-start | bytes 786440 | tf_op jit(solution)/shard_map/ppermute | solution.py:25
  67.4 29.0 %collective-permute-start.16 = (bf16[512,128]{1,0:T(8,128)(2,1)S(1)}, bf16[512,128]{1,0:T(8,128)(2,1)S(1)}, u32[]{:S(2)}, u32[]{:S(2)}) collective-permute-start(bf16[512,128]{1,0:T(8,128)(2,1)S(1)} %get-tuple-element.91), channel_id=1, source_target_pairs={{0,4},{4,0},{8,12},{12,8},{16,20},{20,16},{24,28},{28,24},{1,5},{5... | collective-permute-start | bytes 393224 | tf_op jit(solution)/shard_map/ppermute | solution.py:25
  79.9 27.8 %collective-permute-start.15 = (bf16[1024,128]{1,0:T(8,128)(2,1)S(1)}, bf16[1024,128]{1,0:T(8,128)(2,1)S(1)}, u32[]{:S(2)}, u32[]{:S(2)}) collective-permute-start(bf16[1024,128]{1,0:T(8,128)(2,1)S(1)} %get-tuple-element.89.refs_4_), channel_id=1, source_target_pairs={{0,24},{4,28},{8,16},{12,20},{16,8},{20,12},{24,0},{28,4},{1,25},{... | collective-permute-start | bytes 786440 | tf_op jit(solution)/shard_map/ppermute | solution.py:25
  83.4 24.3 %collective-permute-start.14 = (bf16[1024,128]{1,0:T(8,128)(2,1)S(1)}, bf16[1024,128]{1,0:T(8,128)(2,1)S(1)}, u32[]{:S(2)}, u32[]{:S(2)}) collective-permute-start(bf16[1024,128]{1,0:T(8,128)(2,1)S(1)} %get-tuple-element.89.refs_4_), channel_id=1, source_target_pairs={{0,16},{4,20},{8,24},{12,28},{16,0},{20,4},{24,8},{28,12},{1,17},{... | collective-permute-start | bytes 786440 | tf_op jit(solution)/shard_map/ppermute | solution.py:25
  103.2 32.1 %collective-permute-start.18 = (bf16[2,1024,128]{2,1,0:T(8,128)(2,1)S(1)}, bf16[2,1024,128]{2,1,0:T(8,128)(2,1)S(1)}, u32[]{:S(2)}, u32[]{:S(2)}) collective-permute-start(bf16[2,1024,128]{2,1,0:T(8,128)(2,1)S(1)} %pad_maximum_fusion), channel_id=1, source_target_pairs={{0,4},{4,0},{8,12},{12,8},{16,20},{20,16},{24,28},{28,24},{1,5},{5... | collective-permute-start | bytes 1572872 | tf_op jit(solution)/shard_map/ppermute | solution.py:25
  107.8 27.6 %collective-permute-start.19 = (bf16[2,1024,128]{2,1,0:T(8,128)(2,1)S(1)}, bf16[2,1024,128]{2,1,0:T(8,128)(2,1)S(1)}, u32[]{:S(2)}, u32[]{:S(2)}) collective-permute-start(bf16[2,1024,128]{2,1,0:T(8,128)(2,1)S(1)} %pad_maximum_fusion.1), channel_id=1, source_target_pairs={{0,4},{4,0},{8,12},{12,8},{16,20},{20,16},{24,28},{28,24},{1,5},{5... | collective-permute-start | bytes 1572872 | tf_op jit(solution)/shard_map/ppermute | solution.py:25
  115.0 22.4 %collective-permute-start.20 = (bf16[2,512,128]{2,1,0:T(8,128)(2,1)S(1)}, bf16[2,512,128]{2,1,0:T(8,128)(2,1)S(1)}, u32[]{:S(2)}, u32[]{:S(2)}) collective-permute-start(bf16[2,512,128]{2,1,0:T(8,128)(2,1)S(1)} %pad_maximum_fusion.2), channel_id=1, source_target_pairs={{0,8},{4,12},{8,0},{12,4},{16,24},{20,28},{24,16},{28,20},{1,9},{5... | collective-permute-start | bytes 786440 | tf_op jit(solution)/shard_map/ppermute | solution.py:25
  117.3 21.5 %collective-permute-start.25 = (bf16[2,512,128]{2,1,0:T(8,128)(2,1)S(1)}, bf16[2,512,128]{2,1,0:T(8,128)(2,1)S(1)}, u32[]{:S(2)}, u32[]{:S(2)}) collective-permute-start(bf16[2,512,128]{2,1,0:T(8,128)(2,1)S(1)} %pad_maximum_fusion.2), channel_id=1, source_target_pairs={{0,24},{4,28},{8,16},{12,20},{16,8},{20,12},{24,0},{28,4},{1,25},{... | collective-permute-start | bytes 786440 | tf_op jit(solution)/shard_map/ppermute | solution.py:25
  153.6 25.6 %collective-permute-start.29 = (s16[4,1040,128]{2,1,0:T(8,128)(2,1)S(1)}, s16[4,1040,128]{2,1,0:T(8,128)(2,1)S(1)}, u32[]{:S(2)}, u32[]{:S(2)}) collective-permute-start(s16[4,1040,128]{2,1,0:T(8,128)(2,1)S(1)} %shard_map.62), channel_id=1, source_target_pairs={{0,4},{4,0},{8,12},{12,8},{16,20},{20,16},{24,28},{28,24},{1,5},{5... | collective-permute-start | bytes 3194888 | tf_op jit(solution)/shard_map/ppermute | solution.py:25
  157.0 20.7 %collective-permute-start.31 = (s16[1040,128]{1,0:T(8,128)(2,1)S(1)}, s16[1040,128]{1,0:T(8,128)(2,1)S(1)}, u32[]{:S(2)}, u32[]{:S(2)}) collective-permute-start(s16[1040,128]{1,0:T(8,128)(2,1)S(1)} %get-tuple-element.103), channel_id=1, source_target_pairs={{0,16},{4,20},{8,24},{12,28},{16,0},{20,4},{24,8},{28,12},{1,17},{... | collective-permute-start | bytes 798728 | tf_op jit(solution)/shard_map/ppermute | solution.py:25
  159.9 17.8 %collective-permute-start.32 = (s16[1040,128]{1,0:T(8,128)(2,1)S(1)}, s16[1040,128]{1,0:T(8,128)(2,1)S(1)}, u32[]{:S(2)}, u32[]{:S(2)}) collective-permute-start(s16[1040,128]{1,0:T(8,128)(2,1)S(1)} %get-tuple-element.104), channel_id=1, source_target_pairs={{0,24},{4,28},{8,16},{12,20},{16,8},{20,12},{24,0},{28,4},{1,25},{... | collective-permute-start | bytes 798728 | tf_op jit(solution)/shard_map/ppermute | solution.py:25
  159.9 19.2 %collective-permute-start.30 = (s16[1040,128]{1,0:T(8,128)(2,1)S(1)}, s16[1040,128]{1,0:T(8,128)(2,1)S(1)}, u32[]{:S(2)}, u32[]{:S(2)}) collective-permute-start(s16[1040,128]{1,0:T(8,128)(2,1)S(1)} %get-tuple-element.102), channel_id=1, source_target_pairs={{0,8},{4,12},{8,0},{12,4},{16,24},{20,28},{24,16},{28,20},{1,9},{5... | collective-permute-start | bytes 798728 | tf_op jit(solution)/shard_map/ppermute | solution.py:25
  186.5 21.6 %collective-permute-start.34 = (s16[1040,128]{1,0:T(8,128)(2,1)S(1)}, s16[1040,128]{1,0:T(8,128)(2,1)S(1)}, u32[]{:S(2)}, u32[]{:S(2)}) collective-permute-start(s16[1040,128]{1,0:T(8,128)(2,1)S(1)} %get-tuple-element.110), channel_id=1, source_target_pairs={{0,16},{4,20},{8,24},{12,28},{16,0},{20,4},{24,8},{28,12},{1,17},{... | collective-permute-start | bytes 798728 | tf_op jit(solution)/shard_map/ppermute | solution.py:25
  187.7 20.4 %collective-permute-start.35 = (s16[1040,128]{1,0:T(8,128)(2,1)S(1)}, s16[1040,128]{1,0:T(8,128)(2,1)S(1)}, u32[]{:S(2)}, u32[]{:S(2)}) collective-permute-start(s16[1040,128]{1,0:T(8,128)(2,1)S(1)} %get-tuple-element.111), channel_id=1, source_target_pairs={{0,24},{4,28},{8,16},{12,20},{16,8},{20,12},{24,0},{28,4},{1,25},{... | collective-permute-start | bytes 798728 | tf_op jit(solution)/shard_map/ppermute | solution.py:25
  189.5 25.9 %collective-permute-start.39 = (s16[528,128]{1,0:T(8,128)(2,1)S(1)}, s16[528,128]{1,0:T(8,128)(2,1)S(1)}, u32[]{:S(2)}, u32[]{:S(2)}) collective-permute-start(s16[528,128]{1,0:T(8,128)(2,1)S(1)} %get-tuple-element.119), channel_id=1, source_target_pairs={{0,4},{4,0},{8,12},{12,8},{16,20},{20,16},{24,28},{28,24},{1,5},{5... | collective-permute-start | bytes 405512 | tf_op jit(solution)/shard_map/ppermute | solution.py:25
  215.4 22.1 %collective-permute-start.36 = (s16[1040,128]{1,0:T(8,128)(2,1)S(1)}, s16[1040,128]{1,0:T(8,128)(2,1)S(1)}, u32[]{:S(2)}, u32[]{:S(2)}) collective-permute-start(s16[1040,128]{1,0:T(8,128)(2,1)S(1)} %get-tuple-element.124.refs_0_), channel_id=1, source_target_pairs={{0,16},{4,20},{8,24},{12,28},{16,0},{20,4},{24,8},{28,12},{1,17},{... | collective-permute-start | bytes 798728 | tf_op jit(solution)/shard_map/ppermute | solution.py:25
  224.0 37.5 %collective-permute-start.47 = (s16[2,1040,128]{2,1,0:T(8,128)(2,1)S(1)}, s16[2,1040,128]{2,1,0:T(8,128)(2,1)S(1)}, u32[]{:S(2)}, u32[]{:S(2)}) collective-permute-start(s16[2,1040,128]{2,1,0:T(8,128)(2,1)S(1)} %pad_add_fusion), channel_id=1, source_target_pairs={{0,4},{4,0},{8,12},{12,8},{16,20},{20,16},{24,28},{28,24},{1,5},{5... | collective-permute-start | bytes 1597448 | tf_op jit(solution)/shard_map/ppermute | solution.py:25
  237.6 23.9 %collective-permute-start.48 = (s16[2,1040,128]{2,1,0:T(8,128)(2,1)S(1)}, s16[2,1040,128]{2,1,0:T(8,128)(2,1)S(1)}, u32[]{:S(2)}, u32[]{:S(2)}) collective-permute-start(s16[2,1040,128]{2,1,0:T(8,128)(2,1)S(1)} %pad_add_fusion.1), channel_id=1, source_target_pairs={{0,4},{4,0},{8,12},{12,8},{16,20},{20,16},{24,28},{28,24},{1,5},{5... | collective-permute-start | bytes 1597448 | tf_op jit(solution)/shard_map/ppermute | solution.py:25
  245.8 21.2 %collective-permute-start.51 = (s16[2,528,128]{2,1,0:T(8,128)(2,1)S(1)}, s16[2,528,128]{2,1,0:T(8,128)(2,1)S(1)}, u32[]{:S(2)}, u32[]{:S(2)}) collective-permute-start(s16[2,528,128]{2,1,0:T(8,128)(2,1)S(1)} %pad_add_fusion.2.refs_1_), channel_id=1, source_target_pairs={{0,24},{4,28},{8,16},{12,20},{16,8},{20,12},{24,0},{28,4},{1,25},{... | collective-permute-start | bytes 811016 | tf_op jit(solution)/shard_map/ppermute | solution.py:25
  (33 other events, 275.7 us)

commit v12 on v11

--- a/solution.py
+++ b/solution.py
@@ -461,16 +461,18 @@
                 gram = gram + swap_vox(gram, mask=mask)
                 mask *= 2
             near_in, gram = lax.optimization_barrier((near_in, gram))
+            gram = gram + swap(gram, mask=1)
+            grams = [gram] + [swap(gram, mask=k * LOW) for k in ks[1:]]
+            far_in, near_in, pair, grams = lax.optimization_barrier(
+                (far_in, near_in, pair, grams)
+            )
             low_near = swap(jnp.stack(near_in), mask=1)
-            gram = gram + swap(gram, mask=1)
-            far_in, pair, gram = lax.optimization_barrier((far_in, pair, gram))
             low_far = swap(jnp.stack(far_in), mask=1)
             seconds = [pair] + [swap(pair, mask=k * LOW) for k in ks[1:]]
-            gram = [gram] + [swap(gram, mask=k * LOW) for k in ks[1:]]
             early = [(0, [k], array) for k, array in zip(near + far, near_in + far_in)]
             late = [(1, near, low_near), (1, far, low_far)]
             pairs = [(None, [k], array) for k, array in zip(ks, seconds)]
-            return early, late, pairs, gram
+            return early, late, pairs, grams
 
         def sum_scores(mine, send, *factor):
             mine = mine + swap_vox(send, mask=1)

time: 273 us -> 287 us (1.051)
  waiting for transfers between devices: 115 us -> 143 us
  starting transfers between devices: 87.4 us -> 73.2 us
    ppermute x52, waiting for transfers between devices: 115 us -> 143 us  [exchange(): return lax.ppermute(value, axis, [(i, i ^ mask) for i in range(size)])]
    ppermute x52, starting transfers between devices: 87.4 us -> 73.2 us  [exchange(): return lax.ppermute(value, axis, [(i, i ^ mask) for i in range(size)])]
  transfers between devices with their start and end apart: 52 -> 52, of which waited for: 32 -> 27; matrix products, arithmetic and copies ran while one was open for 0% -> 0% of each run, Pallas kernels for 14% -> 13%
where the time goes in v12:
time: 287 us
  waiting for transfers between devices  143 us (50%)
  starting transfers between devices  73.2 us (26%)
  Pallas kernels  62 us (22%)
  local copies, waits for them, and re-layouts  7.37 us (3%)
    ppermute x52, waiting for transfers between devices, exchange(): return lax.ppermute(value, axis, [(i, i ^ mask) for i in range(size)])  143 us
    ppermute x52, starting transfers between devices, exchange(): return lax.ppermute(value, axis, [(i, i ^ mask) for i in range(size)])  73.2 us
    pallas_call x8, Pallas kernels, sketch_part(): pl.pallas_call(functools.partial(sketch_kernel, code, apart, per_step), o...  22.2 us
    pallas_call x8, Pallas kernels, small_call(): pl.pallas_call(kernel, out_shape=out_shape, in_specs=[WHOLE] * len(args),...  11.8 us
    pallas_call x2, Pallas kernels, finish(): pl.pallas_call(functools.partial(finish_kernel, layout, items, base is no...  9.12 us
    pallas_call x1, Pallas kernels, first_project(): pl.pallas_call(functools.partial(first_kernel, count), out_shape=[half, h...  8.72 us
    unnamed x10, local copies, waits for them, and re-layouts  7.37 us
    pallas_call x4, Pallas kernels, project(): pl.pallas_call(functools.partial(project_kernel, base is not None, split,...  6.91 us
  transfers between devices with their start and end apart: 52, of which 27 were waited for; matrix products, arithmetic and copies ran while one was open for 0% of the time, Pallas kernels for 13%

profile of v12, /device:TPU:0, one launch (start us, length us, event | category | flops | bytes accessed | tf_op | source)
XLA Modules:
  0.0 286.9 jit_solution(8688600138156886398)
XLA Ops:
  2.0 8.7 %shard_map.46 = (f32[320,128]{1,0:T(8,128)S(1)}, f32[320,128]{1,0:T(8,128)S(1)}) custom-call(s32[3]{0:T(128)S(1)} %pad_add_fusion.3.pos_ref, bf16[12288,128]{1,0:T(8,128)(2,1)S(1)} %copy-done.2, bf16[640,12288]{1,0:T(8,128)(2,1)} %refs_0_.19, bf16[640,12288]{1,0:T(8,128)(2,1)} %refs_0_.19, bf16[640,12288]{1,0:T(8,128)(2,1)} %refs_0_.19, ...), custom_call_target="tpu_custom_call" | custom-call | flops 1 | bytes 1 | tf_op jit(solution)/shard_map/pallas_call | solution.py:206
  15.2 4.5 %collective-permute-done.1 = f32[320,128]{1,0:T(8,128)S(1)} collective-permute-done((f32[320,128]{1,0:T(8,128)S(1)}, f32[320,128]{1,0:T(8,128)S(1)}, u32[]{:S(2)}, u32[]{:S(2)}) %collective-permute-start.1) | collective-permute-done | bytes 163872 | tf_op jit(solution)/shard_map/ppermute | solution.py:25
  21.8 3.8 %shard_map.48 = bf16[4,1024,128]{2,1,0:T(8,128)(2,1)S(1)} custom-call(s32[3]{0:T(128)S(1)} %pad_add_fusion.3.pos_ref, bf16[640,128]{1,0:T(8,128)(2,1)S(1)} %shard_map.47.scores_ref, bf16[640,12288]{1,0:T(8,128)(2,1)} %refs_0_.19, bf16[640,12288]{1,0:T(8,128)(2,1)} %refs_0_.19), custom_call_target="tpu_custom_call" | custom-call | flops 1 | bytes 1 | tf_op jit(solution)/shard_map/pallas_call | solution.py:112
  37.6 4.0 %shard_map.50.own_ref = bf16[4,1024,128]{2,1,0:T(8,128)(2,1)S(1)} custom-call(s32[3]{0:T(128)S(1)} %pad_add_fusion.3.pos_ref, bf16[640,128]{1,0:T(8,128)(2,1)S(1)} %shard_map.47.scores_ref, bf16[640,12288]{1,0:T(8,128)(2,1)} %refs_0_.19, bf16[640,12288]{1,0:T(8,128)(2,1)} %refs_0_.19), custom_call_target="tpu_custom_call" | custom-call | flops 1 | bytes 1 | tf_op jit(solution)/shard_map/pallas_call | solution.py:112
  41.5 10.9 %collective-permute-done.5.refs_2_ = bf16[1024,128]{1,0:T(8,128)(2,1)S(1)} collective-permute-done((bf16[1024,128]{1,0:T(8,128)(2,1)S(1)}, bf16[1024,128]{1,0:T(8,128)(2,1)S(1)}, u32[]{:S(2)}, u32[]{:S(2)}) %collective-permute-start.5) | collective-permute-done | bytes 262176 | tf_op jit(solution)/shard_map/ppermute | solution.py:25
  52.9 5.0 %collective-permute-start.7 = (bf16[1024,128]{1,0:T(8,128)(2,1)S(1)}, bf16[1024,128]{1,0:T(8,128)(2,1)S(1)}, u32[]{:S(2)}, u32[]{:S(2)}) collective-permute-start(bf16[1024,128]{1,0:T(8,128)(2,1)S(1)} %get-tuple-element.87), channel_id=1, source_target_pairs={{0,8},{4,12},{8,0},{12,4},{16,24},{20,28},{24,16},{28,20},{1,9},{5... | collective-permute-start | bytes 786440 | tf_op jit(solution)/shard_map/ppermute | solution.py:25
  62.6 7.2 %collective-permute-done.7.refs_1_ = bf16[1024,128]{1,0:T(8,128)(2,1)S(1)} collective-permute-done((bf16[1024,128]{1,0:T(8,128)(2,1)S(1)}, bf16[1024,128]{1,0:T(8,128)(2,1)S(1)}, u32[]{:S(2)}, u32[]{:S(2)}) %collective-permute-start.7) | collective-permute-done | bytes 262176 | tf_op jit(solution)/shard_map/ppermute | solution.py:25
  69.8 9.5 %collective-permute-done.8.refs_2_ = bf16[1024,128]{1,0:T(8,128)(2,1)S(1)} collective-permute-done((bf16[1024,128]{1,0:T(8,128)(2,1)S(1)}, bf16[1024,128]{1,0:T(8,128)(2,1)S(1)}, u32[]{:S(2)}, u32[]{:S(2)}) %collective-permute-start.8) | collective-permute-done | bytes 262176 | tf_op jit(solution)/shard_map/ppermute | solution.py:25
  79.9 5.0 %collective-permute-start.12 = (bf16[1024,128]{1,0:T(8,128)(2,1)S(1)}, bf16[1024,128]{1,0:T(8,128)(2,1)S(1)}, u32[]{:S(2)}, u32[]{:S(2)}) collective-permute-start(bf16[1024,128]{1,0:T(8,128)(2,1)S(1)} %get-tuple-element.103.refs_4_), channel_id=1, source_target_pairs={{0,8},{4,12},{8,0},{12,4},{16,24},{20,28},{24,16},{28,20},{1,9},{5... | collective-permute-start | bytes 786440 | tf_op jit(solution)/shard_map/ppermute | solution.py:25
  100.5 16.5 %collective-permute-done.10.refs_6_ = bf16[1024,128]{1,0:T(8,128)(2,1)S(1)} collective-permute-done((bf16[1024,128]{1,0:T(8,128)(2,1)S(1)}, bf16[1024,128]{1,0:T(8,128)(2,1)S(1)}, u32[]{:S(2)}, u32[]{:S(2)}) %collective-permute-start.10) | collective-permute-done | bytes 262176 | tf_op jit(solution)/shard_map/ppermute | solution.py:25
  124.8 5.5 %copy-done = bf16[640,12288]{1,0:T(8,128)(2,1)S(1)} copy-done((bf16[640,12288]{1,0:T(8,128)(2,1)S(1)}, bf16[640,12288]{1,0:T(8,128)(2,1)}, u32[]{:S(2)}) %copy-start) | copy-done | bytes 15728664
  132.3 4.1 %shard_map.59.refs_0_ = f32[128,128]{1,0:T(8,128)S(1)} custom-call(f32[128,128]{1,0:T(8,128)S(1)} %add.51.refs_0_, f32[128,128]{1,0:T(8,128)S(1)} %collective-permute-done.18.refs_1_, f32[128,128]{1,0:T(8,128)S(1)} %collective-permute-done.19.refs_2_, f32[128,128]{1,0:T(8,128)S(1)} %collective-permute-done.20.refs_3_), custom_call_target="tpu_custom_call" | custom-call | flops 1 | bytes 1 | tf_op jit(solution)/shard_map/pallas_call | solution.py:128
  136.4 6.8 %collective-permute-done.22.refs_6_ = bf16[2,1024,128]{2,1,0:T(8,128)(2,1)S(1)} collective-permute-done((bf16[2,1024,128]{2,1,0:T(8,128)(2,1)S(1)}, bf16[2,1024,128]{2,1,0:T(8,128)(2,1)S(1)}, u32[]{:S(2)}, u32[]{:S(2)}) %collective-permute-start.22) | collective-permute-done | bytes 524320 | tf_op jit(solution)/shard_map/ppermute | solution.py:25
  150.3 5.7 %collective-permute-done.27 = f32[320,128]{1,0:T(8,128)S(1)} collective-permute-done((f32[320,128]{1,0:T(8,128)S(1)}, f32[320,128]{1,0:T(8,128)S(1)}, u32[]{:S(2)}, u32[]{:S(2)}) %collective-permute-start.27) | collective-permute-done | bytes 163872 | tf_op jit(solution)/shard_map/ppermute | solution.py:25
  171.6 12.9 %collective-permute-done.31.refs_2_ = s16[1040,128]{1,0:T(8,128)(2,1)S(1)} collective-permute-done((s16[1040,128]{1,0:T(8,128)(2,1)S(1)}, s16[1040,128]{1,0:T(8,128)(2,1)S(1)}, u32[]{:S(2)}, u32[]{:S(2)}) %collective-permute-start.31) | collective-permute-done | bytes 266272 | tf_op jit(solution)/shard_map/ppermute | solution.py:25
  188.0 3.7 %collective-permute-start.33 = (s16[1040,128]{1,0:T(8,128)(2,1)S(1)}, s16[1040,128]{1,0:T(8,128)(2,1)S(1)}, u32[]{:S(2)}, u32[]{:S(2)}) collective-permute-start(s16[1040,128]{1,0:T(8,128)(2,1)S(1)} %get-tuple-element.124), channel_id=1, source_target_pairs={{0,8},{4,12},{8,0},{12,4},{16,24},{20,28},{24,16},{28,20},{1,9},{5... | collective-permute-start | bytes 798728 | tf_op jit(solution)/shard_map/ppermute | solution.py:25
  196.3 6.5 %collective-permute-done.33.refs_1_ = s16[1040,128]{1,0:T(8,128)(2,1)S(1)} collective-permute-done((s16[1040,128]{1,0:T(8,128)(2,1)S(1)}, s16[1040,128]{1,0:T(8,128)(2,1)S(1)}, u32[]{:S(2)}, u32[]{:S(2)}) %collective-permute-start.33) | collective-permute-done | bytes 266272 | tf_op jit(solution)/shard_map/ppermute | solution.py:25
  202.9 10.5 %collective-permute-done.34.refs_2_ = s16[1040,128]{1,0:T(8,128)(2,1)S(1)} collective-permute-done((s16[1040,128]{1,0:T(8,128)(2,1)S(1)}, s16[1040,128]{1,0:T(8,128)(2,1)S(1)}, u32[]{:S(2)}, u32[]{:S(2)}) %collective-permute-start.34) | collective-permute-done | bytes 266272 | tf_op jit(solution)/shard_map/ppermute | solution.py:25
  214.2 5.1 %collective-permute-start.38 = (s16[1040,128]{1,0:T(8,128)(2,1)S(1)}, s16[1040,128]{1,0:T(8,128)(2,1)S(1)}, u32[]{:S(2)}, u32[]{:S(2)}) collective-permute-start(s16[1040,128]{1,0:T(8,128)(2,1)S(1)} %get-tuple-element.144.refs_0_), channel_id=1, source_target_pairs={{0,8},{4,12},{8,0},{12,4},{16,24},{20,28},{24,16},{28,20},{1,9},{5... | collective-permute-start | bytes 798728 | tf_op jit(solution)/shard_map/ppermute | solution.py:25
  235.5 16.1 %collective-permute-done.36.refs_2_ = s16[1040,128]{1,0:T(8,128)(2,1)S(1)} collective-permute-done((s16[1040,128]{1,0:T(8,128)(2,1)S(1)}, s16[1040,128]{1,0:T(8,128)(2,1)S(1)}, u32[]{:S(2)}, u32[]{:S(2)}) %collective-permute-start.36) | collective-permute-done | bytes 266272 | tf_op jit(solution)/shard_map/ppermute | solution.py:25
  259.9 4.1 %shard_map.70.inverse_ref = f32[128,128]{1,0:T(8,128)S(1)} custom-call(f32[128,128]{1,0:T(8,128)S(1)} %add.57.refs_0_, f32[128,128]{1,0:T(8,128)S(1)} %collective-permute-done.44.refs_1_, f32[128,128]{1,0:T(8,128)S(1)} %collective-permute-done.45.refs_2_, f32[128,128]{1,0:T(8,128)S(1)} %collective-permute-done.46.refs_3_), custom_call_target="tpu_custom_call" | custom-call | flops 1 | bytes 1 | tf_op jit(solution)/shard_map/pallas_call | solution.py:128
  264.0 4.4 %collective-permute-done.47.refs_4_ = s16[2,1040,128]{2,1,0:T(8,128)(2,1)S(1)} collective-permute-done((s16[2,1040,128]{2,1,0:T(8,128)(2,1)S(1)}, s16[2,1040,128]{2,1,0:T(8,128)(2,1)S(1)}, u32[]{:S(2)}, u32[]{:S(2)}) %collective-permute-start.47) | collective-permute-done | bytes 532512 | tf_op jit(solution)/shard_map/ppermute | solution.py:25
  268.4 9.1 %collective-permute-done.48.refs_5_ = s16[2,1040,128]{2,1,0:T(8,128)(2,1)S(1)} collective-permute-done((s16[2,1040,128]{2,1,0:T(8,128)(2,1)S(1)}, s16[2,1040,128]{2,1,0:T(8,128)(2,1)S(1)}, u32[]{:S(2)}, u32[]{:S(2)}) %collective-permute-start.48) | collective-permute-done | bytes 532512 | tf_op jit(solution)/shard_map/ppermute | solution.py:25
  277.5 5.5 %shard_map.71.refs_0_ = f32[12288,128]{1,0:T(8,128)} custom-call(s32[3]{0:T(128)S(1)} %pad_add_fusion.3.pos_ref, f32[128,128]{1,0:T(8,128)S(1)} %shard_map.70.inverse_ref, s16[1040,128]{1,0:T(8,128)(2,1)S(1)} %get-tuple-element.144.refs_0_, s16[1040,128]{1,0:T(8,128)(2,1)S(1)} %collective-permute-done.38.refs_1_, ...), custom_call_target="tpu_custom_call" | custom-call | tf_op jit(solution)/shard_map/pallas_call | solution.py:310
  (138 shorter events, 111.2 us)
Async XLA Ops:
  25.6 27.0 %collective-permute-start.3 = (bf16[4,1024,128]{2,1,0:T(8,128)(2,1)S(1)}, bf16[4,1024,128]{2,1,0:T(8,128)(2,1)S(1)}, u32[]{:S(2)}, u32[]{:S(2)}) collective-permute-start(bf16[4,1024,128]{2,1,0:T(8,128)(2,1)S(1)} %shard_map.48), channel_id=1, source_target_pairs={{0,4},{4,0},{8,12},{12,8},{16,20},{20,16},{24,28},{28,24},{1,5},{5... | collective-permute-start | bytes 3145736 | tf_op jit(solution)/shard_map/ppermute | solution.py:25
  31.0 21.4 %collective-permute-start.5 = (bf16[1024,128]{1,0:T(8,128)(2,1)S(1)}, bf16[1024,128]{1,0:T(8,128)(2,1)S(1)}, u32[]{:S(2)}, u32[]{:S(2)}) collective-permute-start(bf16[1024,128]{1,0:T(8,128)(2,1)S(1)} %get-tuple-element.81), channel_id=1, source_target_pairs={{0,16},{4,20},{8,24},{12,28},{16,0},{20,4},{24,8},{28,12},{1,17},{... | collective-permute-start | bytes 786440 | tf_op jit(solution)/shard_map/ppermute | solution.py:25
  57.9 21.3 %collective-permute-start.8 = (bf16[1024,128]{1,0:T(8,128)(2,1)S(1)}, bf16[1024,128]{1,0:T(8,128)(2,1)S(1)}, u32[]{:S(2)}, u32[]{:S(2)}) collective-permute-start(bf16[1024,128]{1,0:T(8,128)(2,1)S(1)} %get-tuple-element.88), channel_id=1, source_target_pairs={{0,16},{4,20},{8,24},{12,28},{16,0},{20,4},{24,8},{28,12},{1,17},{... | collective-permute-start | bytes 786440 | tf_op jit(solution)/shard_map/ppermute | solution.py:25
  62.0 23.0 %collective-permute-start.13 = (bf16[512,128]{1,0:T(8,128)(2,1)S(1)}, bf16[512,128]{1,0:T(8,128)(2,1)S(1)}, u32[]{:S(2)}, u32[]{:S(2)}) collective-permute-start(bf16[512,128]{1,0:T(8,128)(2,1)S(1)} %get-tuple-element.97), channel_id=1, source_target_pairs={{0,4},{4,0},{8,12},{12,8},{16,20},{20,16},{24,28},{28,24},{1,5},{5... | collective-permute-start | bytes 393224 | tf_op jit(solution)/shard_map/ppermute | solution.py:25
  91.7 25.4 %collective-permute-start.10 = (bf16[1024,128]{1,0:T(8,128)(2,1)S(1)}, bf16[1024,128]{1,0:T(8,128)(2,1)S(1)}, u32[]{:S(2)}, u32[]{:S(2)}) collective-permute-start(bf16[1024,128]{1,0:T(8,128)(2,1)S(1)} %get-tuple-element.103.refs_4_), channel_id=1, source_target_pairs={{0,16},{4,20},{8,24},{12,28},{16,0},{20,4},{24,8},{28,12},{1,17},{... | collective-permute-start | bytes 786440 | tf_op jit(solution)/shard_map/ppermute | solution.py:25
  96.0 21.0 %collective-permute-start.20 = (f32[128,128]{1,0:T(8,128)S(1)}, f32[128,128]{1,0:T(8,128)S(1)}, u32[]{:S(2)}, u32[]{:S(2)}) collective-permute-start(f32[128,128]{1,0:T(8,128)S(1)} %add.51.refs_0_), channel_id=1, source_target_pairs={{0,24},{4,28},{8,16},{12,20},{16,8},{20,12},{24,0},{28,4},{1,25},{... | collective-permute-start | bytes 196616 | tf_op jit(solution)/shard_map/ppermute | solution.py:25
  98.9 20.2 %collective-permute-start.19 = (f32[128,128]{1,0:T(8,128)S(1)}, f32[128,128]{1,0:T(8,128)S(1)}, u32[]{:S(2)}, u32[]{:S(2)}) collective-permute-start(f32[128,128]{1,0:T(8,128)S(1)} %add.51.refs_0_), channel_id=1, source_target_pairs={{0,16},{4,20},{8,24},{12,28},{16,0},{20,4},{24,8},{28,12},{1,17},{... | collective-permute-start | bytes 196616 | tf_op jit(solution)/shard_map/ppermute | solution.py:25
  120.1 23.2 %collective-permute-start.22 = (bf16[2,1024,128]{2,1,0:T(8,128)(2,1)S(1)}, bf16[2,1024,128]{2,1,0:T(8,128)(2,1)S(1)}, u32[]{:S(2)}, u32[]{:S(2)}) collective-permute-start(bf16[2,1024,128]{2,1,0:T(8,128)(2,1)S(1)} %pad_maximum_fusion.1), channel_id=1, source_target_pairs={{0,4},{4,0},{8,12},{12,8},{16,20},{20,16},{24,28},{28,24},{1,5},{5... | collective-permute-start | bytes 1572872 | tf_op jit(solution)/shard_map/ppermute | solution.py:25
  121.3 24.1 %collective-permute-start.23 = (bf16[2,512,128]{2,1,0:T(8,128)(2,1)S(1)}, bf16[2,512,128]{2,1,0:T(8,128)(2,1)S(1)}, u32[]{:S(2)}, u32[]{:S(2)}) collective-permute-start(bf16[2,512,128]{2,1,0:T(8,128)(2,1)S(1)} %pad_maximum_fusion.2), channel_id=1, source_target_pairs={{0,8},{4,12},{8,0},{12,4},{16,24},{20,28},{24,16},{28,20},{1,9},{5... | collective-permute-start | bytes 786440 | tf_op jit(solution)/shard_map/ppermute | solution.py:25
  121.3 25.4 %collective-permute-start.25 = (bf16[2,512,128]{2,1,0:T(8,128)(2,1)S(1)}, bf16[2,512,128]{2,1,0:T(8,128)(2,1)S(1)}, u32[]{:S(2)}, u32[]{:S(2)}) collective-permute-start(bf16[2,512,128]{2,1,0:T(8,128)(2,1)S(1)} %pad_maximum_fusion.2), channel_id=1, source_target_pairs={{0,24},{4,28},{8,16},{12,20},{16,8},{20,12},{24,0},{28,4},{1,25},{... | collective-permute-start | bytes 786440 | tf_op jit(solution)/shard_map/ppermute | solution.py:25
  124.0 22.8 %collective-permute-start.24 = (bf16[2,512,128]{2,1,0:T(8,128)(2,1)S(1)}, bf16[2,512,128]{2,1,0:T(8,128)(2,1)S(1)}, u32[]{:S(2)}, u32[]{:S(2)}) collective-permute-start(bf16[2,512,128]{2,1,0:T(8,128)(2,1)S(1)} %pad_maximum_fusion.2), channel_id=1, source_target_pairs={{0,16},{4,20},{8,24},{12,28},{16,0},{20,4},{24,8},{28,12},{1,17},{... | collective-permute-start | bytes 786440 | tf_op jit(solution)/shard_map/ppermute | solution.py:25
  161.4 25.6 %collective-permute-start.29 = (s16[4,1040,128]{2,1,0:T(8,128)(2,1)S(1)}, s16[4,1040,128]{2,1,0:T(8,128)(2,1)S(1)}, u32[]{:S(2)}, u32[]{:S(2)}) collective-permute-start(s16[4,1040,128]{2,1,0:T(8,128)(2,1)S(1)} %shard_map.62), channel_id=1, source_target_pairs={{0,4},{4,0},{8,12},{12,8},{16,20},{20,16},{24,28},{28,24},{1,5},{5... | collective-permute-start | bytes 3194888 | tf_op jit(solution)/shard_map/ppermute | solution.py:25
  164.1 20.4 %collective-permute-start.31 = (s16[1040,128]{1,0:T(8,128)(2,1)S(1)}, s16[1040,128]{1,0:T(8,128)(2,1)S(1)}, u32[]{:S(2)}, u32[]{:S(2)}) collective-permute-start(s16[1040,128]{1,0:T(8,128)(2,1)S(1)} %get-tuple-element.118), channel_id=1, source_target_pairs={{0,16},{4,20},{8,24},{12,28},{16,0},{20,4},{24,8},{28,12},{1,17},{... | collective-permute-start | bytes 798728 | tf_op jit(solution)/shard_map/ppermute | solution.py:25
  164.2 20.3 %collective-permute-start.32 = (s16[1040,128]{1,0:T(8,128)(2,1)S(1)}, s16[1040,128]{1,0:T(8,128)(2,1)S(1)}, u32[]{:S(2)}, u32[]{:S(2)}) collective-permute-start(s16[1040,128]{1,0:T(8,128)(2,1)S(1)} %get-tuple-element.119), channel_id=1, source_target_pairs={{0,24},{4,28},{8,16},{12,20},{16,8},{20,12},{24,0},{28,4},{1,25},{... | collective-permute-start | bytes 798728 | tf_op jit(solution)/shard_map/ppermute | solution.py:25
  191.7 21.6 %collective-permute-start.34 = (s16[1040,128]{1,0:T(8,128)(2,1)S(1)}, s16[1040,128]{1,0:T(8,128)(2,1)S(1)}, u32[]{:S(2)}, u32[]{:S(2)}) collective-permute-start(s16[1040,128]{1,0:T(8,128)(2,1)S(1)} %get-tuple-element.125), channel_id=1, source_target_pairs={{0,16},{4,20},{8,24},{12,28},{16,0},{20,4},{24,8},{28,12},{1,17},{... | collective-permute-start | bytes 798728 | tf_op jit(solution)/shard_map/ppermute | solution.py:25
  191.8 21.5 %collective-permute-start.35 = (s16[1040,128]{1,0:T(8,128)(2,1)S(1)}, s16[1040,128]{1,0:T(8,128)(2,1)S(1)}, u32[]{:S(2)}, u32[]{:S(2)}) collective-permute-start(s16[1040,128]{1,0:T(8,128)(2,1)S(1)} %get-tuple-element.126), channel_id=1, source_target_pairs={{0,24},{4,28},{8,16},{12,20},{16,8},{20,12},{24,0},{28,4},{1,25},{... | collective-permute-start | bytes 798728 | tf_op jit(solution)/shard_map/ppermute | solution.py:25
  195.1 24.2 %collective-permute-start.39 = (s16[528,128]{1,0:T(8,128)(2,1)S(1)}, s16[528,128]{1,0:T(8,128)(2,1)S(1)}, u32[]{:S(2)}, u32[]{:S(2)}) collective-permute-start(s16[528,128]{1,0:T(8,128)(2,1)S(1)} %get-tuple-element.134), channel_id=1, source_target_pairs={{0,4},{4,0},{8,12},{12,8},{16,20},{20,16},{24,28},{28,24},{1,5},{5... | collective-permute-start | bytes 405512 | tf_op jit(solution)/shard_map/ppermute | solution.py:25
  224.4 27.2 %collective-permute-start.36 = (s16[1040,128]{1,0:T(8,128)(2,1)S(1)}, s16[1040,128]{1,0:T(8,128)(2,1)S(1)}, u32[]{:S(2)}, u32[]{:S(2)}) collective-permute-start(s16[1040,128]{1,0:T(8,128)(2,1)S(1)} %get-tuple-element.144.refs_0_), channel_id=1, source_target_pairs={{0,16},{4,20},{8,24},{12,28},{16,0},{20,4},{24,8},{28,12},{1,17},{... | collective-permute-start | bytes 798728 | tf_op jit(solution)/shard_map/ppermute | solution.py:25
  231.0 20.6 %collective-permute-start.46 = (f32[128,128]{1,0:T(8,128)S(1)}, f32[128,128]{1,0:T(8,128)S(1)}, u32[]{:S(2)}, u32[]{:S(2)}) collective-permute-start(f32[128,128]{1,0:T(8,128)S(1)} %add.57.refs_0_), channel_id=1, source_target_pairs={{0,24},{4,28},{8,16},{12,20},{16,8},{20,12},{24,0},{28,4},{1,25},{... | collective-permute-start | bytes 196616 | tf_op jit(solution)/shard_map/ppermute | solution.py:25
  232.6 20.7 %collective-permute-start.45 = (f32[128,128]{1,0:T(8,128)S(1)}, f32[128,128]{1,0:T(8,128)S(1)}, u32[]{:S(2)}, u32[]{:S(2)}) collective-permute-start(f32[128,128]{1,0:T(8,128)S(1)} %add.57.refs_0_), channel_id=1, source_target_pairs={{0,16},{4,20},{8,24},{12,28},{16,0},{20,4},{24,8},{28,12},{1,17},{... | collective-permute-start | bytes 196616 | tf_op jit(solution)/shard_map/ppermute | solution.py:25
  254.3 23.2 %collective-permute-start.48 = (s16[2,1040,128]{2,1,0:T(8,128)(2,1)S(1)}, s16[2,1040,128]{2,1,0:T(8,128)(2,1)S(1)}, u32[]{:S(2)}, u32[]{:S(2)}) collective-permute-start(s16[2,1040,128]{2,1,0:T(8,128)(2,1)S(1)} %pad_add_fusion.1), channel_id=1, source_target_pairs={{0,4},{4,0},{8,12},{12,8},{16,20},{20,16},{24,28},{28,24},{1,5},{5... | collective-permute-start | bytes 1597448 | tf_op jit(solution)/shard_map/ppermute | solution.py:25
  255.5 27.5 %collective-permute-start.51 = (s16[2,528,128]{2,1,0:T(8,128)(2,1)S(1)}, s16[2,528,128]{2,1,0:T(8,128)(2,1)S(1)}, u32[]{:S(2)}, u32[]{:S(2)}) collective-permute-start(s16[2,528,128]{2,1,0:T(8,128)(2,1)S(1)} %pad_add_fusion.2.refs_1_), channel_id=1, source_target_pairs={{0,24},{4,28},{8,16},{12,20},{16,8},{20,12},{24,0},{28,4},{1,25},{... | collective-permute-start | bytes 811016 | tf_op jit(solution)/shard_map/ppermute | solution.py:25
  257.0 26.0 %collective-permute-start.50 = (s16[2,528,128]{2,1,0:T(8,128)(2,1)S(1)}, s16[2,528,128]{2,1,0:T(8,128)(2,1)S(1)}, u32[]{:S(2)}, u32[]{:S(2)}) collective-permute-start(s16[2,528,128]{2,1,0:T(8,128)(2,1)S(1)} %pad_add_fusion.2.refs_1_), channel_id=1, source_target_pairs={{0,16},{4,20},{8,24},{12,28},{16,0},{20,4},{24,8},{28,12},{1,17},{... | collective-permute-start | bytes 811016 | tf_op jit(solution)/shard_map/ppermute | solution.py:25
  257.0 26.1 %collective-permute-start.49 = (s16[2,528,128]{2,1,0:T(8,128)(2,1)S(1)}, s16[2,528,128]{2,1,0:T(8,128)(2,1)S(1)}, u32[]{:S(2)}, u32[]{:S(2)}) collective-permute-start(s16[2,528,128]{2,1,0:T(8,128)(2,1)S(1)} %pad_add_fusion.2.refs_1_), channel_id=1, source_target_pairs={{0,8},{4,12},{8,0},{12,4},{16,24},{20,28},{24,16},{28,20},{1,9},{5... | collective-permute-start | bytes 811016 | tf_op jit(solution)/shard_map/ppermute | solution.py:25
  (33 other events, 342.1 us)

commit v13 on v11

--- a/solution.py
+++ b/solution.py
@@ -68,7 +68,7 @@
     def __init__(self, voxels, subjects):
         self.high = subjects // LOW
         unit = subjects * LANES
-        for top, bottom in ((2, 3), (1, 2)):
+        for top, bottom in ((3, 4), (2, 3), (1, 2)):
             self.cut = voxels * top // bottom
             self.pair = (voxels - self.cut) // self.high
             if self.cut % unit == 0 and voxels % unit == 0 and self.cut % self.pair == 0:

time: 273 us -> 277 us (1.015)
  waiting for transfers between devices: 115 us -> 132 us
  starting transfers between devices: 87.4 us -> 71.2 us
  Pallas kernels: 62 us -> 65.5 us
    ppermute x52, waiting for transfers between devices: 115 us -> 132 us  [exchange(): return lax.ppermute(value, axis, [(i, i ^ mask) for i in range(size)])]
    ppermute x52, starting transfers between devices: 87.4 us -> 71.2 us  [exchange(): return lax.ppermute(value, axis, [(i, i ^ mask) for i in range(size)])]
  transfers between devices with their start and end apart: 52 -> 52, of which waited for: 32 -> 32; matrix products, arithmetic and copies ran while one was open for 0% -> 0% of each run, Pallas kernels for 14% -> 15%
where the time goes in v13:
time: 277 us
  waiting for transfers between devices  132 us (48%)
  starting transfers between devices  71.2 us (26%)
  Pallas kernels  65.5 us (24%)
  local copies, waits for them, and re-layouts  7.37 us (3%)
    ppermute x52, waiting for transfers between devices, exchange(): return lax.ppermute(value, axis, [(i, i ^ mask) for i in range(size)])  132 us
    ppermute x52, starting transfers between devices, exchange(): return lax.ppermute(value, axis, [(i, i ^ mask) for i in range(size)])  71.2 us
    pallas_call x8, Pallas kernels, sketch_part(): pl.pallas_call(functools.partial(sketch_kernel, code, apart, per_step), o...  23.4 us
    pallas_call x8, Pallas kernels, small_call(): pl.pallas_call(kernel, out_shape=out_shape, in_specs=[WHOLE] * len(args),...  12 us
    pallas_call x4, Pallas kernels, project(): pl.pallas_call(functools.partial(project_kernel, base is not None, split,...  9.33 us
    pallas_call x2, Pallas kernels, finish(): pl.pallas_call(functools.partial(finish_kernel, layout, items, base is no...  9.05 us
    pallas_call x1, Pallas kernels, first_project(): pl.pallas_call(functools.partial(first_kernel, count), out_shape=[half, h...  8.72 us
    unnamed x10, local copies, waits for them, and re-layouts  7.37 us
  transfers between devices with their start and end apart: 52, of which 32 were waited for; matrix products, arithmetic and copies ran while one was open for 0% of the time, Pallas kernels for 15%

profile of v13, /device:TPU:0, one launch (start us, length us, event | category | flops | bytes accessed | tf_op | source)
XLA Modules:
  0.0 277.2 jit_solution(18291587871861654074)
XLA Ops:
  2.0 8.7 %shard_map.46 = (f32[320,128]{1,0:T(8,128)S(1)}, f32[320,128]{1,0:T(8,128)S(1)}) custom-call(s32[3]{0:T(128)S(1)} %pad_add_fusion.3.pos_ref, bf16[12288,128]{1,0:T(8,128)(2,1)S(1)} %copy-done.2, bf16[640,12288]{1,0:T(8,128)(2,1)} %refs_0_.19, bf16[640,12288]{1,0:T(8,128)(2,1)} %refs_0_.19, bf16[640,12288]{1,0:T(8,128)(2,1)} %refs_0_.19, ...), custom_call_target="tpu_custom_call" | custom-call | flops 1 | bytes 1 | tf_op jit(solution)/shard_map/pallas_call | solution.py:206
  15.2 4.5 %collective-permute-done.1 = f32[320,128]{1,0:T(8,128)S(1)} collective-permute-done((f32[320,128]{1,0:T(8,128)S(1)}, f32[320,128]{1,0:T(8,128)S(1)}, u32[]{:S(2)}, u32[]{:S(2)}) %collective-permute-start.1) | collective-permute-done | bytes 163872 | tf_op jit(solution)/shard_map/ppermute | solution.py:25
  21.8 4.1 %shard_map.48 = bf16[4,1152,128]{2,1,0:T(8,128)(2,1)S(1)} custom-call(s32[3]{0:T(128)S(1)} %pad_add_fusion.3.pos_ref, bf16[640,128]{1,0:T(8,128)(2,1)S(1)} %shard_map.47.scores_ref, bf16[640,12288]{1,0:T(8,128)(2,1)} %refs_0_.19, bf16[640,12288]{1,0:T(8,128)(2,1)} %refs_0_.19), custom_call_target="tpu_custom_call" | custom-call | flops 1 | bytes 1 | tf_op jit(solution)/shard_map/pallas_call | solution.py:112
  37.3 4.1 %shard_map.50.own_ref = bf16[4,1152,128]{2,1,0:T(8,128)(2,1)S(1)} custom-call(s32[3]{0:T(128)S(1)} %pad_add_fusion.3.pos_ref, bf16[640,128]{1,0:T(8,128)(2,1)S(1)} %shard_map.47.scores_ref, bf16[640,12288]{1,0:T(8,128)(2,1)} %refs_0_.19, bf16[640,12288]{1,0:T(8,128)(2,1)} %refs_0_.19), custom_call_target="tpu_custom_call" | custom-call | flops 1 | bytes 1 | tf_op jit(solution)/shard_map/pallas_call | solution.py:112
  41.4 6.7 %collective-permute-done.5.refs_2_ = bf16[768,128]{1,0:T(8,128)(2,1)S(1)} collective-permute-done((bf16[768,128]{1,0:T(8,128)(2,1)S(1)}, bf16[768,128]{1,0:T(8,128)(2,1)S(1)}, u32[]{:S(2)}, u32[]{:S(2)}) %collective-permute-start.5) | collective-permute-done | bytes 196640 | tf_op jit(solution)/shard_map/ppermute | solution.py:25
  48.3 5.7 %collective-permute-done.3.got_ref = bf16[4,1152,128]{2,1,0:T(8,128)(2,1)S(1)} collective-permute-done((bf16[4,1152,128]{2,1,0:T(8,128)(2,1)S(1)}, bf16[4,1152,128]{2,1,0:T(8,128)(2,1)S(1)}, u32[]{:S(2)}, u32[]{:S(2)}) %collective-permute-start.3) | collective-permute-done | bytes 1179680 | tf_op jit(solution)/shard_map/ppermute | solution.py:25
  67.9 11.7 %collective-permute-done.8.refs_2_ = bf16[1152,128]{1,0:T(8,128)(2,1)S(1)} collective-permute-done((bf16[1152,128]{1,0:T(8,128)(2,1)S(1)}, bf16[1152,128]{1,0:T(8,128)(2,1)S(1)}, u32[]{:S(2)}, u32[]{:S(2)}) %collective-permute-start.8) | collective-permute-done | bytes 294944 | tf_op jit(solution)/shard_map/ppermute | solution.py:25
  80.5 5.0 %collective-permute-start.10 = (bf16[1152,128]{1,0:T(8,128)(2,1)S(1)}, bf16[1152,128]{1,0:T(8,128)(2,1)S(1)}, u32[]{:S(2)}, u32[]{:S(2)}) collective-permute-start(bf16[1152,128]{1,0:T(8,128)(2,1)S(1)} %get-tuple-element.89.refs_4_), channel_id=1, source_target_pairs={{0,8},{4,12},{8,0},{12,4},{16,24},{20,28},{24,16},{28,20},{1,9},{5... | collective-permute-start | bytes 884744 | tf_op jit(solution)/shard_map/ppermute | solution.py:25
  97.8 4.3 %collective-permute-done.15.refs_7_ = bf16[1152,128]{1,0:T(8,128)(2,1)S(1)} collective-permute-done((bf16[1152,128]{1,0:T(8,128)(2,1)S(1)}, bf16[1152,128]{1,0:T(8,128)(2,1)S(1)}, u32[]{:S(2)}, u32[]{:S(2)}) %collective-permute-start.15) | collective-permute-done | bytes 294944 | tf_op jit(solution)/shard_map/ppermute | solution.py:25
  102.2 11.2 %collective-permute-done.14.refs_6_ = bf16[1152,128]{1,0:T(8,128)(2,1)S(1)} collective-permute-done((bf16[1152,128]{1,0:T(8,128)(2,1)S(1)}, bf16[1152,128]{1,0:T(8,128)(2,1)S(1)}, u32[]{:S(2)}, u32[]{:S(2)}) %collective-permute-start.14) | collective-permute-done | bytes 294944 | tf_op jit(solution)/shard_map/ppermute | solution.py:25
  125.4 5.5 %copy-done = bf16[640,12288]{1,0:T(8,128)(2,1)S(1)} copy-done((bf16[640,12288]{1,0:T(8,128)(2,1)S(1)}, bf16[640,12288]{1,0:T(8,128)(2,1)}, u32[]{:S(2)}) %copy-start) | copy-done | bytes 15728664
  134.3 4.1 %shard_map.59.refs_0_ = f32[128,128]{1,0:T(8,128)S(1)} custom-call(f32[128,128]{1,0:T(8,128)S(1)} %add.51.refs_0_, f32[128,128]{1,0:T(8,128)S(1)} %collective-permute-done.21.refs_1_, f32[128,128]{1,0:T(8,128)S(1)} %collective-permute-done.22.refs_2_, f32[128,128]{1,0:T(8,128)S(1)} %collective-permute-done.23.refs_3_), custom_call_target="tpu_custom_call" | custom-call | flops 1 | bytes 1 | tf_op jit(solution)/shard_map/pallas_call | solution.py:128
  147.4 4.8 %collective-permute-done.27 = f32[320,128]{1,0:T(8,128)S(1)} collective-permute-done((f32[320,128]{1,0:T(8,128)S(1)}, f32[320,128]{1,0:T(8,128)S(1)}, u32[]{:S(2)}, u32[]{:S(2)}) %collective-permute-start.27) | collective-permute-done | bytes 163872 | tf_op jit(solution)/shard_map/ppermute | solution.py:25
  165.7 3.8 %shard_map.64.own_ref = s16[4,1168,128]{2,1,0:T(8,128)(2,1)S(1)} custom-call(s32[3]{0:T(128)S(1)} %pad_add_fusion.3.pos_ref, bf16[640,128]{1,0:T(8,128)(2,1)S(1)} %shard_map.61.scores_ref, bf16[640,12288]{1,0:T(8,128)(2,1)S(1)} %copy-done.1, bf16[640,12288]{1,0:T(8,128)(2,1)S(1)} %copy-done.1), custom_call_target="tpu_custom_call" | custom-call | flops 1 | bytes 1 | tf_op jit(solution)/shard_map/pallas_call | solution.py:112
  169.5 8.2 %collective-permute-done.31.refs_2_ = s16[784,128]{1,0:T(8,128)(2,1)S(1)} collective-permute-done((s16[784,128]{1,0:T(8,128)(2,1)S(1)}, s16[784,128]{1,0:T(8,128)(2,1)S(1)}, u32[]{:S(2)}, u32[]{:S(2)}) %collective-permute-start.31) | collective-permute-done | bytes 200736 | tf_op jit(solution)/shard_map/ppermute | solution.py:25
  178.2 8.4 %collective-permute-done.29.got_ref = s16[4,1168,128]{2,1,0:T(8,128)(2,1)S(1)} collective-permute-done((s16[4,1168,128]{2,1,0:T(8,128)(2,1)S(1)}, s16[4,1168,128]{2,1,0:T(8,128)(2,1)S(1)}, u32[]{:S(2)}, u32[]{:S(2)}) %collective-permute-start.29) | collective-permute-done | bytes 1196064 | tf_op jit(solution)/shard_map/ppermute | solution.py:25
  193.7 4.1 %collective-permute-done.38.refs_1_ = s16[400,128]{1,0:T(8,128)(2,1)S(1)} collective-permute-done((s16[400,128]{1,0:T(8,128)(2,1)S(1)}, s16[400,128]{1,0:T(8,128)(2,1)S(1)}, u32[]{:S(2)}, u32[]{:S(2)}) %collective-permute-start.38) | collective-permute-done | bytes 102432 | tf_op jit(solution)/shard_map/ppermute | solution.py:25
  201.7 11.9 %collective-permute-done.34.refs_2_ = s16[1168,128]{1,0:T(8,128)(2,1)S(1)} collective-permute-done((s16[1168,128]{1,0:T(8,128)(2,1)S(1)}, s16[1168,128]{1,0:T(8,128)(2,1)S(1)}, u32[]{:S(2)}, u32[]{:S(2)}) %collective-permute-start.34) | collective-permute-done | bytes 299040 | tf_op jit(solution)/shard_map/ppermute | solution.py:25
  214.6 5.1 %collective-permute-start.40 = (s16[1168,128]{1,0:T(8,128)(2,1)S(1)}, s16[1168,128]{1,0:T(8,128)(2,1)S(1)}, u32[]{:S(2)}, u32[]{:S(2)}) collective-permute-start(s16[1168,128]{1,0:T(8,128)(2,1)S(1)} %get-tuple-element.124.refs_0_), channel_id=1, source_target_pairs={{0,8},{4,12},{8,0},{12,4},{16,24},{20,28},{24,16},{28,20},{1,9},{5... | collective-permute-start | bytes 897032 | tf_op jit(solution)/shard_map/ppermute | solution.py:25
  232.3 4.1 %collective-permute-done.37.refs_3_ = s16[1168,128]{1,0:T(8,128)(2,1)S(1)} collective-permute-done((s16[1168,128]{1,0:T(8,128)(2,1)S(1)}, s16[1168,128]{1,0:T(8,128)(2,1)S(1)}, u32[]{:S(2)}, u32[]{:S(2)}) %collective-permute-start.37) | collective-permute-done | bytes 299040 | tf_op jit(solution)/shard_map/ppermute | solution.py:25
  236.4 11.5 %collective-permute-done.36.refs_2_ = s16[1168,128]{1,0:T(8,128)(2,1)S(1)} collective-permute-done((s16[1168,128]{1,0:T(8,128)(2,1)S(1)}, s16[1168,128]{1,0:T(8,128)(2,1)S(1)}, u32[]{:S(2)}, u32[]{:S(2)}) %collective-permute-start.36) | collective-permute-done | bytes 299040 | tf_op jit(solution)/shard_map/ppermute | solution.py:25
  260.0 4.1 %shard_map.70.inverse_ref = f32[128,128]{1,0:T(8,128)S(1)} custom-call(f32[128,128]{1,0:T(8,128)S(1)} %add.57.refs_0_, f32[128,128]{1,0:T(8,128)S(1)} %collective-permute-done.44.refs_1_, f32[128,128]{1,0:T(8,128)S(1)} %collective-permute-done.45.refs_2_, f32[128,128]{1,0:T(8,128)S(1)} %collective-permute-done.46.refs_3_), custom_call_target="tpu_custom_call" | custom-call | flops 1 | bytes 1 | tf_op jit(solution)/shard_map/pallas_call | solution.py:128
  264.1 6.0 %shard_map.71.refs_0_ = f32[12288,128]{1,0:T(8,128)} custom-call(s32[3]{0:T(128)S(1)} %pad_add_fusion.3.pos_ref, f32[128,128]{1,0:T(8,128)S(1)} %shard_map.70.inverse_ref, s16[1168,128]{1,0:T(8,128)(2,1)S(1)} %get-tuple-element.124.refs_0_, s16[1168,128]{1,0:T(8,128)(2,1)S(1)} %collective-permute-done.40.refs_1_, ...), custom_call_target="tpu_custom_call" | custom-call | tf_op jit(solution)/shard_map/pallas_call | solution.py:310
  270.1 3.9 %collective-permute-done.50.refs_3_ = s16[2,400,128]{2,1,0:T(8,128)(2,1)S(1)} collective-permute-done((s16[2,400,128]{2,1,0:T(8,128)(2,1)S(1)}, s16[2,400,128]{2,1,0:T(8,128)(2,1)S(1)}, u32[]{:S(2)}, u32[]{:S(2)}) %collective-permute-start.50) | collective-permute-done | bytes 204832 | tf_op jit(solution)/shard_map/ppermute | solution.py:25
  (138 shorter events, 125.2 us)
Async XLA Ops:
  25.9 28.1 %collective-permute-start.3 = (bf16[4,1152,128]{2,1,0:T(8,128)(2,1)S(1)}, bf16[4,1152,128]{2,1,0:T(8,128)(2,1)S(1)}, u32[]{:S(2)}, u32[]{:S(2)}) collective-permute-start(bf16[4,1152,128]{2,1,0:T(8,128)(2,1)S(1)} %shard_map.48), channel_id=1, source_target_pairs={{0,4},{4,0},{8,12},{12,8},{16,20},{20,16},{24,28},{28,24},{1,5},{5... | collective-permute-start | bytes 3538952 | tf_op jit(solution)/shard_map/ppermute | solution.py:25
  30.9 17.2 %collective-permute-start.5 = (bf16[768,128]{1,0:T(8,128)(2,1)S(1)}, bf16[768,128]{1,0:T(8,128)(2,1)S(1)}, u32[]{:S(2)}, u32[]{:S(2)}) collective-permute-start(bf16[768,128]{1,0:T(8,128)(2,1)S(1)} %get-tuple-element.71), channel_id=1, source_target_pairs={{0,16},{4,20},{8,24},{12,28},{16,0},{20,4},{24,8},{28,12},{1,17},{... | collective-permute-start | bytes 589832 | tf_op jit(solution)/shard_map/ppermute | solution.py:25
  56.2 23.5 %collective-permute-start.8 = (bf16[1152,128]{1,0:T(8,128)(2,1)S(1)}, bf16[1152,128]{1,0:T(8,128)(2,1)S(1)}, u32[]{:S(2)}, u32[]{:S(2)}) collective-permute-start(bf16[1152,128]{1,0:T(8,128)(2,1)S(1)} %get-tuple-element.78), channel_id=1, source_target_pairs={{0,16},{4,20},{8,24},{12,28},{16,0},{20,4},{24,8},{28,12},{1,17},{... | collective-permute-start | bytes 884744 | tf_op jit(solution)/shard_map/ppermute | solution.py:25
  58.8 20.9 %collective-permute-start.9 = (bf16[1152,128]{1,0:T(8,128)(2,1)S(1)}, bf16[1152,128]{1,0:T(8,128)(2,1)S(1)}, u32[]{:S(2)}, u32[]{:S(2)}) collective-permute-start(bf16[1152,128]{1,0:T(8,128)(2,1)S(1)} %get-tuple-element.79), channel_id=1, source_target_pairs={{0,24},{4,28},{8,16},{12,20},{16,8},{20,12},{24,0},{28,4},{1,25},{... | collective-permute-start | bytes 884744 | tf_op jit(solution)/shard_map/ppermute | solution.py:25
  64.5 21.0 %collective-permute-start.16 = (bf16[384,128]{1,0:T(8,128)(2,1)S(1)}, bf16[384,128]{1,0:T(8,128)(2,1)S(1)}, u32[]{:S(2)}, u32[]{:S(2)}) collective-permute-start(bf16[384,128]{1,0:T(8,128)(2,1)S(1)} %get-tuple-element.91), channel_id=1, source_target_pairs={{0,4},{4,0},{8,12},{12,8},{16,20},{20,16},{24,28},{28,24},{1,5},{5... | collective-permute-start | bytes 294920 | tf_op jit(solution)/shard_map/ppermute | solution.py:25
  85.5 16.6 %collective-permute-start.15 = (bf16[1152,128]{1,0:T(8,128)(2,1)S(1)}, bf16[1152,128]{1,0:T(8,128)(2,1)S(1)}, u32[]{:S(2)}, u32[]{:S(2)}) collective-permute-start(bf16[1152,128]{1,0:T(8,128)(2,1)S(1)} %get-tuple-element.89.refs_4_), channel_id=1, source_target_pairs={{0,24},{4,28},{8,16},{12,20},{16,8},{20,12},{24,0},{28,4},{1,25},{... | collective-permute-start | bytes 884744 | tf_op jit(solution)/shard_map/ppermute | solution.py:25
  88.0 25.3 %collective-permute-start.14 = (bf16[1152,128]{1,0:T(8,128)(2,1)S(1)}, bf16[1152,128]{1,0:T(8,128)(2,1)S(1)}, u32[]{:S(2)}, u32[]{:S(2)}) collective-permute-start(bf16[1152,128]{1,0:T(8,128)(2,1)S(1)} %get-tuple-element.89.refs_4_), channel_id=1, source_target_pairs={{0,16},{4,20},{8,24},{12,28},{16,0},{20,4},{24,8},{28,12},{1,17},{... | collective-permute-start | bytes 884744 | tf_op jit(solution)/shard_map/ppermute | solution.py:25
  94.7 43.7 %collective-permute-start.18 = (bf16[2,1152,128]{2,1,0:T(8,128)(2,1)S(1)}, bf16[2,1152,128]{2,1,0:T(8,128)(2,1)S(1)}, u32[]{:S(2)}, u32[]{:S(2)}) collective-permute-start(bf16[2,1152,128]{2,1,0:T(8,128)(2,1)S(1)} %pad_maximum_fusion), channel_id=1, source_target_pairs={{0,4},{4,0},{8,12},{12,8},{16,20},{20,16},{24,28},{28,24},{1,5},{5... | collective-permute-start | bytes 1769480 | tf_op jit(solution)/shard_map/ppermute | solution.py:25
  113.4 25.0 %collective-permute-start.19 = (bf16[2,1152,128]{2,1,0:T(8,128)(2,1)S(1)}, bf16[2,1152,128]{2,1,0:T(8,128)(2,1)S(1)}, u32[]{:S(2)}, u32[]{:S(2)}) collective-permute-start(bf16[2,1152,128]{2,1,0:T(8,128)(2,1)S(1)} %pad_maximum_fusion.1), channel_id=1, source_target_pairs={{0,4},{4,0},{8,12},{12,8},{16,20},{20,16},{24,28},{28,24},{1,5},{5... | collective-permute-start | bytes 1769480 | tf_op jit(solution)/shard_map/ppermute | solution.py:25
  121.0 20.8 %collective-permute-start.20 = (bf16[2,384,128]{2,1,0:T(8,128)(2,1)S(1)}, bf16[2,384,128]{2,1,0:T(8,128)(2,1)S(1)}, u32[]{:S(2)}, u32[]{:S(2)}) collective-permute-start(bf16[2,384,128]{2,1,0:T(8,128)(2,1)S(1)} %pad_maximum_fusion.2), channel_id=1, source_target_pairs={{0,8},{4,12},{8,0},{12,4},{16,24},{20,28},{24,16},{28,20},{1,9},{5... | collective-permute-start | bytes 589832 | tf_op jit(solution)/shard_map/ppermute | solution.py:25
  123.0 20.1 %collective-permute-start.25 = (bf16[2,384,128]{2,1,0:T(8,128)(2,1)S(1)}, bf16[2,384,128]{2,1,0:T(8,128)(2,1)S(1)}, u32[]{:S(2)}, u32[]{:S(2)}) collective-permute-start(bf16[2,384,128]{2,1,0:T(8,128)(2,1)S(1)} %pad_maximum_fusion.2), channel_id=1, source_target_pairs={{0,24},{4,28},{8,16},{12,20},{16,8},{20,12},{24,0},{28,4},{1,25},{... | collective-permute-start | bytes 589832 | tf_op jit(solution)/shard_map/ppermute | solution.py:25
  125.4 17.7 %collective-permute-start.24 = (bf16[2,384,128]{2,1,0:T(8,128)(2,1)S(1)}, bf16[2,384,128]{2,1,0:T(8,128)(2,1)S(1)}, u32[]{:S(2)}, u32[]{:S(2)}) collective-permute-start(bf16[2,384,128]{2,1,0:T(8,128)(2,1)S(1)} %pad_maximum_fusion.2), channel_id=1, source_target_pairs={{0,16},{4,20},{8,24},{12,28},{16,0},{20,4},{24,8},{28,12},{1,17},{... | collective-permute-start | bytes 589832 | tf_op jit(solution)/shard_map/ppermute | solution.py:25
  158.1 28.4 %collective-permute-start.29 = (s16[4,1168,128]{2,1,0:T(8,128)(2,1)S(1)}, s16[4,1168,128]{2,1,0:T(8,128)(2,1)S(1)}, u32[]{:S(2)}, u32[]{:S(2)}) collective-permute-start(s16[4,1168,128]{2,1,0:T(8,128)(2,1)S(1)} %shard_map.62), channel_id=1, source_target_pairs={{0,4},{4,0},{8,12},{12,8},{16,20},{20,16},{24,28},{28,24},{1,5},{5... | collective-permute-start | bytes 3588104 | tf_op jit(solution)/shard_map/ppermute | solution.py:25
  160.2 17.5 %collective-permute-start.31 = (s16[784,128]{1,0:T(8,128)(2,1)S(1)}, s16[784,128]{1,0:T(8,128)(2,1)S(1)}, u32[]{:S(2)}, u32[]{:S(2)}) collective-permute-start(s16[784,128]{1,0:T(8,128)(2,1)S(1)} %get-tuple-element.103), channel_id=1, source_target_pairs={{0,16},{4,20},{8,24},{12,28},{16,0},{20,4},{24,8},{28,12},{1,17},{... | collective-permute-start | bytes 602120 | tf_op jit(solution)/shard_map/ppermute | solution.py:25
  189.8 23.8 %collective-permute-start.34 = (s16[1168,128]{1,0:T(8,128)(2,1)S(1)}, s16[1168,128]{1,0:T(8,128)(2,1)S(1)}, u32[]{:S(2)}, u32[]{:S(2)}) collective-permute-start(s16[1168,128]{1,0:T(8,128)(2,1)S(1)} %get-tuple-element.110), channel_id=1, source_target_pairs={{0,16},{4,20},{8,24},{12,28},{16,0},{20,4},{24,8},{28,12},{1,17},{... | collective-permute-start | bytes 897032 | tf_op jit(solution)/shard_map/ppermute | solution.py:25
  190.8 22.8 %collective-permute-start.35 = (s16[1168,128]{1,0:T(8,128)(2,1)S(1)}, s16[1168,128]{1,0:T(8,128)(2,1)S(1)}, u32[]{:S(2)}, u32[]{:S(2)}) collective-permute-start(s16[1168,128]{1,0:T(8,128)(2,1)S(1)} %get-tuple-element.111), channel_id=1, source_target_pairs={{0,24},{4,28},{8,16},{12,20},{16,8},{20,12},{24,0},{28,4},{1,25},{... | collective-permute-start | bytes 897032 | tf_op jit(solution)/shard_map/ppermute | solution.py:25
  198.2 21.5 %collective-permute-start.39 = (s16[400,128]{1,0:T(8,128)(2,1)S(1)}, s16[400,128]{1,0:T(8,128)(2,1)S(1)}, u32[]{:S(2)}, u32[]{:S(2)}) collective-permute-start(s16[400,128]{1,0:T(8,128)(2,1)S(1)} %get-tuple-element.119), channel_id=1, source_target_pairs={{0,4},{4,0},{8,12},{12,8},{16,20},{20,16},{24,28},{28,24},{1,5},{5... | collective-permute-start | bytes 307208 | tf_op jit(solution)/shard_map/ppermute | solution.py:25
  219.7 16.7 %collective-permute-start.37 = (s16[1168,128]{1,0:T(8,128)(2,1)S(1)}, s16[1168,128]{1,0:T(8,128)(2,1)S(1)}, u32[]{:S(2)}, u32[]{:S(2)}) collective-permute-start(s16[1168,128]{1,0:T(8,128)(2,1)S(1)} %get-tuple-element.124.refs_0_), channel_id=1, source_target_pairs={{0,24},{4,28},{8,16},{12,20},{16,8},{20,12},{24,0},{28,4},{1,25},{... | collective-permute-start | bytes 897032 | tf_op jit(solution)/shard_map/ppermute | solution.py:25
  222.1 25.7 %collective-permute-start.36 = (s16[1168,128]{1,0:T(8,128)(2,1)S(1)}, s16[1168,128]{1,0:T(8,128)(2,1)S(1)}, u32[]{:S(2)}, u32[]{:S(2)}) collective-permute-start(s16[1168,128]{1,0:T(8,128)(2,1)S(1)} %get-tuple-element.124.refs_0_), channel_id=1, source_target_pairs={{0,16},{4,20},{8,24},{12,28},{16,0},{20,4},{24,8},{28,12},{1,17},{... | collective-permute-start | bytes 897032 | tf_op jit(solution)/shard_map/ppermute | solution.py:25
  227.9 36.1 %collective-permute-start.47 = (s16[2,1168,128]{2,1,0:T(8,128)(2,1)S(1)}, s16[2,1168,128]{2,1,0:T(8,128)(2,1)S(1)}, u32[]{:S(2)}, u32[]{:S(2)}) collective-permute-start(s16[2,1168,128]{2,1,0:T(8,128)(2,1)S(1)} %pad_add_fusion), channel_id=1, source_target_pairs={{0,4},{4,0},{8,12},{12,8},{16,20},{20,16},{24,28},{28,24},{1,5},{5... | collective-permute-start | bytes 1794056 | tf_op jit(solution)/shard_map/ppermute | solution.py:25
  247.9 16.1 %collective-permute-start.48 = (s16[2,1168,128]{2,1,0:T(8,128)(2,1)S(1)}, s16[2,1168,128]{2,1,0:T(8,128)(2,1)S(1)}, u32[]{:S(2)}, u32[]{:S(2)}) collective-permute-start(s16[2,1168,128]{2,1,0:T(8,128)(2,1)S(1)} %pad_add_fusion.1), channel_id=1, source_target_pairs={{0,4},{4,0},{8,12},{12,8},{16,20},{20,16},{24,28},{28,24},{1,5},{5... | collective-permute-start | bytes 1794056 | tf_op jit(solution)/shard_map/ppermute | solution.py:25
  254.6 15.5 %collective-permute-start.51 = (s16[2,400,128]{2,1,0:T(8,128)(2,1)S(1)}, s16[2,400,128]{2,1,0:T(8,128)(2,1)S(1)}, u32[]{:S(2)}, u32[]{:S(2)}) collective-permute-start(s16[2,400,128]{2,1,0:T(8,128)(2,1)S(1)} %pad_add_fusion.2.refs_1_), channel_id=1, source_target_pairs={{0,24},{4,28},{8,16},{12,20},{16,8},{20,12},{24,0},{28,4},{1,25},{... | collective-permute-start | bytes 614408 | tf_op jit(solution)/shard_map/ppermute | solution.py:25
  257.6 16.5 %collective-permute-start.50 = (s16[2,400,128]{2,1,0:T(8,128)(2,1)S(1)}, s16[2,400,128]{2,1,0:T(8,128)(2,1)S(1)}, u32[]{:S(2)}, u32[]{:S(2)}) collective-permute-start(s16[2,400,128]{2,1,0:T(8,128)(2,1)S(1)} %pad_add_fusion.2.refs_1_), channel_id=1, source_target_pairs={{0,16},{4,20},{8,24},{12,28},{16,0},{20,4},{24,8},{28,12},{1,17},{... | collective-permute-start | bytes 614408 | tf_op jit(solution)/shard_map/ppermute | solution.py:25
  257.6 16.5 %collective-permute-start.49 = (s16[2,400,128]{2,1,0:T(8,128)(2,1)S(1)}, s16[2,400,128]{2,1,0:T(8,128)(2,1)S(1)}, u32[]{:S(2)}, u32[]{:S(2)}) collective-permute-start(s16[2,400,128]{2,1,0:T(8,128)(2,1)S(1)} %pad_add_fusion.2.refs_1_), channel_id=1, source_target_pairs={{0,8},{4,12},{8,0},{12,4},{16,24},{20,28},{24,16},{28,20},{1,9},{5... | collective-permute-start | bytes 614408 | tf_op jit(solution)/shard_map/ppermute | solution.py:25
  (33 other events, 263.9 us)

commit v14 on v11

--- a/solution.py
+++ b/solution.py
@@ -18,6 +18,7 @@
 VMEM_BYTES = 20 << 20
 VMEM_FIRST = 48 << 20
 LIGHT = pl.CostEstimate(flops=1, bytes_accessed=1, transcendentals=0)
+LONG = pl.CostEstimate(flops=4 * 10**9, bytes_accessed=1, transcendentals=0)
 WHOLE = pl.BlockSpec(memory_space=pltpu.VMEM)
 
 
@@ -124,14 +125,14 @@
     )(pos, scores, *([scans] * per_step))
 
 
-def small_call(kernel, out_shape, *args):
+def small_call(kernel, out_shape, *args, cost=LIGHT):
     return pl.pallas_call(
         kernel,
         out_shape=out_shape,
         in_specs=[WHOLE] * len(args),
         out_specs=jax.tree.map(lambda _: WHOLE, out_shape),
         compiler_params=params(),
-        cost_estimate=LIGHT,
+        cost_estimate=cost,
     )(*args)
 
 
@@ -489,25 +490,28 @@
                 cost_estimate=LIGHT,
             )(lengths, block_subject, pos, mine, other, *factor)
 
+        def invert(grams, cost):
+            return small_call(
+                functools.partial(invert_kernel, all_voxels),
+                jax.ShapeDtypeStruct((rank, rank), F32), *grams, cost=cost,
+            )
+
         def pass_over(scores, code):
             (first, gram_first), (second, gram_second) = sketch_sum(scores, code)
             early, late, pairs, grams = gather(first, second, gram_first + gram_second)
-            inverse = small_call(
-                functools.partial(invert_kernel, all_voxels),
-                jax.ShapeDtypeStruct((rank, rank), F32), *grams,
-            )
-            return early, late, pairs, inverse
+            return early, late, pairs, grams
 
         scores = sum_scores(*first_project(scans, pos, test_matrix))
-        early, late, pairs, inverse = pass_over(scores, Plain)
+        early, late, pairs, grams = pass_over(scores, Plain)
         pairs = [(j, k, array.reshape(layout.pair, rank)) for j, k, array in pairs]
         total = project(scans, layout, pos, early)
         total = project(scans, layout, pos, late, total)
         total = project(scans, layout, pos, pairs[: high // 2], total)
-        total, inverse = lax.optimization_barrier((total, inverse))
+        total, grams = lax.optimization_barrier((total, grams))
         halves = project(scans, layout, pos, pairs[high // 2 :], total, True)
-        scores = sum_scores(*halves, inverse)
-        early, late, pairs, inverse = pass_over(scores, Fixed)
+        scores = sum_scores(*halves, invert(grams, LONG))
+        early, late, pairs, grams = pass_over(scores, Fixed)
+        inverse = invert(grams, LIGHT)
         out = finish(layout, pos, early + late, inverse, voxels)
         return finish(layout, pos, pairs, inverse, voxels, out)
 

time: 273 us -> 277 us (1.015)
  waiting for transfers between devices: 115 us -> 118 us
    ppermute x52, waiting for transfers between devices: 115 us -> 118 us  [exchange(): return lax.ppermute(value, axis, [(i, i ^ mask) for i in range(size)])]
    unnamed x10 -> x16, local copies, waits for them, and re-layouts: 7.37 us -> 7.39 us
  transfers between devices with their start and end apart: 52 -> 52, of which waited for: 32 -> 29; matrix products, arithmetic and copies ran while one was open for 0% -> 0% of each run, Pallas kernels for 14% -> 14%
where the time goes in v14:
time: 277 us
  waiting for transfers between devices  118 us (43%)
  starting transfers between devices  87.9 us (32%)
  Pallas kernels  62 us (22%)
  local copies, waits for them, and re-layouts  7.39 us (3%)
    ppermute x52, waiting for transfers between devices, exchange(): return lax.ppermute(value, axis, [(i, i ^ mask) for i in range(size)])  118 us
    ppermute x52, starting transfers between devices, exchange(): return lax.ppermute(value, axis, [(i, i ^ mask) for i in range(size)])  87.9 us
    pallas_call x8, Pallas kernels, sketch_part(): pl.pallas_call(functools.partial(sketch_kernel, code, apart, per_step), o...  22.2 us
    pallas_call x8, Pallas kernels, small_call(): pl.pallas_call(kernel, out_shape=out_shape, in_specs=[WHOLE] * len(args),...  11.8 us
    pallas_call x2, Pallas kernels, finish(): pl.pallas_call(functools.partial(finish_kernel, layout, items, base is no...  9.12 us
    pallas_call x1, Pallas kernels, first_project(): pl.pallas_call(functools.partial(first_kernel, count), out_shape=[half, h...  8.72 us
    unnamed x16, local copies, waits for them, and re-layouts  7.39 us
    pallas_call x4, Pallas kernels, project(): pl.pallas_call(functools.partial(project_kernel, base is not None, split,...  6.91 us
  transfers between devices with their start and end apart: 52, of which 29 were waited for; matrix products, arithmetic and copies ran while one was open for 0% of the time, Pallas kernels for 14%

profile of v14, /device:TPU:0, one launch (start us, length us, event | category | flops | bytes accessed | tf_op | source)
XLA Modules:
  0.0 276.7 jit_solution(15891635774200994496)
XLA Ops:
  2.0 8.7 %shard_map.46 = (f32[320,128]{1,0:T(8,128)S(1)}, f32[320,128]{1,0:T(8,128)S(1)}) custom-call(s32[3]{0:T(128)S(1)} %pad_add_fusion.3.pos_ref, bf16[12288,128]{1,0:T(8,128)(2,1)S(1)} %copy-done.1, bf16[640,12288]{1,0:T(8,128)(2,1)} %refs_0_.19, bf16[640,12288]{1,0:T(8,128)(2,1)} %refs_0_.19, bf16[640,12288]{1,0:T(8,128)(2,1)} %refs_0_.19, ...), custom_call_target="tpu_custom_call" | custom-call | flops 1 | bytes 1 | tf_op jit(solution)/shard_map/pallas_call | solution.py:207
  15.2 4.5 %collective-permute-done.1 = f32[320,128]{1,0:T(8,128)S(1)} collective-permute-done((f32[320,128]{1,0:T(8,128)S(1)}, f32[320,128]{1,0:T(8,128)S(1)}, u32[]{:S(2)}, u32[]{:S(2)}) %collective-permute-start.1) | collective-permute-done | bytes 163872 | tf_op jit(solution)/shard_map/ppermute | solution.py:26
  21.8 3.8 %shard_map.48 = bf16[4,1024,128]{2,1,0:T(8,128)(2,1)S(1)} custom-call(s32[3]{0:T(128)S(1)} %pad_add_fusion.3.pos_ref, bf16[640,128]{1,0:T(8,128)(2,1)S(1)} %shard_map.47.scores_ref, bf16[640,12288]{1,0:T(8,128)(2,1)} %refs_0_.19, bf16[640,12288]{1,0:T(8,128)(2,1)} %refs_0_.19), custom_call_target="tpu_custom_call" | custom-call | flops 1 | bytes 1 | tf_op jit(solution)/shard_map/pallas_call | solution.py:113
  37.6 4.0 %shard_map.50.own_ref = bf16[4,1024,128]{2,1,0:T(8,128)(2,1)S(1)} custom-call(s32[3]{0:T(128)S(1)} %pad_add_fusion.3.pos_ref, bf16[640,128]{1,0:T(8,128)(2,1)S(1)} %shard_map.47.scores_ref, bf16[640,12288]{1,0:T(8,128)(2,1)} %refs_0_.19, bf16[640,12288]{1,0:T(8,128)(2,1)} %refs_0_.19), custom_call_target="tpu_custom_call" | custom-call | flops 1 | bytes 1 | tf_op jit(solution)/shard_map/pallas_call | solution.py:113
  41.5 10.9 %collective-permute-done.5.refs_2_ = bf16[1024,128]{1,0:T(8,128)(2,1)S(1)} collective-permute-done((bf16[1024,128]{1,0:T(8,128)(2,1)S(1)}, bf16[1024,128]{1,0:T(8,128)(2,1)S(1)}, u32[]{:S(2)}, u32[]{:S(2)}) %collective-permute-start.5) | collective-permute-done | bytes 262176 | tf_op jit(solution)/shard_map/ppermute | solution.py:26
  52.9 5.0 %collective-permute-start.7 = (bf16[1024,128]{1,0:T(8,128)(2,1)S(1)}, bf16[1024,128]{1,0:T(8,128)(2,1)S(1)}, u32[]{:S(2)}, u32[]{:S(2)}) collective-permute-start(bf16[1024,128]{1,0:T(8,128)(2,1)S(1)} %get-tuple-element.80), channel_id=1, source_target_pairs={{0,8},{4,12},{8,0},{12,4},{16,24},{20,28},{24,16},{28,20},{1,9},{5... | collective-permute-start | bytes 786440 | tf_op jit(solution)/shard_map/ppermute | solution.py:26
  62.6 4.5 %collective-permute-done.11.refs_1_ = bf16[512,128]{1,0:T(8,128)(2,1)S(1)} collective-permute-done((bf16[512,128]{1,0:T(8,128)(2,1)S(1)}, bf16[512,128]{1,0:T(8,128)(2,1)S(1)}, u32[]{:S(2)}, u32[]{:S(2)}) %collective-permute-start.11) | collective-permute-done | bytes 131104 | tf_op jit(solution)/shard_map/ppermute | solution.py:26
  69.8 9.5 %collective-permute-done.8.refs_2_ = bf16[1024,128]{1,0:T(8,128)(2,1)S(1)} collective-permute-done((bf16[1024,128]{1,0:T(8,128)(2,1)S(1)}, bf16[1024,128]{1,0:T(8,128)(2,1)S(1)}, u32[]{:S(2)}, u32[]{:S(2)}) %collective-permute-start.8) | collective-permute-done | bytes 262176 | tf_op jit(solution)/shard_map/ppermute | solution.py:26
  83.4 12.5 %collective-permute-start.14 = (bf16[1024,128]{1,0:T(8,128)(2,1)S(1)}, bf16[1024,128]{1,0:T(8,128)(2,1)S(1)}, u32[]{:S(2)}, u32[]{:S(2)}) collective-permute-start(bf16[1024,128]{1,0:T(8,128)(2,1)S(1)} %get-tuple-element.92.refs_4_), channel_id=1, source_target_pairs={{0,16},{4,20},{8,24},{12,28},{16,0},{20,4},{24,8},{28,12},{1,17},{... | collective-permute-start | bytes 786440 | tf_op jit(solution)/shard_map/ppermute | solution.py:26
  113.7 5.8 %collective-permute-done.20 = bf16[2,512,128]{2,1,0:T(8,128)(2,1)S(1)} collective-permute-done((bf16[2,512,128]{2,1,0:T(8,128)(2,1)S(1)}, bf16[2,512,128]{2,1,0:T(8,128)(2,1)S(1)}, u32[]{:S(2)}, u32[]{:S(2)}) %collective-permute-start.20) | collective-permute-done | bytes 262176 | tf_op jit(solution)/shard_map/ppermute | solution.py:26
  122.8 5.1 %collective-permute-done.19.refs_6_ = bf16[2,1024,128]{2,1,0:T(8,128)(2,1)S(1)} collective-permute-done((bf16[2,1024,128]{2,1,0:T(8,128)(2,1)S(1)}, bf16[2,1024,128]{2,1,0:T(8,128)(2,1)S(1)}, u32[]{:S(2)}, u32[]{:S(2)}) %collective-permute-start.19) | collective-permute-done | bytes 524320 | tf_op jit(solution)/shard_map/ppermute | solution.py:26
  129.5 5.5 %copy-done = bf16[640,12288]{1,0:T(8,128)(2,1)S(1)} copy-done((bf16[640,12288]{1,0:T(8,128)(2,1)S(1)}, bf16[640,12288]{1,0:T(8,128)(2,1)}, u32[]{:S(2)}) %copy-start) | copy-done | bytes 15728664
  145.0 4.8 %collective-permute-done.27 = f32[320,128]{1,0:T(8,128)S(1)} collective-permute-done((f32[320,128]{1,0:T(8,128)S(1)}, f32[320,128]{1,0:T(8,128)S(1)}, u32[]{:S(2)}, u32[]{:S(2)}) %collective-permute-start.27) | collective-permute-done | bytes 163872 | tf_op jit(solution)/shard_map/ppermute | solution.py:26
  149.9 4.1 %shard_map.60.refs_0_ = f32[128,128]{1,0:T(8,128)S(1)} custom-call(f32[128,128]{1,0:T(8,128)S(1)} %add.51.refs_0_, f32[128,128]{1,0:T(8,128)S(1)} %collective-permute-done.21.refs_1_, f32[128,128]{1,0:T(8,128)S(1)} %collective-permute-done.22.refs_2_, f32[128,128]{1,0:T(8,128)S(1)} %collective-permute-done.23.refs_3_), custom_call_target="tpu_custom_call" | custom-call | flops 4000000000 | bytes 1 | tf_op jit(solution)/shard_map/pallas_call | solution.py:129
  168.4 13.7 %collective-permute-done.31.refs_2_ = s16[1040,128]{1,0:T(8,128)(2,1)S(1)} collective-permute-done((s16[1040,128]{1,0:T(8,128)(2,1)S(1)}, s16[1040,128]{1,0:T(8,128)(2,1)S(1)}, u32[]{:S(2)}, u32[]{:S(2)}) %collective-permute-start.31) | collective-permute-done | bytes 266272 | tf_op jit(solution)/shard_map/ppermute | solution.py:26
  187.1 4.0 %collective-permute-start.33 = (s16[1040,128]{1,0:T(8,128)(2,1)S(1)}, s16[1040,128]{1,0:T(8,128)(2,1)S(1)}, u32[]{:S(2)}, u32[]{:S(2)}) collective-permute-start(s16[1040,128]{1,0:T(8,128)(2,1)S(1)} %get-tuple-element.115), channel_id=1, source_target_pairs={{0,8},{4,12},{8,0},{12,4},{16,24},{20,28},{24,16},{28,20},{1,9},{5... | collective-permute-start | bytes 798728 | tf_op jit(solution)/shard_map/ppermute | solution.py:26
  195.2 6.8 %collective-permute-done.33.refs_1_ = s16[1040,128]{1,0:T(8,128)(2,1)S(1)} collective-permute-done((s16[1040,128]{1,0:T(8,128)(2,1)S(1)}, s16[1040,128]{1,0:T(8,128)(2,1)S(1)}, u32[]{:S(2)}, u32[]{:S(2)}) %collective-permute-start.33) | collective-permute-done | bytes 266272 | tf_op jit(solution)/shard_map/ppermute | solution.py:26
  202.0 10.8 %collective-permute-done.34.refs_2_ = s16[1040,128]{1,0:T(8,128)(2,1)S(1)} collective-permute-done((s16[1040,128]{1,0:T(8,128)(2,1)S(1)}, s16[1040,128]{1,0:T(8,128)(2,1)S(1)}, u32[]{:S(2)}, u32[]{:S(2)}) %collective-permute-start.34) | collective-permute-done | bytes 266272 | tf_op jit(solution)/shard_map/ppermute | solution.py:26
  213.6 4.6 %collective-permute-start.40 = (s16[1040,128]{1,0:T(8,128)(2,1)S(1)}, s16[1040,128]{1,0:T(8,128)(2,1)S(1)}, u32[]{:S(2)}, u32[]{:S(2)}) collective-permute-start(s16[1040,128]{1,0:T(8,128)(2,1)S(1)} %get-tuple-element.130.refs_0_), channel_id=1, source_target_pairs={{0,8},{4,12},{8,0},{12,4},{16,24},{20,28},{24,16},{28,20},{1,9},{5... | collective-permute-start | bytes 798728 | tf_op jit(solution)/shard_map/ppermute | solution.py:26
  233.8 7.8 %collective-permute-done.36.refs_2_ = s16[1040,128]{1,0:T(8,128)(2,1)S(1)} collective-permute-done((s16[1040,128]{1,0:T(8,128)(2,1)S(1)}, s16[1040,128]{1,0:T(8,128)(2,1)S(1)}, u32[]{:S(2)}, u32[]{:S(2)}) %collective-permute-start.36) | collective-permute-done | bytes 266272 | tf_op jit(solution)/shard_map/ppermute | solution.py:26
  252.4 7.3 %collective-permute-done.45.refs_2_ = f32[128,128]{1,0:T(8,128)S(1)} collective-permute-done((f32[128,128]{1,0:T(8,128)S(1)}, f32[128,128]{1,0:T(8,128)S(1)}, u32[]{:S(2)}, u32[]{:S(2)}) %collective-permute-start.45) | collective-permute-done | bytes 65568 | tf_op jit(solution)/shard_map/ppermute | solution.py:26
  262.4 4.1 %shard_map.70.inverse_ref = f32[128,128]{1,0:T(8,128)S(1)} custom-call(f32[128,128]{1,0:T(8,128)S(1)} %add.57.refs_0_, f32[128,128]{1,0:T(8,128)S(1)} %collective-permute-done.44.refs_1_, f32[128,128]{1,0:T(8,128)S(1)} %collective-permute-done.45.refs_2_, f32[128,128]{1,0:T(8,128)S(1)} %collective-permute-done.46.refs_3_), custom_call_target="tpu_custom_call" | custom-call | flops 1 | bytes 1 | tf_op jit(solution)/shard_map/pallas_call | solution.py:129
  266.5 5.5 %shard_map.71.refs_0_ = f32[12288,128]{1,0:T(8,128)} custom-call(s32[3]{0:T(128)S(1)} %pad_add_fusion.3.pos_ref, f32[128,128]{1,0:T(8,128)S(1)} %shard_map.70.inverse_ref, s16[1040,128]{1,0:T(8,128)(2,1)S(1)} %get-tuple-element.130.refs_0_, s16[1040,128]{1,0:T(8,128)(2,1)S(1)} %collective-permute-done.40.refs_1_, ...), custom_call_target="tpu_custom_call" | custom-call | tf_op jit(solution)/shard_map/pallas_call | solution.py:311
  273.0 3.6 %shard_map.72 = f32[12288,128]{1,0:T(8,128)} custom-call(s32[3]{0:T(128)S(1)} %pad_add_fusion.3.pos_ref, f32[128,128]{1,0:T(8,128)S(1)} %shard_map.70.inverse_ref, f32[12288,128]{1,0:T(8,128)} %shard_map.71.refs_0_, s16[2,528,128]{2,1,0:T(8,128)(2,1)S(1)} %pad_add_fusion.2.refs_1_, ...), custom_call_target="tpu_custom_call", output_to_operand_aliasing={{}: (2, {})} | custom-call | tf_op jit(solution)/shard_map/pallas_call | solution.py:311
  (145 shorter events, 119.3 us)
Async XLA Ops:
  25.6 27.0 %collective-permute-start.3 = (bf16[4,1024,128]{2,1,0:T(8,128)(2,1)S(1)}, bf16[4,1024,128]{2,1,0:T(8,128)(2,1)S(1)}, u32[]{:S(2)}, u32[]{:S(2)}) collective-permute-start(bf16[4,1024,128]{2,1,0:T(8,128)(2,1)S(1)} %shard_map.48), channel_id=1, source_target_pairs={{0,4},{4,0},{8,12},{12,8},{16,20},{20,16},{24,28},{28,24},{1,5},{5... | collective-permute-start | bytes 3145736 | tf_op jit(solution)/shard_map/ppermute | solution.py:26
  31.0 21.4 %collective-permute-start.5 = (bf16[1024,128]{1,0:T(8,128)(2,1)S(1)}, bf16[1024,128]{1,0:T(8,128)(2,1)S(1)}, u32[]{:S(2)}, u32[]{:S(2)}) collective-permute-start(bf16[1024,128]{1,0:T(8,128)(2,1)S(1)} %get-tuple-element.74), channel_id=1, source_target_pairs={{0,16},{4,20},{8,24},{12,28},{16,0},{20,4},{24,8},{28,12},{1,17},{... | collective-permute-start | bytes 786440 | tf_op jit(solution)/shard_map/ppermute | solution.py:26
  33.6 18.8 %collective-permute-start.6 = (bf16[1024,128]{1,0:T(8,128)(2,1)S(1)}, bf16[1024,128]{1,0:T(8,128)(2,1)S(1)}, u32[]{:S(2)}, u32[]{:S(2)}) collective-permute-start(bf16[1024,128]{1,0:T(8,128)(2,1)S(1)} %get-tuple-element.75), channel_id=1, source_target_pairs={{0,24},{4,28},{8,16},{12,20},{16,8},{20,12},{24,0},{28,4},{1,25},{... | collective-permute-start | bytes 786440 | tf_op jit(solution)/shard_map/ppermute | solution.py:26
  57.9 21.3 %collective-permute-start.8 = (bf16[1024,128]{1,0:T(8,128)(2,1)S(1)}, bf16[1024,128]{1,0:T(8,128)(2,1)S(1)}, u32[]{:S(2)}, u32[]{:S(2)}) collective-permute-start(bf16[1024,128]{1,0:T(8,128)(2,1)S(1)} %get-tuple-element.81), channel_id=1, source_target_pairs={{0,16},{4,20},{8,24},{12,28},{16,0},{20,4},{24,8},{28,12},{1,17},{... | collective-permute-start | bytes 786440 | tf_op jit(solution)/shard_map/ppermute | solution.py:26
  59.9 19.3 %collective-permute-start.9 = (bf16[1024,128]{1,0:T(8,128)(2,1)S(1)}, bf16[1024,128]{1,0:T(8,128)(2,1)S(1)}, u32[]{:S(2)}, u32[]{:S(2)}) collective-permute-start(bf16[1024,128]{1,0:T(8,128)(2,1)S(1)} %get-tuple-element.82), channel_id=1, source_target_pairs={{0,24},{4,28},{8,16},{12,20},{16,8},{20,12},{24,0},{28,4},{1,25},{... | collective-permute-start | bytes 786440 | tf_op jit(solution)/shard_map/ppermute | solution.py:26
  67.4 29.0 %collective-permute-start.16 = (bf16[512,128]{1,0:T(8,128)(2,1)S(1)}, bf16[512,128]{1,0:T(8,128)(2,1)S(1)}, u32[]{:S(2)}, u32[]{:S(2)}) collective-permute-start(bf16[512,128]{1,0:T(8,128)(2,1)S(1)} %get-tuple-element.94), channel_id=1, source_target_pairs={{0,4},{4,0},{8,12},{12,8},{16,20},{20,16},{24,28},{28,24},{1,5},{5... | collective-permute-start | bytes 393224 | tf_op jit(solution)/shard_map/ppermute | solution.py:26
  79.9 27.8 %collective-permute-start.15 = (bf16[1024,128]{1,0:T(8,128)(2,1)S(1)}, bf16[1024,128]{1,0:T(8,128)(2,1)S(1)}, u32[]{:S(2)}, u32[]{:S(2)}) collective-permute-start(bf16[1024,128]{1,0:T(8,128)(2,1)S(1)} %get-tuple-element.92.refs_4_), channel_id=1, source_target_pairs={{0,24},{4,28},{8,16},{12,20},{16,8},{20,12},{24,0},{28,4},{1,25},{... | collective-permute-start | bytes 786440 | tf_op jit(solution)/shard_map/ppermute | solution.py:26
  83.4 24.3 %collective-permute-start.14 = (bf16[1024,128]{1,0:T(8,128)(2,1)S(1)}, bf16[1024,128]{1,0:T(8,128)(2,1)S(1)}, u32[]{:S(2)}, u32[]{:S(2)}) collective-permute-start(bf16[1024,128]{1,0:T(8,128)(2,1)S(1)} %get-tuple-element.92.refs_4_), channel_id=1, source_target_pairs={{0,16},{4,20},{8,24},{12,28},{16,0},{20,4},{24,8},{28,12},{1,17},{... | collective-permute-start | bytes 786440 | tf_op jit(solution)/shard_map/ppermute | solution.py:26
  107.8 20.2 %collective-permute-start.19 = (bf16[2,1024,128]{2,1,0:T(8,128)(2,1)S(1)}, bf16[2,1024,128]{2,1,0:T(8,128)(2,1)S(1)}, u32[]{:S(2)}, u32[]{:S(2)}) collective-permute-start(bf16[2,1024,128]{2,1,0:T(8,128)(2,1)S(1)} %pad_maximum_fusion.1), channel_id=1, source_target_pairs={{0,4},{4,0},{8,12},{12,8},{16,20},{20,16},{24,28},{28,24},{1,5},{5... | collective-permute-start | bytes 1572872 | tf_op jit(solution)/shard_map/ppermute | solution.py:26
  110.8 29.7 %collective-permute-start.25 = (bf16[2,512,128]{2,1,0:T(8,128)(2,1)S(1)}, bf16[2,512,128]{2,1,0:T(8,128)(2,1)S(1)}, u32[]{:S(2)}, u32[]{:S(2)}) collective-permute-start(bf16[2,512,128]{2,1,0:T(8,128)(2,1)S(1)} %pad_maximum_fusion.2), channel_id=1, source_target_pairs={{0,24},{4,28},{8,16},{12,20},{16,8},{20,12},{24,0},{28,4},{1,25},{... | collective-permute-start | bytes 786440 | tf_op jit(solution)/shard_map/ppermute | solution.py:26
  113.7 26.8 %collective-permute-start.24 = (bf16[2,512,128]{2,1,0:T(8,128)(2,1)S(1)}, bf16[2,512,128]{2,1,0:T(8,128)(2,1)S(1)}, u32[]{:S(2)}, u32[]{:S(2)}) collective-permute-start(bf16[2,512,128]{2,1,0:T(8,128)(2,1)S(1)} %pad_maximum_fusion.2), channel_id=1, source_target_pairs={{0,16},{4,20},{8,24},{12,28},{16,0},{20,4},{24,8},{28,12},{1,17},{... | collective-permute-start | bytes 786440 | tf_op jit(solution)/shard_map/ppermute | solution.py:26
  119.5 21.0 %collective-permute-start.23 = (f32[128,128]{1,0:T(8,128)S(1)}, f32[128,128]{1,0:T(8,128)S(1)}, u32[]{:S(2)}, u32[]{:S(2)}) collective-permute-start(f32[128,128]{1,0:T(8,128)S(1)} %add.51.refs_0_), channel_id=1, source_target_pairs={{0,24},{4,28},{8,16},{12,20},{16,8},{20,12},{24,0},{28,4},{1,25},{... | collective-permute-start | bytes 196616 | tf_op jit(solution)/shard_map/ppermute | solution.py:26
  120.4 20.0 %collective-permute-start.22 = (f32[128,128]{1,0:T(8,128)S(1)}, f32[128,128]{1,0:T(8,128)S(1)}, u32[]{:S(2)}, u32[]{:S(2)}) collective-permute-start(f32[128,128]{1,0:T(8,128)S(1)} %add.51.refs_0_), channel_id=1, source_target_pairs={{0,16},{4,20},{8,24},{12,28},{16,0},{20,4},{24,8},{28,12},{1,17},{... | collective-permute-start | bytes 196616 | tf_op jit(solution)/shard_map/ppermute | solution.py:26
  158.0 26.0 %collective-permute-start.29 = (s16[4,1040,128]{2,1,0:T(8,128)(2,1)S(1)}, s16[4,1040,128]{2,1,0:T(8,128)(2,1)S(1)}, u32[]{:S(2)}, u32[]{:S(2)}) collective-permute-start(s16[4,1040,128]{2,1,0:T(8,128)(2,1)S(1)} %shard_map.62), channel_id=1, source_target_pairs={{0,4},{4,0},{8,12},{12,8},{16,20},{20,16},{24,28},{28,24},{1,5},{5... | collective-permute-start | bytes 3194888 | tf_op jit(solution)/shard_map/ppermute | solution.py:26
  161.0 21.2 %collective-permute-start.31 = (s16[1040,128]{1,0:T(8,128)(2,1)S(1)}, s16[1040,128]{1,0:T(8,128)(2,1)S(1)}, u32[]{:S(2)}, u32[]{:S(2)}) collective-permute-start(s16[1040,128]{1,0:T(8,128)(2,1)S(1)} %get-tuple-element.109), channel_id=1, source_target_pairs={{0,16},{4,20},{8,24},{12,28},{16,0},{20,4},{24,8},{28,12},{1,17},{... | collective-permute-start | bytes 798728 | tf_op jit(solution)/shard_map/ppermute | solution.py:26
  162.4 19.8 %collective-permute-start.32 = (s16[1040,128]{1,0:T(8,128)(2,1)S(1)}, s16[1040,128]{1,0:T(8,128)(2,1)S(1)}, u32[]{:S(2)}, u32[]{:S(2)}) collective-permute-start(s16[1040,128]{1,0:T(8,128)(2,1)S(1)} %get-tuple-element.110), channel_id=1, source_target_pairs={{0,24},{4,28},{8,16},{12,20},{16,8},{20,12},{24,0},{28,4},{1,25},{... | collective-permute-start | bytes 798728 | tf_op jit(solution)/shard_map/ppermute | solution.py:26
  163.9 19.4 %collective-permute-start.30 = (s16[1040,128]{1,0:T(8,128)(2,1)S(1)}, s16[1040,128]{1,0:T(8,128)(2,1)S(1)}, u32[]{:S(2)}, u32[]{:S(2)}) collective-permute-start(s16[1040,128]{1,0:T(8,128)(2,1)S(1)} %get-tuple-element.108), channel_id=1, source_target_pairs={{0,8},{4,12},{8,0},{12,4},{16,24},{20,28},{24,16},{28,20},{1,9},{5... | collective-permute-start | bytes 798728 | tf_op jit(solution)/shard_map/ppermute | solution.py:26
  191.1 21.6 %collective-permute-start.34 = (s16[1040,128]{1,0:T(8,128)(2,1)S(1)}, s16[1040,128]{1,0:T(8,128)(2,1)S(1)}, u32[]{:S(2)}, u32[]{:S(2)}) collective-permute-start(s16[1040,128]{1,0:T(8,128)(2,1)S(1)} %get-tuple-element.116), channel_id=1, source_target_pairs={{0,16},{4,20},{8,24},{12,28},{16,0},{20,4},{24,8},{28,12},{1,17},{... | collective-permute-start | bytes 798728 | tf_op jit(solution)/shard_map/ppermute | solution.py:26
  192.0 20.8 %collective-permute-start.35 = (s16[1040,128]{1,0:T(8,128)(2,1)S(1)}, s16[1040,128]{1,0:T(8,128)(2,1)S(1)}, u32[]{:S(2)}, u32[]{:S(2)}) collective-permute-start(s16[1040,128]{1,0:T(8,128)(2,1)S(1)} %get-tuple-element.117), channel_id=1, source_target_pairs={{0,24},{4,28},{8,16},{12,20},{16,8},{20,12},{24,0},{28,4},{1,25},{... | collective-permute-start | bytes 798728 | tf_op jit(solution)/shard_map/ppermute | solution.py:26
  194.0 26.8 %collective-permute-start.39 = (s16[528,128]{1,0:T(8,128)(2,1)S(1)}, s16[528,128]{1,0:T(8,128)(2,1)S(1)}, u32[]{:S(2)}, u32[]{:S(2)}) collective-permute-start(s16[528,128]{1,0:T(8,128)(2,1)S(1)} %get-tuple-element.125), channel_id=1, source_target_pairs={{0,4},{4,0},{8,12},{12,8},{16,20},{20,16},{24,28},{28,24},{1,5},{5... | collective-permute-start | bytes 405512 | tf_op jit(solution)/shard_map/ppermute | solution.py:26
  220.7 20.9 %collective-permute-start.36 = (s16[1040,128]{1,0:T(8,128)(2,1)S(1)}, s16[1040,128]{1,0:T(8,128)(2,1)S(1)}, u32[]{:S(2)}, u32[]{:S(2)}) collective-permute-start(s16[1040,128]{1,0:T(8,128)(2,1)S(1)} %get-tuple-element.130.refs_0_), channel_id=1, source_target_pairs={{0,16},{4,20},{8,24},{12,28},{16,0},{20,4},{24,8},{28,12},{1,17},{... | collective-permute-start | bytes 798728 | tf_op jit(solution)/shard_map/ppermute | solution.py:26
  227.7 38.8 %collective-permute-start.47 = (s16[2,1040,128]{2,1,0:T(8,128)(2,1)S(1)}, s16[2,1040,128]{2,1,0:T(8,128)(2,1)S(1)}, u32[]{:S(2)}, u32[]{:S(2)}) collective-permute-start(s16[2,1040,128]{2,1,0:T(8,128)(2,1)S(1)} %pad_add_fusion), channel_id=1, source_target_pairs={{0,4},{4,0},{8,12},{12,8},{16,20},{20,16},{24,28},{28,24},{1,5},{5... | collective-permute-start | bytes 1597448 | tf_op jit(solution)/shard_map/ppermute | solution.py:26
  241.6 24.9 %collective-permute-start.48 = (s16[2,1040,128]{2,1,0:T(8,128)(2,1)S(1)}, s16[2,1040,128]{2,1,0:T(8,128)(2,1)S(1)}, u32[]{:S(2)}, u32[]{:S(2)}) collective-permute-start(s16[2,1040,128]{2,1,0:T(8,128)(2,1)S(1)} %pad_add_fusion.1), channel_id=1, source_target_pairs={{0,4},{4,0},{8,12},{12,8},{16,20},{20,16},{24,28},{28,24},{1,5},{5... | collective-permute-start | bytes 1597448 | tf_op jit(solution)/shard_map/ppermute | solution.py:26
  249.1 23.0 %collective-permute-start.51 = (s16[2,528,128]{2,1,0:T(8,128)(2,1)S(1)}, s16[2,528,128]{2,1,0:T(8,128)(2,1)S(1)}, u32[]{:S(2)}, u32[]{:S(2)}) collective-permute-start(s16[2,528,128]{2,1,0:T(8,128)(2,1)S(1)} %pad_add_fusion.2.refs_1_), channel_id=1, source_target_pairs={{0,24},{4,28},{8,16},{12,20},{16,8},{20,12},{24,0},{28,4},{1,25},{... | collective-permute-start | bytes 811016 | tf_op jit(solution)/shard_map/ppermute | solution.py:26
  (36 other events, 336.9 us)

commit v15 on v11

--- a/solution.py
+++ b/solution.py
@@ -450,7 +450,7 @@
                 add_all(code, [keep, got_send]),
             )
 
-        def gather(first, second, gram):
+        def gather(first, second, gram, near_first):
             far_in = [swap(first, mask=k * LOW) for k in far]
             near_in = [first] + [swap(first, mask=k * LOW) for k in near[1:]]
             got = swap(second, mask=1)
@@ -464,6 +464,10 @@
             low_near = swap(jnp.stack(near_in), mask=1)
             gram = gram + swap(gram, mask=1)
             far_in, pair, gram = lax.optimization_barrier((far_in, pair, gram))
+            if near_first:
+                low_near, far_in, pair, gram = lax.optimization_barrier(
+                    (low_near, far_in, pair, gram)
+                )
             low_far = swap(jnp.stack(far_in), mask=1)
             seconds = [pair] + [swap(pair, mask=k * LOW) for k in ks[1:]]
             gram = [gram] + [swap(gram, mask=k * LOW) for k in ks[1:]]
@@ -489,9 +493,11 @@
                 cost_estimate=LIGHT,
             )(lengths, block_subject, pos, mine, other, *factor)
 
-        def pass_over(scores, code):
+        def pass_over(scores, code, near_first):
             (first, gram_first), (second, gram_second) = sketch_sum(scores, code)
-            early, late, pairs, grams = gather(first, second, gram_first + gram_second)
+            early, late, pairs, grams = gather(
+                first, second, gram_first + gram_second, near_first
+            )
             inverse = small_call(
                 functools.partial(invert_kernel, all_voxels),
                 jax.ShapeDtypeStruct((rank, rank), F32), *grams,
@@ -499,7 +505,7 @@
             return early, late, pairs, inverse
 
         scores = sum_scores(*first_project(scans, pos, test_matrix))
-        early, late, pairs, inverse = pass_over(scores, Plain)
+        early, late, pairs, inverse = pass_over(scores, Plain, False)
         pairs = [(j, k, array.reshape(layout.pair, rank)) for j, k, array in pairs]
         total = project(scans, layout, pos, early)
         total = project(scans, layout, pos, late, total)
@@ -507,7 +513,7 @@
         total, inverse = lax.optimization_barrier((total, inverse))
         halves = project(scans, layout, pos, pairs[high // 2 :], total, True)
         scores = sum_scores(*halves, inverse)
-        early, late, pairs, inverse = pass_over(scores, Fixed)
+        early, late, pairs, inverse = pass_over(scores, Fixed, True)
         out = finish(layout, pos, early + late, inverse, voxels)
         return finish(layout, pos, pairs, inverse, voxels, out)
 

time: 273 us -> 293 us (1.073)
  waiting for transfers between devices: 115 us -> 129 us
  starting transfers between devices: 87.4 us -> 93.2 us
    ppermute x52, waiting for transfers between devices: 115 us -> 129 us  [exchange(): return lax.ppermute(value, axis, [(i, i ^ mask) for i in range(size)])]
    ppermute x52, starting transfers between devices: 87.4 us -> 93.2 us  [exchange(): return lax.ppermute(value, axis, [(i, i ^ mask) for i in range(size)])]
  transfers between devices with their start and end apart: 52 -> 52, of which waited for: 32 -> 31; matrix products, arithmetic and copies ran while one was open for 0% -> 0% of each run, Pallas kernels for 14% -> 13%
where the time goes in v15:
time: 293 us
  waiting for transfers between devices  129 us (44%)
  starting transfers between devices  93.2 us (32%)
  Pallas kernels  62 us (21%)
  local copies, waits for them, and re-layouts  7.37 us (3%)
    ppermute x52, waiting for transfers between devices, exchange(): return lax.ppermute(value, axis, [(i, i ^ mask) for i in range(size)])  129 us
    ppermute x52, starting transfers between devices, exchange(): return lax.ppermute(value, axis, [(i, i ^ mask) for i in range(size)])  93.2 us
    pallas_call x8, Pallas kernels, sketch_part(): pl.pallas_call(functools.partial(sketch_kernel, code, apart, per_step), o...  22.2 us
    pallas_call x8, Pallas kernels, small_call(): pl.pallas_call(kernel, out_shape=out_shape, in_specs=[WHOLE] * len(args),...  11.8 us
    pallas_call x2, Pallas kernels, finish(): pl.pallas_call(functools.partial(finish_kernel, layout, items, base is no...  9.12 us
    pallas_call x1, Pallas kernels, first_project(): pl.pallas_call(functools.partial(first_kernel, count), out_shape=[half, h...  8.72 us
    unnamed x10, local copies, waits for them, and re-layouts  7.37 us
    pallas_call x4, Pallas kernels, project(): pl.pallas_call(functools.partial(project_kernel, base is not None, split,...  6.92 us
  transfers between devices with their start and end apart: 52, of which 31 were waited for; matrix products, arithmetic and copies ran while one was open for 0% of the time, Pallas kernels for 13%

profile of v15, /device:TPU:0, one launch (start us, length us, event | category | flops | bytes accessed | tf_op | source)
XLA Modules:
  0.0 292.5 jit_solution(778952365180952245)
XLA Ops:
  2.0 8.7 %shard_map.46 = (f32[320,128]{1,0:T(8,128)S(1)}, f32[320,128]{1,0:T(8,128)S(1)}) custom-call(s32[3]{0:T(128)S(1)} %pad_add_fusion.3.pos_ref, bf16[12288,128]{1,0:T(8,128)(2,1)S(1)} %copy-done.2, bf16[640,12288]{1,0:T(8,128)(2,1)} %refs_0_.19, bf16[640,12288]{1,0:T(8,128)(2,1)} %refs_0_.19, bf16[640,12288]{1,0:T(8,128)(2,1)} %refs_0_.19, ...), custom_call_target="tpu_custom_call" | custom-call | flops 1 | bytes 1 | tf_op jit(solution)/shard_map/pallas_call | solution.py:206
  15.2 4.5 %collective-permute-done.1 = f32[320,128]{1,0:T(8,128)S(1)} collective-permute-done((f32[320,128]{1,0:T(8,128)S(1)}, f32[320,128]{1,0:T(8,128)S(1)}, u32[]{:S(2)}, u32[]{:S(2)}) %collective-permute-start.1) | collective-permute-done | bytes 163872 | tf_op jit(solution)/shard_map/ppermute | solution.py:25
  21.8 3.8 %shard_map.48 = bf16[4,1024,128]{2,1,0:T(8,128)(2,1)S(1)} custom-call(s32[3]{0:T(128)S(1)} %pad_add_fusion.3.pos_ref, bf16[640,128]{1,0:T(8,128)(2,1)S(1)} %shard_map.47.scores_ref, bf16[640,12288]{1,0:T(8,128)(2,1)} %refs_0_.19, bf16[640,12288]{1,0:T(8,128)(2,1)} %refs_0_.19), custom_call_target="tpu_custom_call" | custom-call | flops 1 | bytes 1 | tf_op jit(solution)/shard_map/pallas_call | solution.py:112
  37.6 4.0 %shard_map.50.own_ref = bf16[4,1024,128]{2,1,0:T(8,128)(2,1)S(1)} custom-call(s32[3]{0:T(128)S(1)} %pad_add_fusion.3.pos_ref, bf16[640,128]{1,0:T(8,128)(2,1)S(1)} %shard_map.47.scores_ref, bf16[640,12288]{1,0:T(8,128)(2,1)} %refs_0_.19, bf16[640,12288]{1,0:T(8,128)(2,1)} %refs_0_.19), custom_call_target="tpu_custom_call" | custom-call | flops 1 | bytes 1 | tf_op jit(solution)/shard_map/pallas_call | solution.py:112
  41.5 10.9 %collective-permute-done.5.refs_2_ = bf16[1024,128]{1,0:T(8,128)(2,1)S(1)} collective-permute-done((bf16[1024,128]{1,0:T(8,128)(2,1)S(1)}, bf16[1024,128]{1,0:T(8,128)(2,1)S(1)}, u32[]{:S(2)}, u32[]{:S(2)}) %collective-permute-start.5) | collective-permute-done | bytes 262176 | tf_op jit(solution)/shard_map/ppermute | solution.py:25
  52.9 5.0 %collective-permute-start.7 = (bf16[1024,128]{1,0:T(8,128)(2,1)S(1)}, bf16[1024,128]{1,0:T(8,128)(2,1)S(1)}, u32[]{:S(2)}, u32[]{:S(2)}) collective-permute-start(bf16[1024,128]{1,0:T(8,128)(2,1)S(1)} %get-tuple-element.82), channel_id=1, source_target_pairs={{0,8},{4,12},{8,0},{12,4},{16,24},{20,28},{24,16},{28,20},{1,9},{5... | collective-permute-start | bytes 786440 | tf_op jit(solution)/shard_map/ppermute | solution.py:25
  62.6 4.5 %collective-permute-done.11.refs_1_ = bf16[512,128]{1,0:T(8,128)(2,1)S(1)} collective-permute-done((bf16[512,128]{1,0:T(8,128)(2,1)S(1)}, bf16[512,128]{1,0:T(8,128)(2,1)S(1)}, u32[]{:S(2)}, u32[]{:S(2)}) %collective-permute-start.11) | collective-permute-done | bytes 131104 | tf_op jit(solution)/shard_map/ppermute | solution.py:25
  69.8 9.5 %collective-permute-done.8.refs_2_ = bf16[1024,128]{1,0:T(8,128)(2,1)S(1)} collective-permute-done((bf16[1024,128]{1,0:T(8,128)(2,1)S(1)}, bf16[1024,128]{1,0:T(8,128)(2,1)S(1)}, u32[]{:S(2)}, u32[]{:S(2)}) %collective-permute-start.8) | collective-permute-done | bytes 262176 | tf_op jit(solution)/shard_map/ppermute | solution.py:25
  83.4 12.5 %collective-permute-start.14 = (bf16[1024,128]{1,0:T(8,128)(2,1)S(1)}, bf16[1024,128]{1,0:T(8,128)(2,1)S(1)}, u32[]{:S(2)}, u32[]{:S(2)}) collective-permute-start(bf16[1024,128]{1,0:T(8,128)(2,1)S(1)} %get-tuple-element.94.refs_4_), channel_id=1, source_target_pairs={{0,16},{4,20},{8,24},{12,28},{16,0},{20,4},{24,8},{28,12},{1,17},{... | collective-permute-start | bytes 786440 | tf_op jit(solution)/shard_map/ppermute | solution.py:25
  117.3 6.4 %collective-permute-start.25 = (bf16[2,512,128]{2,1,0:T(8,128)(2,1)S(1)}, bf16[2,512,128]{2,1,0:T(8,128)(2,1)S(1)}, u32[]{:S(2)}, u32[]{:S(2)}) collective-permute-start(bf16[2,512,128]{2,1,0:T(8,128)(2,1)S(1)} %pad_maximum_fusion.2), channel_id=1, source_target_pairs={{0,24},{4,28},{8,16},{12,20},{16,8},{20,12},{24,0},{28,4},{1,25},{... | collective-permute-start | bytes 786440 | tf_op jit(solution)/shard_map/ppermute | solution.py:25
  123.7 5.5 %copy-done = bf16[640,12288]{1,0:T(8,128)(2,1)S(1)} copy-done((bf16[640,12288]{1,0:T(8,128)(2,1)S(1)}, bf16[640,12288]{1,0:T(8,128)(2,1)}, u32[]{:S(2)}) %copy-start) | copy-done | bytes 15728664
  131.2 4.1 %shard_map.59.refs_0_ = f32[128,128]{1,0:T(8,128)S(1)} custom-call(f32[128,128]{1,0:T(8,128)S(1)} %add.51.refs_0_, f32[128,128]{1,0:T(8,128)S(1)} %collective-permute-done.21.refs_1_, f32[128,128]{1,0:T(8,128)S(1)} %collective-permute-done.22.refs_2_, f32[128,128]{1,0:T(8,128)S(1)} %collective-permute-done.23.refs_3_), custom_call_target="tpu_custom_call" | custom-call | flops 1 | bytes 1 | tf_op jit(solution)/shard_map/pallas_call | solution.py:128
  143.4 4.7 %collective-permute-done.27 = f32[320,128]{1,0:T(8,128)S(1)} collective-permute-done((f32[320,128]{1,0:T(8,128)S(1)}, f32[320,128]{1,0:T(8,128)S(1)}, u32[]{:S(2)}, u32[]{:S(2)}) %collective-permute-start.27) | collective-permute-done | bytes 163872 | tf_op jit(solution)/shard_map/ppermute | solution.py:25
  164.5 13.2 %collective-permute-done.31.refs_2_ = s16[1040,128]{1,0:T(8,128)(2,1)S(1)} collective-permute-done((s16[1040,128]{1,0:T(8,128)(2,1)S(1)}, s16[1040,128]{1,0:T(8,128)(2,1)S(1)}, u32[]{:S(2)}, u32[]{:S(2)}) %collective-permute-start.31) | collective-permute-done | bytes 266272 | tf_op jit(solution)/shard_map/ppermute | solution.py:25
  180.2 4.7 %collective-permute-start.33 = (s16[1040,128]{1,0:T(8,128)(2,1)S(1)}, s16[1040,128]{1,0:T(8,128)(2,1)S(1)}, u32[]{:S(2)}, u32[]{:S(2)}) collective-permute-start(s16[1040,128]{1,0:T(8,128)(2,1)S(1)} %get-tuple-element.114), channel_id=1, source_target_pairs={{0,8},{4,12},{8,0},{12,4},{16,24},{20,28},{24,16},{28,20},{1,9},{5... | collective-permute-start | bytes 798728 | tf_op jit(solution)/shard_map/ppermute | solution.py:25
  189.1 7.0 %collective-permute-done.33.refs_1_ = s16[1040,128]{1,0:T(8,128)(2,1)S(1)} collective-permute-done((s16[1040,128]{1,0:T(8,128)(2,1)S(1)}, s16[1040,128]{1,0:T(8,128)(2,1)S(1)}, u32[]{:S(2)}, u32[]{:S(2)}) %collective-permute-start.33) | collective-permute-done | bytes 266272 | tf_op jit(solution)/shard_map/ppermute | solution.py:25
  196.1 10.4 %collective-permute-done.34.refs_2_ = s16[1040,128]{1,0:T(8,128)(2,1)S(1)} collective-permute-done((s16[1040,128]{1,0:T(8,128)(2,1)S(1)}, s16[1040,128]{1,0:T(8,128)(2,1)S(1)}, u32[]{:S(2)}, u32[]{:S(2)}) %collective-permute-start.34) | collective-permute-done | bytes 266272 | tf_op jit(solution)/shard_map/ppermute | solution.py:25
  207.4 5.1 %collective-permute-start.36 = (s16[1040,128]{1,0:T(8,128)(2,1)S(1)}, s16[1040,128]{1,0:T(8,128)(2,1)S(1)}, u32[]{:S(2)}, u32[]{:S(2)}) collective-permute-start(s16[1040,128]{1,0:T(8,128)(2,1)S(1)} %get-tuple-element.126.refs_0_), channel_id=1, source_target_pairs={{0,8},{4,12},{8,0},{12,4},{16,24},{20,28},{24,16},{28,20},{1,9},{5... | collective-permute-start | bytes 798728 | tf_op jit(solution)/shard_map/ppermute | solution.py:25
  223.4 11.6 %collective-permute-done.43 = s16[528,128]{1,0:T(8,128)(2,1)S(1)} collective-permute-done((s16[528,128]{1,0:T(8,128)(2,1)S(1)}, s16[528,128]{1,0:T(8,128)(2,1)S(1)}, u32[]{:S(2)}, u32[]{:S(2)}) %collective-permute-start.43) | collective-permute-done | bytes 135200 | tf_op jit(solution)/shard_map/ppermute | solution.py:25
  239.4 5.9 %collective-permute-done.41.refs_2_ = s16[1040,128]{1,0:T(8,128)(2,1)S(1)} collective-permute-done((s16[1040,128]{1,0:T(8,128)(2,1)S(1)}, s16[1040,128]{1,0:T(8,128)(2,1)S(1)}, u32[]{:S(2)}, u32[]{:S(2)}) %collective-permute-start.41) | collective-permute-done | bytes 266272 | tf_op jit(solution)/shard_map/ppermute | solution.py:25
  251.2 14.6 %collective-permute-done.47.refs_3_ = f32[128,128]{1,0:T(8,128)S(1)} collective-permute-done((f32[128,128]{1,0:T(8,128)S(1)}, f32[128,128]{1,0:T(8,128)S(1)}, u32[]{:S(2)}, u32[]{:S(2)}) %collective-permute-start.47) | collective-permute-done | bytes 65568 | tf_op jit(solution)/shard_map/ppermute | solution.py:25
  265.8 5.8 %collective-permute-start.46 = (f32[128,128]{1,0:T(8,128)S(1)}, f32[128,128]{1,0:T(8,128)S(1)}, u32[]{:S(2)}, u32[]{:S(2)}) collective-permute-start(f32[128,128]{1,0:T(8,128)S(1)} %add.57.refs_0_), channel_id=1, source_target_pairs={{0,16},{4,20},{8,24},{12,28},{16,0},{20,4},{24,8},{28,12},{1,17},{... | collective-permute-start | bytes 196616 | tf_op jit(solution)/shard_map/ppermute | solution.py:25
  279.1 4.1 %shard_map.70.inverse_ref = f32[128,128]{1,0:T(8,128)S(1)} custom-call(f32[128,128]{1,0:T(8,128)S(1)} %add.57.refs_0_, f32[128,128]{1,0:T(8,128)S(1)} %collective-permute-done.45.refs_1_, f32[128,128]{1,0:T(8,128)S(1)} %collective-permute-done.46.refs_2_, f32[128,128]{1,0:T(8,128)S(1)} %collective-permute-done.47.refs_3_), custom_call_target="tpu_custom_call" | custom-call | flops 1 | bytes 1 | tf_op jit(solution)/shard_map/pallas_call | solution.py:128
  283.2 5.5 %shard_map.71.refs_0_ = f32[12288,128]{1,0:T(8,128)} custom-call(s32[3]{0:T(128)S(1)} %pad_add_fusion.3.pos_ref, f32[128,128]{1,0:T(8,128)S(1)} %shard_map.70.inverse_ref, s16[1040,128]{1,0:T(8,128)(2,1)S(1)} %get-tuple-element.126.refs_0_, s16[1040,128]{1,0:T(8,128)(2,1)S(1)} %collective-permute-done.36.refs_1_, ...), custom_call_target="tpu_custom_call" | custom-call | tf_op jit(solution)/shard_map/pallas_call | solution.py:310
  (138 shorter events, 120.0 us)
Async XLA Ops:
  25.6 27.0 %collective-permute-start.3 = (bf16[4,1024,128]{2,1,0:T(8,128)(2,1)S(1)}, bf16[4,1024,128]{2,1,0:T(8,128)(2,1)S(1)}, u32[]{:S(2)}, u32[]{:S(2)}) collective-permute-start(bf16[4,1024,128]{2,1,0:T(8,128)(2,1)S(1)} %shard_map.48), channel_id=1, source_target_pairs={{0,4},{4,0},{8,12},{12,8},{16,20},{20,16},{24,28},{28,24},{1,5},{5... | collective-permute-start | bytes 3145736 | tf_op jit(solution)/shard_map/ppermute | solution.py:25
  31.0 21.4 %collective-permute-start.5 = (bf16[1024,128]{1,0:T(8,128)(2,1)S(1)}, bf16[1024,128]{1,0:T(8,128)(2,1)S(1)}, u32[]{:S(2)}, u32[]{:S(2)}) collective-permute-start(bf16[1024,128]{1,0:T(8,128)(2,1)S(1)} %get-tuple-element.76), channel_id=1, source_target_pairs={{0,16},{4,20},{8,24},{12,28},{16,0},{20,4},{24,8},{28,12},{1,17},{... | collective-permute-start | bytes 786440 | tf_op jit(solution)/shard_map/ppermute | solution.py:25
  33.6 18.8 %collective-permute-start.6 = (bf16[1024,128]{1,0:T(8,128)(2,1)S(1)}, bf16[1024,128]{1,0:T(8,128)(2,1)S(1)}, u32[]{:S(2)}, u32[]{:S(2)}) collective-permute-start(bf16[1024,128]{1,0:T(8,128)(2,1)S(1)} %get-tuple-element.77), channel_id=1, source_target_pairs={{0,24},{4,28},{8,16},{12,20},{16,8},{20,12},{24,0},{28,4},{1,25},{... | collective-permute-start | bytes 786440 | tf_op jit(solution)/shard_map/ppermute | solution.py:25
  57.9 21.3 %collective-permute-start.8 = (bf16[1024,128]{1,0:T(8,128)(2,1)S(1)}, bf16[1024,128]{1,0:T(8,128)(2,1)S(1)}, u32[]{:S(2)}, u32[]{:S(2)}) collective-permute-start(bf16[1024,128]{1,0:T(8,128)(2,1)S(1)} %get-tuple-element.83), channel_id=1, source_target_pairs={{0,16},{4,20},{8,24},{12,28},{16,0},{20,4},{24,8},{28,12},{1,17},{... | collective-permute-start | bytes 786440 | tf_op jit(solution)/shard_map/ppermute | solution.py:25
  59.9 19.3 %collective-permute-start.9 = (bf16[1024,128]{1,0:T(8,128)(2,1)S(1)}, bf16[1024,128]{1,0:T(8,128)(2,1)S(1)}, u32[]{:S(2)}, u32[]{:S(2)}) collective-permute-start(bf16[1024,128]{1,0:T(8,128)(2,1)S(1)} %get-tuple-element.84), channel_id=1, source_target_pairs={{0,24},{4,28},{8,16},{12,20},{16,8},{20,12},{24,0},{28,4},{1,25},{... | collective-permute-start | bytes 786440 | tf_op jit(solution)/shard_map/ppermute | solution.py:25
  67.4 29.0 %collective-permute-start.16 = (bf16[512,128]{1,0:T(8,128)(2,1)S(1)}, bf16[512,128]{1,0:T(8,128)(2,1)S(1)}, u32[]{:S(2)}, u32[]{:S(2)}) collective-permute-start(bf16[512,128]{1,0:T(8,128)(2,1)S(1)} %get-tuple-element.96), channel_id=1, source_target_pairs={{0,4},{4,0},{8,12},{12,8},{16,20},{20,16},{24,28},{28,24},{1,5},{5... | collective-permute-start | bytes 393224 | tf_op jit(solution)/shard_map/ppermute | solution.py:25
  79.9 27.8 %collective-permute-start.15 = (bf16[1024,128]{1,0:T(8,128)(2,1)S(1)}, bf16[1024,128]{1,0:T(8,128)(2,1)S(1)}, u32[]{:S(2)}, u32[]{:S(2)}) collective-permute-start(bf16[1024,128]{1,0:T(8,128)(2,1)S(1)} %get-tuple-element.94.refs_4_), channel_id=1, source_target_pairs={{0,24},{4,28},{8,16},{12,20},{16,8},{20,12},{24,0},{28,4},{1,25},{... | collective-permute-start | bytes 786440 | tf_op jit(solution)/shard_map/ppermute | solution.py:25
  83.4 24.3 %collective-permute-start.14 = (bf16[1024,128]{1,0:T(8,128)(2,1)S(1)}, bf16[1024,128]{1,0:T(8,128)(2,1)S(1)}, u32[]{:S(2)}, u32[]{:S(2)}) collective-permute-start(bf16[1024,128]{1,0:T(8,128)(2,1)S(1)} %get-tuple-element.94.refs_4_), channel_id=1, source_target_pairs={{0,16},{4,20},{8,24},{12,28},{16,0},{20,4},{24,8},{28,12},{1,17},{... | collective-permute-start | bytes 786440 | tf_op jit(solution)/shard_map/ppermute | solution.py:25
  103.2 32.1 %collective-permute-start.18 = (bf16[2,1024,128]{2,1,0:T(8,128)(2,1)S(1)}, bf16[2,1024,128]{2,1,0:T(8,128)(2,1)S(1)}, u32[]{:S(2)}, u32[]{:S(2)}) collective-permute-start(bf16[2,1024,128]{2,1,0:T(8,128)(2,1)S(1)} %pad_maximum_fusion), channel_id=1, source_target_pairs={{0,4},{4,0},{8,12},{12,8},{16,20},{20,16},{24,28},{28,24},{1,5},{5... | collective-permute-start | bytes 1572872 | tf_op jit(solution)/shard_map/ppermute | solution.py:25
  107.8 27.6 %collective-permute-start.19 = (bf16[2,1024,128]{2,1,0:T(8,128)(2,1)S(1)}, bf16[2,1024,128]{2,1,0:T(8,128)(2,1)S(1)}, u32[]{:S(2)}, u32[]{:S(2)}) collective-permute-start(bf16[2,1024,128]{2,1,0:T(8,128)(2,1)S(1)} %pad_maximum_fusion.1), channel_id=1, source_target_pairs={{0,4},{4,0},{8,12},{12,8},{16,20},{20,16},{24,28},{28,24},{1,5},{5... | collective-permute-start | bytes 1572872 | tf_op jit(solution)/shard_map/ppermute | solution.py:25
  115.0 22.4 %collective-permute-start.20 = (bf16[2,512,128]{2,1,0:T(8,128)(2,1)S(1)}, bf16[2,512,128]{2,1,0:T(8,128)(2,1)S(1)}, u32[]{:S(2)}, u32[]{:S(2)}) collective-permute-start(bf16[2,512,128]{2,1,0:T(8,128)(2,1)S(1)} %pad_maximum_fusion.2), channel_id=1, source_target_pairs={{0,8},{4,12},{8,0},{12,4},{16,24},{20,28},{24,16},{28,20},{1,9},{5... | collective-permute-start | bytes 786440 | tf_op jit(solution)/shard_map/ppermute | solution.py:25
  117.3 21.5 %collective-permute-start.25 = (bf16[2,512,128]{2,1,0:T(8,128)(2,1)S(1)}, bf16[2,512,128]{2,1,0:T(8,128)(2,1)S(1)}, u32[]{:S(2)}, u32[]{:S(2)}) collective-permute-start(bf16[2,512,128]{2,1,0:T(8,128)(2,1)S(1)} %pad_maximum_fusion.2), channel_id=1, source_target_pairs={{0,24},{4,28},{8,16},{12,20},{16,8},{20,12},{24,0},{28,4},{1,25},{... | collective-permute-start | bytes 786440 | tf_op jit(solution)/shard_map/ppermute | solution.py:25
  153.6 25.6 %collective-permute-start.29 = (s16[4,1040,128]{2,1,0:T(8,128)(2,1)S(1)}, s16[4,1040,128]{2,1,0:T(8,128)(2,1)S(1)}, u32[]{:S(2)}, u32[]{:S(2)}) collective-permute-start(s16[4,1040,128]{2,1,0:T(8,128)(2,1)S(1)} %shard_map.62), channel_id=1, source_target_pairs={{0,4},{4,0},{8,12},{12,8},{16,20},{20,16},{24,28},{28,24},{1,5},{5... | collective-permute-start | bytes 3194888 | tf_op jit(solution)/shard_map/ppermute | solution.py:25
  157.0 20.7 %collective-permute-start.31 = (s16[1040,128]{1,0:T(8,128)(2,1)S(1)}, s16[1040,128]{1,0:T(8,128)(2,1)S(1)}, u32[]{:S(2)}, u32[]{:S(2)}) collective-permute-start(s16[1040,128]{1,0:T(8,128)(2,1)S(1)} %get-tuple-element.108), channel_id=1, source_target_pairs={{0,16},{4,20},{8,24},{12,28},{16,0},{20,4},{24,8},{28,12},{1,17},{... | collective-permute-start | bytes 798728 | tf_op jit(solution)/shard_map/ppermute | solution.py:25
  159.9 19.2 %collective-permute-start.30 = (s16[1040,128]{1,0:T(8,128)(2,1)S(1)}, s16[1040,128]{1,0:T(8,128)(2,1)S(1)}, u32[]{:S(2)}, u32[]{:S(2)}) collective-permute-start(s16[1040,128]{1,0:T(8,128)(2,1)S(1)} %get-tuple-element.107), channel_id=1, source_target_pairs={{0,8},{4,12},{8,0},{12,4},{16,24},{20,28},{24,16},{28,20},{1,9},{5... | collective-permute-start | bytes 798728 | tf_op jit(solution)/shard_map/ppermute | solution.py:25
  184.9 21.6 %collective-permute-start.34 = (s16[1040,128]{1,0:T(8,128)(2,1)S(1)}, s16[1040,128]{1,0:T(8,128)(2,1)S(1)}, u32[]{:S(2)}, u32[]{:S(2)}) collective-permute-start(s16[1040,128]{1,0:T(8,128)(2,1)S(1)} %get-tuple-element.115), channel_id=1, source_target_pairs={{0,16},{4,20},{8,24},{12,28},{16,0},{20,4},{24,8},{28,12},{1,17},{... | collective-permute-start | bytes 798728 | tf_op jit(solution)/shard_map/ppermute | solution.py:25
  186.2 20.4 %collective-permute-start.35 = (s16[1040,128]{1,0:T(8,128)(2,1)S(1)}, s16[1040,128]{1,0:T(8,128)(2,1)S(1)}, u32[]{:S(2)}, u32[]{:S(2)}) collective-permute-start(s16[1040,128]{1,0:T(8,128)(2,1)S(1)} %get-tuple-element.116), channel_id=1, source_target_pairs={{0,24},{4,28},{8,16},{12,20},{16,8},{20,12},{24,0},{28,4},{1,25},{... | collective-permute-start | bytes 798728 | tf_op jit(solution)/shard_map/ppermute | solution.py:25
  188.5 24.0 %collective-permute-start.37 = (s16[528,128]{1,0:T(8,128)(2,1)S(1)}, s16[528,128]{1,0:T(8,128)(2,1)S(1)}, u32[]{:S(2)}, u32[]{:S(2)}) collective-permute-start(s16[528,128]{1,0:T(8,128)(2,1)S(1)} %get-tuple-element.124), channel_id=1, source_target_pairs={{0,4},{4,0},{8,12},{12,8},{16,20},{20,16},{24,28},{28,24},{1,5},{5... | collective-permute-start | bytes 405512 | tf_op jit(solution)/shard_map/ppermute | solution.py:25
  218.7 26.6 %collective-permute-start.40 = (s16[2,1040,128]{2,1,0:T(8,128)(2,1)S(1)}, s16[2,1040,128]{2,1,0:T(8,128)(2,1)S(1)}, u32[]{:S(2)}, u32[]{:S(2)}) collective-permute-start(s16[2,1040,128]{2,1,0:T(8,128)(2,1)S(1)} %pad_add_fusion), channel_id=1, source_target_pairs={{0,4},{4,0},{8,12},{12,8},{16,20},{20,16},{24,28},{28,24},{1,5},{5... | collective-permute-start | bytes 1597448 | tf_op jit(solution)/shard_map/ppermute | solution.py:25
  222.4 22.9 %collective-permute-start.41 = (s16[1040,128]{1,0:T(8,128)(2,1)S(1)}, s16[1040,128]{1,0:T(8,128)(2,1)S(1)}, u32[]{:S(2)}, u32[]{:S(2)}) collective-permute-start(s16[1040,128]{1,0:T(8,128)(2,1)S(1)} %get-tuple-element.126.refs_0_), channel_id=1, source_target_pairs={{0,16},{4,20},{8,24},{12,28},{16,0},{20,4},{24,8},{28,12},{1,17},{... | collective-permute-start | bytes 798728 | tf_op jit(solution)/shard_map/ppermute | solution.py:25
  245.3 37.9 %collective-permute-start.48 = (s16[2,1040,128]{2,1,0:T(8,128)(2,1)S(1)}, s16[2,1040,128]{2,1,0:T(8,128)(2,1)S(1)}, u32[]{:S(2)}, u32[]{:S(2)}) collective-permute-start(s16[2,1040,128]{2,1,0:T(8,128)(2,1)S(1)} %pad_add_fusion.1), channel_id=1, source_target_pairs={{0,4},{4,0},{8,12},{12,8},{16,20},{20,16},{24,28},{28,24},{1,5},{5... | collective-permute-start | bytes 1597448 | tf_op jit(solution)/shard_map/ppermute | solution.py:25
  245.4 43.3 %collective-permute-start.51 = (s16[2,528,128]{2,1,0:T(8,128)(2,1)S(1)}, s16[2,528,128]{2,1,0:T(8,128)(2,1)S(1)}, u32[]{:S(2)}, u32[]{:S(2)}) collective-permute-start(s16[2,528,128]{2,1,0:T(8,128)(2,1)S(1)} %pad_add_fusion.2.refs_1_), channel_id=1, source_target_pairs={{0,24},{4,28},{8,16},{12,20},{16,8},{20,12},{24,0},{28,4},{1,25},{... | collective-permute-start | bytes 811016 | tf_op jit(solution)/shard_map/ppermute | solution.py:25
  246.8 41.9 %collective-permute-start.50 = (s16[2,528,128]{2,1,0:T(8,128)(2,1)S(1)}, s16[2,528,128]{2,1,0:T(8,128)(2,1)S(1)}, u32[]{:S(2)}, u32[]{:S(2)}) collective-permute-start(s16[2,528,128]{2,1,0:T(8,128)(2,1)S(1)} %pad_add_fusion.2.refs_1_), channel_id=1, source_target_pairs={{0,16},{4,20},{8,24},{12,28},{16,0},{20,4},{24,8},{28,12},{1,17},{... | collective-permute-start | bytes 811016 | tf_op jit(solution)/shard_map/ppermute | solution.py:25
  246.8 41.9 %collective-permute-start.49 = (s16[2,528,128]{2,1,0:T(8,128)(2,1)S(1)}, s16[2,528,128]{2,1,0:T(8,128)(2,1)S(1)}, u32[]{:S(2)}, u32[]{:S(2)}) collective-permute-start(s16[2,528,128]{2,1,0:T(8,128)(2,1)S(1)} %pad_add_fusion.2.refs_1_), channel_id=1, source_target_pairs={{0,8},{4,12},{8,0},{12,4},{16,24},{20,28},{24,16},{28,20},{1,9},{5... | collective-permute-start | bytes 811016 | tf_op jit(solution)/shard_map/ppermute | solution.py:25
  (33 other events, 286.7 us)

commit v16 on v11

--- a/solution.py
+++ b/solution.py
@@ -508,8 +508,8 @@
         halves = project(scans, layout, pos, pairs[high // 2 :], total, True)
         scores = sum_scores(*halves, inverse)
         early, late, pairs, inverse = pass_over(scores, Fixed)
-        out = finish(layout, pos, early + late, inverse, voxels)
-        return finish(layout, pos, pairs, inverse, voxels, out)
+        out = finish(layout, pos, early + late + pairs[:1], inverse, voxels)
+        return finish(layout, pos, pairs[1:], inverse, voxels, out)
 
     return on_device
 

time: 273 us -> 272 us (level)
  no operation moved by 1% of the time
where the time goes in v16:
time: 272 us
  waiting for transfers between devices  114 us (42%)
  starting transfers between devices  87.4 us (32%)
  Pallas kernels  61.8 us (23%)
  local copies, waits for them, and re-layouts  7.37 us (3%)
    ppermute x52, waiting for transfers between devices, exchange(): return lax.ppermute(value, axis, [(i, i ^ mask) for i in range(size)])  114 us
    ppermute x52, starting transfers between devices, exchange(): return lax.ppermute(value, axis, [(i, i ^ mask) for i in range(size)])  87.4 us
    pallas_call x8, Pallas kernels, sketch_part(): pl.pallas_call(functools.partial(sketch_kernel, code, apart, per_step), o...  22.2 us
    pallas_call x8, Pallas kernels, small_call(): pl.pallas_call(kernel, out_shape=out_shape, in_specs=[WHOLE] * len(args),...  11.8 us
    pallas_call x2, Pallas kernels, finish(): pl.pallas_call(functools.partial(finish_kernel, layout, items, base is no...  8.98 us
    pallas_call x1, Pallas kernels, first_project(): pl.pallas_call(functools.partial(first_kernel, count), out_shape=[half, h...  8.72 us
    unnamed x10, local copies, waits for them, and re-layouts  7.37 us
    pallas_call x4, Pallas kernels, project(): pl.pallas_call(functools.partial(project_kernel, base is not None, split,...  6.92 us
  transfers between devices with their start and end apart: 52, of which 32 were waited for; matrix products, arithmetic and copies ran while one was open for 0% of the time, Pallas kernels for 14%

profile of v16, /device:TPU:0, one launch (start us, length us, event | category | flops | bytes accessed | tf_op | source)
XLA Modules:
  0.0 272.0 jit_solution(2685052313137741065)
XLA Ops:
  2.0 8.7 %shard_map.46 = (f32[320,128]{1,0:T(8,128)S(1)}, f32[320,128]{1,0:T(8,128)S(1)}) custom-call(s32[3]{0:T(128)S(1)} %pad_add_fusion.3.pos_ref, bf16[12288,128]{1,0:T(8,128)(2,1)S(1)} %copy-done.2, bf16[640,12288]{1,0:T(8,128)(2,1)} %refs_0_.19, bf16[640,12288]{1,0:T(8,128)(2,1)} %refs_0_.19, bf16[640,12288]{1,0:T(8,128)(2,1)} %refs_0_.19, ...), custom_call_target="tpu_custom_call" | custom-call | flops 1 | bytes 1 | tf_op jit(solution)/shard_map/pallas_call | solution.py:206
  15.2 4.5 %collective-permute-done.1 = f32[320,128]{1,0:T(8,128)S(1)} collective-permute-done((f32[320,128]{1,0:T(8,128)S(1)}, f32[320,128]{1,0:T(8,128)S(1)}, u32[]{:S(2)}, u32[]{:S(2)}) %collective-permute-start.1) | collective-permute-done | bytes 163872 | tf_op jit(solution)/shard_map/ppermute | solution.py:25
  21.8 3.8 %shard_map.48 = bf16[4,1024,128]{2,1,0:T(8,128)(2,1)S(1)} custom-call(s32[3]{0:T(128)S(1)} %pad_add_fusion.3.pos_ref, bf16[640,128]{1,0:T(8,128)(2,1)S(1)} %shard_map.47.scores_ref, bf16[640,12288]{1,0:T(8,128)(2,1)} %refs_0_.19, bf16[640,12288]{1,0:T(8,128)(2,1)} %refs_0_.19), custom_call_target="tpu_custom_call" | custom-call | flops 1 | bytes 1 | tf_op jit(solution)/shard_map/pallas_call | solution.py:112
  27.4 3.5 %shard_map.49 = (bf16[1024,128]{1,0:T(8,128)(2,1)S(1)}, bf16[1024,128]{1,0:T(8,128)(2,1)S(1)}, bf16[1024,128]{1,0:T(8,128)(2,1)S(1)}) custom-call(s32[3]{0:T(128)S(1)} %pad_add_fusion.3.pos_ref, bf16[640,128]{1,0:T(8,128)(2,1)S(1)} %shard_map.47.scores_ref, bf16[640,12288]{1,0:T(8,128)(2,1)} %refs_0_.19, bf16[640,12288]{1,0:T(8,128)(2,1)} %refs_0_.19, ...), custom_call_target="tpu_custom_call" | custom-call | flops 1 | bytes 1 | tf_op jit(solution)/shard_map/pallas_call | solution.py:112
  37.6 4.0 %shard_map.50.own_ref = bf16[4,1024,128]{2,1,0:T(8,128)(2,1)S(1)} custom-call(s32[3]{0:T(128)S(1)} %pad_add_fusion.3.pos_ref, bf16[640,128]{1,0:T(8,128)(2,1)S(1)} %shard_map.47.scores_ref, bf16[640,12288]{1,0:T(8,128)(2,1)} %refs_0_.19, bf16[640,12288]{1,0:T(8,128)(2,1)} %refs_0_.19), custom_call_target="tpu_custom_call" | custom-call | flops 1 | bytes 1 | tf_op jit(solution)/shard_map/pallas_call | solution.py:112
  41.5 10.9 %collective-permute-done.5.refs_2_ = bf16[1024,128]{1,0:T(8,128)(2,1)S(1)} collective-permute-done((bf16[1024,128]{1,0:T(8,128)(2,1)S(1)}, bf16[1024,128]{1,0:T(8,128)(2,1)S(1)}, u32[]{:S(2)}, u32[]{:S(2)}) %collective-permute-start.5) | collective-permute-done | bytes 262176 | tf_op jit(solution)/shard_map/ppermute | solution.py:25
  52.9 5.0 %collective-permute-start.7 = (bf16[1024,128]{1,0:T(8,128)(2,1)S(1)}, bf16[1024,128]{1,0:T(8,128)(2,1)S(1)}, u32[]{:S(2)}, u32[]{:S(2)}) collective-permute-start(bf16[1024,128]{1,0:T(8,128)(2,1)S(1)} %get-tuple-element.77), channel_id=1, source_target_pairs={{0,8},{4,12},{8,0},{12,4},{16,24},{20,28},{24,16},{28,20},{1,9},{5... | collective-permute-start | bytes 786440 | tf_op jit(solution)/shard_map/ppermute | solution.py:25
  62.6 4.5 %collective-permute-done.11.refs_1_ = bf16[512,128]{1,0:T(8,128)(2,1)S(1)} collective-permute-done((bf16[512,128]{1,0:T(8,128)(2,1)S(1)}, bf16[512,128]{1,0:T(8,128)(2,1)S(1)}, u32[]{:S(2)}, u32[]{:S(2)}) %collective-permute-start.11) | collective-permute-done | bytes 131104 | tf_op jit(solution)/shard_map/ppermute | solution.py:25
  69.8 9.5 %collective-permute-done.8.refs_2_ = bf16[1024,128]{1,0:T(8,128)(2,1)S(1)} collective-permute-done((bf16[1024,128]{1,0:T(8,128)(2,1)S(1)}, bf16[1024,128]{1,0:T(8,128)(2,1)S(1)}, u32[]{:S(2)}, u32[]{:S(2)}) %collective-permute-start.8) | collective-permute-done | bytes 262176 | tf_op jit(solution)/shard_map/ppermute | solution.py:25
  83.4 12.5 %collective-permute-start.14 = (bf16[1024,128]{1,0:T(8,128)(2,1)S(1)}, bf16[1024,128]{1,0:T(8,128)(2,1)S(1)}, u32[]{:S(2)}, u32[]{:S(2)}) collective-permute-start(bf16[1024,128]{1,0:T(8,128)(2,1)S(1)} %get-tuple-element.89.refs_4_), channel_id=1, source_target_pairs={{0,16},{4,20},{8,24},{12,28},{16,0},{20,4},{24,8},{28,12},{1,17},{... | collective-permute-start | bytes 786440 | tf_op jit(solution)/shard_map/ppermute | solution.py:25
  117.3 6.4 %collective-permute-start.25 = (bf16[2,512,128]{2,1,0:T(8,128)(2,1)S(1)}, bf16[2,512,128]{2,1,0:T(8,128)(2,1)S(1)}, u32[]{:S(2)}, u32[]{:S(2)}) collective-permute-start(bf16[2,512,128]{2,1,0:T(8,128)(2,1)S(1)} %pad_maximum_fusion.2), channel_id=1, source_target_pairs={{0,24},{4,28},{8,16},{12,20},{16,8},{20,12},{24,0},{28,4},{1,25},{... | collective-permute-start | bytes 786440 | tf_op jit(solution)/shard_map/ppermute | solution.py:25
  123.7 5.5 %copy-done = bf16[640,12288]{1,0:T(8,128)(2,1)S(1)} copy-done((bf16[640,12288]{1,0:T(8,128)(2,1)S(1)}, bf16[640,12288]{1,0:T(8,128)(2,1)}, u32[]{:S(2)}) %copy-start) | copy-done | bytes 15728664
  131.2 4.1 %shard_map.59.refs_0_ = f32[128,128]{1,0:T(8,128)S(1)} custom-call(f32[128,128]{1,0:T(8,128)S(1)} %add.51.refs_0_, f32[128,128]{1,0:T(8,128)S(1)} %collective-permute-done.21.refs_1_, f32[128,128]{1,0:T(8,128)S(1)} %collective-permute-done.22.refs_2_, f32[128,128]{1,0:T(8,128)S(1)} %collective-permute-done.23.refs_3_), custom_call_target="tpu_custom_call" | custom-call | flops 1 | bytes 1 | tf_op jit(solution)/shard_map/pallas_call | solution.py:128
  143.4 4.7 %collective-permute-done.27 = f32[320,128]{1,0:T(8,128)S(1)} collective-permute-done((f32[320,128]{1,0:T(8,128)S(1)}, f32[320,128]{1,0:T(8,128)S(1)}, u32[]{:S(2)}, u32[]{:S(2)}) %collective-permute-start.27) | collective-permute-done | bytes 163872 | tf_op jit(solution)/shard_map/ppermute | solution.py:25
  164.5 13.2 %collective-permute-done.31.refs_2_ = s16[1040,128]{1,0:T(8,128)(2,1)S(1)} collective-permute-done((s16[1040,128]{1,0:T(8,128)(2,1)S(1)}, s16[1040,128]{1,0:T(8,128)(2,1)S(1)}, u32[]{:S(2)}, u32[]{:S(2)}) %collective-permute-start.31) | collective-permute-done | bytes 266272 | tf_op jit(solution)/shard_map/ppermute | solution.py:25
  182.8 3.6 %collective-permute-start.33 = (s16[1040,128]{1,0:T(8,128)(2,1)S(1)}, s16[1040,128]{1,0:T(8,128)(2,1)S(1)}, u32[]{:S(2)}, u32[]{:S(2)}) collective-permute-start(s16[1040,128]{1,0:T(8,128)(2,1)S(1)} %get-tuple-element.109), channel_id=1, source_target_pairs={{0,8},{4,12},{8,0},{12,4},{16,24},{20,28},{24,16},{28,20},{1,9},{5... | collective-permute-start | bytes 798728 | tf_op jit(solution)/shard_map/ppermute | solution.py:25
  191.1 6.1 %collective-permute-done.33.refs_1_ = s16[1040,128]{1,0:T(8,128)(2,1)S(1)} collective-permute-done((s16[1040,128]{1,0:T(8,128)(2,1)S(1)}, s16[1040,128]{1,0:T(8,128)(2,1)S(1)}, u32[]{:S(2)}, u32[]{:S(2)}) %collective-permute-start.33) | collective-permute-done | bytes 266272 | tf_op jit(solution)/shard_map/ppermute | solution.py:25
  197.2 10.9 %collective-permute-done.34.refs_2_ = s16[1040,128]{1,0:T(8,128)(2,1)S(1)} collective-permute-done((s16[1040,128]{1,0:T(8,128)(2,1)S(1)}, s16[1040,128]{1,0:T(8,128)(2,1)S(1)}, u32[]{:S(2)}, u32[]{:S(2)}) %collective-permute-start.34) | collective-permute-done | bytes 266272 | tf_op jit(solution)/shard_map/ppermute | solution.py:25
  209.0 4.8 %collective-permute-start.40 = (s16[1040,128]{1,0:T(8,128)(2,1)S(1)}, s16[1040,128]{1,0:T(8,128)(2,1)S(1)}, u32[]{:S(2)}, u32[]{:S(2)}) collective-permute-start(s16[1040,128]{1,0:T(8,128)(2,1)S(1)} %get-tuple-element.124.refs_0_), channel_id=1, source_target_pairs={{0,8},{4,12},{8,0},{12,4},{16,24},{20,28},{24,16},{28,20},{1,9},{5... | collective-permute-start | bytes 798728 | tf_op jit(solution)/shard_map/ppermute | solution.py:25
  227.9 9.6 %collective-permute-done.36.refs_2_ = s16[1040,128]{1,0:T(8,128)(2,1)S(1)} collective-permute-done((s16[1040,128]{1,0:T(8,128)(2,1)S(1)}, s16[1040,128]{1,0:T(8,128)(2,1)S(1)}, u32[]{:S(2)}, u32[]{:S(2)}) %collective-permute-start.36) | collective-permute-done | bytes 266272 | tf_op jit(solution)/shard_map/ppermute | solution.py:25
  240.1 3.9 %collective-permute-start.44 = (f32[128,128]{1,0:T(8,128)S(1)}, f32[128,128]{1,0:T(8,128)S(1)}, u32[]{:S(2)}, u32[]{:S(2)}) collective-permute-start(f32[128,128]{1,0:T(8,128)S(1)} %add.57.refs_0_), channel_id=1, source_target_pairs={{0,8},{4,12},{8,0},{12,4},{16,24},{20,28},{24,16},{28,20},{1,9},{5... | collective-permute-start | bytes 196616 | tf_op jit(solution)/shard_map/ppermute | solution.py:25
  246.3 9.0 %collective-permute-done.45.refs_2_ = f32[128,128]{1,0:T(8,128)S(1)} collective-permute-done((f32[128,128]{1,0:T(8,128)S(1)}, f32[128,128]{1,0:T(8,128)S(1)}, u32[]{:S(2)}, u32[]{:S(2)}) %collective-permute-start.45) | collective-permute-done | bytes 65568 | tf_op jit(solution)/shard_map/ppermute | solution.py:25
  257.4 4.1 %shard_map.70.inverse_ref = f32[128,128]{1,0:T(8,128)S(1)} custom-call(f32[128,128]{1,0:T(8,128)S(1)} %add.57.refs_0_, f32[128,128]{1,0:T(8,128)S(1)} %collective-permute-done.44.refs_1_, f32[128,128]{1,0:T(8,128)S(1)} %collective-permute-done.45.refs_2_, f32[128,128]{1,0:T(8,128)S(1)} %collective-permute-done.46.refs_3_), custom_call_target="tpu_custom_call" | custom-call | flops 1 | bytes 1 | tf_op jit(solution)/shard_map/pallas_call | solution.py:128
  261.5 5.9 %shard_map.71.refs_0_ = f32[12288,128]{1,0:T(8,128)} custom-call(s32[3]{0:T(128)S(1)} %pad_add_fusion.3.pos_ref, f32[128,128]{1,0:T(8,128)S(1)} %shard_map.70.inverse_ref, s16[1040,128]{1,0:T(8,128)(2,1)S(1)} %get-tuple-element.124.refs_0_, s16[1040,128]{1,0:T(8,128)(2,1)S(1)} %collective-permute-done.40.refs_1_, ...), custom_call_target="tpu_custom_call" | custom-call | tf_op jit(solution)/shard_map/pallas_call | solution.py:310
  (138 shorter events, 112.7 us)
Async XLA Ops:
  25.6 27.0 %collective-permute-start.3 = (bf16[4,1024,128]{2,1,0:T(8,128)(2,1)S(1)}, bf16[4,1024,128]{2,1,0:T(8,128)(2,1)S(1)}, u32[]{:S(2)}, u32[]{:S(2)}) collective-permute-start(bf16[4,1024,128]{2,1,0:T(8,128)(2,1)S(1)} %shard_map.48), channel_id=1, source_target_pairs={{0,4},{4,0},{8,12},{12,8},{16,20},{20,16},{24,28},{28,24},{1,5},{5... | collective-permute-start | bytes 3145736 | tf_op jit(solution)/shard_map/ppermute | solution.py:25
  31.0 21.4 %collective-permute-start.5 = (bf16[1024,128]{1,0:T(8,128)(2,1)S(1)}, bf16[1024,128]{1,0:T(8,128)(2,1)S(1)}, u32[]{:S(2)}, u32[]{:S(2)}) collective-permute-start(bf16[1024,128]{1,0:T(8,128)(2,1)S(1)} %get-tuple-element.71), channel_id=1, source_target_pairs={{0,16},{4,20},{8,24},{12,28},{16,0},{20,4},{24,8},{28,12},{1,17},{... | collective-permute-start | bytes 786440 | tf_op jit(solution)/shard_map/ppermute | solution.py:25
  33.6 18.8 %collective-permute-start.6 = (bf16[1024,128]{1,0:T(8,128)(2,1)S(1)}, bf16[1024,128]{1,0:T(8,128)(2,1)S(1)}, u32[]{:S(2)}, u32[]{:S(2)}) collective-permute-start(bf16[1024,128]{1,0:T(8,128)(2,1)S(1)} %get-tuple-element.72), channel_id=1, source_target_pairs={{0,24},{4,28},{8,16},{12,20},{16,8},{20,12},{24,0},{28,4},{1,25},{... | collective-permute-start | bytes 786440 | tf_op jit(solution)/shard_map/ppermute | solution.py:25
  35.0 17.6 %collective-permute-start.4 = (bf16[1024,128]{1,0:T(8,128)(2,1)S(1)}, bf16[1024,128]{1,0:T(8,128)(2,1)S(1)}, u32[]{:S(2)}, u32[]{:S(2)}) collective-permute-start(bf16[1024,128]{1,0:T(8,128)(2,1)S(1)} %get-tuple-element.70), channel_id=1, source_target_pairs={{0,8},{4,12},{8,0},{12,4},{16,24},{20,28},{24,16},{28,20},{1,9},{5... | collective-permute-start | bytes 786440 | tf_op jit(solution)/shard_map/ppermute | solution.py:25
  57.9 21.3 %collective-permute-start.8 = (bf16[1024,128]{1,0:T(8,128)(2,1)S(1)}, bf16[1024,128]{1,0:T(8,128)(2,1)S(1)}, u32[]{:S(2)}, u32[]{:S(2)}) collective-permute-start(bf16[1024,128]{1,0:T(8,128)(2,1)S(1)} %get-tuple-element.78), channel_id=1, source_target_pairs={{0,16},{4,20},{8,24},{12,28},{16,0},{20,4},{24,8},{28,12},{1,17},{... | collective-permute-start | bytes 786440 | tf_op jit(solution)/shard_map/ppermute | solution.py:25
  59.9 19.3 %collective-permute-start.9 = (bf16[1024,128]{1,0:T(8,128)(2,1)S(1)}, bf16[1024,128]{1,0:T(8,128)(2,1)S(1)}, u32[]{:S(2)}, u32[]{:S(2)}) collective-permute-start(bf16[1024,128]{1,0:T(8,128)(2,1)S(1)} %get-tuple-element.79), channel_id=1, source_target_pairs={{0,24},{4,28},{8,16},{12,20},{16,8},{20,12},{24,0},{28,4},{1,25},{... | collective-permute-start | bytes 786440 | tf_op jit(solution)/shard_map/ppermute | solution.py:25
  67.4 29.0 %collective-permute-start.16 = (bf16[512,128]{1,0:T(8,128)(2,1)S(1)}, bf16[512,128]{1,0:T(8,128)(2,1)S(1)}, u32[]{:S(2)}, u32[]{:S(2)}) collective-permute-start(bf16[512,128]{1,0:T(8,128)(2,1)S(1)} %get-tuple-element.91), channel_id=1, source_target_pairs={{0,4},{4,0},{8,12},{12,8},{16,20},{20,16},{24,28},{28,24},{1,5},{5... | collective-permute-start | bytes 393224 | tf_op jit(solution)/shard_map/ppermute | solution.py:25
  79.9 27.8 %collective-permute-start.15 = (bf16[1024,128]{1,0:T(8,128)(2,1)S(1)}, bf16[1024,128]{1,0:T(8,128)(2,1)S(1)}, u32[]{:S(2)}, u32[]{:S(2)}) collective-permute-start(bf16[1024,128]{1,0:T(8,128)(2,1)S(1)} %get-tuple-element.89.refs_4_), channel_id=1, source_target_pairs={{0,24},{4,28},{8,16},{12,20},{16,8},{20,12},{24,0},{28,4},{1,25},{... | collective-permute-start | bytes 786440 | tf_op jit(solution)/shard_map/ppermute | solution.py:25
  83.4 24.3 %collective-permute-start.14 = (bf16[1024,128]{1,0:T(8,128)(2,1)S(1)}, bf16[1024,128]{1,0:T(8,128)(2,1)S(1)}, u32[]{:S(2)}, u32[]{:S(2)}) collective-permute-start(bf16[1024,128]{1,0:T(8,128)(2,1)S(1)} %get-tuple-element.89.refs_4_), channel_id=1, source_target_pairs={{0,16},{4,20},{8,24},{12,28},{16,0},{20,4},{24,8},{28,12},{1,17},{... | collective-permute-start | bytes 786440 | tf_op jit(solution)/shard_map/ppermute | solution.py:25
  103.2 32.1 %collective-permute-start.18 = (bf16[2,1024,128]{2,1,0:T(8,128)(2,1)S(1)}, bf16[2,1024,128]{2,1,0:T(8,128)(2,1)S(1)}, u32[]{:S(2)}, u32[]{:S(2)}) collective-permute-start(bf16[2,1024,128]{2,1,0:T(8,128)(2,1)S(1)} %pad_maximum_fusion), channel_id=1, source_target_pairs={{0,4},{4,0},{8,12},{12,8},{16,20},{20,16},{24,28},{28,24},{1,5},{5... | collective-permute-start | bytes 1572872 | tf_op jit(solution)/shard_map/ppermute | solution.py:25
  107.8 27.6 %collective-permute-start.19 = (bf16[2,1024,128]{2,1,0:T(8,128)(2,1)S(1)}, bf16[2,1024,128]{2,1,0:T(8,128)(2,1)S(1)}, u32[]{:S(2)}, u32[]{:S(2)}) collective-permute-start(bf16[2,1024,128]{2,1,0:T(8,128)(2,1)S(1)} %pad_maximum_fusion.1), channel_id=1, source_target_pairs={{0,4},{4,0},{8,12},{12,8},{16,20},{20,16},{24,28},{28,24},{1,5},{5... | collective-permute-start | bytes 1572872 | tf_op jit(solution)/shard_map/ppermute | solution.py:25
  115.0 22.4 %collective-permute-start.20 = (bf16[2,512,128]{2,1,0:T(8,128)(2,1)S(1)}, bf16[2,512,128]{2,1,0:T(8,128)(2,1)S(1)}, u32[]{:S(2)}, u32[]{:S(2)}) collective-permute-start(bf16[2,512,128]{2,1,0:T(8,128)(2,1)S(1)} %pad_maximum_fusion.2), channel_id=1, source_target_pairs={{0,8},{4,12},{8,0},{12,4},{16,24},{20,28},{24,16},{28,20},{1,9},{5... | collective-permute-start | bytes 786440 | tf_op jit(solution)/shard_map/ppermute | solution.py:25
  117.3 21.5 %collective-permute-start.25 = (bf16[2,512,128]{2,1,0:T(8,128)(2,1)S(1)}, bf16[2,512,128]{2,1,0:T(8,128)(2,1)S(1)}, u32[]{:S(2)}, u32[]{:S(2)}) collective-permute-start(bf16[2,512,128]{2,1,0:T(8,128)(2,1)S(1)} %pad_maximum_fusion.2), channel_id=1, source_target_pairs={{0,24},{4,28},{8,16},{12,20},{16,8},{20,12},{24,0},{28,4},{1,25},{... | collective-permute-start | bytes 786440 | tf_op jit(solution)/shard_map/ppermute | solution.py:25
  153.6 25.6 %collective-permute-start.29 = (s16[4,1040,128]{2,1,0:T(8,128)(2,1)S(1)}, s16[4,1040,128]{2,1,0:T(8,128)(2,1)S(1)}, u32[]{:S(2)}, u32[]{:S(2)}) collective-permute-start(s16[4,1040,128]{2,1,0:T(8,128)(2,1)S(1)} %shard_map.62), channel_id=1, source_target_pairs={{0,4},{4,0},{8,12},{12,8},{16,20},{20,16},{24,28},{28,24},{1,5},{5... | collective-permute-start | bytes 3194888 | tf_op jit(solution)/shard_map/ppermute | solution.py:25
  157.0 20.7 %collective-permute-start.31 = (s16[1040,128]{1,0:T(8,128)(2,1)S(1)}, s16[1040,128]{1,0:T(8,128)(2,1)S(1)}, u32[]{:S(2)}, u32[]{:S(2)}) collective-permute-start(s16[1040,128]{1,0:T(8,128)(2,1)S(1)} %get-tuple-element.103), channel_id=1, source_target_pairs={{0,16},{4,20},{8,24},{12,28},{16,0},{20,4},{24,8},{28,12},{1,17},{... | collective-permute-start | bytes 798728 | tf_op jit(solution)/shard_map/ppermute | solution.py:25
  159.9 17.8 %collective-permute-start.32 = (s16[1040,128]{1,0:T(8,128)(2,1)S(1)}, s16[1040,128]{1,0:T(8,128)(2,1)S(1)}, u32[]{:S(2)}, u32[]{:S(2)}) collective-permute-start(s16[1040,128]{1,0:T(8,128)(2,1)S(1)} %get-tuple-element.104), channel_id=1, source_target_pairs={{0,24},{4,28},{8,16},{12,20},{16,8},{20,12},{24,0},{28,4},{1,25},{... | collective-permute-start | bytes 798728 | tf_op jit(solution)/shard_map/ppermute | solution.py:25
  159.9 19.2 %collective-permute-start.30 = (s16[1040,128]{1,0:T(8,128)(2,1)S(1)}, s16[1040,128]{1,0:T(8,128)(2,1)S(1)}, u32[]{:S(2)}, u32[]{:S(2)}) collective-permute-start(s16[1040,128]{1,0:T(8,128)(2,1)S(1)} %get-tuple-element.102), channel_id=1, source_target_pairs={{0,8},{4,12},{8,0},{12,4},{16,24},{20,28},{24,16},{28,20},{1,9},{5... | collective-permute-start | bytes 798728 | tf_op jit(solution)/shard_map/ppermute | solution.py:25
  186.5 21.6 %collective-permute-start.34 = (s16[1040,128]{1,0:T(8,128)(2,1)S(1)}, s16[1040,128]{1,0:T(8,128)(2,1)S(1)}, u32[]{:S(2)}, u32[]{:S(2)}) collective-permute-start(s16[1040,128]{1,0:T(8,128)(2,1)S(1)} %get-tuple-element.110), channel_id=1, source_target_pairs={{0,16},{4,20},{8,24},{12,28},{16,0},{20,4},{24,8},{28,12},{1,17},{... | collective-permute-start | bytes 798728 | tf_op jit(solution)/shard_map/ppermute | solution.py:25
  187.7 20.4 %collective-permute-start.35 = (s16[1040,128]{1,0:T(8,128)(2,1)S(1)}, s16[1040,128]{1,0:T(8,128)(2,1)S(1)}, u32[]{:S(2)}, u32[]{:S(2)}) collective-permute-start(s16[1040,128]{1,0:T(8,128)(2,1)S(1)} %get-tuple-element.111), channel_id=1, source_target_pairs={{0,24},{4,28},{8,16},{12,20},{16,8},{20,12},{24,0},{28,4},{1,25},{... | collective-permute-start | bytes 798728 | tf_op jit(solution)/shard_map/ppermute | solution.py:25
  189.5 25.9 %collective-permute-start.39 = (s16[528,128]{1,0:T(8,128)(2,1)S(1)}, s16[528,128]{1,0:T(8,128)(2,1)S(1)}, u32[]{:S(2)}, u32[]{:S(2)}) collective-permute-start(s16[528,128]{1,0:T(8,128)(2,1)S(1)} %get-tuple-element.119), channel_id=1, source_target_pairs={{0,4},{4,0},{8,12},{12,8},{16,20},{20,16},{24,28},{28,24},{1,5},{5... | collective-permute-start | bytes 405512 | tf_op jit(solution)/shard_map/ppermute | solution.py:25
  215.4 22.1 %collective-permute-start.36 = (s16[1040,128]{1,0:T(8,128)(2,1)S(1)}, s16[1040,128]{1,0:T(8,128)(2,1)S(1)}, u32[]{:S(2)}, u32[]{:S(2)}) collective-permute-start(s16[1040,128]{1,0:T(8,128)(2,1)S(1)} %get-tuple-element.124.refs_0_), channel_id=1, source_target_pairs={{0,16},{4,20},{8,24},{12,28},{16,0},{20,4},{24,8},{28,12},{1,17},{... | collective-permute-start | bytes 798728 | tf_op jit(solution)/shard_map/ppermute | solution.py:25
  223.9 37.5 %collective-permute-start.47 = (s16[2,1040,128]{2,1,0:T(8,128)(2,1)S(1)}, s16[2,1040,128]{2,1,0:T(8,128)(2,1)S(1)}, u32[]{:S(2)}, u32[]{:S(2)}) collective-permute-start(s16[2,1040,128]{2,1,0:T(8,128)(2,1)S(1)} %pad_add_fusion), channel_id=1, source_target_pairs={{0,4},{4,0},{8,12},{12,8},{16,20},{20,16},{24,28},{28,24},{1,5},{5... | collective-permute-start | bytes 1597448 | tf_op jit(solution)/shard_map/ppermute | solution.py:25
  237.6 23.9 %collective-permute-start.48 = (s16[2,1040,128]{2,1,0:T(8,128)(2,1)S(1)}, s16[2,1040,128]{2,1,0:T(8,128)(2,1)S(1)}, u32[]{:S(2)}, u32[]{:S(2)}) collective-permute-start(s16[2,1040,128]{2,1,0:T(8,128)(2,1)S(1)} %pad_add_fusion.1), channel_id=1, source_target_pairs={{0,4},{4,0},{8,12},{12,8},{16,20},{20,16},{24,28},{28,24},{1,5},{5... | collective-permute-start | bytes 1597448 | tf_op jit(solution)/shard_map/ppermute | solution.py:25
  245.8 21.6 %collective-permute-start.51 = (s16[2,528,128]{2,1,0:T(8,128)(2,1)S(1)}, s16[2,528,128]{2,1,0:T(8,128)(2,1)S(1)}, u32[]{:S(2)}, u32[]{:S(2)}) collective-permute-start(s16[2,528,128]{2,1,0:T(8,128)(2,1)S(1)} %pad_add_fusion.2.refs_6_), channel_id=1, source_target_pairs={{0,24},{4,28},{8,16},{12,20},{16,8},{20,12},{24,0},{28,4},{1,25},{... | collective-permute-start | bytes 811016 | tf_op jit(solution)/shard_map/ppermute | solution.py:25
  (33 other events, 275.7 us)

commit v17 on v11

--- a/solution.py
+++ b/solution.py
@@ -503,9 +503,8 @@
         pairs = [(j, k, array.reshape(layout.pair, rank)) for j, k, array in pairs]
         total = project(scans, layout, pos, early)
         total = project(scans, layout, pos, late, total)
-        total = project(scans, layout, pos, pairs[: high // 2], total)
         total, inverse = lax.optimization_barrier((total, inverse))
-        halves = project(scans, layout, pos, pairs[high // 2 :], total, True)
+        halves = project(scans, layout, pos, pairs, total, True)
         scores = sum_scores(*halves, inverse)
         early, late, pairs, inverse = pass_over(scores, Fixed)
         out = finish(layout, pos, early + late, inverse, voxels)

time: 273 us -> 278 us (1.018)
  waiting for transfers between devices: 115 us -> 122 us
    ppermute x52, waiting for transfers between devices: 115 us -> 122 us  [exchange(): return lax.ppermute(value, axis, [(i, i ^ mask) for i in range(size)])]
    pallas_call x4 -> x3, Pallas kernels: 6.92 us -> 6.23 us  [project(): pl.pallas_call(functools.partial(project_kernel, base is not None, split,...]
  transfers between devices with their start and end apart: 52 -> 52, of which waited for: 32 -> 30; matrix products, arithmetic and copies ran while one was open for 0% -> 0% of each run, Pallas kernels for 14% -> 13%
where the time goes in v17:
time: 278 us; the launch traced here: 277 us
  waiting for transfers between devices  122 us (44%)
  starting transfers between devices  85.6 us (31%)
  Pallas kernels  61.3 us (22%)
  local copies, waits for them, and re-layouts  7.37 us (3%)
    ppermute x52, waiting for transfers between devices, exchange(): return lax.ppermute(value, axis, [(i, i ^ mask) for i in range(size)])  122 us
    ppermute x52, starting transfers between devices, exchange(): return lax.ppermute(value, axis, [(i, i ^ mask) for i in range(size)])  85.6 us
    pallas_call x8, Pallas kernels, sketch_part(): pl.pallas_call(functools.partial(sketch_kernel, code, apart, per_step), o...  22.2 us
    pallas_call x8, Pallas kernels, small_call(): pl.pallas_call(kernel, out_shape=out_shape, in_specs=[WHOLE] * len(args),...  11.8 us
    pallas_call x2, Pallas kernels, finish(): pl.pallas_call(functools.partial(finish_kernel, layout, items, base is no...  9.12 us
    pallas_call x1, Pallas kernels, first_project(): pl.pallas_call(functools.partial(first_kernel, count), out_shape=[half, h...  8.72 us
    unnamed x10, local copies, waits for them, and re-layouts  7.37 us
    pallas_call x3, Pallas kernels, project(): pl.pallas_call(functools.partial(project_kernel, base is not None, split,...  6.23 us
  transfers between devices with their start and end apart: 52, of which 30 were waited for; matrix products, arithmetic and copies ran while one was open for 0% of the time, Pallas kernels for 13%

profile of v17, /device:TPU:0, one launch (start us, length us, event | category | flops | bytes accessed | tf_op | source)
XLA Modules:
  0.0 277.3 jit_solution(15268834814501141327)
XLA Ops:
  2.0 8.7 %shard_map.46 = (f32[320,128]{1,0:T(8,128)S(1)}, f32[320,128]{1,0:T(8,128)S(1)}) custom-call(s32[3]{0:T(128)S(1)} %pad_add_fusion.3.pos_ref, bf16[12288,128]{1,0:T(8,128)(2,1)S(1)} %copy-done.2, bf16[640,12288]{1,0:T(8,128)(2,1)} %refs_0_.19, bf16[640,12288]{1,0:T(8,128)(2,1)} %refs_0_.19, bf16[640,12288]{1,0:T(8,128)(2,1)} %refs_0_.19, ...), custom_call_target="tpu_custom_call" | custom-call | flops 1 | bytes 1 | tf_op jit(solution)/shard_map/pallas_call | solution.py:206
  15.2 4.5 %collective-permute-done.1 = f32[320,128]{1,0:T(8,128)S(1)} collective-permute-done((f32[320,128]{1,0:T(8,128)S(1)}, f32[320,128]{1,0:T(8,128)S(1)}, u32[]{:S(2)}, u32[]{:S(2)}) %collective-permute-start.1) | collective-permute-done | bytes 163872 | tf_op jit(solution)/shard_map/ppermute | solution.py:25
  21.8 3.8 %shard_map.48 = bf16[4,1024,128]{2,1,0:T(8,128)(2,1)S(1)} custom-call(s32[3]{0:T(128)S(1)} %pad_add_fusion.3.pos_ref, bf16[640,128]{1,0:T(8,128)(2,1)S(1)} %shard_map.47.scores_ref, bf16[640,12288]{1,0:T(8,128)(2,1)} %refs_0_.19, bf16[640,12288]{1,0:T(8,128)(2,1)} %refs_0_.19), custom_call_target="tpu_custom_call" | custom-call | flops 1 | bytes 1 | tf_op jit(solution)/shard_map/pallas_call | solution.py:112
  27.4 3.5 %shard_map.49 = (bf16[1024,128]{1,0:T(8,128)(2,1)S(1)}, bf16[1024,128]{1,0:T(8,128)(2,1)S(1)}, bf16[1024,128]{1,0:T(8,128)(2,1)S(1)}) custom-call(s32[3]{0:T(128)S(1)} %pad_add_fusion.3.pos_ref, bf16[640,128]{1,0:T(8,128)(2,1)S(1)} %shard_map.47.scores_ref, bf16[640,12288]{1,0:T(8,128)(2,1)} %refs_0_.19, bf16[640,12288]{1,0:T(8,128)(2,1)} %refs_0_.19, ...), custom_call_target="tpu_custom_call" | custom-call | flops 1 | bytes 1 | tf_op jit(solution)/shard_map/pallas_call | solution.py:112
  37.6 4.0 %shard_map.50.own_ref = bf16[4,1024,128]{2,1,0:T(8,128)(2,1)S(1)} custom-call(s32[3]{0:T(128)S(1)} %pad_add_fusion.3.pos_ref, bf16[640,128]{1,0:T(8,128)(2,1)S(1)} %shard_map.47.scores_ref, bf16[640,12288]{1,0:T(8,128)(2,1)} %refs_0_.19, bf16[640,12288]{1,0:T(8,128)(2,1)} %refs_0_.19), custom_call_target="tpu_custom_call" | custom-call | flops 1 | bytes 1 | tf_op jit(solution)/shard_map/pallas_call | solution.py:112
  41.5 10.9 %collective-permute-done.5.refs_2_ = bf16[1024,128]{1,0:T(8,128)(2,1)S(1)} collective-permute-done((bf16[1024,128]{1,0:T(8,128)(2,1)S(1)}, bf16[1024,128]{1,0:T(8,128)(2,1)S(1)}, u32[]{:S(2)}, u32[]{:S(2)}) %collective-permute-start.5) | collective-permute-done | bytes 262176 | tf_op jit(solution)/shard_map/ppermute | solution.py:25
  52.9 5.0 %collective-permute-start.7 = (bf16[1024,128]{1,0:T(8,128)(2,1)S(1)}, bf16[1024,128]{1,0:T(8,128)(2,1)S(1)}, u32[]{:S(2)}, u32[]{:S(2)}) collective-permute-start(bf16[1024,128]{1,0:T(8,128)(2,1)S(1)} %get-tuple-element.77), channel_id=1, source_target_pairs={{0,8},{4,12},{8,0},{12,4},{16,24},{20,28},{24,16},{28,20},{1,9},{5... | collective-permute-start | bytes 786440 | tf_op jit(solution)/shard_map/ppermute | solution.py:25
  62.6 4.5 %collective-permute-done.11.refs_1_ = bf16[512,128]{1,0:T(8,128)(2,1)S(1)} collective-permute-done((bf16[512,128]{1,0:T(8,128)(2,1)S(1)}, bf16[512,128]{1,0:T(8,128)(2,1)S(1)}, u32[]{:S(2)}, u32[]{:S(2)}) %collective-permute-start.11) | collective-permute-done | bytes 131104 | tf_op jit(solution)/shard_map/ppermute | solution.py:25
  69.8 9.5 %collective-permute-done.8.refs_2_ = bf16[1024,128]{1,0:T(8,128)(2,1)S(1)} collective-permute-done((bf16[1024,128]{1,0:T(8,128)(2,1)S(1)}, bf16[1024,128]{1,0:T(8,128)(2,1)S(1)}, u32[]{:S(2)}, u32[]{:S(2)}) %collective-permute-start.8) | collective-permute-done | bytes 262176 | tf_op jit(solution)/shard_map/ppermute | solution.py:25
  83.4 12.5 %collective-permute-start.14 = (bf16[1024,128]{1,0:T(8,128)(2,1)S(1)}, bf16[1024,128]{1,0:T(8,128)(2,1)S(1)}, u32[]{:S(2)}, u32[]{:S(2)}) collective-permute-start(bf16[1024,128]{1,0:T(8,128)(2,1)S(1)} %get-tuple-element.89.refs_4_), channel_id=1, source_target_pairs={{0,16},{4,20},{8,24},{12,28},{16,0},{20,4},{24,8},{28,12},{1,17},{... | collective-permute-start | bytes 786440 | tf_op jit(solution)/shard_map/ppermute | solution.py:25
  117.6 8.8 %collective-permute-done.21.refs_2_ = f32[128,128]{1,0:T(8,128)S(1)} collective-permute-done((f32[128,128]{1,0:T(8,128)S(1)}, f32[128,128]{1,0:T(8,128)S(1)}, u32[]{:S(2)}, u32[]{:S(2)}) %collective-permute-start.21) | collective-permute-done | bytes 65568 | tf_op jit(solution)/shard_map/ppermute | solution.py:25
  129.9 5.5 %copy-done = bf16[640,12288]{1,0:T(8,128)(2,1)S(1)} copy-done((bf16[640,12288]{1,0:T(8,128)(2,1)S(1)}, bf16[640,12288]{1,0:T(8,128)(2,1)}, u32[]{:S(2)}) %copy-start) | copy-done | bytes 15728664
  137.4 4.1 %shard_map.58.refs_0_ = f32[128,128]{1,0:T(8,128)S(1)} custom-call(f32[128,128]{1,0:T(8,128)S(1)} %add.51.refs_0_, f32[128,128]{1,0:T(8,128)S(1)} %collective-permute-done.20.refs_1_, f32[128,128]{1,0:T(8,128)S(1)} %collective-permute-done.21.refs_2_, f32[128,128]{1,0:T(8,128)S(1)} %collective-permute-done.22.refs_3_), custom_call_target="tpu_custom_call" | custom-call | flops 1 | bytes 1 | tf_op jit(solution)/shard_map/pallas_call | solution.py:128
  148.8 4.7 %collective-permute-done.27 = f32[320,128]{1,0:T(8,128)S(1)} collective-permute-done((f32[320,128]{1,0:T(8,128)S(1)}, f32[320,128]{1,0:T(8,128)S(1)}, u32[]{:S(2)}, u32[]{:S(2)}) %collective-permute-start.27) | collective-permute-done | bytes 163872 | tf_op jit(solution)/shard_map/ppermute | solution.py:25
  169.8 12.6 %collective-permute-done.31.refs_2_ = s16[1040,128]{1,0:T(8,128)(2,1)S(1)} collective-permute-done((s16[1040,128]{1,0:T(8,128)(2,1)S(1)}, s16[1040,128]{1,0:T(8,128)(2,1)S(1)}, u32[]{:S(2)}, u32[]{:S(2)}) %collective-permute-start.31) | collective-permute-done | bytes 266272 | tf_op jit(solution)/shard_map/ppermute | solution.py:25
  195.7 6.1 %collective-permute-done.33.refs_1_ = s16[1040,128]{1,0:T(8,128)(2,1)S(1)} collective-permute-done((s16[1040,128]{1,0:T(8,128)(2,1)S(1)}, s16[1040,128]{1,0:T(8,128)(2,1)S(1)}, u32[]{:S(2)}, u32[]{:S(2)}) %collective-permute-start.33) | collective-permute-done | bytes 266272 | tf_op jit(solution)/shard_map/ppermute | solution.py:25
  201.7 11.1 %collective-permute-done.34.refs_2_ = s16[1040,128]{1,0:T(8,128)(2,1)S(1)} collective-permute-done((s16[1040,128]{1,0:T(8,128)(2,1)S(1)}, s16[1040,128]{1,0:T(8,128)(2,1)S(1)}, u32[]{:S(2)}, u32[]{:S(2)}) %collective-permute-start.34) | collective-permute-done | bytes 266272 | tf_op jit(solution)/shard_map/ppermute | solution.py:25
  213.7 4.8 %collective-permute-start.40 = (s16[1040,128]{1,0:T(8,128)(2,1)S(1)}, s16[1040,128]{1,0:T(8,128)(2,1)S(1)}, u32[]{:S(2)}, u32[]{:S(2)}) collective-permute-start(s16[1040,128]{1,0:T(8,128)(2,1)S(1)} %get-tuple-element.124.refs_0_), channel_id=1, source_target_pairs={{0,8},{4,12},{8,0},{12,4},{16,24},{20,28},{24,16},{28,20},{1,9},{5... | collective-permute-start | bytes 798728 | tf_op jit(solution)/shard_map/ppermute | solution.py:25
  232.9 9.4 %collective-permute-done.36.refs_2_ = s16[1040,128]{1,0:T(8,128)(2,1)S(1)} collective-permute-done((s16[1040,128]{1,0:T(8,128)(2,1)S(1)}, s16[1040,128]{1,0:T(8,128)(2,1)S(1)}, u32[]{:S(2)}, u32[]{:S(2)}) %collective-permute-start.36) | collective-permute-done | bytes 266272 | tf_op jit(solution)/shard_map/ppermute | solution.py:25
  245.0 3.8 %collective-permute-start.44 = (f32[128,128]{1,0:T(8,128)S(1)}, f32[128,128]{1,0:T(8,128)S(1)}, u32[]{:S(2)}, u32[]{:S(2)}) collective-permute-start(f32[128,128]{1,0:T(8,128)S(1)} %add.57.refs_0_), channel_id=1, source_target_pairs={{0,8},{4,12},{8,0},{12,4},{16,24},{20,28},{24,16},{28,20},{1,9},{5... | collective-permute-start | bytes 196616 | tf_op jit(solution)/shard_map/ppermute | solution.py:25
  251.1 9.1 %collective-permute-done.45.refs_2_ = f32[128,128]{1,0:T(8,128)S(1)} collective-permute-done((f32[128,128]{1,0:T(8,128)S(1)}, f32[128,128]{1,0:T(8,128)S(1)}, u32[]{:S(2)}, u32[]{:S(2)}) %collective-permute-start.45) | collective-permute-done | bytes 65568 | tf_op jit(solution)/shard_map/ppermute | solution.py:25
  262.2 4.1 %shard_map.69.inverse_ref = f32[128,128]{1,0:T(8,128)S(1)} custom-call(f32[128,128]{1,0:T(8,128)S(1)} %add.57.refs_0_, f32[128,128]{1,0:T(8,128)S(1)} %collective-permute-done.44.refs_1_, f32[128,128]{1,0:T(8,128)S(1)} %collective-permute-done.45.refs_2_, f32[128,128]{1,0:T(8,128)S(1)} %collective-permute-done.46.refs_3_), custom_call_target="tpu_custom_call" | custom-call | flops 1 | bytes 1 | tf_op jit(solution)/shard_map/pallas_call | solution.py:128
  266.3 5.5 %shard_map.70.refs_0_ = f32[12288,128]{1,0:T(8,128)} custom-call(s32[3]{0:T(128)S(1)} %pad_add_fusion.3.pos_ref, f32[128,128]{1,0:T(8,128)S(1)} %shard_map.69.inverse_ref, s16[1040,128]{1,0:T(8,128)(2,1)S(1)} %get-tuple-element.124.refs_0_, s16[1040,128]{1,0:T(8,128)(2,1)S(1)} %collective-permute-done.40.refs_1_, ...), custom_call_target="tpu_custom_call" | custom-call | tf_op jit(solution)/shard_map/pallas_call | solution.py:310
  273.5 3.6 %shard_map.71 = f32[12288,128]{1,0:T(8,128)} custom-call(s32[3]{0:T(128)S(1)} %pad_add_fusion.3.pos_ref, f32[128,128]{1,0:T(8,128)S(1)} %shard_map.69.inverse_ref, f32[12288,128]{1,0:T(8,128)} %shard_map.70.refs_0_, s16[2,528,128]{2,1,0:T(8,128)(2,1)S(1)} %pad_add_fusion.2.refs_1_, ...), custom_call_target="tpu_custom_call", output_to_operand_aliasing={{}: (2, {})} | custom-call | tf_op jit(solution)/shard_map/pallas_call | solution.py:310
  (137 shorter events, 116.6 us)
Async XLA Ops:
  25.6 27.0 %collective-permute-start.3 = (bf16[4,1024,128]{2,1,0:T(8,128)(2,1)S(1)}, bf16[4,1024,128]{2,1,0:T(8,128)(2,1)S(1)}, u32[]{:S(2)}, u32[]{:S(2)}) collective-permute-start(bf16[4,1024,128]{2,1,0:T(8,128)(2,1)S(1)} %shard_map.48), channel_id=1, source_target_pairs={{0,4},{4,0},{8,12},{12,8},{16,20},{20,16},{24,28},{28,24},{1,5},{5... | collective-permute-start | bytes 3145736 | tf_op jit(solution)/shard_map/ppermute | solution.py:25
  31.0 21.4 %collective-permute-start.5 = (bf16[1024,128]{1,0:T(8,128)(2,1)S(1)}, bf16[1024,128]{1,0:T(8,128)(2,1)S(1)}, u32[]{:S(2)}, u32[]{:S(2)}) collective-permute-start(bf16[1024,128]{1,0:T(8,128)(2,1)S(1)} %get-tuple-element.71), channel_id=1, source_target_pairs={{0,16},{4,20},{8,24},{12,28},{16,0},{20,4},{24,8},{28,12},{1,17},{... | collective-permute-start | bytes 786440 | tf_op jit(solution)/shard_map/ppermute | solution.py:25
  33.6 18.8 %collective-permute-start.6 = (bf16[1024,128]{1,0:T(8,128)(2,1)S(1)}, bf16[1024,128]{1,0:T(8,128)(2,1)S(1)}, u32[]{:S(2)}, u32[]{:S(2)}) collective-permute-start(bf16[1024,128]{1,0:T(8,128)(2,1)S(1)} %get-tuple-element.72), channel_id=1, source_target_pairs={{0,24},{4,28},{8,16},{12,20},{16,8},{20,12},{24,0},{28,4},{1,25},{... | collective-permute-start | bytes 786440 | tf_op jit(solution)/shard_map/ppermute | solution.py:25
  35.0 17.6 %collective-permute-start.4 = (bf16[1024,128]{1,0:T(8,128)(2,1)S(1)}, bf16[1024,128]{1,0:T(8,128)(2,1)S(1)}, u32[]{:S(2)}, u32[]{:S(2)}) collective-permute-start(bf16[1024,128]{1,0:T(8,128)(2,1)S(1)} %get-tuple-element.70), channel_id=1, source_target_pairs={{0,8},{4,12},{8,0},{12,4},{16,24},{20,28},{24,16},{28,20},{1,9},{5... | collective-permute-start | bytes 786440 | tf_op jit(solution)/shard_map/ppermute | solution.py:25
  57.9 21.3 %collective-permute-start.8 = (bf16[1024,128]{1,0:T(8,128)(2,1)S(1)}, bf16[1024,128]{1,0:T(8,128)(2,1)S(1)}, u32[]{:S(2)}, u32[]{:S(2)}) collective-permute-start(bf16[1024,128]{1,0:T(8,128)(2,1)S(1)} %get-tuple-element.78), channel_id=1, source_target_pairs={{0,16},{4,20},{8,24},{12,28},{16,0},{20,4},{24,8},{28,12},{1,17},{... | collective-permute-start | bytes 786440 | tf_op jit(solution)/shard_map/ppermute | solution.py:25
  59.9 19.3 %collective-permute-start.9 = (bf16[1024,128]{1,0:T(8,128)(2,1)S(1)}, bf16[1024,128]{1,0:T(8,128)(2,1)S(1)}, u32[]{:S(2)}, u32[]{:S(2)}) collective-permute-start(bf16[1024,128]{1,0:T(8,128)(2,1)S(1)} %get-tuple-element.79), channel_id=1, source_target_pairs={{0,24},{4,28},{8,16},{12,20},{16,8},{20,12},{24,0},{28,4},{1,25},{... | collective-permute-start | bytes 786440 | tf_op jit(solution)/shard_map/ppermute | solution.py:25
  67.4 29.0 %collective-permute-start.16 = (bf16[512,128]{1,0:T(8,128)(2,1)S(1)}, bf16[512,128]{1,0:T(8,128)(2,1)S(1)}, u32[]{:S(2)}, u32[]{:S(2)}) collective-permute-start(bf16[512,128]{1,0:T(8,128)(2,1)S(1)} %get-tuple-element.91), channel_id=1, source_target_pairs={{0,4},{4,0},{8,12},{12,8},{16,20},{20,16},{24,28},{28,24},{1,5},{5... | collective-permute-start | bytes 393224 | tf_op jit(solution)/shard_map/ppermute | solution.py:25
  79.9 27.8 %collective-permute-start.15 = (bf16[1024,128]{1,0:T(8,128)(2,1)S(1)}, bf16[1024,128]{1,0:T(8,128)(2,1)S(1)}, u32[]{:S(2)}, u32[]{:S(2)}) collective-permute-start(bf16[1024,128]{1,0:T(8,128)(2,1)S(1)} %get-tuple-element.89.refs_4_), channel_id=1, source_target_pairs={{0,24},{4,28},{8,16},{12,20},{16,8},{20,12},{24,0},{28,4},{1,25},{... | collective-permute-start | bytes 786440 | tf_op jit(solution)/shard_map/ppermute | solution.py:25
  83.4 24.3 %collective-permute-start.14 = (bf16[1024,128]{1,0:T(8,128)(2,1)S(1)}, bf16[1024,128]{1,0:T(8,128)(2,1)S(1)}, u32[]{:S(2)}, u32[]{:S(2)}) collective-permute-start(bf16[1024,128]{1,0:T(8,128)(2,1)S(1)} %get-tuple-element.89.refs_4_), channel_id=1, source_target_pairs={{0,16},{4,20},{8,24},{12,28},{16,0},{20,4},{24,8},{28,12},{1,17},{... | collective-permute-start | bytes 786440 | tf_op jit(solution)/shard_map/ppermute | solution.py:25
  103.2 38.3 %collective-permute-start.18 = (bf16[2,1024,128]{2,1,0:T(8,128)(2,1)S(1)}, bf16[2,1024,128]{2,1,0:T(8,128)(2,1)S(1)}, u32[]{:S(2)}, u32[]{:S(2)}) collective-permute-start(bf16[2,1024,128]{2,1,0:T(8,128)(2,1)S(1)} %pad_maximum_fusion), channel_id=1, source_target_pairs={{0,4},{4,0},{8,12},{12,8},{16,20},{20,16},{24,28},{28,24},{1,5},{5... | collective-permute-start | bytes 1572872 | tf_op jit(solution)/shard_map/ppermute | solution.py:25
  107.8 33.7 %collective-permute-start.19 = (bf16[2,1024,128]{2,1,0:T(8,128)(2,1)S(1)}, bf16[2,1024,128]{2,1,0:T(8,128)(2,1)S(1)}, u32[]{:S(2)}, u32[]{:S(2)}) collective-permute-start(bf16[2,1024,128]{2,1,0:T(8,128)(2,1)S(1)} %pad_maximum_fusion.1), channel_id=1, source_target_pairs={{0,4},{4,0},{8,12},{12,8},{16,20},{20,16},{24,28},{28,24},{1,5},{5... | collective-permute-start | bytes 1572872 | tf_op jit(solution)/shard_map/ppermute | solution.py:25
  114.4 29.2 %collective-permute-start.25 = (bf16[2,512,128]{2,1,0:T(8,128)(2,1)S(1)}, bf16[2,512,128]{2,1,0:T(8,128)(2,1)S(1)}, u32[]{:S(2)}, u32[]{:S(2)}) collective-permute-start(bf16[2,512,128]{2,1,0:T(8,128)(2,1)S(1)} %pad_maximum_fusion.2), channel_id=1, source_target_pairs={{0,24},{4,28},{8,16},{12,20},{16,8},{20,12},{24,0},{28,4},{1,25},{... | collective-permute-start | bytes 786440 | tf_op jit(solution)/shard_map/ppermute | solution.py:25
  126.4 17.2 %collective-permute-start.24 = (bf16[2,512,128]{2,1,0:T(8,128)(2,1)S(1)}, bf16[2,512,128]{2,1,0:T(8,128)(2,1)S(1)}, u32[]{:S(2)}, u32[]{:S(2)}) collective-permute-start(bf16[2,512,128]{2,1,0:T(8,128)(2,1)S(1)} %pad_maximum_fusion.2), channel_id=1, source_target_pairs={{0,16},{4,20},{8,24},{12,28},{16,0},{20,4},{24,8},{28,12},{1,17},{... | collective-permute-start | bytes 786440 | tf_op jit(solution)/shard_map/ppermute | solution.py:25
  159.0 25.6 %collective-permute-start.29 = (s16[4,1040,128]{2,1,0:T(8,128)(2,1)S(1)}, s16[4,1040,128]{2,1,0:T(8,128)(2,1)S(1)}, u32[]{:S(2)}, u32[]{:S(2)}) collective-permute-start(s16[4,1040,128]{2,1,0:T(8,128)(2,1)S(1)} %shard_map.61), channel_id=1, source_target_pairs={{0,4},{4,0},{8,12},{12,8},{16,20},{20,16},{24,28},{28,24},{1,5},{5... | collective-permute-start | bytes 3194888 | tf_op jit(solution)/shard_map/ppermute | solution.py:25
  162.3 20.1 %collective-permute-start.31 = (s16[1040,128]{1,0:T(8,128)(2,1)S(1)}, s16[1040,128]{1,0:T(8,128)(2,1)S(1)}, u32[]{:S(2)}, u32[]{:S(2)}) collective-permute-start(s16[1040,128]{1,0:T(8,128)(2,1)S(1)} %get-tuple-element.103), channel_id=1, source_target_pairs={{0,16},{4,20},{8,24},{12,28},{16,0},{20,4},{24,8},{28,12},{1,17},{... | collective-permute-start | bytes 798728 | tf_op jit(solution)/shard_map/ppermute | solution.py:25
  162.4 20.0 %collective-permute-start.32 = (s16[1040,128]{1,0:T(8,128)(2,1)S(1)}, s16[1040,128]{1,0:T(8,128)(2,1)S(1)}, u32[]{:S(2)}, u32[]{:S(2)}) collective-permute-start(s16[1040,128]{1,0:T(8,128)(2,1)S(1)} %get-tuple-element.104), channel_id=1, source_target_pairs={{0,24},{4,28},{8,16},{12,20},{16,8},{20,12},{24,0},{28,4},{1,25},{... | collective-permute-start | bytes 798728 | tf_op jit(solution)/shard_map/ppermute | solution.py:25
  164.8 18.9 %collective-permute-start.30 = (s16[1040,128]{1,0:T(8,128)(2,1)S(1)}, s16[1040,128]{1,0:T(8,128)(2,1)S(1)}, u32[]{:S(2)}, u32[]{:S(2)}) collective-permute-start(s16[1040,128]{1,0:T(8,128)(2,1)S(1)} %get-tuple-element.102), channel_id=1, source_target_pairs={{0,8},{4,12},{8,0},{12,4},{16,24},{20,28},{24,16},{28,20},{1,9},{5... | collective-permute-start | bytes 798728 | tf_op jit(solution)/shard_map/ppermute | solution.py:25
  191.2 21.6 %collective-permute-start.34 = (s16[1040,128]{1,0:T(8,128)(2,1)S(1)}, s16[1040,128]{1,0:T(8,128)(2,1)S(1)}, u32[]{:S(2)}, u32[]{:S(2)}) collective-permute-start(s16[1040,128]{1,0:T(8,128)(2,1)S(1)} %get-tuple-element.110), channel_id=1, source_target_pairs={{0,16},{4,20},{8,24},{12,28},{16,0},{20,4},{24,8},{28,12},{1,17},{... | collective-permute-start | bytes 798728 | tf_op jit(solution)/shard_map/ppermute | solution.py:25
  191.3 21.5 %collective-permute-start.35 = (s16[1040,128]{1,0:T(8,128)(2,1)S(1)}, s16[1040,128]{1,0:T(8,128)(2,1)S(1)}, u32[]{:S(2)}, u32[]{:S(2)}) collective-permute-start(s16[1040,128]{1,0:T(8,128)(2,1)S(1)} %get-tuple-element.111), channel_id=1, source_target_pairs={{0,24},{4,28},{8,16},{12,20},{16,8},{20,12},{24,0},{28,4},{1,25},{... | collective-permute-start | bytes 798728 | tf_op jit(solution)/shard_map/ppermute | solution.py:25
  194.1 26.1 %collective-permute-start.39 = (s16[528,128]{1,0:T(8,128)(2,1)S(1)}, s16[528,128]{1,0:T(8,128)(2,1)S(1)}, u32[]{:S(2)}, u32[]{:S(2)}) collective-permute-start(s16[528,128]{1,0:T(8,128)(2,1)S(1)} %get-tuple-element.119), channel_id=1, source_target_pairs={{0,4},{4,0},{8,12},{12,8},{16,20},{20,16},{24,28},{28,24},{1,5},{5... | collective-permute-start | bytes 405512 | tf_op jit(solution)/shard_map/ppermute | solution.py:25
  219.7 22.6 %collective-permute-start.36 = (s16[1040,128]{1,0:T(8,128)(2,1)S(1)}, s16[1040,128]{1,0:T(8,128)(2,1)S(1)}, u32[]{:S(2)}, u32[]{:S(2)}) collective-permute-start(s16[1040,128]{1,0:T(8,128)(2,1)S(1)} %get-tuple-element.124.refs_0_), channel_id=1, source_target_pairs={{0,16},{4,20},{8,24},{12,28},{16,0},{20,4},{24,8},{28,12},{1,17},{... | collective-permute-start | bytes 798728 | tf_op jit(solution)/shard_map/ppermute | solution.py:25
  229.5 36.8 %collective-permute-start.47 = (s16[2,1040,128]{2,1,0:T(8,128)(2,1)S(1)}, s16[2,1040,128]{2,1,0:T(8,128)(2,1)S(1)}, u32[]{:S(2)}, u32[]{:S(2)}) collective-permute-start(s16[2,1040,128]{2,1,0:T(8,128)(2,1)S(1)} %pad_add_fusion), channel_id=1, source_target_pairs={{0,4},{4,0},{8,12},{12,8},{16,20},{20,16},{24,28},{28,24},{1,5},{5... | collective-permute-start | bytes 1597448 | tf_op jit(solution)/shard_map/ppermute | solution.py:25
  242.4 23.9 %collective-permute-start.48 = (s16[2,1040,128]{2,1,0:T(8,128)(2,1)S(1)}, s16[2,1040,128]{2,1,0:T(8,128)(2,1)S(1)}, u32[]{:S(2)}, u32[]{:S(2)}) collective-permute-start(s16[2,1040,128]{2,1,0:T(8,128)(2,1)S(1)} %pad_add_fusion.1), channel_id=1, source_target_pairs={{0,4},{4,0},{8,12},{12,8},{16,20},{20,16},{24,28},{28,24},{1,5},{5... | collective-permute-start | bytes 1597448 | tf_op jit(solution)/shard_map/ppermute | solution.py:25
  250.5 21.3 %collective-permute-start.51 = (s16[2,528,128]{2,1,0:T(8,128)(2,1)S(1)}, s16[2,528,128]{2,1,0:T(8,128)(2,1)S(1)}, u32[]{:S(2)}, u32[]{:S(2)}) collective-permute-start(s16[2,528,128]{2,1,0:T(8,128)(2,1)S(1)} %pad_add_fusion.2.refs_1_), channel_id=1, source_target_pairs={{0,24},{4,28},{8,16},{12,20},{16,8},{20,12},{24,0},{28,4},{1,25},{... | collective-permute-start | bytes 811016 | tf_op jit(solution)/shard_map/ppermute | solution.py:25
  (33 other events, 287.9 us)
